TPU v7x, 32 devices: a whole 2x2x4 slice. The times are simulated.
32 devices in a mesh: ctx: 8 (over y, x, core), exp: 4 (over z).
Axes of the slice: x: 2, y: 2, z: 4, core: 2. Of those that a mesh axis runs over, the one named last changes fastest.
Arguments:
- tokens: bfloat16 [4, 4096, 1024], P(None, ('ctx', 'exp')), may hold values from -6 to 6
- doc_lengths: int32 [4, 8], replicated, may hold values from 0 to 4096, as said below
- routes: int32 [4, 4096, 2], P(None, ('ctx', 'exp')), may hold values from 0 to 3, all different within a row
- priority: int32 [4, 4096], P(None, ('ctx', 'exp')), may hold values from 0 to 511, as said below
- norm1_gain: bfloat16 [1024], replicated, may hold values from 0.099609375 to 1.8984375
- w_query: bfloat16 [1024, 1024], replicated, may hold values from -0.1875 to 0.1875
- w_key: bfloat16 [1024, 1024], replicated, may hold values from -0.1875 to 0.1875
- w_value: bfloat16 [1024, 1024], replicated, may hold values from -0.1875 to 0.1875
- w_out: bfloat16 [1024, 1024], replicated, may hold values from -1.5 to 1.5
- bias_table: bfloat16 [512], replicated, may hold values from -4 to 4
- norm2_gain: bfloat16 [1024], replicated, may hold values from 0.099609375 to 1.8984375
- w_router: bfloat16 [1024, 4], replicated, may hold values from -0.125 to 0.125
- w_gate: bfloat16 [4, 1024, 2816], P('exp'), may hold values from -0.1875 to 0.1875
- w_up: bfloat16 [4, 1024, 2816], P('exp'), may hold values from -0.1875 to 0.1875
- w_down: bfloat16 [4, 2816, 1024], P('exp'), may hold values from -0.3125 to 0.3125
- cotangent: bfloat16 [4, 4096, 1024], P(None, ('ctx', 'exp')), may hold values from -6 to 6
Outputs:
- mixed: bfloat16 [4, 4096, 1024], P(None, ('ctx', 'exp'))
- grad_tokens: bfloat16 [4, 4096, 1024], P(None, ('ctx', 'exp'))
- grad_norm1: float32 [1024], P(('ctx', 'exp'))
- grad_query: float32 [1024, 1024], P(('ctx', 'exp'))
- grad_key: float32 [1024, 1024], P(('ctx', 'exp'))
- grad_value: float32 [1024, 1024], P(('ctx', 'exp'))
- grad_out: float32 [1024, 1024], P(('ctx', 'exp'))
- grad_table: float32 [512], P(('ctx', 'exp'))
- grad_norm2: float32 [1024], P(('ctx', 'exp'))
- grad_router: float32 [1024, 4], P(('ctx', 'exp'))
- grad_gate: float32 [4, 1024, 2816], P('exp', 'ctx')
- grad_up: float32 [4, 1024, 2816], P('exp', 'ctx')
- grad_down: float32 [4, 2816, 1024], P('exp', 'ctx')
Inputs may be any that keep to these rules, and one draw needn't show every extreme that they name: `doc_lengths`: the lengths of each sequence sum to 4096; trailing lengths may be zero; one sequence, chosen by the seed, is a single document. `priority`: within each group of positions g * 128 to (g + 1) * 128 - 1 of all sequences, every value appears exactly once. `routes`: the two experts of a position differ.
All inputs are finite; a program needn't handle non-finite values.
Results may differ from a plain program's by a relative error of at most 0.02.
Values may be sent and summed in bfloat16 or wider, within the bound.
No kernel may reach another device: no remote copies, remote signals or barrier semaphores. Data moves between devices by JAX's collectives and lax.ppermute only.
A program may use at most 320 MiB of HBM per device.

v0:
```python
import jax
import jax.numpy as jnp
import numpy as np
from jax import lax
from jax.sharding import PartitionSpec as P

WINDOW = 1024


epsilon = 1e-06
bucket_total = 32
heads_group = 4


def from_behind(x, axis, by):
    count = lax.axis_size(axis)
    pairs = [(i, i + by) for i in range(count) if 0 <= i + by < count]
    return lax.ppermute(x, axis, pairs)


def bucket_of(distance):
    limits = np.ceil(16.0 * 8.0 ** (np.arange(1, 16) / 16.0)).astype(np.int32)
    above = jnp.sum((distance[..., None] >= jnp.asarray(limits)).astype(jnp.int32), axis=-1)
    return jnp.where(distance < 16, distance, 16 + above)


def norm_rows(values, gain):
    return values * lax.rsqrt(jnp.mean(values * values, axis=-1, keepdims=True) + epsilon) * gain


def group_places(route_rows, priority_rows, experts):
    count = priority_rows.shape[0]
    inverse = (
        jnp.zeros((count,), jnp.int32).at[priority_rows].set(jnp.arange(count, dtype=jnp.int32))
    )
    ordered = jnp.concatenate([route_rows[inverse, 0], route_rows[inverse, 1]])
    onehot = (ordered[:, None] == jnp.arange(experts, dtype=jnp.int32)[None, :]).astype(jnp.int32)
    earlier = jnp.cumsum(onehot, axis=0) - onehot
    ranked = jnp.sum(earlier * onehot, axis=1)
    return jnp.stack([ranked[priority_rows], ranked[count + priority_rows]], axis=1)


def activate(gate_pre, up_pre):
    return jax.nn.gelu(gate_pre) * up_pre


def matmul(left, right):
    return jnp.dot(left, right, preferred_element_type=jnp.float32)


def exact_matmul(left, right):
    return jnp.dot(left, right, precision=lax.Precision.HIGHEST, preferred_element_type=jnp.float32)


def on_device(
    tokens,
    doc_lengths,
    routes,
    priority,
    norm1_gain,
    w_query,
    w_key,
    w_value,
    w_out,
    bias_table,
    norm2_gain,
    w_router,
    w_gate,
    w_up,
    w_down,
    cotangent,
):
    seqs, piece_len, model_width = tokens.shape
    exp_count = lax.axis_size("exp")
    block_len = piece_len * exp_count
    window_len = 3 * block_len
    head_count = bias_table.shape[0] // bucket_total
    head_size = model_width // head_count
    group_count = head_count // heads_group
    scale = head_size ** (-0.5)
    ctx_index = lax.axis_index("ctx")
    exp_index = lax.axis_index("exp")
    first_pos = (ctx_index * exp_count + exp_index) * piece_len
    row_count = seqs * piece_len
    x_rows = tokens.reshape(row_count, model_width).astype(jnp.float32)
    gain_one = norm1_gain.astype(jnp.float32)
    normed = norm_rows(x_rows, gain_one).astype(jnp.bfloat16)
    query_rows = matmul(normed, w_query).astype(jnp.bfloat16)
    key_rows = matmul(normed, w_key).astype(jnp.bfloat16)
    value_rows = matmul(normed, w_value).astype(jnp.bfloat16)
    kv_piece = jnp.concatenate([key_rows, value_rows], axis=1).reshape(
        seqs, piece_len, 2 * model_width
    )
    kv_block = lax.all_gather(kv_piece, "exp", axis=1, tiled=True)
    earlier = []
    for back_by in (2, 1):
        earlier.append(from_behind(kv_block, "ctx", back_by))
    kv_window = jnp.concatenate(earlier + [kv_block], axis=1)
    q_pos = first_pos + jnp.arange(piece_len, dtype=jnp.int32)
    k_pos = (ctx_index - 2) * block_len + jnp.arange(window_len, dtype=jnp.int32)
    ends = jnp.cumsum(doc_lengths, axis=1)
    q_doc = jnp.sum((q_pos[None, :, None] >= ends[:, None, :]).astype(jnp.int32), axis=2)
    k_doc = jnp.sum((k_pos[None, :, None] >= ends[:, None, :]).astype(jnp.int32), axis=2)
    distance = q_pos[:, None] - k_pos[None, :]
    allowed = (distance >= 0) & (distance < WINDOW) & (k_pos[None, :] >= 0)
    allowed = allowed[None] & (q_doc[:, :, None] == k_doc[:, None, :])
    onehot = (bucket_of(distance)[..., None] == jnp.arange(bucket_total, dtype=jnp.int32)).astype(
        jnp.bfloat16
    )
    bias = jnp.einsum(
        "qkb,hb->hqk",
        onehot,
        bias_table.reshape(head_count, bucket_total),
        preferred_element_type=jnp.float32,
    )
    bias_grouped = bias.reshape(group_count, heads_group, piece_len, window_len)
    query_grouped = query_rows.reshape(
        seqs, piece_len, group_count, heads_group, head_size
    ).transpose(2, 0, 1, 3, 4)
    key_grouped = (
        kv_window[..., :model_width]
        .reshape(seqs, window_len, group_count, heads_group, head_size)
        .transpose(2, 0, 1, 3, 4)
    )
    value_grouped = (
        kv_window[..., model_width:]
        .reshape(seqs, window_len, group_count, heads_group, head_size)
        .transpose(2, 0, 1, 3, 4)
    )

    def scores_of(query_g, key_g, bias_g):
        scores = (
            jnp.einsum("sqhd,skhd->shqk", query_g, key_g, preferred_element_type=jnp.float32)
            * scale
            + bias_g[None]
        )
        return jnp.where(allowed[:, None], scores, -1e30)

    def forward_group(parts):
        query_g, key_g, value_g, bias_g = parts
        scores = scores_of(query_g, key_g, bias_g)
        row_max = jnp.max(scores, axis=-1, keepdims=True)
        exponent = jnp.exp(scores - row_max)
        row_sum = jnp.sum(exponent, axis=-1, keepdims=True)
        probs = (exponent / row_sum).astype(jnp.bfloat16)
        context = jnp.einsum("shqk,skhd->sqhd", probs, value_g, preferred_element_type=jnp.float32)
        return (context.astype(jnp.bfloat16), (row_max + jnp.log(row_sum))[..., 0])

    context_grouped, log_totals = lax.map(
        forward_group, (query_grouped, key_grouped, value_grouped, bias_grouped)
    )
    context_rows = context_grouped.transpose(1, 2, 0, 3, 4).reshape(row_count, model_width)
    h_rows = x_rows + matmul(context_rows, w_out)
    gain_two = norm2_gain.astype(jnp.float32)
    moe_in = norm_rows(h_rows, gain_two).astype(jnp.bfloat16)
    experts = w_router.shape[1]
    router_probs = jax.nn.softmax(matmul(moe_in, w_router), axis=-1)
    route_rows = routes.reshape(row_count, 2)
    route_hot = (route_rows[..., None] == jnp.arange(experts, dtype=jnp.int32)).astype(jnp.float32)
    gates = jnp.sum(router_probs[:, None, :] * route_hot, axis=-1)
    places = group_places(route_rows, priority.reshape(row_count), experts)
    slot_size = 5 * row_count // (2 * experts)
    kept = places < slot_size
    keep_weight = kept.astype(jnp.float32)
    target = jnp.where(kept, route_rows * slot_size + places, experts * slot_size)
    assign = (
        jnp.full((experts * slot_size,), 2 * row_count, jnp.int32)
        .at[target.reshape(-1)]
        .set(jnp.arange(2 * row_count, dtype=jnp.int32), mode="drop")
    )
    slot_token = jnp.where(assign < 2 * row_count, assign // 2, row_count)
    gate_pad = jnp.concatenate([(gates * keep_weight).reshape(-1), jnp.zeros((1,), jnp.float32)])
    slot_gate = gate_pad[assign]
    pick = jnp.where(kept, target, 0)
    moe_pad = jnp.concatenate([moe_in, jnp.zeros((1, model_width), jnp.bfloat16)], axis=0)
    send_rows = moe_pad[slot_token].reshape(experts, slot_size, model_width)
    received = lax.all_to_all(send_rows, "exp", split_axis=0, concat_axis=0, tiled=True)
    sources = received.shape[0]
    count = received.shape[1]
    inputs = received.reshape(-1, model_width)
    gate_pre = matmul(inputs, w_gate[0])
    up_pre = matmul(inputs, w_up[0])
    activation = activate(gate_pre, up_pre).astype(jnp.bfloat16)
    produced = (
        matmul(activation, w_down[0]).astype(jnp.bfloat16).reshape(sources, count, model_width)
    )
    back = lax.all_to_all(produced, "exp", split_axis=0, concat_axis=0, tiled=True)
    chosen = back.reshape(experts * slot_size, model_width)[pick]
    mix = jnp.sum((gates * keep_weight)[..., None] * chosen.astype(jnp.float32), axis=1)
    mixed = (h_rows + mix).astype(jnp.bfloat16).reshape(seqs, piece_len, model_width)
    grad_y = cotangent.reshape(row_count, model_width).astype(jnp.float32)
    grad_gates = keep_weight * jnp.sum(grad_y[:, None, :] * chosen.astype(jnp.float32), axis=-1)
    grad_pad = jnp.concatenate([grad_y, jnp.zeros((1, model_width), jnp.float32)], axis=0)
    grad_send = (
        (slot_gate[:, None] * grad_pad[slot_token])
        .astype(jnp.bfloat16)
        .reshape(experts, slot_size, model_width)
    )
    grad_received = lax.all_to_all(
        grad_send, "exp", split_axis=0, concat_axis=0, tiled=True
    ).reshape(-1, model_width)
    inputs = received.reshape(-1, model_width)
    gate_pre = matmul(inputs, w_gate[0])
    up_pre = matmul(inputs, w_up[0])
    activation, activation_back = jax.vjp(activate, gate_pre, up_pre)
    activation_low = activation.astype(jnp.bfloat16)
    grad_activation = matmul(grad_received, w_down[0].T)
    grad_down_local = matmul(activation_low.T, grad_received)
    grad_gate_pre, grad_up_pre = activation_back(grad_activation)
    grad_gate_low = grad_gate_pre.astype(jnp.bfloat16)
    grad_up_low = grad_up_pre.astype(jnp.bfloat16)
    grad_gate_local = matmul(inputs.T, grad_gate_low)
    grad_up_local = matmul(inputs.T, grad_up_low)
    grad_inputs = (matmul(grad_gate_low, w_gate[0].T) + matmul(grad_up_low, w_up[0].T)).astype(
        jnp.bfloat16
    )
    grad_inputs = grad_inputs.reshape(exp_count, slot_size, model_width)
    grad_back = lax.all_to_all(grad_inputs, "exp", split_axis=0, concat_axis=0, tiled=True).reshape(
        experts * slot_size, model_width
    )
    grad_moe = jnp.sum(keep_weight[..., None] * grad_back[pick].astype(jnp.float32), axis=1)
    grad_choice = jnp.sum(grad_gates[..., None] * route_hot, axis=1)
    grad_logits = router_probs * (
        grad_choice - jnp.sum(router_probs * grad_choice, axis=-1, keepdims=True)
    )
    grad_router_local = exact_matmul(moe_in.astype(jnp.float32).T, grad_logits)
    grad_moe = grad_moe + exact_matmul(grad_logits, w_router.astype(jnp.float32).T)
    norm_two_out, norm_two_back = jax.vjp(norm_rows, h_rows, gain_two)
    grad_hidden_norm, grad_gain_two = norm_two_back(grad_moe)
    grad_hidden = grad_y + grad_hidden_norm
    grad_attn = grad_hidden.astype(jnp.bfloat16)
    grad_out_local = matmul(context_rows.T, grad_attn)
    grad_context = matmul(grad_attn, w_out.T).astype(jnp.bfloat16)
    grad_context_grouped = grad_context.reshape(
        seqs, piece_len, group_count, heads_group, head_size
    ).transpose(2, 0, 1, 3, 4)

    def backward_group(parts):
        query_g, key_g, value_g, bias_g, log_g, grad_g = parts
        scores = scores_of(query_g, key_g, bias_g)
        probs = jnp.exp(scores - log_g[..., None])
        probs_low = probs.astype(jnp.bfloat16)
        grad_probs = jnp.einsum(
            "sqhd,skhd->shqk", grad_g, value_g, preferred_element_type=jnp.float32
        )
        inner = jnp.sum(probs * grad_probs, axis=-1, keepdims=True)
        grad_scores = (probs * (grad_probs - inner)).astype(jnp.bfloat16)
        grad_q = (
            jnp.einsum("shqk,skhd->sqhd", grad_scores, key_g, preferred_element_type=jnp.float32)
            * scale
        )
        grad_k = (
            jnp.einsum("shqk,sqhd->skhd", grad_scores, query_g, preferred_element_type=jnp.float32)
            * scale
        )
        grad_v = jnp.einsum(
            "shqk,sqhd->skhd", probs_low, grad_g, preferred_element_type=jnp.float32
        )
        grad_bias = jnp.einsum(
            "shqk,qkb->hb", grad_scores, onehot, preferred_element_type=jnp.float32
        )
        return (grad_q, grad_k, grad_v, grad_bias)

    grad_q4, grad_k4, grad_v4, grad_table_groups = lax.map(
        backward_group,
        (query_grouped, key_grouped, value_grouped, bias_grouped, log_totals, grad_context_grouped),
    )
    grad_q_low = (
        grad_q4.transpose(1, 2, 0, 3, 4).reshape(row_count, model_width).astype(jnp.bfloat16)
    )
    grad_k_window = grad_k4.transpose(1, 2, 0, 3, 4).reshape(seqs, window_len, model_width)
    grad_v_window = grad_v4.transpose(1, 2, 0, 3, 4).reshape(seqs, window_len, model_width)
    grad_window = jnp.concatenate([grad_k_window, grad_v_window], axis=-1)
    grad_table_local = grad_table_groups.reshape(head_count * bucket_total)
    own_part = grad_window[:, 2 * block_len :]
    for back_by in (2, 1):
        sent_part = grad_window[:, (2 - back_by) * block_len : (3 - back_by) * block_len]
        own_part = own_part + from_behind(sent_part.astype(jnp.bfloat16), "ctx", -back_by).astype(
            sent_part.dtype
        )
    grad_piece = lax.psum_scatter(own_part, "exp", scatter_dimension=1, tiled=True)
    grad_piece = grad_piece.reshape(row_count, 2 * model_width)
    grad_k_low = grad_piece[:, :model_width].astype(jnp.bfloat16)
    grad_v_low = grad_piece[:, model_width:].astype(jnp.bfloat16)
    grad_query_local = matmul(normed.T, grad_q_low)
    grad_key_local = matmul(normed.T, grad_k_low)
    grad_value_local = matmul(normed.T, grad_v_low)
    grad_normed = (
        matmul(grad_q_low, w_query.T) + matmul(grad_k_low, w_key.T) + matmul(grad_v_low, w_value.T)
    )
    norm_one_out, norm_one_back = jax.vjp(norm_rows, x_rows, gain_one)
    grad_x_norm, grad_gain_one = norm_one_back(grad_normed)
    grad_tokens = (
        (grad_hidden + grad_x_norm).astype(jnp.bfloat16).reshape(seqs, piece_len, model_width)
    )
    dense = (
        lax.psum_scatter(grad_gain_one, ("ctx", "exp"), scatter_dimension=0, tiled=True),
        lax.psum_scatter(grad_query_local, ("ctx", "exp"), scatter_dimension=0, tiled=True),
        lax.psum_scatter(grad_key_local, ("ctx", "exp"), scatter_dimension=0, tiled=True),
        lax.psum_scatter(grad_value_local, ("ctx", "exp"), scatter_dimension=0, tiled=True),
        lax.psum_scatter(grad_out_local, ("ctx", "exp"), scatter_dimension=0, tiled=True),
        lax.psum_scatter(grad_table_local, ("ctx", "exp"), scatter_dimension=0, tiled=True),
        lax.psum_scatter(grad_gain_two, ("ctx", "exp"), scatter_dimension=0, tiled=True),
        lax.psum_scatter(grad_router_local, ("ctx", "exp"), scatter_dimension=0, tiled=True),
    )
    expert_sums = (
        lax.psum_scatter(
            grad_gate_local[None].astype(jnp.bfloat16), "ctx", scatter_dimension=1, tiled=True
        ).astype(jnp.float32),
        lax.psum_scatter(
            grad_up_local[None].astype(jnp.bfloat16), "ctx", scatter_dimension=1, tiled=True
        ).astype(jnp.float32),
        lax.psum_scatter(
            grad_down_local[None].astype(jnp.bfloat16), "ctx", scatter_dimension=1, tiled=True
        ).astype(jnp.float32),
    )
    return (
        mixed,
        grad_tokens,
        dense[0],
        dense[1],
        dense[2],
        dense[3],
        dense[4],
        dense[5],
        dense[6],
        dense[7],
        expert_sums[0],
        expert_sums[1],
        expert_sums[2],
    )


def solution(mesh):
    in_specs = (
        P(None, ("ctx", "exp"), None),
        P(),
        P(None, ("ctx", "exp"), None),
        P(None, ("ctx", "exp")),
        P(),
        P(),
        P(),
        P(),
        P(),
        P(),
        P(),
        P(),
        P("exp", None, None),
        P("exp", None, None),
        P("exp", None, None),
        P(None, ("ctx", "exp"), None),
    )
    out_specs = (
        P(None, ("ctx", "exp"), None),
        P(None, ("ctx", "exp"), None),
        P(("ctx", "exp")),
        P(("ctx", "exp"), None),
        P(("ctx", "exp"), None),
        P(("ctx", "exp"), None),
        P(("ctx", "exp"), None),
        P(("ctx", "exp")),
        P(("ctx", "exp")),
        P(("ctx", "exp"), None),
        P("exp", "ctx", None),
        P("exp", "ctx", None),
        P("exp", "ctx", None),
    )
    return jax.shard_map(
        on_device, mesh=mesh, in_specs=in_specs, out_specs=out_specs, check_vma=False
    )
```

profile of v0, /device:TPU:10, one launch (start us, length us, event | category | flops | bytes accessed | tf_op | source)
XLA Modules:
  0.0 2705.8 jit_solution(8604381038129097468)
XLA Ops:
  19.8 147.7 %all-gather.2.cloned.1.call-done = bf16[4,512,2048]{1,2,0:T(8,128)(2,1)} async-done(((bf16[4,128,2048]{1,2,0:T(8,128)(2,1)}), bf16[4,512,2048]{1,2,0:T(8,128)(2,1)}) %all-gather.2.cloned.1.call-update) | async-done | bytes 8388624 | tf_op jit(solution)/shard_map/all_gather | solution.py:94
  212.4 16.3 copy.199
  234.2 118.9 %collective-permute-done = bf16[4,512,2048]{1,2,0:T(8,128)(2,1)} collective-permute-done((bf16[4,512,2048]{1,2,0:T(8,128)(2,1)}, bf16[4,512,2048]{1,2,0:T(8,128)(2,1)}, u32[]{:S(2)}, u32[]{:S(2)}) %collective-permute-start) | collective-permute-done | bytes 8388640 | tf_op jit(solution)/shard_map/ppermute | solution.py:18
  360.4 81.4 %collective-permute-done.1 = bf16[4,512,2048]{1,2,0:T(8,128)(2,1)} collective-permute-done((bf16[4,512,2048]{1,2,0:T(8,128)(2,1)}, bf16[4,512,2048]{1,2,0:T(8,128)(2,1)}, u32[]{:S(2)}, u32[]{:S(2)}) %collective-permute-start.1) | collective-permute-done | bytes 8388640 | tf_op jit(solution)/shard_map/ppermute | solution.py:18
  456.4 10.0 fusion.153
  477.1 110.0 %while.30 = (s32[]{:T(128)}, bf16[4,4,128,4,64]{2,4,3,1,0:T(8,128)(2,1)}, f32[4,4,4,128]{3,2,1,0:T(4,128)}, bf16[4,4,1536,4,64]{2,4,3,1,0:T(8,128)(2,1)}, bf16[4...) while((s32[]{:T(128)}, ...), condition=%wide.region_8.9_spmd.clone, body=%wide.region_5.8_spmd.clone.sunk | while | flops 854194176 | bytes 114061456 | solution.py:149
  493.3 10.7 fusion.207
  520.8 10.7 fusion.207
  548.3 10.7 fusion.207
  575.9 10.7 fusion.207
  631.4 33.2 %all-to-all-done = bf16[4,320,1024]{2,1,0:T(8,128)(2,1)} async-done(((bf16[4,320,1024]{2,1,0:T(8,128)(2,1)}), bf16[4,320,1024]{2,1,0:T(8,128)(2,1)}, u32[]{:S(2)}, u32[]{:S(2)}) %all-to-all-start) | async-done | bytes 2621472 | tf_op jit(solution)/shard_map/all_to_all | solution.py:177
  672.5 13.8 fusion.88
  686.3 41.8 %all-to-all-done.2 = bf16[4,320,1024]{2,1,0:T(8,128)(2,1)} async-done(((bf16[4,320,1024]{2,1,0:T(8,128)(2,1)}), bf16[4,320,1024]{2,1,0:T(8,128)(2,1)}, u32[]{:S(2)}, u32[]{:S(2)}) %all-to-all-start.2) | async-done | bytes 2621472 | tf_op jit(solution)/shard_map/all_to_all | solution.py:199
  728.2 13.8 fusion.82
  742.0 26.9 fusion.79
  768.9 13.0 fusion.96
  789.7 11.6 fusion.86
  801.3 12.7 add_convert_fusion
  814.0 31.3 %all-to-all-done.1 = bf16[4,320,1024]{2,1,0:T(8,128)(2,1)} async-done(((bf16[4,320,1024]{2,1,0:T(8,128)(2,1)}), bf16[4,320,1024]{2,1,0:T(8,128)(2,1)}, u32[]{:S(2)}, u32[]{:S(2)}) %all-to-all-start.1) | async-done | bytes 2621472 | tf_op jit(solution)/shard_map/all_to_all | solution.py:187
  871.4 10.5 multiply_reduce_fusion.1
  882.1 26.8 all-to-all-done.3
  940.6 245.3 %while.31 = (s32[]{:T(128)}, bf16[4,4,128,4,64]{2,4,3,1,0:T(8,128)(2,1)}, f32[4,4,1536,4,64]{2,4,3,0,1:T(8,128)}, f32[4,4,1536,4,64]{2,4,3,0,1:T(8,128)}, f32[4,...) while((s32[]{:T(128)}, ...), condition=%wide.region_27.28_spmd.clone, body=%wide.region_24.27_spmd.clone.sunk | while | flops 2116417536 | bytes 259530032 | solution.py:264
  955.2 9.4 multiply_reduce_fusion.9
  964.6 13.6 convert_reduce_fusion.5
  1016.4 9.3 multiply_reduce_fusion.9
  1025.7 13.6 convert_reduce_fusion.5
  1077.6 9.4 multiply_reduce_fusion.9
  1087.1 13.6 convert_reduce_fusion.5
  1138.9 9.5 multiply_reduce_fusion.9
  1148.3 13.6 convert_reduce_fusion.5
  1185.9 25.3 fusion.68
  1211.2 9.2 fusion.152
  1224.3 179.6 %collective-permute-done.2 = bf16[4,512,2048]{1,2,0:T(8,128)(2,1)S(1)} collective-permute-done((bf16[4,512,2048]{1,2,0:T(8,128)(2,1)}, bf16[4,512,2048]{1,2,0:T(8,128)(2,1)S(1)}, u32[]{:S(2)}, u32[]{:S(2)}) %collective-permute-start.2) | collective-permute-done | bytes 8388640 | tf_op jit(solution)/shard_map/ppermute | solution.py:18
  1404.0 86.8 %collective-permute-done.3 = bf16[4,512,2048]{1,2,0:T(8,128)(2,1)S(1)} collective-permute-done((bf16[4,512,2048]{1,2,0:T(8,128)(2,1)S(1)}, bf16[4,512,2048]{1,2,0:T(8,128)(2,1)S(1)}, u32[]{:S(2)}, u32[]{:S(2)}) %collective-permute-start.3) | collective-permute-done | bytes 8388640 | tf_op jit(solution)/shard_map/ppermute | solution.py:18
  1490.8 12.5 fusion.72
  1506.6 12.4 convert_bitcast_fusion
  1519.0 13.1 convert_bitcast_fusion.2
  1532.2 13.0 convert_bitcast_fusion.1
  1557.4 227.1 %reduce-scatter.12.cloned.1.call-done = f32[4,128,2048]{1,2,0:T(8,128)} async-done(((f32[4,512,2048]{1,2,0:T(8,128)}), f32[4,128,2048]{1,2,0:T(8,128)}) %reduce-scatter.12.cloned.1.call-update) | async-done | bytes 4194320 | tf_op jit(solution)/shard_map/reduce_scatter | solution.py:281
  1806.8 105.8 %reduce-scatter.28.cloned.1.call-done = f32[32,4]{1,0:T(8,128)} async-done(((f32[1024,4]{1,0:T(8,128)}), f32[32,4]{1,0:T(8,128)}) %reduce-scatter.28.cloned.1.call-update) | async-done | bytes 528
  1914.0 69.7 %reduce-scatter.26.cloned.1.call-done = bf16[1,352,1024]{2,1,0:T(8,128)(2,1)} async-done(((bf16[1,2816,1024]{2,1,0:T(8,128)(2,1)}), bf16[1,352,1024]{2,1,0:T(8,128)(2,1)}) %reduce-scatter.26.cloned.1.call-update) | async-done | bytes 720912 | tf_op jit(solution)/shard_map/reduce_scatter | solution.py:313
  1986.1 60.4 %reduce-scatter.22.cloned.1.call-done = bf16[1,128,2816]{2,1,0:T(8,128)(2,1)} async-done(((bf16[1,1024,2816]{2,1,0:T(8,128)(2,1)}), bf16[1,128,2816]{2,1,0:T(8,128)(2,1)}) %reduce-scatter.22.cloned.1.call-update) | async-done | bytes 720912 | tf_op jit(solution)/shard_map/reduce_scatter | solution.py:307
  2048.8 60.1 %reduce-scatter.24.cloned.1.call-done = bf16[1,128,2816]{2,1,0:T(8,128)(2,1)} async-done(((bf16[1,1024,2816]{2,1,0:T(8,128)(2,1)}), bf16[1,128,2816]{2,1,0:T(8,128)(2,1)}) %reduce-scatter.24.cloned.1.call-update) | async-done | bytes 720912 | tf_op jit(solution)/shard_map/reduce_scatter | solution.py:310
  2117.6 41.2 %all-reduce.7 = (f32[1024]{0:T(1024)S(1)}, f32[512]{0:T(512)S(1)}, f32[1024]{0:T(1024)S(1)}) all-reduce(f32[1024]{0:T(1024)S(1)} %get-tuple-element.348, f32[512]{0:T(512)S(1)} %reshape.632, f32[1024]{0:T(1024)S(1)} %copy-done.57), channel_id=3, replica_groups=mesh['ctx'=8,'exp'=4] {'ctx','exp'}, use_global_device_ids=true, to_apply=%region_31.32.clone | all-reduce | flops 2560 | bytes 20480
  2164.3 85.9 %reduce-scatter.20.cloned.1.call-done = f32[32,1024]{1,0:T(8,128)} async-done(((f32[1024,1024]{1,0:T(8,128)}), f32[32,1024]{1,0:T(8,128)}) %reduce-scatter.20.cloned.1.call-update) | async-done | bytes 131088 | tf_op jit(solution)/shard_map/reduce_scatter | solution.py:301
  2250.3 149.5 %reduce-scatter.14.cloned.1.call-done = f32[32,1024]{1,0:T(8,128)} async-done(((f32[1024,1024]{1,0:T(8,128)}), f32[32,1024]{1,0:T(8,128)}) %reduce-scatter.14.cloned.1.call-update) | async-done | bytes 131088 | tf_op jit(solution)/shard_map/reduce_scatter | solution.py:298
  2399.8 148.9 %reduce-scatter.16.cloned.1.call-done = f32[32,1024]{1,0:T(8,128)} async-done(((f32[1024,1024]{1,0:T(8,128)}), f32[32,1024]{1,0:T(8,128)}) %reduce-scatter.16.cloned.1.call-update) | async-done | bytes 131088 | tf_op jit(solution)/shard_map/reduce_scatter | solution.py:299
  2548.7 150.0 %reduce-scatter.18.cloned.1.call-done = f32[32,1024]{1,0:T(8,128)} async-done(((f32[1024,1024]{1,0:T(8,128)}), f32[32,1024]{1,0:T(8,128)}) %reduce-scatter.18.cloned.1.call-update) | async-done | bytes 131088 | tf_op jit(solution)/shard_map/reduce_scatter | solution.py:300
  (392 shorter events, 494.3 us)
Async XLA Ops:
  7.2 160.3 %all-gather.2.cloned.1.call-start = ((), (), s32[]{:S(2)}) async-start(), calls=%async_computation.13 | async-start | bytes 10485760 | tf_op jit(solution)/shard_map/all_gather | solution.py:94
  11.7 182.4 %copy-start.18 = (bf16[512,1024]{1,0:T(8,128)(2,1)}, bf16[512,1024]{1,0:T(8,128)(2,1)S(1)}, u32[]{:S(2)}) copy-start(bf16[512,1024]{1,0:T(8,128)(2,1)S(1)} %fusion.104) | copy-start | bytes 3145732
  14.3 158.6 %copy-start.60 = (s32[4,8]{1,0:T(4,128)S(1)}, s32[4,8]{1,0:T(4,128)}, u32[]{:S(2)}) copy-start(s32[4,8]{1,0:T(4,128)} %param.22) | copy-start | bytes 388
  14.3 158.7 %copy-start.59 = (bf16[1024]{0:T(1024)(128)(2,1)S(1)}, bf16[1024]{0:T(1024)(128)(2,1)}, u32[]{:S(2)}) copy-start(bf16[1024]{0:T(1024)(128)(2,1)} %param.31) | copy-start | bytes 6148
  14.3 159.3 %copy-start.62 = (bf16[512]{0:T(512)(128)(2,1)S(1)}, bf16[512]{0:T(512)(128)(2,1)}, u32[]{:S(2)}) copy-start(bf16[512]{0:T(512)(128)(2,1)} %param.30) | copy-start | bytes 3076
  14.3 159.4 %copy-start.61 = (s32[4,128]{1,0:T(4,128)S(1)}, s32[4,128]{1,0:T(4,128)}, u32[]{:S(2)}) copy-start(s32[4,128]{1,0:T(4,128)} %param.24) | copy-start | bytes 6148
  14.4 161.9 %copy-start.1 = (s32[4,128,2]{1,2,0:T(2,128)S(1)}, s32[4,128,2]{1,2,0:T(2,128)}, u32[]{:S(2)}) copy-start(s32[4,128,2]{1,2,0:T(2,128)} %param.23) | copy-start | bytes 12292
  167.5 185.5 %collective-permute-start = (bf16[4,512,2048]{1,2,0:T(8,128)(2,1)}, bf16[4,512,2048]{1,2,0:T(8,128)(2,1)}, u32[]{:S(2)}, u32[]{:S(2)}) collective-permute-start(bf16[4,512,2048]{1,2,0:T(8,128)(2,1)} %all-gather.2.cloned.1.call-done), channel_id=1, source_target_pairs={{0,8},{4,12},{8,16},{12,20},{16,24},{20,28},{1,9},{5,13},{9,17},{1... | collective-permute-start | bytes 25165832 | tf_op jit(solution)/shard_map/ppermute | solution.py:18
  170.9 270.9 %collective-permute-start.1 = (bf16[4,512,2048]{1,2,0:T(8,128)(2,1)}, bf16[4,512,2048]{1,2,0:T(8,128)(2,1)}, u32[]{:S(2)}, u32[]{:S(2)}) collective-permute-start(bf16[4,512,2048]{1,2,0:T(8,128)(2,1)} %all-gather.2.cloned.1.call-done), channel_id=1, source_target_pairs={{0,4},{4,8},{8,12},{12,16},{16,20},{20,24},{24,28},{1,5},{5,9},{9,... | collective-permute-start | bytes 25165832 | tf_op jit(solution)/shard_map/ppermute | solution.py:18
  477.1 112.3 %copy-start.6 = (bf16[4,128,1024]{2,1,0:T(8,128)(2,1)S(1)}, bf16[4,128,1024]{2,1,0:T(8,128)(2,1)}, u32[]{:S(2)}) copy-start(bf16[4,128,1024]{2,1,0:T(8,128)(2,1)} %param.21) | copy-start | bytes 3145732
  600.6 64.0 %all-to-all-start = ((bf16[4,320,1024]{2,1,0:T(8,128)(2,1)}), bf16[4,320,1024]{2,1,0:T(8,128)(2,1)}, u32[]{:S(2)}, u32[]{:S(2)}) async-start(bf16[4,320,1024]{2,1,0:T(8,128)(2,1)} %bitcast.331), calls=%async_computation | async-start | bytes 5242880 | tf_op jit(solution)/shard_map/all_to_all | solution.py:177
  619.5 310.9 %copy-start.32 = (f32[512,4]{0,1:T(4,128)}, f32[512,4]{0,1:T(4,128)S(1)}, u32[]{:S(2)}) copy-start(f32[512,4]{0,1:T(4,128)S(1)} %fusion.139) | copy-start | bytes 24580
  664.6 63.5 %all-to-all-start.2 = ((bf16[4,320,1024]{2,1,0:T(8,128)(2,1)}), bf16[4,320,1024]{2,1,0:T(8,128)(2,1)}, u32[]{:S(2)}, u32[]{:S(2)}) async-start(bf16[4,320,1024]{2,1,0:T(8,128)(2,1)} %multiply_convert_fusion.3), calls=%async_computation.2 | async-start | bytes 5242880 | tf_op jit(solution)/shard_map/all_to_all | solution.py:199
  781.8 63.5 %all-to-all-start.1 = ((bf16[4,320,1024]{2,1,0:T(8,128)(2,1)}), bf16[4,320,1024]{2,1,0:T(8,128)(2,1)}, u32[]{:S(2)}, u32[]{:S(2)}) async-start(bf16[4,320,1024]{2,1,0:T(8,128)(2,1)} %bitcast.338), calls=%async_computation.1 | async-start | bytes 5242880 | tf_op jit(solution)/shard_map/all_to_all | solution.py:187
  814.0 39.2 %copy-start.20 = (s32[128,1536]{1,0:T(8,128)S(1)}, s32[128,1536]{1,0:T(8,128)}, u32[]{:S(2)}) copy-start(s32[128,1536]{1,0:T(8,128)} %copy-done.19) | copy-start | bytes 2359300
  814.0 43.4 %copy-start.58 = (s32[512,2,1]{0,1,2:T(2,128)S(1)}, s32[512,2,1]{0,1,2:T(2,128)}, u32[]{:S(2)}) copy-start(s32[512,2,1]{0,1,2:T(2,128)} %get-tuple-element.420) | copy-start | bytes 12292
  845.4 63.5 %all-to-all-start.3 = ((bf16[4,320,1024]{2,1,0:T(8,128)(2,1)}), bf16[4,320,1024]{2,1,0:T(8,128)(2,1)}, u32[]{:S(2)}, u32[]{:S(2)}) async-start(bf16[4,320,1024]{2,1,0:T(8,128)(2,1)} %bitcast.337), calls=%async_computation.3 | async-start | bytes 5242880 | tf_op jit(solution)/shard_map/all_to_all | solution.py:218
  853.3 931.2 %reduce-scatter.12.cloned.1.call-start = ((), (), s32[]{:S(2)}) async-start(), calls=%async_computation.14 | async-start | bytes 20971520 | tf_op jit(solution)/shard_map/reduce_scatter | solution.py:281
  882.0 48.4 %copy-start.34 = (f32[512,4]{0,1:T(4,128)}, f32[512,4]{0,1:T(4,128)S(1)}, u32[]{:S(2)}) copy-start(f32[512,4]{0,1:T(4,128)S(1)} %select_reduce_fusion) | copy-start | bytes 24580
  882.1 48.4 %copy-start.53 = (f32[512]{0:T(512)}, f32[512]{0:T(512)S(1)}, u32[]{:S(2)}) copy-start(f32[512]{0:T(512)S(1)} %multiply_reduce_fusion.7) | copy-start | bytes 6148
  917.0 13.4 copy-start.44
  917.0 13.4 copy-start.46
  964.6 13.7 copy-start.3
  964.6 17.4 copy-start.29
  982.0 11.8 copy-start.4
  1025.7 13.7 copy-start.3
  1025.7 17.4 copy-start.29
  1043.1 11.8 copy-start.4
  1048.0 10.6 slice-start
  1087.0 13.7 copy-start.3
  1087.1 17.4 copy-start.29
  1104.5 11.8 copy-start.4
  1109.4 10.5 slice-start
  1148.3 13.7 copy-start.3
  1148.3 17.4 copy-start.29
  1165.7 11.8 copy-start.4
  1170.7 10.6 slice-start
  1220.5 183.5 %collective-permute-start.2 = (bf16[4,512,2048]{1,2,0:T(8,128)(2,1)}, bf16[4,512,2048]{1,2,0:T(8,128)(2,1)S(1)}, u32[]{:S(2)}, u32[]{:S(2)}) collective-permute-start(bf16[4,512,2048]{1,2,0:T(8,128)(2,1)} %get-tuple-element.412), channel_id=1, source_target_pairs={{8,0},{12,4},{16,8},{20,12},{24,16},{28,20},{9,1},{13,5},{17,9},{2... | collective-permute-start | bytes 25165832 | tf_op jit(solution)/shard_map/ppermute | solution.py:18
  1222.4 268.4 %collective-permute-start.3 = (bf16[4,512,2048]{1,2,0:T(8,128)(2,1)S(1)}, bf16[4,512,2048]{1,2,0:T(8,128)(2,1)S(1)}, u32[]{:S(2)}, u32[]{:S(2)}) collective-permute-start(bf16[4,512,2048]{1,2,0:T(8,128)(2,1)S(1)} %get-tuple-element.413), channel_id=1, source_target_pairs={{4,0},{8,4},{12,8},{16,12},{20,16},{24,20},{28,24},{5,1},{9,5},{13... | collective-permute-start | bytes 25165832 | tf_op jit(solution)/shard_map/ppermute | solution.py:18
  1503.3 409.4 %reduce-scatter.28.cloned.1.call-start = ((), (), s32[]{:S(2)}) async-start(), calls=%async_computation.22 | async-start | bytes 540672
  1506.5 477.2 %reduce-scatter.26.cloned.1.call-start = ((), (), s32[]{:S(2)}) async-start(), calls=%async_computation.21 | async-start | bytes 6488064 | tf_op jit(solution)/shard_map/reduce_scatter | solution.py:313
  1519.0 527.5 %reduce-scatter.22.cloned.1.call-start = ((), (), s32[]{:S(2)}) async-start(), calls=%async_computation.19 | async-start | bytes 6488064 | tf_op jit(solution)/shard_map/reduce_scatter | solution.py:307
  1532.2 576.6 %reduce-scatter.24.cloned.1.call-start = ((), (), s32[]{:S(2)}) async-start(), calls=%async_computation.20 | async-start | bytes 6488064 | tf_op jit(solution)/shard_map/reduce_scatter | solution.py:310
  1545.3 705.0 %reduce-scatter.20.cloned.1.call-start = ((), (), s32[]{:S(2)}) async-start(), calls=%async_computation.18 | async-start | bytes 4325376 | tf_op jit(solution)/shard_map/reduce_scatter | solution.py:301
  1550.6 849.2 %reduce-scatter.14.cloned.1.call-start = ((), (), s32[]{:S(2)}) async-start(), calls=%async_computation.15 | async-start | bytes 4325376 | tf_op jit(solution)/shard_map/reduce_scatter | solution.py:298
  1557.4 991.3 %reduce-scatter.16.cloned.1.call-start = ((), (), s32[]{:S(2)}) async-start(), calls=%async_computation.16 | async-start | bytes 4325376 | tf_op jit(solution)/shard_map/reduce_scatter | solution.py:299
  1797.4 901.3 %reduce-scatter.18.cloned.1.call-start = ((), (), s32[]{:S(2)}) async-start(), calls=%async_computation.17 | async-start | bytes 4325376 | tf_op jit(solution)/shard_map/reduce_scatter | solution.py:300
  2048.8 65.7 %copy-start.52 = (f32[512]{0:T(512)S(1)}, f32[512]{0:T(512)}, u32[]{:S(2)}) copy-start(f32[512]{0:T(512)} %copy-done.51) | copy-start | bytes 6148
  (55 other events, 278.5 us)
Sparse Core Ops, SparseCore 0:
  20.0 147.5 all-gather.1
  1503.4 281.0 reduce-scatter.11
  1787.4 125.1 reduce-scatter.27
  1916.0 67.7 reduce-scatter.25
  1987.4 59.0 reduce-scatter.21
  2049.8 59.0 reduce-scatter.23
  2111.8 138.4 reduce-scatter.19
  2253.2 146.5 reduce-scatter.13
  2402.8 145.8 reduce-scatter.15
  2551.5 147.1 reduce-scatter.17
where the time goes:
time: 2730 us; the launch traced here: 2710 us
  waiting for transfers between devices  1810 us (66%)
  matrix products  397 us (15%)
  local copies, waits for them, and re-layouts  237 us (9%)
  other arithmetic  168 us (6%)
  starting transfers between devices  41.5 us (2%)
  blocking collectives  41.2 us (2%)
    ppermute x4, waiting for transfers between devices, from_behind(): return lax.ppermute(x, axis, pairs)  467 us
    reduce_scatter x1, waiting for transfers between devices, on_device(): lax.psum_scatter(own_part, 'exp', scatter_dimension=1, tiled=True)  227 us
    dot_general x22, matrix products, matmul(): return jnp.dot(left, right, preferred_element_type=jnp.float32)  172 us
    reduce_scatter x1, waiting for transfers between devices, on_device(): lax.psum_scatter(grad_value_local, ('ctx', 'exp'), scatter_dimension=0, t...  150 us
    reduce_scatter x1, waiting for transfers between devices, on_device(): lax.psum_scatter(grad_query_local, ('ctx', 'exp'), scatter_dimension=0, t...  150 us
    reduce_scatter x1, waiting for transfers between devices, on_device(): lax.psum_scatter(grad_key_local, ('ctx', 'exp'), scatter_dimension=0, til...  149 us
    all_gather x1, waiting for transfers between devices, on_device(): kv_block = lax.all_gather(kv_piece, 'exp', axis=1, tiled=True)  148 us
    unnamed x11, waiting for transfers between devices  106 us
  transfers between devices with their start and end apart: 18, of which 18 were waited for; matrix products, arithmetic and copies ran while one was open for 9% of the time, Pallas kernels for 0%

commit v1 on v0

v1 whole, which is shorter than its diff:
```python
import functools

import jax
import jax.numpy as jnp
import numpy as np
from jax import lax
from jax.experimental import pallas as pl
from jax.experimental.pallas import tpu as pltpu
from jax.sharding import PartitionSpec as P

WINDOW = 1024
TILE = 128
TILES_SEEN = WINDOW // TILE + 1
epsilon = 1e-06
bucket_total = 32
NEG = -1e30
f32 = jnp.float32
bf16 = jnp.bfloat16
VMEM = 56 * 1024 * 1024


def dot(left, right):
    return jnp.dot(left, right, preferred_element_type=f32)


def dot_nt(left, right):
    return lax.dot_general(left, right, (((1,), (1,)), ((), ())), preferred_element_type=f32)


def dot_tn(left, right):
    return lax.dot_general(left, right, (((0,), (0,)), ((), ())), preferred_element_type=f32)


def exact_dot(left, right):
    return jnp.dot(left, right, precision=lax.Precision.HIGHEST, preferred_element_type=f32)


def bucket_of(distance):
    limits = np.ceil(16.0 * 8.0 ** (np.arange(1, 16) / 16.0)).astype(np.int32)
    above = np.sum(distance[..., None] >= limits, axis=-1)
    return np.where(distance < 16, distance, 16 + above)


def bias_kernel(vec_ref, out_ref):
    for a in range(TILES_SEEN):
        first = (TILES_SEEN - 1 - a) * TILE
        for h in range(2):
            row = vec_ref[0, h : h + 1, first : first + 2 * TILE]
            wide = jnp.broadcast_to(row, (TILE, 2 * TILE))
            rolled = pltpu.roll(wide, TILE, 1, stride=1, stride_axis=0)
            out_ref[0, a, :, h * TILE : (h + 1) * TILE] = rolled[:, :TILE].astype(bf16)


def split_heads(x):
    lane = lax.broadcasted_iota(jnp.int32, x.shape, 1)
    zero = jnp.zeros_like(x)
    return jnp.concatenate([jnp.where(lane < 64, x, zero), jnp.where(lane < 64, zero, x)], axis=0)


def merge_heads(xt):
    return jnp.concatenate([xt[:64, :TILE], xt[64:, TILE:]], axis=0).T


def attend_kernel(tiles, lo_ref, q_ref, k_ref, v_ref, b_ref, out_ref, lse_ref, s_ref, p_ref):
    vt = v_ref[...].T
    row = lax.broadcasted_iota(jnp.int32, (TILE, 2 * TILE), 0)
    for t in range(tiles):
        q2 = split_heads(q_ref[t * TILE : (t + 1) * TILE, :])
        lo = lo_ref[:, t * 2 * TILE : (t + 1) * 2 * TILE]
        top = jnp.full((8, 2 * TILE), NEG, f32)
        for a in range(TILES_SEEN):
            kb = t + a
            s = dot_nt(k_ref[kb * TILE : (kb + 1) * TILE, :], q2) + b_ref[0, a].astype(f32)
            s = jnp.where(row >= lo - kb * TILE, s, NEG)
            s_ref[a] = s
            top = jnp.maximum(top, jnp.max(s.reshape(TILE // 8, 8, 2 * TILE), axis=0))
        top = jnp.max(top, axis=0, keepdims=True)
        total = jnp.zeros((8, 2 * TILE), f32)
        for a in range(TILES_SEEN):
            p = jnp.exp(s_ref[a] - top)
            total = total + jnp.sum(p.reshape(TILE // 8, 8, 2 * TILE), axis=0)
            p_ref[a * TILE : (a + 1) * TILE, :] = p.astype(bf16)
        total = jnp.sum(total, axis=0, keepdims=True)
        ct = dot(vt[:, t * TILE : (t + TILES_SEEN) * TILE], p_ref[...]) / total
        out_ref[t * TILE : (t + 1) * TILE, :] = merge_heads(ct).astype(bf16)
        lse_ref[0, :, t * 2 * TILE : (t + 1) * 2 * TILE] = top + jnp.log(total)


def attend_back_kernel(
    tiles, lo_ref, lse_ref, q_ref, k_ref, v_ref, o_ref, do_ref, b_ref,
    dq_ref, dk_ref, dv_ref, tab_ref, q2_ref, do2_ref, ds_ref, p_ref, acc_ref, delta_ref,
):
    row = lax.broadcasted_iota(jnp.int32, (TILE, 2 * TILE), 0)
    for t in range(tiles):
        rows = slice(t * TILE, (t + 1) * TILE)
        both = slice(t * 2 * TILE, (t + 1) * 2 * TILE)
        q2_ref[both, :] = split_heads(q_ref[rows, :])
        do2_ref[both, :] = split_heads(do_ref[rows, :])
        prod = (do_ref[rows, :].astype(f32) * o_ref[rows, :].astype(f32)).T
        delta_ref[:, t * 2 * TILE : t * 2 * TILE + TILE] = jnp.sum(prod[:64], axis=0, keepdims=True)
        delta_ref[:, t * 2 * TILE + TILE : (t + 1) * 2 * TILE] = jnp.sum(prod[64:], axis=0, keepdims=True)
    acc_ref[...] = jnp.zeros_like(acc_ref)
    keys = tiles + TILES_SEEN - 1
    for kb in range(keys):
        first, last = max(0, kb - TILES_SEEN + 1), min(tiles - 1, kb)
        krows = slice(kb * TILE, (kb + 1) * TILE)
        cols = slice(first * 2 * TILE, (last + 1) * 2 * TILE)
        key, value = k_ref[krows, :], v_ref[krows, :]
        for t in range(first, last + 1):
            both = slice(t * 2 * TILE, (t + 1) * 2 * TILE)
            a = kb - t
            s = dot_nt(key, q2_ref[both, :]) + b_ref[0, a].astype(f32)
            s = jnp.where(row >= lo_ref[:, both] - kb * TILE, s, NEG)
            p = jnp.exp(s - lse_ref[0, :, both])
            dp = dot_nt(value, do2_ref[both, :])
            ds = p * (dp - delta_ref[:, both])
            acc_ref[a] += ds
            p_ref[:, both] = p.astype(bf16)
            ds_ref[krows, both] = ds.astype(bf16)
        dk_ref[krows, :] = dot(ds_ref[krows, cols], q2_ref[cols, :]).astype(bf16)
        dv_ref[krows, :] = dot(p_ref[:, cols], do2_ref[cols, :]).astype(bf16)
    kt = k_ref[...].T
    for t in range(tiles):
        both = slice(t * 2 * TILE, (t + 1) * 2 * TILE)
        span = slice(t * TILE, (t + TILES_SEEN) * TILE)
        dqt = dot(kt[:, span], ds_ref[span, both]) * 0.125
        dq_ref[t * TILE : (t + 1) * TILE, :] = merge_heads(dqt).astype(bf16)
    for a in range(TILES_SEEN):
        for h in range(2):
            part = acc_ref[a, :, h * TILE : (h + 1) * TILE]
            part = jnp.concatenate([part, jnp.zeros_like(part)], axis=1)
            half = TILE // 2
            while half >= 1:
                part = part[:half] + pltpu.roll(part[half:], 2 * TILE - half, 1)
                half //= 2
            tab_ref[0, h, a : a + 1, :] = pltpu.roll(part, TILE, 1)


def bias_tiles(vec):
    pairs = vec.shape[0]
    return pl.pallas_call(
        bias_kernel,
        grid=(pairs,),
        in_specs=[pl.BlockSpec((1, 2, vec.shape[2]), lambda g: (g, 0, 0))],
        out_specs=pl.BlockSpec((1, TILES_SEEN, TILE, 2 * TILE), lambda g: (g, 0, 0, 0)),
        out_shape=jax.ShapeDtypeStruct((pairs, TILES_SEEN, TILE, 2 * TILE), bf16),
        compiler_params=pltpu.CompilerParams(vmem_limit_bytes=VMEM),
        name="bias_tiles",
    )(vec)


def attend(lo, q, k, v, bias):
    rows, width = q.shape
    keys = k.shape[0]
    pairs, tiles = width // TILE, rows // TILE
    half = lambda n: pl.BlockSpec((n, TILE), lambda g: (0, g))
    return pl.pallas_call(
        functools.partial(attend_kernel, tiles),
        grid=(pairs,),
        in_specs=[
            pl.BlockSpec((1, 2 * rows), lambda g: (0, 0)),
            half(rows), half(keys), half(keys),
            pl.BlockSpec((1, TILES_SEEN, TILE, 2 * TILE), lambda g: (g, 0, 0, 0)),
        ],
        out_specs=[half(rows), pl.BlockSpec((1, 1, 2 * rows), lambda g: (g, 0, 0))],
        out_shape=[
            jax.ShapeDtypeStruct((rows, width), bf16),
            jax.ShapeDtypeStruct((pairs, 1, 2 * rows), f32),
        ],
        scratch_shapes=[
            pltpu.VMEM((TILES_SEEN, TILE, 2 * TILE), f32),
            pltpu.VMEM((TILES_SEEN * TILE, 2 * TILE), bf16),
        ],
        compiler_params=pltpu.CompilerParams(vmem_limit_bytes=VMEM),
        cost_estimate=pl.CostEstimate(flops=20_000_000_000, bytes_accessed=16_000_000, transcendentals=9_400_000),
        name="attend",
    )(lo, q, k, v, bias)


def attend_back(lo, lse, q, k, v, o, do, bias):
    rows, width = q.shape
    keys = k.shape[0]
    pairs, tiles = width // TILE, rows // TILE
    half = lambda n: pl.BlockSpec((n, TILE), lambda g: (0, g))
    return pl.pallas_call(
        functools.partial(attend_back_kernel, tiles),
        grid=(pairs,),
        in_specs=[
            pl.BlockSpec((1, 2 * rows), lambda g: (0, 0)),
            pl.BlockSpec((1, 1, 2 * rows), lambda g: (g, 0, 0)),
            half(rows), half(keys), half(keys), half(rows), half(rows),
            pl.BlockSpec((1, TILES_SEEN, TILE, 2 * TILE), lambda g: (g, 0, 0, 0)),
        ],
        out_specs=[
            half(rows), half(keys), half(keys),
            pl.BlockSpec((1, 2, TILES_SEEN, 2 * TILE), lambda g: (g, 0, 0, 0)),
        ],
        out_shape=[
            jax.ShapeDtypeStruct((rows, width), bf16),
            jax.ShapeDtypeStruct((keys, width), bf16),
            jax.ShapeDtypeStruct((keys, width), bf16),
            jax.ShapeDtypeStruct((pairs, 2, TILES_SEEN, 2 * TILE), f32),
        ],
        scratch_shapes=[
            pltpu.VMEM((2 * rows, TILE), bf16),
            pltpu.VMEM((2 * rows, TILE), bf16),
            pltpu.VMEM((keys, 2 * rows), bf16),
            pltpu.VMEM((TILE, 2 * rows), bf16),
            pltpu.VMEM((TILES_SEEN, TILE, 2 * TILE), f32),
            pltpu.VMEM((1, 2 * rows), f32),
        ],
        compiler_params=pltpu.CompilerParams(vmem_limit_bytes=VMEM),
        cost_estimate=pl.CostEstimate(flops=50_000_000_000, bytes_accessed=24_000_000, transcendentals=9_400_000),
        name="attend_back",
    )(lo, lse, q, k, v, o, do, bias)


def shift(x, by):
    count = lax.axis_size("ctx")
    return lax.ppermute(x, "ctx", [(i, i + by) for i in range(count) if 0 <= i + by < count])


def core_swap(x):
    return lax.ppermute(x, "ctx", [(i, i ^ 1) for i in range(lax.axis_size("ctx"))])


def over_exp(x):
    return lax.all_to_all(x, "exp", split_axis=0, concat_axis=0, tiled=True)


def sum_over_ctx(partial):
    count = lax.axis_size("ctx")
    rows, width = partial.shape
    side = lax.axis_index("ctx") % 2
    parts = partial.reshape(count // 2, 2, rows // count, width)
    other = core_swap(lax.dynamic_index_in_dim(parts, 1 - side, 1, keepdims=False))
    mine = lax.dynamic_index_in_dim(parts, side, 1, keepdims=False)
    pair = (mine.astype(f32) + other.astype(f32)).astype(bf16)
    groups = [list(range(core, count, 2)) for core in range(2)]
    got = lax.all_to_all(pair, "ctx", split_axis=0, concat_axis=0, tiled=True, axis_index_groups=groups)
    return jnp.sum(got.astype(f32), axis=0)


def sum_over_all(partial):
    rows_sum = sum_over_ctx(partial).astype(bf16)
    count = lax.axis_size("exp")
    got = over_exp(rows_sum.reshape(count, -1, rows_sum.shape[-1]))
    return jnp.sum(got.astype(f32), axis=0)


def norm_rows(values, gain):
    return values * lax.rsqrt(jnp.mean(values * values, axis=-1, keepdims=True) + epsilon) * gain


def norm_back(values, gain, grad):
    r = lax.rsqrt(jnp.mean(values * values, axis=-1, keepdims=True) + epsilon)
    u = grad * gain
    inner = jnp.mean(values * u, axis=-1, keepdims=True)
    return r * u - values * (r * r * r) * inner, jnp.sum(grad * values * r, axis=0)


def gelu_parts(v):
    c = np.float32(np.sqrt(2.0 / np.pi))
    t = jnp.tanh(c * (v + 0.044715 * v * v * v))
    half = 0.5 * (1.0 + t)
    return v * half, half + 0.5 * v * (1.0 - t * t) * (c * (1.0 + 3.0 * 0.044715 * v * v))


def on_device(
    tokens, doc_lengths, routes, priority, norm1_gain, w_query, w_key, w_value, w_out, bias_table,
    norm2_gain, w_router, w_gate, w_up, w_down, cotangent,
):
    seqs, piece_len, width = tokens.shape
    exp_count = lax.axis_size("exp")
    ctx_count = lax.axis_size("ctx")
    device_count = exp_count * ctx_count
    block_len = piece_len * exp_count
    rows = seqs * piece_len
    heads = bias_table.shape[0] // bucket_total
    experts = w_router.shape[1]
    slot = 5 * rows // (2 * experts)
    slots = experts * slot
    ctx = lax.axis_index("ctx")
    exp = lax.axis_index("exp")
    side = ctx % 2

    x_own = over_exp(tokens).reshape(block_len, width)
    x_two = shift(x_own, 2)
    x_one = core_swap(jnp.where(side == 0, x_own, x_two))

    route_rows = routes.reshape(rows, 2)
    order = priority.reshape(rows)
    earlier = order[None, :] < order[:, None]
    r0, r1 = route_rows[:, 0], route_rows[:, 1]
    place0 = jnp.sum((earlier & (r0[None, :] == r0[:, None])).astype(jnp.int32), axis=1)
    place1 = jnp.sum((earlier & (r1[None, :] == r1[:, None])).astype(jnp.int32), axis=1) + jnp.sum(
        (r0[None, :] == r1[:, None]).astype(jnp.int32), axis=1
    )
    target0 = jnp.where(place0 < slot, r0 * slot + place0, -1)
    target1 = jnp.where(place1 < slot, r1 * slot + place1, -1)
    slot_index = jnp.arange(slots, dtype=jnp.int32)[:, None]
    spread = ((slot_index == target0[None, :]) | (slot_index == target1[None, :])).astype(bf16)

    def dispatch(values):
        return over_exp(dot(spread, values).astype(bf16).reshape(experts, slot, width)).reshape(slots, width)

    def collect(values):
        return dot_tn(spread, over_exp(values.reshape(experts, slot, width)).reshape(slots, width))

    cot_rows = cotangent.reshape(rows, width)
    cot_slots = dispatch(cot_rows)

    distance = np.arange(-TILE, WINDOW + TILE)
    seen = (distance >= 0) & (distance < WINDOW)
    hot = (bucket_of(np.clip(distance, 0, None))[None, :] == np.arange(bucket_total)[:, None]) & seen[None, :]
    vec = exact_dot(bias_table.astype(f32).reshape(heads, bucket_total), jnp.asarray(hot, f32))
    vec = jnp.where(jnp.asarray(seen)[None, :], vec, NEG).reshape(heads // 2, 2, -1)
    bias = bias_tiles(vec)

    ends = jnp.cumsum(lax.dynamic_index_in_dim(doc_lengths, exp, 0, keepdims=False))
    q_pos = ctx * block_len + jnp.arange(block_len, dtype=jnp.int32)
    start = jnp.max(jnp.where(ends[None, :] <= q_pos[:, None], ends[None, :], 0), axis=1)
    lo = start - (ctx - 2) * block_len
    lo = jnp.broadcast_to(lo.reshape(-1, 1, TILE), (block_len // TILE, 2, TILE)).reshape(1, -1)

    gain_one = norm1_gain.astype(f32)
    x_window = jnp.concatenate([x_two, x_one, x_own], axis=0)
    normed = norm_rows(x_window.astype(f32), gain_one).astype(bf16)
    normed_own = normed[2 * block_len :]
    q = (dot(normed_own, w_query).astype(bf16) * 0.125).astype(bf16)
    k = dot(normed, w_key).astype(bf16)
    v = dot(normed, w_value).astype(bf16)
    context, lse = attend(lo, q, k, v, bias)

    context_rows = over_exp(context.reshape(exp_count, piece_len, width)).reshape(rows, width)
    hidden = tokens.reshape(rows, width).astype(f32) + dot(context_rows, w_out)
    gain_two = norm2_gain.astype(f32)
    moe_in = norm_rows(hidden, gain_two).astype(bf16)

    wg, wu, wd = w_gate[0], w_up[0], w_down[0]
    grad_raw = dot_nt(cot_slots, wd)
    inputs = dispatch(moe_in)
    router_probs = jax.nn.softmax(dot(inputs, w_router), axis=-1)
    own_expert = (jnp.arange(experts) == exp).astype(f32)[None, :]
    gate = jnp.sum(router_probs * own_expert, axis=-1, keepdims=True)
    gate_pre = dot(inputs, wg)
    up_pre = dot(inputs, wu)
    gelu, gelu_slope = gelu_parts(gate_pre)
    activation = gelu * up_pre
    act_low = activation.astype(bf16)
    grad_gates = jnp.sum(activation * grad_raw, axis=-1, keepdims=True)
    grad_act = grad_raw * gate
    grad_gate_pre = (grad_act * up_pre * gelu_slope).astype(bf16)
    grad_up_pre = (grad_act * gelu).astype(bf16)
    grad_logits = grad_gates * router_probs * (own_expert - gate)
    grad_inputs = (
        dot_nt(grad_gate_pre, wg)
        + dot_nt(grad_up_pre, wu)
        + exact_dot(grad_logits, w_router.astype(f32).T)
    ).astype(bf16)
    grad_moe = collect(grad_inputs)
    grad_router_part = lax.dot_general(
        inputs.astype(f32), grad_logits, (((0,), (0,)), ((), ())),
        precision=lax.Precision.HIGHEST, preferred_element_type=f32,
    )
    produced = (dot(act_low, wd) * gate).astype(bf16)
    mixed = (hidden + collect(produced)).astype(bf16).reshape(seqs, piece_len, width)
    grad_out_slots = (gate * cot_slots.astype(f32)).astype(bf16)
    grad_gate = sum_over_ctx(dot_tn(inputs, grad_gate_pre).astype(bf16))
    grad_up = sum_over_ctx(dot_tn(inputs, grad_up_pre).astype(bf16))
    grad_down = sum_over_ctx(dot_tn(act_low, grad_out_slots).astype(bf16))

    grad_norm, grad_gain_two = norm_back(hidden, gain_two, grad_moe)
    grad_hidden = cot_rows.astype(f32) + grad_norm
    grad_attn = grad_hidden.astype(bf16)
    grad_out = sum_over_all(dot_tn(context_rows, grad_attn).astype(bf16))
    grad_context = dot_nt(grad_attn, w_out).astype(bf16)
    grad_context = over_exp(grad_context.reshape(seqs, piece_len, width)).reshape(block_len, width)

    dq, dk, dv, diagonals = attend_back(lo, lse, q, k, v, context, grad_context, bias)
    grad_window = dot_nt(dk, w_key) + dot_nt(dv, w_value)
    part_two = grad_window[:block_len].astype(bf16)
    part_one = grad_window[block_len : 2 * block_len].astype(bf16)
    swapped = core_swap(part_one).astype(f32)
    own_sum = grad_window[2 * block_len :] + dot_nt(dq, w_query)
    own_sum = own_sum + jnp.where(side == 0, swapped, 0.0)
    leave = jnp.where(side == 0, part_two.astype(f32), part_two.astype(f32) + swapped).astype(bf16)
    grad_normed = own_sum + shift(leave, -2).astype(f32)
    grad_query = sum_over_all(dot_tn(normed_own, dq).astype(bf16))
    grad_key = sum_over_all(dot_tn(normed, dk).astype(bf16))
    grad_value = sum_over_all(dot_tn(normed, dv).astype(bf16))
    grad_x, grad_gain_one = norm_back(x_own.astype(f32), gain_one, grad_normed)
    grad_x = over_exp(grad_x.astype(bf16).reshape(exp_count, piece_len, width)).reshape(rows, width)
    grad_tokens = (grad_hidden + grad_x.astype(f32)).astype(bf16).reshape(seqs, piece_len, width)

    places = np.arange((TILES_SEEN) * 2 * TILE).reshape(TILES_SEEN, 2 * TILE)
    block, lane = places // (2 * TILE), places % (2 * TILE)
    where_dist = lane - TILE + (TILES_SEEN - 1 - block) * TILE
    ok = (where_dist >= 0) & (where_dist < WINDOW)
    to_bucket = (bucket_of(np.clip(where_dist, 0, None))[..., None] == np.arange(bucket_total)) & ok[..., None]
    table_part = exact_dot(diagonals.reshape(heads, -1), jnp.asarray(to_bucket.reshape(-1, bucket_total), f32))
    small = [
        grad_gain_one.reshape(device_count, -1),
        grad_gain_two.reshape(device_count, -1),
        table_part.reshape(device_count, -1),
        grad_router_part.reshape(device_count, -1),
    ]
    sizes = [s.shape[1] for s in small]
    packed = jnp.concatenate(small, axis=1)
    packed = jnp.pad(packed, ((0, 0), (0, -packed.shape[1] % 128)))
    packed = lax.all_to_all(packed, ("ctx", "exp"), split_axis=0, concat_axis=0, tiled=True)
    packed = jnp.sum(packed, axis=0)
    cuts = np.cumsum([0] + sizes)
    norm1_out, norm2_out, table_out, router_out = [packed[cuts[i] : cuts[i + 1]] for i in range(4)]
    return (
        mixed, grad_tokens, norm1_out, grad_query, grad_key, grad_value, grad_out, table_out, norm2_out,
        router_out.reshape(-1, experts), grad_gate[None], grad_up[None], grad_down[None],
    )


def solution(mesh):
    rows = P(None, ("ctx", "exp"), None)
    flat = P(("ctx", "exp"))
    in_specs = (
        rows, P(), rows, P(None, ("ctx", "exp")), P(), P(), P(), P(), P(), P(), P(), P(),
        P("exp", None, None), P("exp", None, None), P("exp", None, None), rows,
    )
    out_specs = (
        rows, rows, flat, P(("ctx", "exp"), None), P(("ctx", "exp"), None), P(("ctx", "exp"), None),
        P(("ctx", "exp"), None), flat, flat, P(("ctx", "exp"), None),
        P("exp", "ctx", None), P("exp", "ctx", None), P("exp", "ctx", None),
    )
    return jax.shard_map(on_device, mesh=mesh, in_specs=in_specs, out_specs=out_specs, check_vma=False)
```

time: 2730 us -> 768 us (0.28)
  waiting for transfers between devices: 1810 us -> 217 us
  local copies, waits for them, and re-layouts: 237 us -> 29.2 us
  matrix products: 397 us -> 216 us
  other arithmetic: 168 us -> 72 us
  starting transfers between devices: 41.5 us -> 122 us
  Pallas kernels: 0 us -> 66.9 us
    reduce_scatter x8 -> x0, waiting for transfers between devices: 952 us -> none  [the longest x1 227 us: on_device(): lax.psum_scatter(own_part, 'exp', scatter_dimension=1, tiled=True)]
    ppermute x4 -> x11, waiting for transfers between devices: 467 us -> 22 us  [the longest x2 22 us: shift(): lax.ppermute(x, 'ctx', [(i, i + by) for i in range(count) if 0 <= i + by...]
    dot_general x56 -> x30, matrix products: 395 us -> 216 us  [the longest x7 70.6 us: dot_nt(): lax.dot_general(left, right, (((1,), (1,)), ((), ())), preferred_element_...]
    all_gather x1 -> x0, waiting for transfers between devices: 148 us -> none  [on_device(): kv_block = lax.all_gather(kv_piece, 'exp', axis=1, tiled=True)]
    unnamed x11 -> x0, waiting for transfers between devices: 106 us -> none
    all_to_all x4 -> x19, starting transfers between devices: 32 us -> 116 us  [the longest x11 75.4 us: over_exp(): return lax.all_to_all(x, 'exp', split_axis=0, concat_axis=0, tiled=True)]
    pallas_call x0 -> x3, Pallas kernels: none -> 66.9 us  [the longest x1 38 us: attend_back(): pl.pallas_call(functools.partial(attend_back_kernel, tiles), grid=(pairs,...]
    all_to_all x4 -> x19, waiting for transfers between devices: 133 us -> 195 us  [the longest x11 123 us: over_exp(): return lax.all_to_all(x, 'exp', split_axis=0, concat_axis=0, tiled=True)]
  transfers between devices with their start and end apart: 18 -> 30, of which waited for: 18 -> 16; matrix products, arithmetic and copies ran while one was open for 9% -> 37% of each run, Pallas kernels for 0% -> 6%
where the time goes in v1:
time: 768 us; the launch traced here: 755 us
  waiting for transfers between devices  217 us (28%)
  matrix products  216 us (28%)
  starting transfers between devices  122 us (16%)
  other arithmetic  72 us (9%)
  Pallas kernels  66.9 us (9%)
  blocking collectives  29.4 us (4%)
  local copies, waits for them, and re-layouts  29.2 us (4%)
    all_to_all x11, waiting for transfers between devices, over_exp(): return lax.all_to_all(x, 'exp', split_axis=0, concat_axis=0, tiled=True)  123 us
    all_to_all x11, starting transfers between devices, over_exp(): return lax.all_to_all(x, 'exp', split_axis=0, concat_axis=0, tiled=True)  75.4 us
    dot_general x7, matrix products, dot_nt(): lax.dot_general(left, right, (((1,), (1,)), ((), ())), preferred_element_...  70.6 us
    all_to_all x7, waiting for transfers between devices, sum_over_ctx(): lax.all_to_all(pair, 'ctx', split_axis=0, concat_axis=0, tiled=True, axis...  69.6 us
    dot_general x9, matrix products, dot_tn(): lax.dot_general(left, right, (((0,), (0,)), ((), ())), preferred_element_...  68.5 us
    dot_general x10, matrix products, dot(): return jnp.dot(left, right, preferred_element_type=f32)  65.8 us
    pallas_call x1, Pallas kernels, attend_back(): pl.pallas_call(functools.partial(attend_back_kernel, tiles), grid=(pairs,...  38 us
    all_to_all x7, starting transfers between devices, sum_over_ctx(): lax.all_to_all(pair, 'ctx', split_axis=0, concat_axis=0, tiled=True, axis...  34.4 us
  transfers between devices with their start and end apart: 30, of which 16 were waited for; matrix products, arithmetic and copies ran while one was open for 37% of the time, Pallas kernels for 6%

profile of v1, /device:TPU:10, one launch (start us, length us, event | category | flops | bytes accessed | tf_op | source)
XLA Modules:
  0.0 755.3 jit_solution(4622761271140710559)
XLA Ops:
  0.7 29.4 %all_to_all.104 = bf16[4,128,1024]{2,1,0:T(8,128)(2,1)S(1)} all-to-all(bf16[4,128,1024]{2,1,0:T(8,128)(2,1)} %param.19), channel_id=1, replica_groups=mesh['ctx'=8,'exp'=4] {'exp'}, dimensions={0} | all-to-all | bytes 2097152 | tf_op jit(solution)/shard_map/all_to_all | solution.py:228
  33.5 22.0 %collective-permute-done = bf16[512,1024]{1,0:T(8,128)(2,1)} collective-permute-done((bf16[512,1024]{1,0:T(8,128)(2,1)S(1)}, bf16[512,1024]{1,0:T(8,128)(2,1)}, u32[]{:S(2)}, u32[]{:S(2)}) %collective-permute-start) | collective-permute-done | bytes 1048608 | tf_op jit(solution)/shard_map/ppermute | solution.py:220
  58.5 6.3 bias_tiles.1.b_ref
  81.5 22.6 %attend.1 = (bf16[512,1024]{1,0:T(8,128)(2,1)}, f32[8,1,1024]{2,1,0:T(1,128)}) custom-call(s32[1,1024]{1,0:T(1,128)} %bitcast.193, bf16[512,1024]{1,0:T(8,128)(2,1)} %fusion.49.q_ref, bf16[1536,1024]{1,0:T(8,128)(2,1)} %convolution_convert_fusion.6.k_ref, bf16[1536,1024]{1,0:T(8,128)(2,1)} %convolution_convert_fusion.5.v_ref, ...), custom_call_target="tpu_custom_call" | custom-call | flops 20000000000 | bytes 16000000 | tf_op jit(solution)/shard_map/attend/pallas_call | solution.py:157
  104.2 6.4 all-to-all-start.1
  111.5 22.5 %all-to-all-done.1 = bf16[4,128,1024]{2,1,0:T(8,128)(2,1)} async-done(((bf16[4,128,1024]{2,1,0:T(8,128)(2,1)}), bf16[4,128,1024]{2,1,0:T(8,128)(2,1)}, u32[]{:S(2)}, u32[]{:S(2)}) %all-to-all-start.1) | async-done | bytes 1048608 | tf_op jit(solution)/shard_map/all_to_all | solution.py:228
  141.1 8.4 %all-to-all-start.2 = ((bf16[4,320,1024]{2,1,0:T(8,128)(2,1)}), bf16[4,320,1024]{2,1,0:T(8,128)(2,1)}, u32[]{:S(2)}, u32[]{:S(2)}) async-start(bf16[4,320,1024]{2,1,0:T(8,128)(2,1)} %bitcast.169), calls=%async_computation.2 | async-start | bytes 5242880 | tf_op jit(solution)/shard_map/all_to_all | solution.py:228
  152.5 53.3 %all-to-all-done.2 = bf16[4,320,1024]{2,1,0:T(8,128)(2,1)} async-done(((bf16[4,320,1024]{2,1,0:T(8,128)(2,1)}), bf16[4,320,1024]{2,1,0:T(8,128)(2,1)}, u32[]{:S(2)}, u32[]{:S(2)}) %all-to-all-start.2) | async-done | bytes 2621472 | tf_op jit(solution)/shard_map/all_to_all | solution.py:228
  205.8 7.9 %all-to-all-start.4 = ((bf16[4,320,1024]{2,1,0:T(8,128)(2,1)}), bf16[4,320,1024]{2,1,0:T(8,128)(2,1)}, u32[]{:S(2)}, u32[]{:S(2)}) async-start(bf16[4,320,1024]{2,1,0:T(8,128)(2,1)} %bitcast.167), calls=%async_computation.4 | async-start | bytes 5242880 | tf_op jit(solution)/shard_map/all_to_all | solution.py:228
  216.4 14.0 %fusion.22 = f32[1280,2816]{1,0:T(8,128)} fusion(bf16[1280,1024]{1,0:T(8,128)(2,1)} %bitcast.14, bf16[1,1024,2816]{2,1,0:T(8,128)(2,1)} %param.32), kind=kOutput, calls=%fused_computation.32 | convolution fusion | flops 7381975040 | bytes 22806528 | tf_op jit(solution)/shard_map/dot_general | solution.py:23
  230.5 12.2 %fusion.26 = f32[1280,2816]{1,0:T(8,128)} fusion(bf16[1280,1024]{1,0:T(8,128)(2,1)} %bitcast.14, bf16[1,1024,2816]{2,1,0:T(8,128)(2,1)S(1)} %bitcast.200), kind=kOutput, calls=%fused_computation.36 | convolution fusion | flops 7381975040 | bytes 22806528 | tf_op jit(solution)/shard_map/dot_general | solution.py:23
  242.7 15.8 %multiply_convert_fusion.2 = bf16[1280,1024]{1,0:T(8,128)(2,1)} fusion(bf16[1,2816,1024]{2,1,0:T(8,128)(2,1)S(1)} %bitcast.198, f32[1280]{0:T(1024)S(1)} %get-tuple-element.85, f32[1280,2816]{1,0:T(8,128)} %fusion.22, f32[1280,2816]{1,0:T(8,128)} %fusion.26), kind=kOutput, calls=%fused_computation.46 | convolution fusion | flops 7420641280 | bytes 37229568 | tf_op jit(solution)/shard_map/dot_general | solution.py:23
  258.5 10.9 %all-to-all-done.4 = bf16[4,320,1024]{2,1,0:T(8,128)(2,1)} async-done(((bf16[4,320,1024]{2,1,0:T(8,128)(2,1)}), bf16[4,320,1024]{2,1,0:T(8,128)(2,1)}, u32[]{:S(2)}, u32[]{:S(2)}) %all-to-all-start.4) | async-done | bytes 2621472 | tf_op jit(solution)/shard_map/all_to_all | solution.py:228
  269.4 8.1 %all-to-all-start.3 = ((bf16[4,320,1024]{2,1,0:T(8,128)(2,1)}), bf16[4,320,1024]{2,1,0:T(8,128)(2,1)}, u32[]{:S(2)}, u32[]{:S(2)}) async-start(bf16[4,320,1024]{2,1,0:T(8,128)(2,1)} %bitcast.168), calls=%async_computation.3 | async-start | bytes 5242880 | tf_op jit(solution)/shard_map/all_to_all | solution.py:228
  277.5 26.0 %multiply_reduce_fusion = (f32[1280]{0:T(1024)S(1)}, bf16[1280,2816]{1,0:T(8,128)(2,1)}, bf16[1280,2816]{1,0:T(8,128)(2,1)S(1)}) fusion(f32[1280,2816]{1,0:T(8,128)} %fusion.22, f32[1280,2816]{1,0:T(8,128)} %fusion.26, f32[1280]{0:T(1024)S(1)} %get-tuple-element.85, bf16[1280,1024]{1,0:T(8,128)(2,1)} %bitcast.23, bf16[1,2816,1024]{2,1,0:T(8,128)(2,1)} %param.33), kind=kOutput, calls=%fused_computation.10 | convolution fusion | flops 7479294976 | bytes 51652608 | tf_op jit(solution)/shard_map/dot_general | solution.py:27
  303.4 14.2 %fusion.24 = f32[1280,1024]{1,0:T(8,128)S(1)} fusion(bf16[1280,2816]{1,0:T(8,128)(2,1)} %get-tuple-element.88, bf16[1,1024,2816]{2,1,0:T(8,128)(2,1)} %param.31), kind=kOutput, calls=%fused_computation.34 | convolution fusion | flops 7381975040 | bytes 18219008 | tf_op jit(solution)/shard_map/dot_general | solution.py:27
  317.6 11.2 %fusion.20 = f32[1280,1024]{1,0:T(8,128)S(1)} fusion(bf16[1280,2816]{1,0:T(8,128)(2,1)S(1)} %get-tuple-element.89, bf16[1,1024,2816]{2,1,0:T(8,128)(2,1)} %param.32), kind=kOutput, calls=%fused_computation.30 | convolution fusion | flops 7381975040 | bytes 18219008 | tf_op jit(solution)/shard_map/dot_general | solution.py:27
  333.1 8.1 %all-to-all-start.5 = ((bf16[4,320,1024]{2,1,0:T(8,128)(2,1)}), bf16[4,320,1024]{2,1,0:T(8,128)(2,1)}, u32[]{:S(2)}, u32[]{:S(2)}) async-start(bf16[4,320,1024]{2,1,0:T(8,128)(2,1)} %bitcast.159), calls=%async_computation.5 | async-start | bytes 5242880 | tf_op jit(solution)/shard_map/all_to_all | solution.py:228
  341.2 19.1 %convolution_convert_fusion.2 = bf16[2816,1024]{1,0:T(8,128)(2,1)} fusion(bf16[1280,1024]{1,0:T(8,128)(2,1)} %bitcast.23, f32[1280]{0:T(1024)S(1)} %get-tuple-element.85, f32[1280,2816]{1,0:T(8,128)} %fusion.22, f32[1280,2816]{1,0:T(8,128)} %fusion.26), kind=kOutput, calls=%fused_computation.43 | convolution fusion | flops 7424835584 | bytes 37229568 | tf_op jit(solution)/shard_map/dot_general | solution.py:31
  364.0 11.4 %convolution_convert_fusion.1 = bf16[1024,2816]{1,0:T(8,128)(2,1)S(1)} fusion(bf16[1280,1024]{1,0:T(8,128)(2,1)} %bitcast.14, bf16[1280,2816]{1,0:T(8,128)(2,1)} %get-tuple-element.88), kind=kOutput, calls=%fused_computation.42 | convolution fusion | flops 7384858624 | bytes 15597568 | tf_op jit(solution)/shard_map/dot_general | solution.py:31
  380.2 5.7 fusion.13
  385.9 10.9 %all-to-all-done.5 = bf16[4,320,1024]{2,1,0:T(8,128)(2,1)} async-done(((bf16[4,320,1024]{2,1,0:T(8,128)(2,1)}), bf16[4,320,1024]{2,1,0:T(8,128)(2,1)}, u32[]{:S(2)}, u32[]{:S(2)}) %all-to-all-start.5) | async-done | bytes 2621472 | tf_op jit(solution)/shard_map/all_to_all | solution.py:228
  396.9 5.0 all-to-all-start.19
  401.9 11.4 %convolution_convert_fusion = bf16[1024,2816]{1,0:T(8,128)(2,1)S(1)} fusion(bf16[1280,1024]{1,0:T(8,128)(2,1)} %bitcast.14, bf16[1280,2816]{1,0:T(8,128)(2,1)} %copy-done.50), kind=kOutput, calls=%fused_computation.41 | convolution fusion | flops 7384858624 | bytes 15597568 | tf_op jit(solution)/shard_map/dot_general | solution.py:31
  416.6 4.9 fusion.15
  421.6 12.8 %all-to-all-done.19 = bf16[4,352,1024]{2,1,0:T(8,128)(2,1)} async-done(((bf16[4,352,1024]{2,1,0:T(8,128)(2,1)}), bf16[4,352,1024]{2,1,0:T(8,128)(2,1)}, u32[]{:S(2)}, u32[]{:S(2)}) %all-to-all-start.19) | async-done | bytes 2883616 | tf_op jit(solution)/shard_map/all_to_all | solution.py:240
  434.4 5.1 all-to-all-start.17
  448.5 24.3 %all-to-all-done.17 = bf16[4,128,2816]{2,1,0:T(8,128)(2,1)} async-done(((bf16[4,128,2816]{2,1,0:T(8,128)(2,1)}), bf16[4,128,2816]{2,1,0:T(8,128)(2,1)}, u32[]{:S(2)}, u32[]{:S(2)}) %all-to-all-start.17) | async-done | bytes 2883616 | tf_op jit(solution)/shard_map/all_to_all | solution.py:240
  472.8 8.5 %all-to-all-start.6 = ((bf16[4,128,1024]{2,1,0:T(8,128)(2,1)}), bf16[4,128,1024]{2,1,0:T(8,128)(2,1)}, u32[]{:S(2)}, u32[]{:S(2)}) async-start(bf16[4,128,1024]{2,1,0:T(8,128)(2,1)} %bitcast.184), calls=%async_computation.6 | async-start | bytes 2097152 | tf_op jit(solution)/shard_map/all_to_all | solution.py:228
  484.7 5.0 fusion.14
  491.1 12.2 %all-to-all-done.6 = bf16[4,128,1024]{2,1,0:T(8,128)(2,1)} async-done(((bf16[4,128,1024]{2,1,0:T(8,128)(2,1)}), bf16[4,128,1024]{2,1,0:T(8,128)(2,1)}, u32[]{:S(2)}, u32[]{:S(2)}) %all-to-all-start.6) | async-done | bytes 1048608 | tf_op jit(solution)/shard_map/all_to_all | solution.py:228
  503.3 5.0 all-to-all-start.15
  508.4 38.0 %attend_back.1 = (bf16[512,1024]{1,0:T(8,128)(2,1)}, bf16[1536,1024]{1,0:T(8,128)(2,1)}, bf16[1536,1024]{1,0:T(8,128)(2,1)}, f32[8,2,9,256]{3,2,1,0:T(8,128)}) custom-call(s32[1,1024]{1,0:T(1,128)} %bitcast.194, f32[8,1,1024]{2,1,0:T(1,128)} %get-tuple-element.20.lse_ref, bf16[512,1024]{1,0:T(8,128)(2,1)} %fusion.49.q_ref, ...), custom_call_target="tpu_custom_call" | custom-call | flops 49999998976 | bytes 24000000 | tf_op jit(solution)/shard_map/attend_back/pallas_call | solution.py:185
  551.1 6.5 convolution_convert_fusion.9
  561.7 5.4 fusion.80
  570.4 12.1 %all-to-all-done.18 = bf16[4,128,2816]{2,1,0:T(8,128)(2,1)} async-done(((bf16[4,128,2816]{2,1,0:T(8,128)(2,1)}), bf16[4,128,2816]{2,1,0:T(8,128)(2,1)}, u32[]{:S(2)}, u32[]{:S(2)}) %all-to-all-start.18) | async-done | bytes 2883616 | tf_op jit(solution)/shard_map/all_to_all | solution.py:240
  582.5 7.8 %all-to-all-start.16 = ((bf16[4,32,1024]{2,1,0:T(8,128)(2,1)}), bf16[4,32,1024]{2,1,0:T(8,128)(2,1)S(1)}, u32[]{:S(2)}, u32[]{:S(2)}) async-start(bf16[4,32,1024]{2,1,0:T(8,128)(2,1)} %bitcast.48), calls=%async_computation.16 | async-start | bytes 524288 | tf_op jit(solution)/shard_map/all_to_all | solution.py:228
  590.3 8.4 %fusion.79 = (bf16[1536,1024]{1,0:T(8,128)(2,1)S(1)}, f32[1536,1024]{1,0:T(8,128)}) fusion(f32[1536,1024]{1,0:T(8,128)} %fusion.80, bf16[1536,1024]{1,0:T(8,128)(2,1)} %get-tuple-element.22, bf16[1024,1024]{1,0:T(8,128)(2,1)S(1)} %copy-done), kind=kOutput, calls=%fused_computation.160 | convolution fusion | flops 3224371200 | bytes 20971520 | tf_op jit(solution)/shard_map/dot_general | solution.py:27
  604.0 4.8 all-to-all-start.11
  608.8 6.3 convolution_convert_fusion.8
  625.8 5.4 all-to-all-start.9
  631.2 5.4 fusion.64
  644.0 16.7 %all-to-all-done.9 = bf16[4,128,1024]{2,1,0:T(8,128)(2,1)} async-done(((bf16[4,128,1024]{2,1,0:T(8,128)(2,1)}), bf16[4,128,1024]{2,1,0:T(8,128)(2,1)}, u32[]{:S(2)}, u32[]{:S(2)}) %all-to-all-start.9) | async-done | bytes 1048608 | tf_op jit(solution)/shard_map/all_to_all | solution.py:240
  677.5 5.8 all-to-all-start.8
  688.4 5.6 all-to-all-start.12
  696.2 5.3 all-to-all-done.12
  701.5 6.0 all-to-all-start.10
  728.8 4.9 add_convert_fusion.1
  (228 shorter events, 168.5 us)
Async XLA Ops:
  0.6 70.8 %copy-start = (bf16[1024,1024]{1,0:T(8,128)(2,1)S(1)}, bf16[1024,1024]{1,0:T(8,128)(2,1)}, u32[]{:S(2)}) copy-start(bf16[1024,1024]{1,0:T(8,128)(2,1)} %param.26) | copy-start | bytes 6291460
  0.7 57.0 %copy-start.36 = (pred[1280]{0:T(1024)(128)(4,1)S(1)}, pred[1280]{0:T(1024)(128)(4,1)}, u32[]{:S(2)}) copy-start(pred[1280]{0:T(1024)(128)(4,1)} %constant.135.clone) | copy-start | bytes 3844
  0.7 56.9 %copy-start.21 = (f32[32,1280]{1,0:T(8,128)S(1)}, f32[32,1280]{1,0:T(8,128)}, u32[]{:S(2)}) copy-start(f32[32,1280]{1,0:T(8,128)} %constant.134.clone) | copy-start | bytes 491524
  0.7 56.8 %copy-start.37 = (bf16[1024]{0:T(1024)(128)(2,1)S(1)}, bf16[1024]{0:T(1024)(128)(2,1)}, u32[]{:S(2)}) copy-start(bf16[1024]{0:T(1024)(128)(2,1)} %param.23) | copy-start | bytes 6148
  0.7 56.8 %copy-start.43 = (bf16[512]{0:T(512)(128)(2,1)S(1)}, bf16[512]{0:T(512)(128)(2,1)}, u32[]{:S(2)}) copy-start(bf16[512]{0:T(512)(128)(2,1)} %param.28) | copy-start | bytes 3076
  30.1 36.8 %copy-start.1 = (bf16[4,128,1024]{2,1,0:T(8,128)(2,1)}, bf16[4,128,1024]{2,1,0:T(8,128)(2,1)S(1)}, u32[]{:S(2)}) copy-start(bf16[4,128,1024]{2,1,0:T(8,128)(2,1)S(1)} %all_to_all.104) | copy-start | bytes 3145732
  30.1 25.4 %collective-permute-start = (bf16[512,1024]{1,0:T(8,128)(2,1)S(1)}, bf16[512,1024]{1,0:T(8,128)(2,1)}, u32[]{:S(2)}, u32[]{:S(2)}) collective-permute-start(bf16[512,1024]{1,0:T(8,128)(2,1)S(1)} %bitcast.156), channel_id=1, source_target_pairs={{0,8},{4,12},{8,16},{12,20},{16,24},{20,28},{1,9},{5,13},{9,17},{1... | collective-permute-start | bytes 3145736 | tf_op jit(solution)/shard_map/ppermute | solution.py:220
  56.6 8.2 %collective-permute-start.1 = (bf16[512,1024]{1,0:T(8,128)(2,1)}, bf16[512,1024]{1,0:T(8,128)(2,1)}, u32[]{:S(2)}, u32[]{:S(2)}) collective-permute-start(bf16[512,1024]{1,0:T(8,128)(2,1)} %broadcast_select_fusion), channel_id=1, source_target_pairs={{0,4},{4,0},{8,12},{12,8},{16,20},{20,16},{24,28},{28,24},{1,5},{5... | collective-permute-start | bytes 3145736 | tf_op jit(solution)/shard_map/ppermute | solution.py:224
  81.5 29.0 %copy-start.38 = (bf16[1024]{0:T(1024)(128)(2,1)S(1)}, bf16[1024]{0:T(1024)(128)(2,1)}, u32[]{:S(2)}) copy-start(bf16[1024]{0:T(1024)(128)(2,1)} %param.29) | copy-start | bytes 6148
  81.5 29.0 %copy-start.35 = (s32[4,128,2]{1,2,0:T(2,128)S(1)}, s32[4,128,2]{1,2,0:T(2,128)}, u32[]{:S(2)}) copy-start(s32[4,128,2]{1,2,0:T(2,128)} %param.21) | copy-start | bytes 12292
  81.5 29.0 %copy-start.32 = (s32[4,128]{1,0:T(4,128)S(1)}, s32[4,128]{1,0:T(4,128)}, u32[]{:S(2)}) copy-start(s32[4,128]{1,0:T(4,128)} %param.22) | copy-start | bytes 6148
  81.5 52.4 %copy-start.18 = (bf16[4,128,1024]{2,1,0:T(8,128)(2,1)S(1)}, bf16[4,128,1024]{2,1,0:T(8,128)(2,1)}, u32[]{:S(2)}) copy-start(bf16[4,128,1024]{2,1,0:T(8,128)(2,1)} %param.19) | copy-start | bytes 3145732
  104.2 29.8 %all-to-all-start.1 = ((bf16[4,128,1024]{2,1,0:T(8,128)(2,1)}), bf16[4,128,1024]{2,1,0:T(8,128)(2,1)}, u32[]{:S(2)}, u32[]{:S(2)}) async-start(bf16[4,128,1024]{2,1,0:T(8,128)(2,1)} %bitcast.183), calls=%async_computation.1 | async-start | bytes 2097152 | tf_op jit(solution)/shard_map/all_to_all | solution.py:228
  110.5 27.3 %copy-start.27 = (f32[1024]{0:T(1024)}, f32[1024]{0:T(1024)S(1)}, u32[]{:S(2)}) copy-start(f32[1024]{0:T(1024)S(1)} %convert_element_type.269) | copy-start | bytes 12292
  111.4 38.0 %copy-start.39 = (s32[512]{0:T(512)}, s32[512]{0:T(512)S(1)}, u32[]{:S(2)}) copy-start(s32[512]{0:T(512)S(1)} %get-tuple-element.103) | copy-start | bytes 6148
  111.4 38.0 %copy-start.41 = (s32[512]{0:T(512)}, s32[512]{0:T(512)S(1)}, u32[]{:S(2)}) copy-start(s32[512]{0:T(512)S(1)} %get-tuple-element.104) | copy-start | bytes 6148
  141.1 64.7 %all-to-all-start.2 = ((bf16[4,320,1024]{2,1,0:T(8,128)(2,1)}), bf16[4,320,1024]{2,1,0:T(8,128)(2,1)}, u32[]{:S(2)}, u32[]{:S(2)}) async-start(bf16[4,320,1024]{2,1,0:T(8,128)(2,1)} %bitcast.169), calls=%async_computation.2 | async-start | bytes 5242880 | tf_op jit(solution)/shard_map/all_to_all | solution.py:228
  149.5 179.4 %copy-start.33 = (f32[4]{0:T(128)}, f32[4]{0:T(128)S(1)}, u32[]{:S(2)}) copy-start(f32[4]{0:T(128)S(1)} %compare_convert_fusion) | copy-start | bytes 52
  152.5 61.2 %copy-start.24 = (bf16[1024,4]{0,1:T(4,128)(2,1)S(1)}, bf16[1024,4]{0,1:T(4,128)(2,1)}, u32[]{:S(2)}) copy-start(bf16[1024,4]{0,1:T(4,128)(2,1)} %param.30) | copy-start | bytes 24580
  205.8 63.6 %all-to-all-start.4 = ((bf16[4,320,1024]{2,1,0:T(8,128)(2,1)}), bf16[4,320,1024]{2,1,0:T(8,128)(2,1)}, u32[]{:S(2)}, u32[]{:S(2)}) async-start(bf16[4,320,1024]{2,1,0:T(8,128)(2,1)} %bitcast.167), calls=%async_computation.4 | async-start | bytes 5242880 | tf_op jit(solution)/shard_map/all_to_all | solution.py:228
  216.4 26.3 %slice-start = ((s8[5767168]{0:T(1024)(128)(4,1)}), s8[4194304]{0:T(1024)(128)(4,1)S(1)}, s32[]{:S(2)}) async-start(s8[5767168]{0:T(1024)(128)(4,1)} %bitcast.197), calls=%async_computation.20 | async-start | bytes 8388608
  230.5 98.3 %copy-start.19 = (f32[1280,4]{0,1:T(4,128)}, f32[1280,4]{0,1:T(4,128)S(1)}, u32[]{:S(2)}) copy-start(f32[1280,4]{0,1:T(4,128)S(1)} %get-tuple-element.86) | copy-start | bytes 61444
  269.4 63.7 %all-to-all-start.3 = ((bf16[4,320,1024]{2,1,0:T(8,128)(2,1)}), bf16[4,320,1024]{2,1,0:T(8,128)(2,1)}, u32[]{:S(2)}, u32[]{:S(2)}) async-start(bf16[4,320,1024]{2,1,0:T(8,128)(2,1)} %bitcast.168), calls=%async_computation.3 | async-start | bytes 5242880 | tf_op jit(solution)/shard_map/all_to_all | solution.py:228
  303.4 25.4 %copy-start.25 = (f32[1280]{0:T(1024)}, f32[1280]{0:T(1024)S(1)}, u32[]{:S(2)}) copy-start(f32[1280]{0:T(1024)S(1)} %get-tuple-element.87) | copy-start | bytes 15364
  333.1 63.8 %all-to-all-start.5 = ((bf16[4,320,1024]{2,1,0:T(8,128)(2,1)}), bf16[4,320,1024]{2,1,0:T(8,128)(2,1)}, u32[]{:S(2)}, u32[]{:S(2)}) async-start(bf16[4,320,1024]{2,1,0:T(8,128)(2,1)} %bitcast.159), calls=%async_computation.5 | async-start | bytes 5242880 | tf_op jit(solution)/shard_map/all_to_all | solution.py:228
  364.0 16.1 %collective-permute-start.10 = (bf16[4,352,1024]{2,1,0:T(8,128)(2,1)}, bf16[4,352,1024]{2,1,0:T(8,128)(2,1)}, u32[]{:S(2)}, u32[]{:S(2)}) collective-permute-start(bf16[4,352,1024]{2,1,0:T(8,128)(2,1)} %dynamic-slice_bitcast_fusion), channel_id=1, source_target_pairs={{0,4},{4,0},{8,12},{12,8},{16,20},{20,16},{24,28},{28,24},{1,5},{5... | collective-permute-start | bytes 8650760 | tf_op jit(solution)/shard_map/ppermute | solution.py:224
  379.7 35.6 %collective-permute-start.8 = (bf16[4,128,2816]{2,1,0:T(8,128)(2,1)}, bf16[4,128,2816]{2,1,0:T(8,128)(2,1)}, u32[]{:S(2)}, u32[]{:S(2)}) collective-permute-start(bf16[4,128,2816]{2,1,0:T(8,128)(2,1)} %dynamic-slice_bitcast_fusion.2), channel_id=1, source_target_pairs={{0,4},{4,0},{8,12},{12,8},{16,20},{20,16},{24,28},{28,24},{1,5},{5... | collective-permute-start | bytes 8650760 | tf_op jit(solution)/shard_map/ppermute | solution.py:224
  396.9 37.5 %all-to-all-start.19 = ((bf16[4,352,1024]{2,1,0:T(8,128)(2,1)}), bf16[4,352,1024]{2,1,0:T(8,128)(2,1)}, u32[]{:S(2)}, u32[]{:S(2)}) async-start(bf16[4,352,1024]{2,1,0:T(8,128)(2,1)} %fusion.13), calls=%async_computation.19 | async-start | bytes 5767168 | tf_op jit(solution)/shard_map/all_to_all | solution.py:240
  415.2 69.5 %collective-permute-start.9 = (bf16[4,128,2816]{2,1,0:T(8,128)(2,1)}, bf16[4,128,2816]{2,1,0:T(8,128)(2,1)}, u32[]{:S(2)}, u32[]{:S(2)}) collective-permute-start(bf16[4,128,2816]{2,1,0:T(8,128)(2,1)} %dynamic-slice_bitcast_fusion.1), channel_id=1, source_target_pairs={{0,4},{4,0},{8,12},{12,8},{16,20},{20,16},{24,28},{28,24},{1,5},{5... | collective-permute-start | bytes 8650760 | tf_op jit(solution)/shard_map/ppermute | solution.py:224
  434.4 38.4 %all-to-all-start.17 = ((bf16[4,128,2816]{2,1,0:T(8,128)(2,1)}), bf16[4,128,2816]{2,1,0:T(8,128)(2,1)}, u32[]{:S(2)}, u32[]{:S(2)}) async-start(bf16[4,128,2816]{2,1,0:T(8,128)(2,1)} %fusion.15), calls=%async_computation.17 | async-start | bytes 5767168 | tf_op jit(solution)/shard_map/all_to_all | solution.py:240
  472.8 30.5 %all-to-all-start.6 = ((bf16[4,128,1024]{2,1,0:T(8,128)(2,1)}), bf16[4,128,1024]{2,1,0:T(8,128)(2,1)}, u32[]{:S(2)}, u32[]{:S(2)}) async-start(bf16[4,128,1024]{2,1,0:T(8,128)(2,1)} %bitcast.184), calls=%async_computation.6 | async-start | bytes 2097152 | tf_op jit(solution)/shard_map/all_to_all | solution.py:228
  484.6 5.1 collective-permute-start.7
  503.3 43.1 %all-to-all-start.15 = ((bf16[4,128,1024]{2,1,0:T(8,128)(2,1)}), bf16[4,128,1024]{2,1,0:T(8,128)(2,1)}, u32[]{:S(2)}, u32[]{:S(2)}) async-start(bf16[4,128,1024]{2,1,0:T(8,128)(2,1)} %fusion.44), calls=%async_computation.15 | async-start | bytes 2097152 | tf_op jit(solution)/shard_map/all_to_all | solution.py:240
  546.4 36.1 %all-to-all-start.18 = ((bf16[4,128,2816]{2,1,0:T(8,128)(2,1)}), bf16[4,128,2816]{2,1,0:T(8,128)(2,1)}, u32[]{:S(2)}, u32[]{:S(2)}) async-start(bf16[4,128,2816]{2,1,0:T(8,128)(2,1)} %fusion.14), calls=%async_computation.18 | async-start | bytes 5767168 | tf_op jit(solution)/shard_map/all_to_all | solution.py:240
  558.7 42.7 %collective-permute-start.5 = (bf16[4,128,1024]{2,1,0:T(8,128)(2,1)}, bf16[4,128,1024]{2,1,0:T(8,128)(2,1)}, u32[]{:S(2)}, u32[]{:S(2)}) collective-permute-start(bf16[4,128,1024]{2,1,0:T(8,128)(2,1)} %dynamic-slice_bitcast_fusion.5), channel_id=1, source_target_pairs={{0,4},{4,0},{8,12},{12,8},{16,20},{20,16},{24,28},{28,24},{1,5},{5... | collective-permute-start | bytes 3145736 | tf_op jit(solution)/shard_map/ppermute | solution.py:224
  568.2 55.0 %collective-permute-start.4 = (bf16[4,128,1024]{2,1,0:T(8,128)(2,1)}, bf16[4,128,1024]{2,1,0:T(8,128)(2,1)}, u32[]{:S(2)}, u32[]{:S(2)}) collective-permute-start(bf16[4,128,1024]{2,1,0:T(8,128)(2,1)} %dynamic-slice_bitcast_fusion.6), channel_id=1, source_target_pairs={{0,4},{4,0},{8,12},{12,8},{16,20},{20,16},{24,28},{28,24},{1,5},{5... | collective-permute-start | bytes 3145736 | tf_op jit(solution)/shard_map/ppermute | solution.py:224
  582.5 21.5 %all-to-all-start.16 = ((bf16[4,32,1024]{2,1,0:T(8,128)(2,1)}), bf16[4,32,1024]{2,1,0:T(8,128)(2,1)S(1)}, u32[]{:S(2)}, u32[]{:S(2)}) async-start(bf16[4,32,1024]{2,1,0:T(8,128)(2,1)} %bitcast.48), calls=%async_computation.16 | async-start | bytes 524288 | tf_op jit(solution)/shard_map/all_to_all | solution.py:228
  601.4 16.5 %collective-permute-start.2 = (bf16[512,1024]{1,0:T(8,128)(2,1)}, bf16[512,1024]{1,0:T(8,128)(2,1)}, u32[]{:S(2)}, u32[]{:S(2)}) collective-permute-start(bf16[512,1024]{1,0:T(8,128)(2,1)} %slice.54), channel_id=1, source_target_pairs={{0,4},{4,0},{8,12},{12,8},{16,20},{20,16},{24,28},{28,24},{1,5},{5... | collective-permute-start | bytes 3145736 | tf_op jit(solution)/shard_map/ppermute | solution.py:224
  604.0 21.8 %all-to-all-start.11 = ((bf16[4,128,1024]{2,1,0:T(8,128)(2,1)}), bf16[4,128,1024]{2,1,0:T(8,128)(2,1)}, u32[]{:S(2)}, u32[]{:S(2)}) async-start(bf16[4,128,1024]{2,1,0:T(8,128)(2,1)} %fusion.46), calls=%async_computation.11 | async-start | bytes 2097152 | tf_op jit(solution)/shard_map/all_to_all | solution.py:240
  617.6 23.4 %collective-permute-start.6 = (bf16[4,128,1024]{2,1,0:T(8,128)(2,1)}, bf16[4,128,1024]{2,1,0:T(8,128)(2,1)}, u32[]{:S(2)}, u32[]{:S(2)}) collective-permute-start(bf16[4,128,1024]{2,1,0:T(8,128)(2,1)} %dynamic-slice_bitcast_fusion.4), channel_id=1, source_target_pairs={{0,4},{4,0},{8,12},{12,8},{16,20},{20,16},{24,28},{28,24},{1,5},{5... | collective-permute-start | bytes 3145736 | tf_op jit(solution)/shard_map/ppermute | solution.py:224
  620.8 47.6 %collective-permute-start.3 = (bf16[512,1024]{1,0:T(8,128)(2,1)}, bf16[512,1024]{1,0:T(8,128)(2,1)}, u32[]{:S(2)}, u32[]{:S(2)}) collective-permute-start(bf16[512,1024]{1,0:T(8,128)(2,1)} %fusion.37), channel_id=1, source_target_pairs={{8,0},{12,4},{16,8},{20,12},{24,16},{28,20},{9,1},{13,5},{17,9},{2... | collective-permute-start | bytes 3145736 | tf_op jit(solution)/shard_map/ppermute | solution.py:220
  625.8 34.9 %all-to-all-start.9 = ((bf16[4,128,1024]{2,1,0:T(8,128)(2,1)}), bf16[4,128,1024]{2,1,0:T(8,128)(2,1)}, u32[]{:S(2)}, u32[]{:S(2)}) async-start(bf16[4,128,1024]{2,1,0:T(8,128)(2,1)} %fusion.47), calls=%async_computation.9 | async-start | bytes 2097152 | tf_op jit(solution)/shard_map/all_to_all | solution.py:240
  660.7 16.9 %all-to-all-start.13 = ((bf16[4,128,1024]{2,1,0:T(8,128)(2,1)}), bf16[4,128,1024]{2,1,0:T(8,128)(2,1)}, u32[]{:S(2)}, u32[]{:S(2)}) async-start(bf16[4,128,1024]{2,1,0:T(8,128)(2,1)} %fusion.45), calls=%async_computation.13 | async-start | bytes 2097152 | tf_op jit(solution)/shard_map/all_to_all | solution.py:240
  677.5 10.9 %all-to-all-start.8 = ((f32[32,1,256]{2,1,0:T(1,128)}), f32[32,1,256]{2,1,0:T(1,128)S(1)}, u32[]{:S(2)}, u32[]{:S(2)}) async-start(f32[32,1,256]{2,1,0:T(1,128)} %copy.42), calls=%async_computation.8 | async-start | bytes 65536 | tf_op jit(solution)/shard_map/all_to_all | solution.py:411
  688.4 13.1 %all-to-all-start.12 = ((bf16[4,32,1024]{2,1,0:T(8,128)(2,1)}), bf16[4,32,1024]{2,1,0:T(8,128)(2,1)}, u32[]{:S(2)}, u32[]{:S(2)}) async-start(bf16[4,32,1024]{2,1,0:T(8,128)(2,1)} %bitcast.40), calls=%async_computation.12 | async-start | bytes 524288 | tf_op jit(solution)/shard_map/all_to_all | solution.py:228
  701.5 12.3 %all-to-all-start.10 = ((bf16[4,32,1024]{2,1,0:T(8,128)(2,1)}), bf16[4,32,1024]{2,1,0:T(8,128)(2,1)}, u32[]{:S(2)}, u32[]{:S(2)}) async-start(bf16[4,32,1024]{2,1,0:T(8,128)(2,1)} %bitcast.36), calls=%async_computation.10 | async-start | bytes 524288 | tf_op jit(solution)/shard_map/all_to_all | solution.py:228
  713.8 10.9 %all-to-all-start.14 = ((bf16[4,32,1024]{2,1,0:T(8,128)(2,1)}), bf16[4,32,1024]{2,1,0:T(8,128)(2,1)}, u32[]{:S(2)}, u32[]{:S(2)}) async-start(bf16[4,32,1024]{2,1,0:T(8,128)(2,1)} %bitcast.44), calls=%async_computation.14 | async-start | bytes 524288 | tf_op jit(solution)/shard_map/all_to_all | solution.py:228
  724.7 27.2 %all-to-all-start.7 = ((bf16[4,128,1024]{2,1,0:T(8,128)(2,1)}), bf16[4,128,1024]{2,1,0:T(8,128)(2,1)S(1)}, u32[]{:S(2)}, u32[]{:S(2)}) async-start(bf16[4,128,1024]{2,1,0:T(8,128)(2,1)} %bitcast.166), calls=%async_computation.7 | async-start | bytes 2097152 | tf_op jit(solution)/shard_map/all_to_all | solution.py:228
  (37 other events, 294.0 us)

commit v2 on v1

v2 whole, which is shorter than its diff:
```python
import functools

import jax
import jax.numpy as jnp
import numpy as np
from jax import lax
from jax.experimental import pallas as pl
from jax.experimental.pallas import tpu as pltpu
from jax.sharding import PartitionSpec as P

WINDOW = 1024
TILE = 128
TILES_SEEN = WINDOW // TILE + 1
epsilon = 1e-06
bucket_total = 32
NEG = -1e30
f32 = jnp.float32
bf16 = jnp.bfloat16
VMEM = 56 * 1024 * 1024


def cost(us):
    return pl.CostEstimate(flops=int(us * 1.15e9), bytes_accessed=0, transcendentals=0)


def behind(kernel, inputs, others):
    return lambda *refs: kernel(*refs[:inputs], *refs[inputs + len(others) :])


def anywhere(others):
    return [pl.BlockSpec(memory_space=pl.ANY)] * len(others)


def dot(left, right):
    return jnp.dot(left, right, preferred_element_type=f32)


def dot_nt(left, right):
    return lax.dot_general(left, right, (((1,), (1,)), ((), ())), preferred_element_type=f32)


def dot_tn(left, right):
    return lax.dot_general(left, right, (((0,), (0,)), ((), ())), preferred_element_type=f32)


def exact_dot(left, right):
    return jnp.dot(left, right, precision=lax.Precision.HIGHEST, preferred_element_type=f32)


def bucket_of(distance):
    limits = np.ceil(16.0 * 8.0 ** (np.arange(1, 16) / 16.0)).astype(np.int32)
    above = np.sum(distance[..., None] >= limits, axis=-1)
    return np.where(distance < 16, distance, 16 + above)


def bias_kernel(vec_ref, out_ref):
    for a in range(TILES_SEEN):
        first = (TILES_SEEN - 1 - a) * TILE
        for h in range(2):
            row = vec_ref[0, h : h + 1, first : first + 2 * TILE]
            wide = jnp.broadcast_to(row, (TILE, 2 * TILE))
            rolled = pltpu.roll(wide, TILE, 1, stride=1, stride_axis=0)
            out_ref[0, a, :, h * TILE : (h + 1) * TILE] = rolled[:, :TILE].astype(bf16)


def split_heads(x):
    lane = lax.broadcasted_iota(jnp.int32, x.shape, 1)
    zero = jnp.zeros_like(x)
    return jnp.concatenate([jnp.where(lane < 64, x, zero), jnp.where(lane < 64, zero, x)], axis=0)


def merge_heads(xt):
    return jnp.concatenate([xt[:64, :TILE], xt[64:, TILE:]], axis=0).T


def key_block(kb, z):
    return (kb // 4) * 4 + ((kb % 4) ^ z)


def attend_kernel(ks, z_ref, lo_ref, q_ref, k_ref, v_ref, b_ref, *refs):
    outs, (lse_ref, s_ref, p_ref, v_s) = refs[: len(ks)], refs[len(ks) :]
    z = z_ref[0]
    row = lax.broadcasted_iota(jnp.int32, (TILE, 2 * TILE), 0)
    for n, k in enumerate(ks):
        t = z ^ k
        q2 = split_heads(q_ref[n])
        lo = lo_ref[n] - t * TILE
        top = jnp.full((8, 2 * TILE), NEG, f32)
        for a in range(TILES_SEEN):
            at = key_block(t + a, z)
            v_s[a * TILE : (a + 1) * TILE, :] = v_ref[at]
            s = dot_nt(k_ref[at], q2) + b_ref[0, a].astype(f32)
            s = jnp.where(row >= lo - a * TILE, s, NEG)
            s_ref[a] = s
            top = jnp.maximum(top, jnp.max(s.reshape(TILE // 8, 8, 2 * TILE), axis=0))
        top = jnp.max(top, axis=0, keepdims=True)
        total = jnp.zeros((8, 2 * TILE), f32)
        for a in range(TILES_SEEN):
            p = jnp.exp(s_ref[a] - top)
            total = total + jnp.sum(p.reshape(TILE // 8, 8, 2 * TILE), axis=0)
            p_ref[a * TILE : (a + 1) * TILE, :] = p.astype(bf16)
        total = jnp.sum(total, axis=0, keepdims=True)
        ct = dot(v_s[...].T, p_ref[...]) / total
        outs[n][...] = merge_heads(ct).astype(bf16)
        lse_ref[0, n] = top + jnp.log(total)


def attend_back_kernel(pieces, z_ref, lo_ref, lse_a, lse_b, q_ref, k_ref, v_ref, b_ref, *refs):
    o_refs, do_refs = refs[:pieces], refs[pieces : 2 * pieces]
    dq_ref, dk_ref, dv_ref, tab_ref, q2_ref, do2_ref, ds_ref, p_ref, acc_ref, row_ref, k_s = refs[2 * pieces :]
    z = z_ref[0]
    row = lax.broadcasted_iota(jnp.int32, (TILE, 2 * TILE), 0)
    for k in range(pieces):
        both = pl.ds(pl.multiple_of((z ^ k) * 2 * TILE, 2 * TILE), 2 * TILE)
        out, grad = o_refs[k][...], do_refs[k][...]
        q2_ref[both, :] = split_heads(q_ref[k])
        do2_ref[both, :] = split_heads(grad)
        prod = (grad.astype(f32) * out.astype(f32)).T
        lse_ref = lse_a if k < pieces // 2 else lse_b
        row_ref[0:1, both] = lse_ref[0, k % (pieces // 2)]
        row_ref[1:2, both] = jnp.concatenate(
            [jnp.sum(prod[:64], axis=0, keepdims=True), jnp.sum(prod[64:], axis=0, keepdims=True)], axis=1
        )
    acc_ref[...] = jnp.zeros_like(acc_ref)
    keys = pieces + TILES_SEEN - 1
    for kb in range(keys):
        first, last = max(0, kb - TILES_SEEN + 1), min(pieces - 1, kb)
        krows = slice(kb * TILE, (kb + 1) * TILE)
        cols = slice(first * 2 * TILE, (last + 1) * 2 * TILE)
        at = key_block(kb, z)
        key, value = k_ref[at], v_ref[at]
        k_s[krows, :] = key
        for t in range(first, last + 1):
            both = slice(t * 2 * TILE, (t + 1) * 2 * TILE)
            a = kb - t
            s = dot_nt(key, q2_ref[both, :]) + b_ref[0, a].astype(f32)
            s = jnp.where(row >= lo_ref[z ^ t] - kb * TILE, s, NEG)
            p = jnp.exp(s - row_ref[0:1, both])
            dp = dot_nt(value, do2_ref[both, :])
            ds = p * (dp - row_ref[1:2, both])
            acc_ref[a] += ds
            p_ref[:, both] = p.astype(bf16)
            ds_ref[krows, both] = ds.astype(bf16)
        dk_ref[at] = dot(ds_ref[krows, cols], q2_ref[cols, :]).astype(bf16)
        dv_ref[at] = dot(p_ref[:, cols], do2_ref[cols, :]).astype(bf16)
    kt = k_s[...].T
    for t in range(pieces):
        both = slice(t * 2 * TILE, (t + 1) * 2 * TILE)
        span = slice(t * TILE, (t + TILES_SEEN) * TILE)
        dqt = dot(kt[:, span], ds_ref[span, both]) * 0.125
        dq_ref[z ^ t] = merge_heads(dqt).astype(bf16)
    for a in range(TILES_SEEN):
        for h in range(2):
            part = acc_ref[a, :, h * TILE : (h + 1) * TILE]
            part = jnp.concatenate([part, jnp.zeros_like(part)], axis=1)
            half = TILE // 2
            while half >= 1:
                part = part[:half] + pltpu.roll(part[half:], 2 * TILE - half, 1)
                half //= 2
            tab_ref[0, h, a : a + 1, :] = pltpu.roll(part, TILE, 1)


def bias_tiles(vec):
    pairs = vec.shape[0]
    return pl.pallas_call(
        bias_kernel,
        grid=(pairs,),
        in_specs=[pl.BlockSpec((1, 2, vec.shape[2]), lambda g: (g, 0, 0))],
        out_specs=pl.BlockSpec((1, TILES_SEEN, TILE, 2 * TILE), lambda g: (g, 0, 0, 0)),
        out_shape=jax.ShapeDtypeStruct((pairs, TILES_SEEN, TILE, 2 * TILE), bf16),
        compiler_params=pltpu.CompilerParams(vmem_limit_bytes=VMEM),
        cost_estimate=cost(6),
        name="bias_tiles",
    )(vec)


SMEM = pl.BlockSpec(memory_space=pltpu.SMEM)


def attend(ks, z, lo, q, k, v, bias, others=()):
    count, _, width = q.shape
    blocks, pairs = k.shape[0], width // TILE
    part = lambda n: pl.BlockSpec((n, TILE, TILE), lambda g: (0, 0, g))
    return pl.pallas_call(
        behind(functools.partial(attend_kernel, ks), 6, others),
        grid=(pairs,),
        in_specs=[
            SMEM,
            pl.BlockSpec((count, 1, 2 * TILE), lambda g: (0, 0, 0)),
            part(count), part(blocks), part(blocks),
            pl.BlockSpec((1, TILES_SEEN, TILE, 2 * TILE), lambda g: (g, 0, 0, 0)),
        ] + anywhere(others),
        out_specs=[pl.BlockSpec((TILE, TILE), lambda g: (0, g))] * count
        + [pl.BlockSpec((1, count, 1, 2 * TILE), lambda g: (g, 0, 0, 0))],
        out_shape=[jax.ShapeDtypeStruct((TILE, width), bf16)] * count
        + [
            jax.ShapeDtypeStruct((pairs, count, 1, 2 * TILE), f32),
        ],
        scratch_shapes=[
            pltpu.VMEM((TILES_SEEN, TILE, 2 * TILE), f32),
            pltpu.VMEM((TILES_SEEN * TILE, 2 * TILE), bf16),
            pltpu.VMEM((TILES_SEEN * TILE, TILE), bf16),
        ],
        compiler_params=pltpu.CompilerParams(vmem_limit_bytes=VMEM),
        cost_estimate=cost(7.4 * count),
        name="attend",
    )(z, lo, q, k, v, bias, *others)


def attend_back(part_index, part_count, z, lo, lses, q, k, v, bias, o, do, others=()):
    pieces, _, width = q.shape
    blocks, pairs = k.shape[0], width // TILE // part_count
    base = part_index * pairs
    part = lambda n: pl.BlockSpec((n, TILE, TILE), lambda g: (0, 0, base + g))
    alone = lambda n: pl.BlockSpec((n, TILE, TILE), lambda g: (0, 0, g))
    columns = pieces * 2 * TILE
    return pl.pallas_call(
        behind(functools.partial(attend_back_kernel, pieces), 8 + 2 * pieces, others),
        grid=(pairs,),
        in_specs=[
            SMEM,
            pl.BlockSpec((pieces, 1, 2 * TILE), lambda g: (0, 0, 0)),
            pl.BlockSpec((1, pieces // 2, 1, 2 * TILE), lambda g: (base + g, 0, 0, 0)),
            pl.BlockSpec((1, pieces // 2, 1, 2 * TILE), lambda g: (base + g, 0, 0, 0)),
            part(pieces), part(blocks), part(blocks),
            pl.BlockSpec((1, TILES_SEEN, TILE, 2 * TILE), lambda g: (base + g, 0, 0, 0)),
        ]
        + [pl.BlockSpec((TILE, TILE), lambda g: (0, base + g))] * pieces
        + [pl.BlockSpec((TILE, TILE), lambda g: (0, g))] * pieces
        + anywhere(others),
        out_specs=[
            alone(pieces), alone(blocks), alone(blocks),
            pl.BlockSpec((1, 2, TILES_SEEN, 2 * TILE), lambda g: (g, 0, 0, 0)),
        ],
        out_shape=[
            jax.ShapeDtypeStruct((pieces, TILE, width // part_count), bf16),
            jax.ShapeDtypeStruct((blocks, TILE, width // part_count), bf16),
            jax.ShapeDtypeStruct((blocks, TILE, width // part_count), bf16),
            jax.ShapeDtypeStruct((pairs, 2, TILES_SEEN, 2 * TILE), f32),
        ],
        scratch_shapes=[
            pltpu.VMEM((columns, TILE), bf16),
            pltpu.VMEM((columns, TILE), bf16),
            pltpu.VMEM((blocks * TILE, columns), bf16),
            pltpu.VMEM((TILE, columns), bf16),
            pltpu.VMEM((TILES_SEEN, TILE, 2 * TILE), f32),
            pltpu.VMEM((8, columns), f32),
            pltpu.VMEM((blocks * TILE, TILE), bf16),
        ],
        compiler_params=pltpu.CompilerParams(vmem_limit_bytes=VMEM),
        cost_estimate=cost(42 / part_count),
        name="attend_back",
    )(z, lo, *lses, q, k, v, bias, *o, *do, *others)


def gelu_parts(v):
    c = np.float32(np.sqrt(2.0 / np.pi))
    t = jnp.tanh(c * (v + 0.044715 * v * v * v))
    half = 0.5 * (1.0 + t)
    return v * half, half + 0.5 * v * (1.0 - t * t) * (c * (1.0 + 3.0 * 0.044715 * v * v))


def expert_kernel(
    experts, held, z_ref, x_ref, c_ref, wg_ref, wu_ref, wd_ref, wr_ref, *refs,
):
    gin_ref, kept_ref, act_ref, dgp_ref, dup_ref, gcot_ref, gate_out, glog_ref, acc_ref, gg_ref, rp_ref, gate_ref = refs[held:]
    step = pl.program_id(0)
    lane = lax.broadcasted_iota(jnp.int32, (x_ref.shape[0], TILE), 1)
    x, c = x_ref[...], c_ref[...]

    @pl.when(step == 0)
    def _():
        logits = jnp.where(lane < experts, dot(x, wr_ref[...]), NEG)
        e = jnp.exp(logits - jnp.max(logits, axis=1, keepdims=True))
        probs = e / jnp.sum(e, axis=1, keepdims=True)
        rp_ref[...] = probs
        gate = jnp.sum(jnp.where(lane == z_ref[0], probs, 0.0), axis=1, keepdims=True)
        gate_ref[...] = jnp.broadcast_to(gate, gate_ref.shape)
        gate_out[...] = gate_ref[...]
        kept_ref[...] = x
        gcot_ref[...] = (gate * c.astype(f32)).astype(bf16)
        acc_ref[...] = jnp.zeros_like(acc_ref)
        gg_ref[...] = jnp.zeros_like(gg_ref)

    raw = dot_nt(c, wd_ref[0])
    gate_pre = dot(x, wg_ref[0])
    up_pre = dot(x, wu_ref[0])
    gelu, slope = gelu_parts(gate_pre)
    act = gelu * up_pre
    act_ref[...] = act.astype(bf16)
    prod = act * raw
    gg_ref[...] += prod[:, :TILE] + prod[:, TILE:]
    scaled = raw * gate_ref[:, :1]
    dgp = (scaled * up_pre * slope).astype(bf16)
    dup = (scaled * gelu).astype(bf16)
    dgp_ref[...] = dgp
    dup_ref[...] = dup
    acc_ref[...] += dot_nt(dgp, wg_ref[0]) + dot_nt(dup, wu_ref[0])

    @pl.when(step == pl.num_programs(0) - 1)
    def _():
        gg = jnp.sum(gg_ref[...], axis=1, keepdims=True)
        own = jnp.where(lane == z_ref[0], 1.0, 0.0)
        glog = gg * rp_ref[...] * (own - gate_ref[...])
        glog_ref[...] = glog
        high = glog.astype(bf16)
        low = (glog - high.astype(f32)).astype(bf16)
        gin_ref[...] = (acc_ref[...] + dot_nt(high, wr_ref[...]) + dot_nt(low, wr_ref[...])).astype(bf16)


def expert(chunk, chunks, held, z, x, c, wg, wu, wd, wr, experts, others=()):
    rows, width = x.shape
    hidden = wg.shape[2]
    wide = 2 * TILE
    whole = pl.BlockSpec((rows, width), lambda f: (0, 0))
    kept = pl.BlockSpec((rows, width), lambda f: (chunk, 0))
    thin = pl.BlockSpec((rows, TILE), lambda f: (chunk, 0))
    tile = pl.BlockSpec((rows, wide), lambda f: (chunk, f))
    full = lambda n, t: jax.ShapeDtypeStruct((chunks * rows, n), t)
    held = [] if held is None else list(held)
    return pl.pallas_call(
        functools.partial(expert_kernel, experts, len(held) + len(others)),
        grid=(hidden // wide,),
        in_specs=[
            SMEM, whole, whole,
            pl.BlockSpec((1, width, wide), lambda f: (0, 0, f)),
            pl.BlockSpec((1, width, wide), lambda f: (0, 0, f)),
            pl.BlockSpec((1, wide, width), lambda f: (0, f, 0)),
            pl.BlockSpec((width, TILE), lambda f: (0, 0)),
        ] + anywhere(held) + anywhere(others),
        out_specs=[whole, kept, tile, tile, tile, kept, thin, thin],
        out_shape=[
            jax.ShapeDtypeStruct((rows, width), bf16),
            full(width, bf16), full(hidden, bf16), full(hidden, bf16), full(hidden, bf16), full(width, bf16),
            full(TILE, f32), full(TILE, f32),
        ],
        input_output_aliases={7 + i: 1 + i for i in range(len(held))},
        scratch_shapes=[
            pltpu.VMEM((rows, width), f32), pltpu.VMEM((rows, TILE), f32), pltpu.VMEM((rows, TILE), f32),
            pltpu.VMEM((rows, TILE), f32),
        ],
        compiler_params=pltpu.CompilerParams(vmem_limit_bytes=VMEM),
        cost_estimate=cost(23),
        name="expert",
    )(z, x, c, wg, wu, wd, wr, *held, *others)


def gate_up_kernel(x_ref, dgp_ref, dup_ref, gate_ref, up_ref, xt_ref):
    @pl.when(pl.program_id(0) == 0)
    def _():
        xt_ref[...] = x_ref[...].T

    gate_ref[...] = dot(xt_ref[...], dgp_ref[...]).astype(bf16)
    up_ref[...] = dot(xt_ref[...], dup_ref[...]).astype(bf16)


def gate_up_grads(x, dgp, dup, others=()):
    rows, width = x.shape
    hidden, wide = dgp.shape[1], 2 * TILE
    tile = pl.BlockSpec((rows, wide), lambda f: (0, f))
    out = pl.BlockSpec((width, wide), lambda f: (0, f))
    return pl.pallas_call(
        behind(gate_up_kernel, 3, others),
        grid=(hidden // wide,),
        in_specs=[pl.BlockSpec((rows, width), lambda f: (0, 0)), tile, tile] + anywhere(others),
        out_specs=[out, out],
        out_shape=[jax.ShapeDtypeStruct((width, hidden), bf16)] * 2,
        scratch_shapes=[pltpu.VMEM((width, rows), bf16)],
        compiler_params=pltpu.CompilerParams(vmem_limit_bytes=VMEM),
        cost_estimate=cost(26),
        name="gate_up_grads",
    )(x, dgp, dup, *others)


def down_kernel(act_ref, gcot_ref, wd_ref, gate_ref, down_ref, *refs):
    outs, acc_ref = refs[:-1], refs[-1]
    step = pl.program_id(0)
    act = act_ref[...]
    down_ref[...] = dot(act.T, gcot_ref[...]).astype(bf16)
    more = dot(act, wd_ref[0])

    @pl.when(step == 0)
    def _():
        acc_ref[...] = more

    @pl.when(step > 0)
    def _():
        acc_ref[...] += more

    @pl.when(step == pl.num_programs(0) - 1)
    def _():
        rows = outs[0].shape[0]
        for n, out in enumerate(outs):
            part = slice(n * rows, (n + 1) * rows)
            out[...] = (acc_ref[part, :] * gate_ref[part, :1]).astype(bf16)


def down_and_out(act, gcot, wd, gate, chunks, others=()):
    rows, hidden = act.shape
    width, wide = gcot.shape[1], 2 * TILE
    fixed = lambda r, c: pl.BlockSpec((r, c), lambda f: (0, 0))
    return pl.pallas_call(
        behind(down_kernel, 4, others),
        grid=(hidden // wide,),
        in_specs=[
            pl.BlockSpec((rows, wide), lambda f: (0, f)), fixed(rows, width),
            pl.BlockSpec((1, wide, width), lambda f: (0, f, 0)), fixed(rows, TILE),
        ] + anywhere(others),
        out_specs=[pl.BlockSpec((wide, width), lambda f: (f, 0))] + [fixed(rows // chunks, width)] * chunks,
        out_shape=[jax.ShapeDtypeStruct((hidden, width), bf16)]
        + [jax.ShapeDtypeStruct((rows // chunks, width), bf16)] * chunks,
        scratch_shapes=[pltpu.VMEM((rows, width), f32)],
        compiler_params=pltpu.CompilerParams(vmem_limit_bytes=VMEM),
        cost_estimate=cost(26),
        name="down_and_out",
    )(act, gcot, wd, gate, *others)


def norm_kernel(per_block, two_ref, one_ref, own_ref, gain_ref, out_ref, turned_ref):
    step = pl.program_id(0)

    def put(ref):
        x = ref[0].astype(f32)
        r = lax.rsqrt(jnp.mean(x * x, axis=-1, keepdims=True) + epsilon)
        normed = (x * r * gain_ref[...]).astype(bf16)
        out_ref[0] = normed
        turned_ref[...] = normed.T.reshape(turned_ref.shape)

    for n, ref in enumerate((two_ref, one_ref, own_ref)):
        pl.when(step // per_block == n)(functools.partial(put, ref))


def norm_window(two, one, own, gain, chips):
    pieces, rows, width = own.shape
    at = lambda n: pl.BlockSpec((1, rows, width), lambda f: (jnp.clip(f - n * pieces, 0, pieces - 1), 0, 0))
    return pl.pallas_call(
        functools.partial(norm_kernel, pieces),
        grid=(3 * pieces,),
        in_specs=[at(0), at(1), at(2), pl.BlockSpec((1, width), lambda f: (0, 0))],
        out_specs=[
            pl.BlockSpec((1, rows, width), lambda f: (f, 0, 0)),
            pl.BlockSpec((chips, 2, width // chips // 2, rows), lambda f: (0, 0, 0, f)),
        ],
        out_shape=[
            jax.ShapeDtypeStruct((3 * pieces, rows, width), bf16),
            jax.ShapeDtypeStruct((chips, 2, width // chips // 2, 3 * pieces * rows), bf16),
        ],
        compiler_params=pltpu.CompilerParams(vmem_limit_bytes=VMEM),
        cost_estimate=cost(10),
        name="norm_window",
    )(two, one, own, gain)


def slot_rows(t_ref, k, slot):
    index = lax.broadcasted_iota(jnp.int32, (slot, t_ref.shape[1]), 0) + k * slot
    return ((index == t_ref[0:1, :]) | (index == t_ref[1:2, :])).astype(bf16)


def row_slots(t_ref, k, slot):
    index = lax.broadcasted_iota(jnp.int32, (t_ref.shape[0], slot), 1) + k * slot
    return ((index == t_ref[:, 0:1]) | (index == t_ref[:, 1:2])).astype(bf16)


def collect(t_ref, refs):
    total = None
    for k, ref in enumerate(refs):
        part = dot(row_slots(t_ref, k, ref.shape[0]), ref[...])
        total = part if total is None else total + part
    return total


def turned(ref, z):
    return jnp.concatenate([ref[z ^ k] for k in range(ref.shape[0])], axis=0)


def call(kernel, ins, outs, us, name, others=(), scratch=()):
    specs = [SMEM if a.ndim == 1 else pl.BlockSpec(memory_space=pltpu.VMEM) for a in ins]
    return pl.pallas_call(
        behind(kernel, len(ins), others),
        in_specs=specs + anywhere(others),
        out_specs=[pl.BlockSpec(memory_space=pltpu.VMEM)] * len(outs),
        out_shape=[jax.ShapeDtypeStruct(shape, dtype) for shape, dtype in outs],
        scratch_shapes=list(scratch),
        compiler_params=pltpu.CompilerParams(vmem_limit_bytes=VMEM),
        cost_estimate=cost(us),
        name=name,
    )(*ins, *others)


def cot_kernel(ks, slot, z_ref, t_ref, cot_ref, *outs):
    values = turned(cot_ref, z_ref[0])
    for k, out in zip(ks, outs):
        out[...] = dot(slot_rows(t_ref, k, slot), values).astype(bf16)


def rows_kernel(ks, slot, t_ref, value_ref, *outs):
    for k, out in zip(ks, outs):
        out[...] = dot(slot_rows(t_ref, k, slot), value_ref[...]).astype(bf16)


def hidden_kernel(ks, slot, z_ref, t_ref, tok_ref, w_ref, gain_ref, *refs):
    pieces = tok_ref.shape[0]
    context, hidden_ref, moe_ref, outs = refs[:pieces], refs[pieces], refs[pieces + 1], refs[pieces + 2 :]
    left = jnp.concatenate([ref[...] for ref in context], axis=0)
    hidden = turned(tok_ref, z_ref[0]).astype(f32) + dot(left, w_ref[...])
    hidden_ref[...] = hidden
    moe_in = norm_rows(hidden, gain_ref[...]).astype(bf16)
    moe_ref[...] = moe_in
    for k, out in zip(ks, outs):
        out[...] = dot(slot_rows(t_ref, k, slot), moe_in).astype(bf16)


def middle_kernel(parts, z_ref, t_ref, hidden_ref, cot_ref, w_ref, gain_ref, *refs):
    pieces = cot_ref.shape[0]
    grad_ref, attn_ref, gain_grad_ref, outs = refs[pieces], refs[pieces + 1], refs[pieces + 2], refs[pieces + 3 :]
    grad_moe = collect(t_ref, refs[:pieces])
    grad_norm, gain_grad = norm_back(hidden_ref[...], gain_ref[...], grad_moe)
    gain_grad_ref[...] = gain_grad[None]
    grad = turned(cot_ref, z_ref[0]).astype(f32) + grad_norm
    grad_ref[...] = grad
    low = grad.astype(bf16)
    attn_ref[...] = low
    context = dot_nt(low, w_ref[...]).astype(bf16)
    rows, width = context.shape[0] // pieces, context.shape[1] // parts
    for n in range(parts):
        for k in range(pieces):
            outs[n * pieces + k][...] = context[k * rows : (k + 1) * rows, n * width : (n + 1) * width]


def mix_kernel(z_ref, t_ref, hidden_ref, *refs):
    out_ref = refs[-1]
    rows = out_ref.shape[1]
    mixed = (hidden_ref[...] + collect(t_ref, refs[:-1])).astype(bf16)
    for k in range(out_ref.shape[0]):
        out_ref[z_ref[0] ^ k] = mixed[k * rows : (k + 1) * rows]


def inputs_kernel(last, dq_ref, dk_ref, dv_ref, wq_ref, wk_ref, wv_ref, *refs):
    step = pl.program_id(0)
    flat = lambda ref: ref[...].reshape(-1, ref.shape[-1])
    grad = dot_nt(flat(dk_ref), wk_ref[...]) + dot_nt(flat(dv_ref), wv_ref[...])
    if not last:
        refs[0][...] = grad

        @pl.when(step == 2)
        def _():
            refs[0][...] = grad + dot_nt(flat(dq_ref), wq_ref[...])

        return
    acc_ref, normed_ref, two_ref, one_ref, own_ref, gain_ref = refs
    grad = grad + acc_ref[...]

    def gain(total):
        return jnp.sum(total * flat(normed_ref).astype(f32), axis=0, keepdims=True)

    @pl.when(step == 0)
    def _():
        two_ref[...] = grad.astype(bf16)
        gain_ref[...] = gain(grad)

    @pl.when(step == 1)
    def _():
        one_ref[...] = grad.astype(bf16)
        gain_ref[...] += gain(grad)

    @pl.when(step == 2)
    def _():
        total = grad + dot_nt(flat(dq_ref), wq_ref[...])
        own_ref[...] = total
        gain_ref[...] += gain(total)


def input_grads(part, dq, dk, dv, wq, wk, wv, acc=None, normed=None, others=()):
    pieces, rows, some = dq.shape
    width = wq.shape[0]
    block = pieces * rows
    window = pl.BlockSpec((pieces, rows, some), lambda f: (f, 0, 0))
    weight = pl.BlockSpec((width, some), lambda f: (0, part))
    once = pl.BlockSpec((block, width), lambda f: (0, 0))
    step = pl.BlockSpec((block, width), lambda f: (f, 0))
    specs = [pl.BlockSpec((pieces, rows, some), lambda f: (0, 0, 0)), window, window, weight, weight, weight]
    ins, outs = [dq, dk, dv, wq, wk, wv], [(step, (3 * block, width), f32)]
    if acc is not None:
        specs += [step, pl.BlockSpec((pieces, rows, width), lambda f: (f, 0, 0))]
        ins += [acc, normed]
        outs = [(once, (block, width), bf16)] * 2 + [(once, (block, width), f32)]
        outs += [(pl.BlockSpec((1, width), lambda f: (0, 0)), (1, width), f32)]
    return pl.pallas_call(
        behind(functools.partial(inputs_kernel, acc is not None), len(ins), others),
        grid=(3,),
        in_specs=specs + anywhere(others),
        out_specs=[o[0] for o in outs],
        out_shape=[jax.ShapeDtypeStruct(o[1], o[2]) for o in outs],
        compiler_params=pltpu.CompilerParams(vmem_limit_bytes=VMEM),
        cost_estimate=cost(7),
        name="input_grads",
    )(*ins, *others)


def tail_kernel(x_ref, sum_ref, swapped_ref, gain_ref, *refs):
    count = len(refs) // 2
    rows = x_ref.shape[1]
    for k in range(count):
        part = slice(k * rows, (k + 1) * rows)
        grad = sum_ref[part, :] + swapped_ref[part, :].astype(f32) + refs[k][...].astype(f32)
        refs[count + k][...] = norm_back(x_ref[k].astype(f32), gain_ref[...], grad)[0].astype(bf16)


def end_kernel(z_ref, grad_ref, *refs):
    out_ref = refs[-1]
    rows = out_ref.shape[1]
    for k in range(out_ref.shape[0]):
        out_ref[z_ref[0] ^ k] = (grad_ref[k * rows : (k + 1) * rows, :] + refs[k][...].astype(f32)).astype(bf16)


def projection_kernel(third, small, s_ref, nt_ref, dq_ref, dk_ref, dv_ref, *refs):
    other_ref, mine_ref = refs[-2:]
    step = pl.program_id(0)
    keys = nt_ref.shape[3]
    own = dq_ref.shape[0]

    def put(grad_ref, first):
        for where, ref in ((1 - s_ref[0], other_ref), (s_ref[0], mine_ref)):
            left = nt_ref[:, where, :, first:].reshape(-1, keys - first)
            ref[...] = dot(left, grad_ref[...]).astype(bf16).reshape(ref.shape)

    @pl.when(step < third)
    def _():
        put(dq_ref, keys - own)

    @pl.when((step >= third) & (step < 2 * third))
    def _():
        put(dk_ref, 0)

    @pl.when((step >= 2 * third) & (step < 3 * third))
    def _():
        put(dv_ref, 0)

    if small:

        @pl.when(step == 3 * third)
        def _():
            other_ref[...] = refs[0][:, 1 - s_ref[0]]
            mine_ref[...] = refs[0][:, s_ref[0]]


def projection_grads(side, normed_t, dq, dk, dv, small=(), others=()):
    chips, _, rows, keys = normed_t.shape
    own, width = dq.shape
    wide = 2 * TILE
    third = width // wide
    at = lambda j: (lambda f: (0, jnp.clip(f - j * third, 0, third - 1)))
    out = pl.BlockSpec((chips, rows, wide), lambda f: (0, 0, f))
    shape = jax.ShapeDtypeStruct((chips, rows, 3 * width + wide * len(small)), bf16)
    return pl.pallas_call(
        behind(functools.partial(projection_kernel, third, len(small)), 5 + len(small), others),
        grid=(3 * third + len(small),),
        in_specs=[
            SMEM,
            pl.BlockSpec((chips, 2, rows, keys), lambda f: (0, 0, 0, 0)),
            pl.BlockSpec((own, wide), at(0)),
            pl.BlockSpec((keys, wide), at(1)),
            pl.BlockSpec((keys, wide), at(2)),
        ] + [pl.BlockSpec((chips, 2, rows, wide), lambda f: (0, 0, 0, 0))] * len(small) + anywhere(others),
        out_specs=[out, out],
        out_shape=[shape, shape],
        compiler_params=pltpu.CompilerParams(vmem_limit_bytes=VMEM),
        cost_estimate=cost(9.3),
        name="projection_grads",
    )(side, normed_t, dq, dk, dv, *small, *others)


def shift(x, by):
    count = lax.axis_size("ctx")
    return lax.ppermute(x, "ctx", [(i, i + by) for i in range(count) if 0 <= i + by < count])


def core_swap(x):
    return lax.ppermute(x, "ctx", [(i, i ^ 1) for i in range(lax.axis_size("ctx"))])


def z_swap(x, k):
    if k == 0:
        return x
    return lax.ppermute(x, "exp", [(i, i ^ k) for i in range(lax.axis_size("exp"))])


def sum_over_chips(pair):
    chips = pair.shape[0]
    count = lax.axis_size("ctx")
    if chips > 4 or chips & (chips - 1):
        groups = [list(range(core, count, 2)) for core in range(2)]
        got = lax.all_to_all(pair, "ctx", split_axis=0, concat_axis=0, tiled=True, axis_index_groups=groups)
        return jnp.sum(got.astype(f32), axis=0)
    chip = lax.axis_index("ctx") // 2
    total = None
    for d in range(chips - 1, -1, -1):
        block = lax.dynamic_index_in_dim(pair, chip ^ d, 0, keepdims=False)
        if d:
            block = lax.ppermute(block, "ctx", [(i, i ^ (2 * d)) for i in range(count)])
        total = block.astype(f32) if total is None else total + block.astype(f32)
    return total


def sum_over_ctx(partial):
    count = lax.axis_size("ctx")
    rows, width = partial.shape
    side = lax.axis_index("ctx") % 2
    parts = partial.reshape(count // 2, 2, rows // count, width)
    other = core_swap(lax.dynamic_index_in_dim(parts, 1 - side, 1, keepdims=False))
    mine = lax.dynamic_index_in_dim(parts, side, 1, keepdims=False)
    return sum_over_chips((mine.astype(f32) + other.astype(f32)).astype(bf16))


def sum_over_exp(partial):
    count = lax.axis_size("exp")
    z = lax.axis_index("exp")
    parts = partial.reshape(count, -1, partial.shape[-1])
    total = None
    for k in range(count - 1, -1, -1):
        block = z_swap(lax.dynamic_index_in_dim(parts, z ^ k, 0, keepdims=False), k).astype(f32)
        total = block if total is None else total + block
    return total


def sum_over_all(partial):
    return sum_over_exp(sum_over_ctx(partial).astype(bf16))


def norm_rows(values, gain):
    return values * lax.rsqrt(jnp.mean(values * values, axis=-1, keepdims=True) + epsilon) * gain


def norm_back(values, gain, grad):
    r = lax.rsqrt(jnp.mean(values * values, axis=-1, keepdims=True) + epsilon)
    u = grad * gain
    inner = jnp.mean(values * u, axis=-1, keepdims=True)
    return r * u - values * (r * r * r) * inner, jnp.sum(grad * values * r, axis=0)


def on_device(
    tokens, doc_lengths, routes, priority, norm1_gain, w_query, w_key, w_value, w_out, bias_table,
    norm2_gain, w_router, w_gate, w_up, w_down, cotangent,
):
    seqs, piece_len, width = tokens.shape
    exp_count = lax.axis_size("exp")
    ctx_count = lax.axis_size("ctx")
    device_count = exp_count * ctx_count
    block_len = piece_len * exp_count
    rows = seqs * piece_len
    heads = bias_table.shape[0] // bucket_total
    experts = w_router.shape[1]
    slot = 5 * rows // (2 * experts)
    slots = experts * slot
    ctx = lax.axis_index("ctx")
    exp = lax.axis_index("exp")
    side = ctx % 2

    z = jnp.reshape(exp, (1,))
    far_first = [2, 3, 1]

    turn = jnp.arange(seqs, dtype=jnp.int32) ^ exp
    pick = lambda array, k: lax.dynamic_index_in_dim(array, exp ^ k, 0, keepdims=False)

    x_own = [None] * seqs
    for k in [0, 2, 3, 1]:
        x_own[k] = z_swap(pick(tokens, k), k)
    x_pieces = x_own
    x_two = [shift(piece, 2) for piece in x_own]
    x_own, x_two = jnp.stack(x_own), jnp.stack(x_two)
    x_one = core_swap(jnp.where(side == 0, x_own, x_two))

    route_rows = jnp.take(routes, turn, axis=0).reshape(rows, 2)
    order = jnp.take(priority, turn, axis=0).reshape(rows)
    earlier = order[None, :] < order[:, None]
    r0, r1 = route_rows[:, 0], route_rows[:, 1]
    place0 = jnp.sum((earlier & (r0[None, :] == r0[:, None])).astype(jnp.int32), axis=1)
    place1 = jnp.sum((earlier & (r1[None, :] == r1[:, None])).astype(jnp.int32), axis=1) + jnp.sum(
        (r0[None, :] == r1[:, None]).astype(jnp.int32), axis=1
    )
    target0 = jnp.where(place0 < slot, (r0 ^ exp) * slot + place0, -1)
    target1 = jnp.where(place1 < slot, (r1 ^ exp) * slot + place1, -1)
    targets = jnp.stack([target0, target1])
    targets_t = targets.T
    slot_shape = ((slot, width), bf16)
    sent = call(
        functools.partial(cot_kernel, far_first + [0], slot), [z, targets, cotangent], [slot_shape] * experts, 4, "cot_rows", x_pieces[1:]
    )
    cot_slots = [None] * experts
    for k, rows_k in zip(far_first + [0], sent):
        cot_slots[k] = z_swap(rows_k, k)

    distance = np.arange(-TILE, WINDOW + TILE)
    seen = (distance >= 0) & (distance < WINDOW)
    hot = (bucket_of(np.clip(distance, 0, None))[None, :] == np.arange(bucket_total)[:, None]) & seen[None, :]
    vec = exact_dot(bias_table.astype(f32).reshape(heads, bucket_total), jnp.asarray(hot, f32))
    vec = jnp.where(jnp.asarray(seen)[None, :], vec, NEG).reshape(heads // 2, 2, -1)
    bias = bias_tiles(vec)

    ends = jnp.cumsum(lax.dynamic_index_in_dim(doc_lengths, exp, 0, keepdims=False))
    piece_start = ctx * block_len + turn[:, None] * piece_len
    q_pos = piece_start + jnp.arange(piece_len, dtype=jnp.int32)[None, :]
    start = jnp.max(jnp.where(ends <= q_pos[..., None], ends, 0), axis=2)
    lo = start - (ctx - 2) * block_len
    lo = jnp.broadcast_to(lo[:, None, None, :], (seqs, 1, 2, TILE)).reshape(seqs, 1, 2 * TILE)

    gain_one = norm1_gain.astype(f32)
    normed, normed_t = norm_window(x_two, x_one, x_own, gain_one[None], ctx_count // 2)
    normed = normed.reshape(-1, width)
    normed_own = normed[2 * block_len :]
    q = (dot(normed_own, w_query).astype(bf16) * 0.125).astype(bf16).reshape(seqs, piece_len, width)
    k_win = dot(normed, w_key).astype(bf16).reshape(-1, TILE, width)
    v_win = dot(normed, w_value).astype(bf16).reshape(-1, TILE, width)
    contexts, lses, context_rows = [None] * seqs, [], [None] * seqs
    for first in (2, 0):
        others = [contexts[2], cot_slots[3], cot_slots[1]] if first == 0 else [cot_slots[2]]
        *c, l = attend((first, first + 1), z, lo[first : first + 2], q[first : first + 2], k_win, v_win, bias, others)
        lses.insert(0, l)
        for k in (first, first + 1):
            contexts[k] = c[k - first]
            context_rows[k] = z_swap(contexts[k], k)
    router_wide = jnp.pad(w_router, ((0, 0), (0, TILE - experts)))
    gain_two = norm2_gain.astype(f32)[None]
    hidden, moe_in, *sent = call(
        functools.partial(hidden_kernel, [2, 0], slot),
        [z, targets, tokens, w_out, gain_two] + context_rows,
        [((rows, width), f32), ((rows, width), bf16), slot_shape, slot_shape], 9, "hidden_rows",
    )
    inputs = [sent[1], None, z_swap(sent[0], 2), None]
    held, returned, turns = None, [None] * experts, [0, 2, 1, 3]
    for i, k in enumerate(turns):
        back, *held = expert(k, experts, held, z, inputs[k], cot_slots[k], w_gate, w_up, w_down, router_wide, experts)
        returned[k] = z_swap(back, k)
        if i == 0:
            sent = call(functools.partial(rows_kernel, [3, 1], slot), [targets, moe_in], [slot_shape] * 2, 3, "moe_rows", [back])
            inputs[3], inputs[1] = z_swap(sent[0], 3), z_swap(sent[1], 1)
    all_inputs, act_low, grad_gate_pre, grad_up_pre, grad_out_slots, gate, grad_logits = held
    grad_logits = grad_logits[:, :experts]
    scatter = lambda partial: lax.psum_scatter(partial, "ctx", scatter_dimension=0, tiled=True).astype(f32)
    gate_part, up_part = gate_up_grads(all_inputs, grad_gate_pre, grad_up_pre, [returned[turns[1]], returned[turns[2]]])
    grad_gate, grad_up = scatter(gate_part), scatter(up_part)

    part_count = 2
    part_width = width // part_count
    grad_hidden, grad_attn, grad_gain_two, *sent_back = call(
        functools.partial(middle_kernel, part_count),
        [z, targets_t, hidden, cotangent, w_out, gain_two] + returned,
        [((rows, width), f32), ((rows, width), bf16), ((1, width), f32)] + [((piece_len, part_width), bf16)] * (seqs * part_count),
        12, "middle_rows", [gate_part],
    )
    arrived = [[z_swap(sent_back[n * seqs + k], k) for k in range(seqs)] for n in range(part_count)]
    down_part, *produced = down_and_out(act_low, grad_out_slots, w_down, gate, experts, [sent_back[-1]])
    grad_down = scatter(down_part)
    grad_out = sum_over_ctx(dot_tn(jnp.concatenate(context_rows), grad_attn).astype(bf16)).astype(bf16)
    grad_router_part = lax.dot_general(
        all_inputs.astype(f32), grad_logits, (((0,), (0,)), ((), ())),
        precision=lax.Precision.HIGHEST, preferred_element_type=f32,
    )
    given = [z_swap(produced[k], k) for k in range(experts)]

    side_ref = jnp.reshape(side, (1,))
    weights = (w_query, w_key, w_value)
    flat = lambda grads: [grad.reshape(-1, part_width) for grad in grads]
    back = lambda n, others: attend_back(n, part_count, z, lo, lses, q, k_win, v_win, bias, contexts, arrived[n], others)
    *grads, diagonal = back(0, [down_part] + arrived[1])
    other, mine = projection_grads(side_ref, normed_t, *flat(grads), (), [given[2], given[1]])
    first_pair = (mine.astype(f32) + core_swap(other).astype(f32)).astype(bf16)
    first_sum = sum_over_chips(first_pair).astype(bf16)
    acc = input_grads(0, *grads, *weights, others=[other])[0]
    *grads, more = back(1, [acc, grad_out, first_pair])
    part_two, part_one, own_sum, gain_part = input_grads(1, *grads, *weights, acc, normed.reshape(-1, piece_len, width), [first_sum])
    grad_gain_one = gain_part / gain_one
    diagonals = jnp.concatenate([diagonal, more])
    places = np.arange((TILES_SEEN) * 2 * TILE).reshape(TILES_SEEN, 2 * TILE)
    block, lane = places // (2 * TILE), places % (2 * TILE)
    where_dist = lane - TILE + (TILES_SEEN - 1 - block) * TILE
    ok = (where_dist >= 0) & (where_dist < WINDOW)
    to_bucket = (bucket_of(np.clip(where_dist, 0, None))[..., None] == np.arange(bucket_total)) & ok[..., None]
    table_part = exact_dot(diagonals.reshape(heads, -1), jnp.asarray(to_bucket.reshape(-1, bucket_total), f32))
    small = [
        grad_gain_one.reshape(device_count, -1),
        grad_gain_two.reshape(device_count, -1),
        table_part.reshape(device_count, -1),
        grad_router_part.reshape(device_count, -1),
    ]
    cuts = np.cumsum([0] + [item.shape[1] for item in small])
    packed = jnp.concatenate(small, axis=1)
    share = width // device_count
    packed = jnp.pad(packed, ((0, 0), (0, -packed.shape[1] % share))).reshape(width, -1)
    packed = jnp.pad(packed.astype(bf16), ((0, 0), (0, 2 * TILE - packed.shape[1])))
    packed = packed.reshape(ctx_count // 2, 2, -1, 2 * TILE)
    other, mine = projection_grads(side_ref, normed_t, *flat(grads), [packed])
    pair = (mine.astype(f32) + core_swap(other).astype(f32)).astype(bf16)
    last_sum = sum_over_chips(pair).astype(bf16)
    swapped = core_swap(part_one)
    leave = jnp.where(side == 0, part_two.astype(f32), part_two.astype(f32) + swapped.astype(f32)).astype(bf16)
    swapped = jnp.where(side == 0, swapped, jnp.zeros_like(swapped))
    came = [shift(leave[k * piece_len : (k + 1) * piece_len], -2) for k in range(seqs)]
    mixed = call(
        mix_kernel, [z, targets_t, hidden] + given, [((seqs, piece_len, width), bf16)], 8, "mixed_rows", [leave, pair]
    )[0]
    pieces = call(
        tail_kernel, [x_own, own_sum, swapped, gain_one[None]] + came, [((piece_len, width), bf16)] * seqs, 6, "tail_rows", [mixed, last_sum]
    )
    pieces = [z_swap(piece, k) for k, piece in enumerate(pieces)]
    grad_tokens = call(end_kernel, [z, grad_hidden] + pieces, [((seqs, piece_len, width), bf16)], 4, "end_rows")[0]
    dense = sum_over_exp(jnp.concatenate([grad_out, first_sum, last_sum], axis=1))
    grad_out = dense[:, :width]
    parts = [dense[:, width + i * part_width : width + (i + 1) * part_width] for i in range(3 * part_count)]
    grad_query, grad_key, grad_value = [jnp.concatenate(parts[i::3], axis=1) for i in range(3)]
    packed = dense[:, 4 * width :].reshape(-1, 2 * TILE)[:, : -(-cuts[-1] // share)].reshape(-1)
    norm1_out, norm2_out, table_out, router_out = [packed[cuts[i] : cuts[i + 1]] for i in range(4)]
    return (
        mixed, grad_tokens, norm1_out, grad_query, grad_key, grad_value, grad_out, table_out, norm2_out,
        router_out.reshape(-1, experts), grad_gate[None], grad_up[None], grad_down[None],
    )


def solution(mesh):
    rows = P(None, ("ctx", "exp"), None)
    flat = P(("ctx", "exp"))
    in_specs = (
        rows, P(), rows, P(None, ("ctx", "exp")), P(), P(), P(), P(), P(), P(), P(), P(),
        P("exp", None, None), P("exp", None, None), P("exp", None, None), rows,
    )
    out_specs = (
        rows, rows, flat, P(("ctx", "exp"), None), P(("ctx", "exp"), None), P(("ctx", "exp"), None),
        P(("ctx", "exp"), None), flat, flat, P(("ctx", "exp"), None),
        P("exp", "ctx", None), P("exp", "ctx", None), P("exp", "ctx", None),
    )
    return jax.shard_map(on_device, mesh=mesh, in_specs=in_specs, out_specs=out_specs, check_vma=False)
```

time: 768 us -> 631 us (0.82)
  Pallas kernels: 66.9 us -> 305 us
  matrix products: 216 us -> 15.7 us
  waiting for transfers between devices: 217 us -> 148 us
  other arithmetic: 72 us -> 26.6 us
  starting transfers between devices: 122 us -> 84 us
  blocking collectives: 29.4 us -> 0 us
  between operations: 1.92 us -> 14.9 us
    pallas_call x2 -> x22, Pallas kernels: 60.7 us -> 299 us  [the longest x4 93.2 us: expert(): pl.pallas_call(functools.partial(expert_kernel, experts, len(held) + len(...]
    all_to_all x19 -> x0, waiting for transfers between devices: 195 us -> none  [the longest x11 123 us: over_exp(): return lax.all_to_all(x, 'exp', split_axis=0, concat_axis=0, tiled=True)]
    ppermute x0 -> x39, waiting for transfers between devices: none -> 130 us  [the longest x30 102 us: z_swap(): lax.ppermute(x, 'exp', [(i, i ^ k) for i in range(lax.axis_size('exp'))])]
    all_to_all x19 -> x0, starting transfers between devices: 116 us -> none  [the longest x11 75.4 us: over_exp(): return lax.all_to_all(x, 'exp', split_axis=0, concat_axis=0, tiled=True)]
    dot_general x8 -> x1, matrix products: 76 us -> 1.17 us  [on_device(): lax.dot_general(all_inputs.astype(f32), grad_logits, (((0,), (0,)), ((),...]
    dot_general x9 -> x1, matrix products: 68.5 us -> 2.87 us  [dot_tn(): lax.dot_general(left, right, (((0,), (0,)), ((), ())), preferred_element_...]
    ppermute x0 -> x39, starting transfers between devices: none -> 61.4 us  [the longest x30 49.1 us: z_swap(): lax.ppermute(x, 'exp', [(i, i ^ k) for i in range(lax.axis_size('exp'))])]
    dot_general x10 -> x3, matrix products: 65.8 us -> 10.8 us  [dot(): return jnp.dot(left, right, preferred_element_type=f32)]
  transfers between devices with their start and end apart: 30 -> 55, of which waited for: 16 -> 25; matrix products, arithmetic and copies ran while one was open for 37% -> 9% of each run, Pallas kernels for 6% -> 42%
where the time goes in v2:
time: 631 us; the launch traced here: 623 us
  Pallas kernels  305 us (48%)
  waiting for transfers between devices  148 us (23%)
  starting transfers between devices  84 us (13%)
  local copies, waits for them, and re-layouts  28.9 us (5%)
  other arithmetic  26.6 us (4%)
  matrix products  15.7 us (2%)
  between operations  14.9 us (2%)
    ppermute x30, waiting for transfers between devices, z_swap(): lax.ppermute(x, 'exp', [(i, i ^ k) for i in range(lax.axis_size('exp'))])  102 us
    pallas_call x4, Pallas kernels, expert(): pl.pallas_call(functools.partial(expert_kernel, experts, len(held) + len(...  93.2 us
    ppermute x30, starting transfers between devices, z_swap(): lax.ppermute(x, 'exp', [(i, i ^ k) for i in range(lax.axis_size('exp'))])  49.1 us
    pallas_call x2, Pallas kernels, attend_back(): pl.pallas_call(behind(functools.partial(attend_back_kernel, pieces), 8 +...  42.9 us
    pallas_call x7, Pallas kernels, call(): pl.pallas_call(behind(kernel, len(ins), others), in_specs=specs + anywher...  34 us
    pallas_call x2, Pallas kernels, attend(): pl.pallas_call(behind(functools.partial(attend_kernel, ks), 6, others), g...  29.9 us
    pallas_call x1, Pallas kernels, down_and_out(): pl.pallas_call(behind(down_kernel, 4, others), grid=(hidden // wide,), in...  27.1 us
    ppermute x9, waiting for transfers between devices, sum_over_chips(): block = lax.ppermute(block, 'ctx', [(i, i ^ 2 * d) for i in range(count)])  27.1 us
  transfers between devices with their start and end apart: 55, of which 25 were waited for; matrix products, arithmetic and copies ran while one was open for 9% of the time, Pallas kernels for 42%

profile of v2, /device:TPU:10, one launch (start us, length us, event | category | flops | bytes accessed | tf_op | source)
XLA Modules:
  0.0 623.3 jit_solution(7674387785336720115)
XLA Ops:
  12.2 3.4 collective-permute-start
  19.5 3.4 collective-permute-start.2
  22.9 6.8 %collective-permute-done.3.refs_4_ = bf16[128,1024]{1,0:T(8,128)(2,1)S(1)} collective-permute-done((bf16[128,1024]{1,0:T(8,128)(2,1)S(1)}, bf16[128,1024]{1,0:T(8,128)(2,1)S(1)}, u32[]{:S(2)}, u32[]{:S(2)}) %collective-permute-start.3) | collective-permute-done | bytes 262176 | tf_op jit(solution)/shard_map/ppermute | solution.py:685
  29.7 3.4 collective-permute-start.4
  34.8 3.4 collective-permute-start.6
  40.1 3.5 collective-permute-done.6
  45.3 6.4 %bias_tiles.1.refs_5_.refs_7_ = bf16[8,9,128,256]{3,2,1,0:T(8,128)(2,1)} custom-call(f32[8,2,1280]{2,1,0:T(2,128)} %reshape.320.vec_ref), custom_call_target="tpu_custom_call" | custom-call | flops 6899999744 | tf_op jit(solution)/shard_map/bias_tiles/pallas_call | solution.py:165
  51.7 3.6 cot_rows.1
  59.8 9.9 %norm_window.1 = (bf16[12,128,1024]{2,1,0:T(8,128)(2,1)}, bf16[4,2,128,1536]{3,2,1,0:T(8,128)(2,1)}) custom-call(bf16[4,128,1024]{2,1,0:T(8,128)(2,1)} %get-tuple-element.264.two_ref, bf16[4,128,1024]{2,1,0:T(8,128)(2,1)} %copy-done.34, bf16[4,128,1024]{2,1,0:T(8,128)(2,1)} %get-tuple-element.262.own_ref.refs_0_, f32[1,1024]{1,0:T(1,128)} %bitcast.157), custom_call_target="tpu_custom_call" | custom-call | flops 11500000256 | tf_op jit(solution)/shard_map/norm_window/pallas_call | solution.py:436
  75.8 4.8 convolution_convert_fusion.1
  80.6 4.8 convolution_convert_fusion
  86.7 14.9 %attend.2 = (bf16[128,1024]{1,0:T(8,128)(2,1)}, bf16[128,1024]{1,0:T(8,128)(2,1)}, f32[8,2,1,256]{3,2,1,0:T(1,128)}) custom-call(s32[1]{0:T(128)} %bitcast.refs_0_.z_ref, s32[2,1,256]{2,1,0:T(1,128)} %bitcast.166, bf16[2,128,1024]{2,1,0:T(8,128)(2,1)} %bitcast.143, bf16[12,128,1024]{2,1,0:T(8,128)(2,1)} %bitcast.169, bf16[12,128,1024]{2,1,0:T(8,128)(2,1)} %bitcast.173, ...), custom_call_target="tpu_custom_call" | custom-call | flops 17020000256 | tf_op jit(solution)/shard_map/attend/pallas_call | solution.py:184
  101.6 3.3 collective-permute-start.12
  104.9 15.6 %collective-permute-done.9.refs_7_.c_ref = bf16[320,1024]{1,0:T(8,128)(2,1)S(1)} collective-permute-done((bf16[320,1024]{1,0:T(8,128)(2,1)}, bf16[320,1024]{1,0:T(8,128)(2,1)S(1)}, u32[]{:S(2)}, u32[]{:S(2)}) %collective-permute-start.9) | collective-permute-done | bytes 655392 | tf_op jit(solution)/shard_map/ppermute | solution.py:685
  121.4 15.0 %attend.3 = (bf16[128,1024]{1,0:T(8,128)(2,1)}, bf16[128,1024]{1,0:T(8,128)(2,1)}, f32[8,2,1,256]{3,2,1,0:T(1,128)}) custom-call(s32[1]{0:T(128)} %bitcast.refs_0_.z_ref, s32[2,1,256]{2,1,0:T(1,128)} %bitcast.167, bf16[2,128,1024]{2,1,0:T(8,128)(2,1)} %bitcast.142, bf16[12,128,1024]{2,1,0:T(8,128)(2,1)} %bitcast.170, bf16[12,128,1024]{2,1,0:T(8,128)(2,1)} %bitcast.174, ...), custom_call_target="tpu_custom_call" | custom-call | flops 17020000256 | tf_op jit(solution)/shard_map/attend/pallas_call | solution.py:184
  140.4 5.4 collective-permute-done.11.refs_6_
  146.7 5.6 hidden_rows.1
  152.2 6.4 %collective-permute-start.16 = (bf16[320,1024]{1,0:T(8,128)(2,1)}, bf16[320,1024]{1,0:T(8,128)(2,1)S(1)}, u32[]{:S(2)}, u32[]{:S(2)}) collective-permute-start(bf16[320,1024]{1,0:T(8,128)(2,1)} %get-tuple-element.116), channel_id=1, source_target_pairs={{0,2},{1,3},{2,0},{3,1},{4,6},{5,7},{6,4},{7,5},{8,10},{9,11},{10,... | collective-permute-start | bytes 1966088 | tf_op jit(solution)/shard_map/ppermute | solution.py:685
  158.6 23.5 %expert.4 = (bf16[320,1024]{1,0:T(8,128)(2,1)}, bf16[1280,1024]{1,0:T(8,128)(2,1)}, bf16[1280,2816]{1,0:T(8,128)(2,1)}, bf16[1280,2816]{1,0:T(8,128)(2,1)}, bf16...) custom-call(s32[1]{0:T(128)} %bitcast.refs_0_.z_ref, ...), custom_call_target="tpu_custom_call" | custom-call | flops 26449999872 | tf_op jit(solution)/shard_map/expert/pallas_call | solution.py:321
  182.1 3.0 moe_rows.1
  187.0 23.3 %expert.5 = (bf16[320,1024]{1,0:T(8,128)(2,1)}, bf16[1280,1024]{1,0:T(8,128)(2,1)}, bf16[1280,2816]{1,0:T(8,128)(2,1)}, bf16[1280,2816]{1,0:T(8,128)(2,1)}, bf16...) custom-call(s32[1]{0:T(128)} %bitcast.refs_0_.z_ref, ...), custom_call_target="tpu_custom_call", output_to_operand_aliasing={{1}: (7, {}), {2}: (8, {}), {3}: (9, {}), {4}: (10, {}), {5... | custom-call | flops 26449999872 | tf_op jit(solution)/shard_map/expert/pallas_call | solution.py:321
  211.2 23.2 %expert.6 = (bf16[320,1024]{1,0:T(8,128)(2,1)}, bf16[1280,1024]{1,0:T(8,128)(2,1)}, bf16[1280,2816]{1,0:T(8,128)(2,1)}, bf16[1280,2816]{1,0:T(8,128)(2,1)}, bf16...) custom-call(s32[1]{0:T(128)} %bitcast.refs_0_.z_ref, ...), custom_call_target="tpu_custom_call", output_to_operand_aliasing={{1}: (7, {}), {2}: (8, {}), {3}: (9, {}), {4}: (10, {}), {5... | custom-call | flops 26449999872 | tf_op jit(solution)/shard_map/expert/pallas_call | solution.py:321
  234.4 3.0 collective-permute-start.17
  238.7 23.2 %expert.7 = (bf16[320,1024]{1,0:T(8,128)(2,1)}, bf16[1280,1024]{1,0:T(8,128)(2,1)}, bf16[1280,2816]{1,0:T(8,128)(2,1)}, bf16[1280,2816]{1,0:T(8,128)(2,1)}, bf16...) custom-call(s32[1]{0:T(128)} %bitcast.refs_0_.z_ref, ...), custom_call_target="tpu_custom_call", output_to_operand_aliasing={{1}: (7, {}), {2}: (8, {}), {3}: (9, {}), {4}: (10, {}), {5... | custom-call | flops 26449999872 | tf_op jit(solution)/shard_map/expert/pallas_call | solution.py:321
  263.9 14.9 %collective-permute-done.18.refs_3_.refs_8_ = bf16[320,1024]{1,0:T(8,128)(2,1)S(1)} collective-permute-done((bf16[320,1024]{1,0:T(8,128)(2,1)S(1)}, bf16[320,1024]{1,0:T(8,128)(2,1)S(1)}, u32[]{:S(2)}, u32[]{:S(2)}) %collective-permute-start.18) | collective-permute-done | bytes 655392 | tf_op jit(solution)/shard_map/ppermute | solution.py:685
  279.6 22.2 %gate_up_grads.1 = (bf16[1024,2816]{1,0:T(8,128)(2,1)}, bf16[1024,2816]{1,0:T(8,128)(2,1)}) custom-call(bf16[1280,1024]{1,0:T(8,128)(2,1)} %get-tuple-element.144.refs_0_, bf16[1280,2816]{1,0:T(8,128)(2,1)} %get-tuple-element.145.refs_1_, bf16[1280,2816]{1,0:T(8,128)(2,1)} %get-tuple-element.146.refs_2_, bf16[320,1024]{1,0:T(8,128)(2,1)} %copy-done.45, ...), custom_call_target="tpu_custom_call" | custom-call | flops 29899999232 | tf_op jit(solution)/shard_map/gate_up_grads/pallas_call | solution.py:362
  302.6 8.7 %middle_rows.1 = (f32[512,1024]{1,0:T(8,128)}, bf16[512,1024]{1,0:T(8,128)(2,1)}, f32[1,1024]{1,0:T(1,128)}, bf16[128,512]{1,0:T(8,128)(2,1)}, bf16[128,512]{1,0...) custom-call(s32[1]{0:T(128)} %bitcast.refs_0_.z_ref, ...), custom_call_target="tpu_custom_call" | custom-call | flops 13799999488 | tf_op jit(solution)/shard_map/middle_rows/pallas_call | solution.py:478
  311.4 27.1 %down_and_out.1 = (bf16[2816,1024]{1,0:T(8,128)(2,1)}, bf16[320,1024]{1,0:T(8,128)(2,1)}, bf16[320,1024]{1,0:T(8,128)(2,1)}, bf16[320,1024]{1,0:T(8,128)(2,1)}, bf16[320,1024]{1,0:T(8,128)(2,1)}) custom-call(bf16[1280,2816]{1,0:T(8,128)(2,1)} %get-tuple-element.138.refs_0_, bf16[1280,1024]{1,0:T(8,128)(2,1)} %get-tuple-element.139.refs_1_, ...), custom_call_target="tpu_custom_call" | custom-call | flops 29899999232 | tf_op jit(solution)/shard_map/down_and_out/pallas_call | solution.py:402
  351.1 4.5 collective-permute-done.23.refs_18_.refs_13_
  358.0 3.6 collective-permute-start.20
  361.7 7.9 %collective-permute-done.28.refs_15_ = bf16[128,512]{1,0:T(8,128)(2,1)S(1)} collective-permute-done((bf16[128,512]{1,0:T(8,128)(2,1)S(1)}, bf16[128,512]{1,0:T(8,128)(2,1)S(1)}, u32[]{:S(2)}, u32[]{:S(2)}) %collective-permute-start.28) | collective-permute-done | bytes 131104 | tf_op jit(solution)/shard_map/ppermute | solution.py:685
  370.3 21.2 %attend_back.2 = (bf16[4,128,512]{2,1,0:T(8,128)(2,1)}, bf16[12,128,512]{2,1,0:T(8,128)(2,1)}, bf16[12,128,512]{2,1,0:T(8,128)(2,1)}, f32[4,2,9,256]{3,2,1,0:T(8,128)}) custom-call(s32[1]{0:T(128)} %bitcast.refs_0_.z_ref, s32[4,1,256]{2,1,0:T(1,128)} %bitcast.164, f32[8,2,1,256]{3,2,1,0:T(1,128)} %get-tuple-element.153.refs_2_, ...), custom_call_target="tpu_custom_call" | custom-call | flops 24149999616 | tf_op jit(solution)/shard_map/attend_back/pallas_call | solution.py:217
  392.6 9.3 %projection_grads.2 = (bf16[4,128,1536]{2,1,0:T(8,128)(2,1)}, bf16[4,128,1536]{2,1,0:T(8,128)(2,1)}) custom-call(s32[1]{0:T(128)} %bitcast.38.refs_0_, bf16[4,2,128,1536]{3,2,1,0:T(8,128)(2,1)} %get-tuple-element.166.refs_1_, bf16[512,512]{1,0:T(8,128)(2,1)} %bitcast.182, bf16[1536,512]{1,0:T(8,128)(2,1)} %bitcast.179, bf16[1536,512]{1,0:T(8,128)(2,1)} %bitcast.180, ...), custom_call_target="tpu_custom_call" | custom-call | flops 10695000064 | tf_op jit(solution)/shard_map/projection_grads/pallas_call | solution.py:655
  409.0 9.7 %input_grads.2.refs_16_.refs_6_ = f32[1536,1024]{1,0:T(8,128)} custom-call(bf16[4,128,512]{2,1,0:T(8,128)(2,1)} %get-tuple-element.163.refs_0_, bf16[12,128,512]{2,1,0:T(8,128)(2,1)} %get-tuple-element.164.refs_1_, bf16[12,128,512]{2,1,0:T(8,128)(2,1)} %get-tuple-element.165.refs_2_, bf16[1024,1024]{1,0:T(8,128)(2,1)} %refs_3_.7, ...), custom_call_target="tpu_custom_call" | custom-call | flops 8049999872 | tf_op jit(solution)/shard_map/input_grads/pallas_call | solution.py:588
  427.2 21.8 %attend_back.3 = (bf16[4,128,512]{2,1,0:T(8,128)(2,1)}, bf16[12,128,512]{2,1,0:T(8,128)(2,1)}, bf16[12,128,512]{2,1,0:T(8,128)(2,1)}, f32[4,2,9,256]{3,2,1,0:T(8,128)}) custom-call(s32[1]{0:T(128)} %bitcast.refs_0_.z_ref, s32[4,1,256]{2,1,0:T(1,128)} %bitcast.165, f32[8,2,1,256]{3,2,1,0:T(1,128)} %get-tuple-element.153.refs_2_, ...), custom_call_target="tpu_custom_call" | custom-call | flops 24149999616 | tf_op jit(solution)/shard_map/attend_back/pallas_call | solution.py:217
  452.4 7.0 %collective-permute-done.36 = bf16[128,1536]{1,0:T(8,128)(2,1)S(1)} collective-permute-done((bf16[128,1536]{1,0:T(8,128)(2,1)S(1)}, bf16[128,1536]{1,0:T(8,128)(2,1)S(1)}, u32[]{:S(2)}, u32[]{:S(2)}) %collective-permute-start.36) | collective-permute-done | bytes 393248 | tf_op jit(solution)/shard_map/ppermute | solution.py:700
  461.4 11.5 %input_grads.3 = (bf16[512,1024]{1,0:T(8,128)(2,1)}, bf16[512,1024]{1,0:T(8,128)(2,1)}, f32[512,1024]{1,0:T(8,128)}, f32[1,1024]{1,0:T(1,128)}) custom-call(bf16[4,128,512]{2,1,0:T(8,128)(2,1)} %get-tuple-element.170.refs_0_, bf16[12,128,512]{2,1,0:T(8,128)(2,1)} %get-tuple-element.171.refs_1_, bf16[12,128,512]{2,1,0:T(8,128)(2,1)} %get-tuple-element.172.refs_2_, ...), custom_call_target="tpu_custom_call" | custom-call | flops 8049999872 | tf_op jit(solution)/shard_map/input_grads/pallas_call | solution.py:588
  475.2 9.4 %projection_grads.3 = (bf16[4,128,1792]{2,1,0:T(8,128)(2,1)}, bf16[4,128,1792]{2,1,0:T(8,128)(2,1)}) custom-call(s32[1]{0:T(128)} %bitcast.38.refs_0_, bf16[4,2,128,1536]{3,2,1,0:T(8,128)(2,1)} %get-tuple-element.166.refs_1_, bf16[512,512]{1,0:T(8,128)(2,1)} %bitcast.181, bf16[1536,512]{1,0:T(8,128)(2,1)} %bitcast.177, bf16[1536,512]{1,0:T(8,128)(2,1)} %bitcast.178, ...), custom_call_target="tpu_custom_call" | custom-call | flops 10695000064 | tf_op jit(solution)/shard_map/projection_grads/pallas_call | solution.py:655
  495.0 3.0 collective-permute-start.43
  499.0 12.7 %collective-permute-done.22.refs_6_ = bf16[320,1024]{1,0:T(8,128)(2,1)S(1)} collective-permute-done((bf16[320,1024]{1,0:T(8,128)(2,1)}, bf16[320,1024]{1,0:T(8,128)(2,1)S(1)}, u32[]{:S(2)}, u32[]{:S(2)}) %collective-permute-start.22) | collective-permute-done | bytes 655392 | tf_op jit(solution)/shard_map/ppermute | solution.py:685
  512.8 5.8 mixed_rows.1.refs_8_
  518.6 5.2 collective-permute-done.43
  525.7 9.3 %collective-permute-done.44 = bf16[128,1792]{1,0:T(8,128)(2,1)S(1)} collective-permute-done((bf16[128,1792]{1,0:T(8,128)(2,1)S(1)}, bf16[128,1792]{1,0:T(8,128)(2,1)S(1)}, u32[]{:S(2)}, u32[]{:S(2)}) %collective-permute-start.44) | collective-permute-done | bytes 458784 | tf_op jit(solution)/shard_map/ppermute | solution.py:700
  540.9 6.6 %collective-permute-done.41.refs_6_ = bf16[128,1024]{1,0:T(8,128)(2,1)S(1)} collective-permute-done((bf16[128,1024]{1,0:T(8,128)(2,1)S(1)}, bf16[128,1024]{1,0:T(8,128)(2,1)S(1)}, u32[]{:S(2)}, u32[]{:S(2)}) %collective-permute-start.41) | collective-permute-done | bytes 262176 | tf_op jit(solution)/shard_map/ppermute | solution.py:675
  547.5 8.0 %collective-permute-done.42.refs_7_ = bf16[128,1024]{1,0:T(8,128)(2,1)S(1)} collective-permute-done((bf16[128,1024]{1,0:T(8,128)(2,1)S(1)}, bf16[128,1024]{1,0:T(8,128)(2,1)S(1)}, u32[]{:S(2)}, u32[]{:S(2)}) %collective-permute-start.42) | collective-permute-done | bytes 262176 | tf_op jit(solution)/shard_map/ppermute | solution.py:675
  556.2 4.4 tail_rows.1
  572.9 15.8 %collective-permute-done.47.refs_4_ = bf16[128,1024]{1,0:T(8,128)(2,1)S(1)} collective-permute-done((bf16[128,1024]{1,0:T(8,128)(2,1)}, bf16[128,1024]{1,0:T(8,128)(2,1)S(1)}, u32[]{:S(2)}, u32[]{:S(2)}) %collective-permute-start.47) | collective-permute-done | bytes 262176 | tf_op jit(solution)/shard_map/ppermute | solution.py:685
  588.7 9.0 %collective-permute-done.48.refs_5_ = bf16[128,1024]{1,0:T(8,128)(2,1)S(1)} collective-permute-done((bf16[128,1024]{1,0:T(8,128)(2,1)}, bf16[128,1024]{1,0:T(8,128)(2,1)S(1)}, u32[]{:S(2)}, u32[]{:S(2)}) %collective-permute-start.48) | collective-permute-done | bytes 262176 | tf_op jit(solution)/shard_map/ppermute | solution.py:685
  (307 shorter events, 131.5 us)
Async XLA Ops:
  7.3 602.2 %reduce-scatter.8.cloned.1.call-start = ((), (), s32[]{:S(2)}) async-start(), calls=%async_computation.5 | async-start | bytes 6488064 | tf_op jit(solution)/shard_map/reduce_scatter | solution.py:839
  9.1 20.6 %collective-permute-start.3 = (bf16[128,1024]{1,0:T(8,128)(2,1)S(1)}, bf16[128,1024]{1,0:T(8,128)(2,1)S(1)}, u32[]{:S(2)}, u32[]{:S(2)}) collective-permute-start(bf16[128,1024]{1,0:T(8,128)(2,1)S(1)} %get-tuple-element.266), channel_id=1, source_target_pairs={{0,2},{1,3},{2,0},{3,1},{4,6},{5,7},{6,4},{7,5},{8,10},{9,11},{10,... | collective-permute-start | bytes 786440 | tf_op jit(solution)/shard_map/ppermute | solution.py:685
  11.7 23.1 %collective-permute-start.5 = (bf16[128,1024]{1,0:T(8,128)(2,1)S(1)}, bf16[128,1024]{1,0:T(8,128)(2,1)S(1)}, u32[]{:S(2)}, u32[]{:S(2)}) collective-permute-start(bf16[128,1024]{1,0:T(8,128)(2,1)S(1)} %get-tuple-element.268), channel_id=1, source_target_pairs={{0,3},{1,2},{2,1},{3,0},{4,7},{5,6},{6,5},{7,4},{8,11},{9,10},{10,... | collective-permute-start | bytes 786440 | tf_op jit(solution)/shard_map/ppermute | solution.py:685
  12.2 27.9 %collective-permute-start = (bf16[128,1024]{1,0:T(8,128)(2,1)S(1)}, bf16[128,1024]{1,0:T(8,128)(2,1)S(1)}, u32[]{:S(2)}, u32[]{:S(2)}) collective-permute-start(bf16[128,1024]{1,0:T(8,128)(2,1)S(1)} %bitcast.139), channel_id=1, source_target_pairs={{0,8},{4,12},{8,16},{12,20},{16,24},{20,28},{1,9},{5,13},{9,17},{1... | collective-permute-start | bytes 786440 | tf_op jit(solution)/shard_map/ppermute | solution.py:675
  19.5 20.5 %collective-permute-start.2 = (bf16[128,1024]{1,0:T(8,128)(2,1)S(1)}, bf16[128,1024]{1,0:T(8,128)(2,1)S(1)}, u32[]{:S(2)}, u32[]{:S(2)}) collective-permute-start(bf16[128,1024]{1,0:T(8,128)(2,1)S(1)} %collective-permute-done.1.refs_3_), channel_id=1, source_target_pairs={{0,8},{4,12},{8,16},{12,20},{16,24},{20,28},{1,9},{5,13},{9,17},{1... | collective-permute-start | bytes 786440 | tf_op jit(solution)/shard_map/ppermute | solution.py:675
  45.2 13.6 %collective-permute-start.7 = (bf16[4,128,1024]{2,1,0:T(8,128)(2,1)S(1)}, bf16[4,128,1024]{2,1,0:T(8,128)(2,1)S(1)}, u32[]{:S(2)}, u32[]{:S(2)}) collective-permute-start(bf16[4,128,1024]{2,1,0:T(8,128)(2,1)S(1)} %get-tuple-element.263), channel_id=1, source_target_pairs={{0,4},{4,0},{8,12},{12,8},{16,20},{20,16},{24,28},{28,24},{1,5},{5... | collective-permute-start | bytes 3145736 | tf_op jit(solution)/shard_map/ppermute | solution.py:679
  55.3 30.6 %collective-permute-start.8 = (bf16[320,1024]{1,0:T(8,128)(2,1)}, bf16[320,1024]{1,0:T(8,128)(2,1)S(1)}, u32[]{:S(2)}, u32[]{:S(2)}) collective-permute-start(bf16[320,1024]{1,0:T(8,128)(2,1)} %get-tuple-element.102), channel_id=1, source_target_pairs={{0,2},{1,3},{2,0},{3,1},{4,6},{5,7},{6,4},{7,5},{8,10},{9,11},{10,... | collective-permute-start | bytes 1966088 | tf_op jit(solution)/shard_map/ppermute | solution.py:685
  56.5 48.4 %collective-permute-start.10 = (bf16[320,1024]{1,0:T(8,128)(2,1)}, bf16[320,1024]{1,0:T(8,128)(2,1)S(1)}, u32[]{:S(2)}, u32[]{:S(2)}) collective-permute-start(bf16[320,1024]{1,0:T(8,128)(2,1)} %get-tuple-element.105), channel_id=1, source_target_pairs={{0,1},{1,0},{2,3},{3,2},{4,5},{5,4},{6,7},{7,6},{8,9},{9,8},{10,11... | collective-permute-start | bytes 1966088 | tf_op jit(solution)/shard_map/ppermute | solution.py:685
  58.3 62.2 %collective-permute-start.9 = (bf16[320,1024]{1,0:T(8,128)(2,1)}, bf16[320,1024]{1,0:T(8,128)(2,1)S(1)}, u32[]{:S(2)}, u32[]{:S(2)}) collective-permute-start(bf16[320,1024]{1,0:T(8,128)(2,1)} %get-tuple-element.104), channel_id=1, source_target_pairs={{0,3},{1,2},{2,1},{3,0},{4,7},{5,6},{6,5},{7,4},{8,11},{9,10},{10,... | collective-permute-start | bytes 1966088 | tf_op jit(solution)/shard_map/ppermute | solution.py:685
  101.6 44.1 %collective-permute-start.12 = (bf16[128,1024]{1,0:T(8,128)(2,1)}, bf16[128,1024]{1,0:T(8,128)(2,1)S(1)}, u32[]{:S(2)}, u32[]{:S(2)}) collective-permute-start(bf16[128,1024]{1,0:T(8,128)(2,1)} %get-tuple-element.103.refs_6_.refs_10_), channel_id=1, source_target_pairs={{0,2},{1,3},{2,0},{3,1},{4,6},{5,7},{6,4},{7,5},{8,10},{9,11},{10,... | collective-permute-start | bytes 786440 | tf_op jit(solution)/shard_map/ppermute | solution.py:685
  152.2 34.0 %collective-permute-start.16 = (bf16[320,1024]{1,0:T(8,128)(2,1)}, bf16[320,1024]{1,0:T(8,128)(2,1)S(1)}, u32[]{:S(2)}, u32[]{:S(2)}) collective-permute-start(bf16[320,1024]{1,0:T(8,128)(2,1)} %get-tuple-element.116), channel_id=1, source_target_pairs={{0,2},{1,3},{2,0},{3,1},{4,6},{5,7},{6,4},{7,5},{8,10},{9,11},{10,... | collective-permute-start | bytes 1966088 | tf_op jit(solution)/shard_map/ppermute | solution.py:685
  185.1 25.3 %collective-permute-start.15 = (bf16[320,1024]{1,0:T(8,128)(2,1)}, bf16[320,1024]{1,0:T(8,128)(2,1)S(1)}, u32[]{:S(2)}, u32[]{:S(2)}) collective-permute-start(bf16[320,1024]{1,0:T(8,128)(2,1)} %get-tuple-element.115), channel_id=1, source_target_pairs={{0,1},{1,0},{2,3},{3,2},{4,5},{5,4},{6,7},{7,6},{8,9},{9,8},{10,11... | collective-permute-start | bytes 1966088 | tf_op jit(solution)/shard_map/ppermute | solution.py:685
  185.1 52.7 %collective-permute-start.14 = (bf16[320,1024]{1,0:T(8,128)(2,1)}, bf16[320,1024]{1,0:T(8,128)(2,1)S(1)}, u32[]{:S(2)}, u32[]{:S(2)}) collective-permute-start(bf16[320,1024]{1,0:T(8,128)(2,1)} %get-tuple-element.114), channel_id=1, source_target_pairs={{0,3},{1,2},{2,1},{3,0},{4,7},{5,6},{6,5},{7,4},{8,11},{9,10},{10,... | collective-permute-start | bytes 1966088 | tf_op jit(solution)/shard_map/ppermute | solution.py:685
  234.4 29.5 %collective-permute-start.17 = (bf16[320,1024]{1,0:T(8,128)(2,1)}, bf16[320,1024]{1,0:T(8,128)(2,1)S(1)}, u32[]{:S(2)}, u32[]{:S(2)}) collective-permute-start(bf16[320,1024]{1,0:T(8,128)(2,1)} %get-tuple-element.141), channel_id=1, source_target_pairs={{0,1},{1,0},{2,3},{3,2},{4,5},{5,4},{6,7},{7,6},{8,9},{9,8},{10,11... | collective-permute-start | bytes 1966088 | tf_op jit(solution)/shard_map/ppermute | solution.py:685
  237.4 41.4 %collective-permute-start.18 = (bf16[320,1024]{1,0:T(8,128)(2,1)S(1)}, bf16[320,1024]{1,0:T(8,128)(2,1)S(1)}, u32[]{:S(2)}, u32[]{:S(2)}) collective-permute-start(bf16[320,1024]{1,0:T(8,128)(2,1)S(1)} %copy-done.42), channel_id=1, source_target_pairs={{0,2},{1,3},{2,0},{3,1},{4,6},{5,7},{6,4},{7,5},{8,10},{9,11},{10,... | collective-permute-start | bytes 1966088 | tf_op jit(solution)/shard_map/ppermute | solution.py:685
  261.9 39.9 %collective-permute-start.19 = (bf16[320,1024]{1,0:T(8,128)(2,1)}, bf16[320,1024]{1,0:T(8,128)(2,1)S(1)}, u32[]{:S(2)}, u32[]{:S(2)}) collective-permute-start(bf16[320,1024]{1,0:T(8,128)(2,1)} %get-tuple-element.143), channel_id=1, source_target_pairs={{0,3},{1,2},{2,1},{3,0},{4,7},{5,6},{6,5},{7,4},{8,11},{9,10},{10,... | collective-permute-start | bytes 1966088 | tf_op jit(solution)/shard_map/ppermute | solution.py:685
  338.5 273.4 %reduce-scatter.6.cloned.1.call-start = ((), (), s32[]{:S(2)}) async-start(), calls=%async_computation.4 | async-start | bytes 6488064 | tf_op jit(solution)/shard_map/reduce_scatter | solution.py:839
  338.6 23.0 %collective-permute-start.25 = (bf16[128,512]{1,0:T(8,128)(2,1)}, bf16[128,512]{1,0:T(8,128)(2,1)S(1)}, u32[]{:S(2)}, u32[]{:S(2)}) collective-permute-start(bf16[128,512]{1,0:T(8,128)(2,1)} %get-tuple-element.148.refs_4_), channel_id=1, source_target_pairs={{0,3},{1,2},{2,1},{3,0},{4,7},{5,6},{6,5},{7,4},{8,11},{9,10},{10,... | collective-permute-start | bytes 393224 | tf_op jit(solution)/shard_map/ppermute | solution.py:685
  340.8 14.9 %collective-permute-start.23 = (bf16[128,512]{1,0:T(8,128)(2,1)S(1)}, bf16[128,512]{1,0:T(8,128)(2,1)S(1)}, u32[]{:S(2)}, u32[]{:S(2)}) collective-permute-start(bf16[128,512]{1,0:T(8,128)(2,1)S(1)} %copy-done.66), channel_id=1, source_target_pairs={{0,1},{1,0},{2,3},{3,2},{4,5},{5,4},{6,7},{7,6},{8,9},{9,8},{10,11... | collective-permute-start | bytes 393224 | tf_op jit(solution)/shard_map/ppermute | solution.py:685
  343.6 14.3 %collective-permute-start.24 = (bf16[128,512]{1,0:T(8,128)(2,1)}, bf16[128,512]{1,0:T(8,128)(2,1)S(1)}, u32[]{:S(2)}, u32[]{:S(2)}) collective-permute-start(bf16[128,512]{1,0:T(8,128)(2,1)} %get-tuple-element.157), channel_id=1, source_target_pairs={{0,2},{1,3},{2,0},{3,1},{4,6},{5,7},{6,4},{7,5},{8,10},{9,11},{10,... | collective-permute-start | bytes 393224 | tf_op jit(solution)/shard_map/ppermute | solution.py:685
  345.1 16.6 %collective-permute-start.26 = (bf16[128,512]{1,0:T(8,128)(2,1)}, bf16[128,512]{1,0:T(8,128)(2,1)}, u32[]{:S(2)}, u32[]{:S(2)}) collective-permute-start(bf16[128,512]{1,0:T(8,128)(2,1)} %get-tuple-element.159), channel_id=1, source_target_pairs={{0,1},{1,0},{2,3},{3,2},{4,5},{5,4},{6,7},{7,6},{8,9},{9,8},{10,11... | collective-permute-start | bytes 393224 | tf_op jit(solution)/shard_map/ppermute | solution.py:685
  347.1 14.6 %collective-permute-start.27 = (bf16[128,512]{1,0:T(8,128)(2,1)}, bf16[128,512]{1,0:T(8,128)(2,1)}, u32[]{:S(2)}, u32[]{:S(2)}) collective-permute-start(bf16[128,512]{1,0:T(8,128)(2,1)} %get-tuple-element.160), channel_id=1, source_target_pairs={{0,2},{1,3},{2,0},{3,1},{4,6},{5,7},{6,4},{7,5},{8,10},{9,11},{10,... | collective-permute-start | bytes 393224 | tf_op jit(solution)/shard_map/ppermute | solution.py:685
  347.1 267.0 %reduce-scatter.4.cloned.1.call-start = ((), (), s32[]{:S(2)}) async-start(), calls=%async_computation.3 | async-start | bytes 6488064 | tf_op jit(solution)/shard_map/reduce_scatter | solution.py:839
  355.7 14.0 %collective-permute-start.28 = (bf16[128,512]{1,0:T(8,128)(2,1)S(1)}, bf16[128,512]{1,0:T(8,128)(2,1)S(1)}, u32[]{:S(2)}, u32[]{:S(2)}) collective-permute-start(bf16[128,512]{1,0:T(8,128)(2,1)S(1)} %copy-done.65), channel_id=1, source_target_pairs={{0,3},{1,2},{2,1},{3,0},{4,7},{5,6},{6,5},{7,4},{8,11},{9,10},{10,... | collective-permute-start | bytes 393224 | tf_op jit(solution)/shard_map/ppermute | solution.py:685
  358.0 33.5 %collective-permute-start.20 = (bf16[320,1024]{1,0:T(8,128)(2,1)S(1)}, bf16[320,1024]{1,0:T(8,128)(2,1)S(1)}, u32[]{:S(2)}, u32[]{:S(2)}) collective-permute-start(bf16[320,1024]{1,0:T(8,128)(2,1)S(1)} %copy-done.39), channel_id=1, source_target_pairs={{0,1},{1,0},{2,3},{3,2},{4,5},{5,4},{6,7},{7,6},{8,9},{9,8},{10,11... | collective-permute-start | bytes 1966088 | tf_op jit(solution)/shard_map/ppermute | solution.py:685
  361.6 30.0 %collective-permute-start.21 = (bf16[320,1024]{1,0:T(8,128)(2,1)S(1)}, bf16[320,1024]{1,0:T(8,128)(2,1)S(1)}, u32[]{:S(2)}, u32[]{:S(2)}) collective-permute-start(bf16[320,1024]{1,0:T(8,128)(2,1)S(1)} %copy-done.38), channel_id=1, source_target_pairs={{0,2},{1,3},{2,0},{3,1},{4,6},{5,7},{6,4},{7,5},{8,10},{9,11},{10,... | collective-permute-start | bytes 1966088 | tf_op jit(solution)/shard_map/ppermute | solution.py:685
  361.7 42.1 %collective-permute-start.29 = (bf16[4,128,1024]{2,1,0:T(8,128)(2,1)S(1)}, bf16[4,128,1024]{2,1,0:T(8,128)(2,1)}, u32[]{:S(2)}, u32[]{:S(2)}) collective-permute-start(bf16[4,128,1024]{2,1,0:T(8,128)(2,1)S(1)} %dynamic-slice_bitcast_fusion), channel_id=1, source_target_pairs={{0,4},{4,0},{8,12},{12,8},{16,20},{20,16},{24,28},{28,24},{1,5},{5... | collective-permute-start | bytes 3145736 | tf_op jit(solution)/shard_map/ppermute | solution.py:679
  401.9 19.7 %collective-permute-start.33 = (bf16[4,128,1536]{2,1,0:T(8,128)(2,1)}, bf16[4,128,1536]{2,1,0:T(8,128)(2,1)}, u32[]{:S(2)}, u32[]{:S(2)}) collective-permute-start(bf16[4,128,1536]{2,1,0:T(8,128)(2,1)} %get-tuple-element.167.refs_6_), channel_id=1, source_target_pairs={{0,4},{4,0},{8,12},{12,8},{16,20},{20,16},{24,28},{28,24},{1,5},{5... | collective-permute-start | bytes 4718600 | tf_op jit(solution)/shard_map/ppermute | solution.py:679
  405.4 13.2 %collective-permute-start.30 = (bf16[128,1024]{1,0:T(8,128)(2,1)S(1)}, bf16[128,1024]{1,0:T(8,128)(2,1)S(1)}, u32[]{:S(2)}, u32[]{:S(2)}) collective-permute-start(bf16[128,1024]{1,0:T(8,128)(2,1)S(1)} %get-tuple-element.257), channel_id=1, source_target_pairs={{0,24},{4,28},{8,16},{12,20},{16,8},{20,12},{24,0},{28,4},{1,25},{... | collective-permute-start | bytes 786440 | tf_op jit(solution)/shard_map/ppermute | solution.py:700
  407.9 12.8 %collective-permute-start.31 = (bf16[128,1024]{1,0:T(8,128)(2,1)S(1)}, bf16[128,1024]{1,0:T(8,128)(2,1)S(1)}, u32[]{:S(2)}, u32[]{:S(2)}) collective-permute-start(bf16[128,1024]{1,0:T(8,128)(2,1)S(1)} %get-tuple-element.259), channel_id=1, source_target_pairs={{0,16},{4,20},{8,24},{12,28},{16,0},{20,4},{24,8},{28,12},{1,17},{... | collective-permute-start | bytes 786440 | tf_op jit(solution)/shard_map/ppermute | solution.py:700
  407.9 12.8 %collective-permute-start.32 = (bf16[128,1024]{1,0:T(8,128)(2,1)S(1)}, bf16[128,1024]{1,0:T(8,128)(2,1)S(1)}, u32[]{:S(2)}, u32[]{:S(2)}) collective-permute-start(bf16[128,1024]{1,0:T(8,128)(2,1)S(1)} %get-tuple-element.258), channel_id=1, source_target_pairs={{0,8},{4,12},{8,0},{12,4},{16,24},{20,28},{24,16},{28,20},{1,9},{5... | collective-permute-start | bytes 786440 | tf_op jit(solution)/shard_map/ppermute | solution.py:700
  423.6 27.2 %collective-permute-start.34 = (bf16[128,1536]{1,0:T(8,128)(2,1)S(1)}, bf16[128,1536]{1,0:T(8,128)(2,1)S(1)}, u32[]{:S(2)}, u32[]{:S(2)}) collective-permute-start(bf16[128,1536]{1,0:T(8,128)(2,1)S(1)} %get-tuple-element.247), channel_id=1, source_target_pairs={{0,24},{4,28},{8,16},{12,20},{16,8},{20,12},{24,0},{28,4},{1,25},{... | collective-permute-start | bytes 1179656 | tf_op jit(solution)/shard_map/ppermute | solution.py:700
  425.4 27.0 %collective-permute-start.35 = (bf16[128,1536]{1,0:T(8,128)(2,1)S(1)}, bf16[128,1536]{1,0:T(8,128)(2,1)S(1)}, u32[]{:S(2)}, u32[]{:S(2)}) collective-permute-start(bf16[128,1536]{1,0:T(8,128)(2,1)S(1)} %get-tuple-element.249), channel_id=1, source_target_pairs={{0,16},{4,20},{8,24},{12,28},{16,0},{20,4},{24,8},{28,12},{1,17},{... | collective-permute-start | bytes 1179656 | tf_op jit(solution)/shard_map/ppermute | solution.py:700
  426.7 32.7 %collective-permute-start.36 = (bf16[128,1536]{1,0:T(8,128)(2,1)S(1)}, bf16[128,1536]{1,0:T(8,128)(2,1)S(1)}, u32[]{:S(2)}, u32[]{:S(2)}) collective-permute-start(bf16[128,1536]{1,0:T(8,128)(2,1)S(1)} %get-tuple-element.248), channel_id=1, source_target_pairs={{0,8},{4,12},{8,0},{12,4},{16,24},{20,28},{24,16},{28,20},{1,9},{5... | collective-permute-start | bytes 1179656 | tf_op jit(solution)/shard_map/ppermute | solution.py:700
  475.2 11.1 %collective-permute-start.37 = (bf16[512,1024]{1,0:T(8,128)(2,1)}, bf16[512,1024]{1,0:T(8,128)(2,1)S(1)}, u32[]{:S(2)}, u32[]{:S(2)}) collective-permute-start(bf16[512,1024]{1,0:T(8,128)(2,1)} %get-tuple-element.174), channel_id=1, source_target_pairs={{0,4},{4,0},{8,12},{12,8},{16,20},{20,16},{24,28},{28,24},{1,5},{5... | collective-permute-start | bytes 3145736 | tf_op jit(solution)/shard_map/ppermute | solution.py:679
  485.1 26.5 %collective-permute-start.22 = (bf16[320,1024]{1,0:T(8,128)(2,1)}, bf16[320,1024]{1,0:T(8,128)(2,1)S(1)}, u32[]{:S(2)}, u32[]{:S(2)}) collective-permute-start(bf16[320,1024]{1,0:T(8,128)(2,1)} %get-tuple-element.152), channel_id=1, source_target_pairs={{0,3},{1,2},{2,1},{3,0},{4,7},{5,6},{6,5},{7,4},{8,11},{9,10},{10,... | collective-permute-start | bytes 1966088 | tf_op jit(solution)/shard_map/ppermute | solution.py:685
  488.8 52.1 %collective-permute-start.39 = (bf16[128,1024]{1,0:T(8,128)(2,1)}, bf16[128,1024]{1,0:T(8,128)(2,1)}, u32[]{:S(2)}, u32[]{:S(2)}) collective-permute-start(bf16[128,1024]{1,0:T(8,128)(2,1)} %get-tuple-element.256), channel_id=1, source_target_pairs={{8,0},{12,4},{16,8},{20,12},{24,16},{28,20},{9,1},{13,5},{17,9},{2... | collective-permute-start | bytes 786440 | tf_op jit(solution)/shard_map/ppermute | solution.py:675
  491.2 49.7 %collective-permute-start.40 = (bf16[128,1024]{1,0:T(8,128)(2,1)}, bf16[128,1024]{1,0:T(8,128)(2,1)}, u32[]{:S(2)}, u32[]{:S(2)}) collective-permute-start(bf16[128,1024]{1,0:T(8,128)(2,1)} %get-tuple-element.255), channel_id=1, source_target_pairs={{8,0},{12,4},{16,8},{20,12},{24,16},{28,20},{9,1},{13,5},{17,9},{2... | collective-permute-start | bytes 786440 | tf_op jit(solution)/shard_map/ppermute | solution.py:675
  495.0 28.8 %collective-permute-start.43 = (bf16[128,1792]{1,0:T(8,128)(2,1)S(1)}, bf16[128,1792]{1,0:T(8,128)(2,1)S(1)}, u32[]{:S(2)}, u32[]{:S(2)}) collective-permute-start(bf16[128,1792]{1,0:T(8,128)(2,1)S(1)} %get-tuple-element.244), channel_id=1, source_target_pairs={{0,24},{4,28},{8,16},{12,20},{16,8},{20,12},{24,0},{28,4},{1,25},{... | collective-permute-start | bytes 1376264 | tf_op jit(solution)/shard_map/ppermute | solution.py:700
  497.9 37.0 %collective-permute-start.44 = (bf16[128,1792]{1,0:T(8,128)(2,1)S(1)}, bf16[128,1792]{1,0:T(8,128)(2,1)S(1)}, u32[]{:S(2)}, u32[]{:S(2)}) collective-permute-start(bf16[128,1792]{1,0:T(8,128)(2,1)S(1)} %get-tuple-element.246), channel_id=1, source_target_pairs={{0,16},{4,20},{8,24},{12,28},{16,0},{20,4},{24,8},{28,12},{1,17},{... | collective-permute-start | bytes 1376264 | tf_op jit(solution)/shard_map/ppermute | solution.py:700
  511.7 27.2 %collective-permute-start.45 = (bf16[128,1792]{1,0:T(8,128)(2,1)S(1)}, bf16[128,1792]{1,0:T(8,128)(2,1)S(1)}, u32[]{:S(2)}, u32[]{:S(2)}) collective-permute-start(bf16[128,1792]{1,0:T(8,128)(2,1)S(1)} %get-tuple-element.245), channel_id=1, source_target_pairs={{0,8},{4,12},{8,0},{12,4},{16,24},{20,28},{24,16},{28,20},{1,9},{5... | collective-permute-start | bytes 1376264 | tf_op jit(solution)/shard_map/ppermute | solution.py:700
  523.8 23.7 %collective-permute-start.41 = (bf16[128,1024]{1,0:T(8,128)(2,1)S(1)}, bf16[128,1024]{1,0:T(8,128)(2,1)S(1)}, u32[]{:S(2)}, u32[]{:S(2)}) collective-permute-start(bf16[128,1024]{1,0:T(8,128)(2,1)S(1)} %get-tuple-element.254), channel_id=1, source_target_pairs={{8,0},{12,4},{16,8},{20,12},{24,16},{28,20},{9,1},{13,5},{17,9},{2... | collective-permute-start | bytes 786440 | tf_op jit(solution)/shard_map/ppermute | solution.py:675
  535.0 20.5 %collective-permute-start.42 = (bf16[128,1024]{1,0:T(8,128)(2,1)S(1)}, bf16[128,1024]{1,0:T(8,128)(2,1)S(1)}, u32[]{:S(2)}, u32[]{:S(2)}) collective-permute-start(bf16[128,1024]{1,0:T(8,128)(2,1)S(1)} %get-tuple-element.253), channel_id=1, source_target_pairs={{8,0},{12,4},{16,8},{20,12},{24,16},{28,20},{9,1},{13,5},{17,9},{2... | collective-permute-start | bytes 786440 | tf_op jit(solution)/shard_map/ppermute | solution.py:675
  560.6 28.1 %collective-permute-start.47 = (bf16[128,1024]{1,0:T(8,128)(2,1)}, bf16[128,1024]{1,0:T(8,128)(2,1)S(1)}, u32[]{:S(2)}, u32[]{:S(2)}) collective-permute-start(bf16[128,1024]{1,0:T(8,128)(2,1)} %get-tuple-element.186), channel_id=1, source_target_pairs={{0,2},{1,3},{2,0},{3,1},{4,6},{5,7},{6,4},{7,5},{8,10},{9,11},{10,... | collective-permute-start | bytes 786440 | tf_op jit(solution)/shard_map/ppermute | solution.py:685
  562.5 35.2 %collective-permute-start.48 = (bf16[128,1024]{1,0:T(8,128)(2,1)}, bf16[128,1024]{1,0:T(8,128)(2,1)S(1)}, u32[]{:S(2)}, u32[]{:S(2)}) collective-permute-start(bf16[128,1024]{1,0:T(8,128)(2,1)} %get-tuple-element.187), channel_id=1, source_target_pairs={{0,3},{1,2},{2,1},{3,0},{4,7},{5,6},{6,5},{7,4},{8,11},{9,10},{10,... | collective-permute-start | bytes 786440 | tf_op jit(solution)/shard_map/ppermute | solution.py:685
  564.2 39.4 %collective-permute-start.49 = (bf16[32,4352]{1,0:T(8,128)(2,1)S(1)}, bf16[32,4352]{1,0:T(8,128)(2,1)S(1)}, u32[]{:S(2)}, u32[]{:S(2)}) collective-permute-start(bf16[32,4352]{1,0:T(8,128)(2,1)S(1)} %get-tuple-element.250), channel_id=1, source_target_pairs={{0,3},{1,2},{2,1},{3,0},{4,7},{5,6},{6,5},{7,4},{8,11},{9,10},{10,... | collective-permute-start | bytes 835592 | tf_op jit(solution)/shard_map/ppermute | solution.py:685
  564.8 40.5 %collective-permute-start.50 = (bf16[32,4352]{1,0:T(8,128)(2,1)S(1)}, bf16[32,4352]{1,0:T(8,128)(2,1)S(1)}, u32[]{:S(2)}, u32[]{:S(2)}) collective-permute-start(bf16[32,4352]{1,0:T(8,128)(2,1)S(1)} %get-tuple-element.252), channel_id=1, source_target_pairs={{0,2},{1,3},{2,0},{3,1},{4,6},{5,7},{6,4},{7,5},{8,10},{9,11},{10,... | collective-permute-start | bytes 835592 | tf_op jit(solution)/shard_map/ppermute | solution.py:685
  570.1 35.2 %collective-permute-start.51 = (bf16[32,4352]{1,0:T(8,128)(2,1)S(1)}, bf16[32,4352]{1,0:T(8,128)(2,1)S(1)}, u32[]{:S(2)}, u32[]{:S(2)}) collective-permute-start(bf16[32,4352]{1,0:T(8,128)(2,1)S(1)} %get-tuple-element.251), channel_id=1, source_target_pairs={{0,1},{1,0},{2,3},{3,2},{4,5},{5,4},{6,7},{7,6},{8,9},{9,8},{10,11... | collective-permute-start | bytes 835592 | tf_op jit(solution)/shard_map/ppermute | solution.py:685
  (75 other events, 666.2 us)
Sparse Core Ops, SparseCore 0:
  338.6 61.5 reduce-scatter.7
  404.1 72.7 reduce-scatter.5
  485.2 75.6 reduce-scatter.3

commit v3 on v2

--- a/solution.py
+++ b/solution.py
@@ -160,18 +160,18 @@
             tab_ref[0, h, a : a + 1, :] = pltpu.roll(part, TILE, 1)
 
 
-def bias_tiles(vec):
+def bias_tiles(vec, others=()):
     pairs = vec.shape[0]
     return pl.pallas_call(
-        bias_kernel,
+        behind(bias_kernel, 1, others),
         grid=(pairs,),
-        in_specs=[pl.BlockSpec((1, 2, vec.shape[2]), lambda g: (g, 0, 0))],
+        in_specs=[pl.BlockSpec((1, 2, vec.shape[2]), lambda g: (g, 0, 0))] + anywhere(others),
         out_specs=pl.BlockSpec((1, TILES_SEEN, TILE, 2 * TILE), lambda g: (g, 0, 0, 0)),
         out_shape=jax.ShapeDtypeStruct((pairs, TILES_SEEN, TILE, 2 * TILE), bf16),
         compiler_params=pltpu.CompilerParams(vmem_limit_bytes=VMEM),
         cost_estimate=cost(6),
         name="bias_tiles",
-    )(vec)
+    )(vec, *others)
 
 
 SMEM = pl.BlockSpec(memory_space=pltpu.SMEM)
@@ -226,7 +226,7 @@
             pl.BlockSpec((1, TILES_SEEN, TILE, 2 * TILE), lambda g: (base + g, 0, 0, 0)),
         ]
         + [pl.BlockSpec((TILE, TILE), lambda g: (0, base + g))] * pieces
-        + [pl.BlockSpec((TILE, TILE), lambda g: (0, g))] * pieces
+        + [pl.BlockSpec((TILE, TILE), lambda g: (0, base + g))] * pieces
         + anywhere(others),
         out_specs=[
             alone(pieces), alone(blocks), alone(blocks),
@@ -260,16 +260,22 @@
     return v * half, half + 0.5 * v * (1.0 - t * t) * (c * (1.0 + 3.0 * 0.044715 * v * v))
 
 
-def expert_kernel(
-    experts, held, z_ref, x_ref, c_ref, wg_ref, wu_ref, wd_ref, wr_ref, *refs,
-):
-    gin_ref, kept_ref, act_ref, dgp_ref, dup_ref, gcot_ref, gate_out, glog_ref, acc_ref, gg_ref, rp_ref, gate_ref = refs[held:]
+def expert_kernel(experts, count, held, z_ref, *refs):
+    x_refs, c_refs, (wg_ref, wu_ref, wd_ref, wr_ref) = refs[:count], refs[count : 2 * count], refs[2 * count : 2 * count + 4]
+    refs = refs[2 * count + 4 + held :]
+    gin_refs, refs = refs[:count], refs[count:]
+    kept_ref, act_ref, dgp_ref, dup_ref, gcot_ref, gate_out, glog_ref, acc_ref, gg_ref, rp_ref, gate_ref, xs_ref, cs_ref = refs
     step = pl.program_id(0)
-    lane = lax.broadcasted_iota(jnp.int32, (x_ref.shape[0], TILE), 1)
-    x, c = x_ref[...], c_ref[...]
+    rows = xs_ref.shape[0]
+    lane = lax.broadcasted_iota(jnp.int32, (rows, TILE), 1)
 
     @pl.when(step == 0)
     def _():
+        for n in range(count):
+            part = slice(n * rows // count, (n + 1) * rows // count)
+            xs_ref[part, :] = x_refs[n][...]
+            cs_ref[part, :] = c_refs[n][...]
+        x = xs_ref[...]
         logits = jnp.where(lane < experts, dot(x, wr_ref[...]), NEG)
         e = jnp.exp(logits - jnp.max(logits, axis=1, keepdims=True))
         probs = e / jnp.sum(e, axis=1, keepdims=True)
@@ -278,10 +284,11 @@
         gate_ref[...] = jnp.broadcast_to(gate, gate_ref.shape)
         gate_out[...] = gate_ref[...]
         kept_ref[...] = x
-        gcot_ref[...] = (gate * c.astype(f32)).astype(bf16)
+        gcot_ref[...] = (gate * cs_ref[...].astype(f32)).astype(bf16)
         acc_ref[...] = jnp.zeros_like(acc_ref)
         gg_ref[...] = jnp.zeros_like(gg_ref)
 
+    x, c = xs_ref[...], cs_ref[...]
     raw = dot_nt(c, wd_ref[0])
     gate_pre = dot(x, wg_ref[0])
     up_pre = dot(x, wu_ref[0])
@@ -305,79 +312,119 @@
         glog_ref[...] = glog
         high = glog.astype(bf16)
         low = (glog - high.astype(f32)).astype(bf16)
-        gin_ref[...] = (acc_ref[...] + dot_nt(high, wr_ref[...]) + dot_nt(low, wr_ref[...])).astype(bf16)
-
-
-def expert(chunk, chunks, held, z, x, c, wg, wu, wd, wr, experts, others=()):
-    rows, width = x.shape
+        gin = (acc_ref[...] + dot_nt(high, wr_ref[...]) + dot_nt(low, wr_ref[...])).astype(bf16)
+        for n in range(count):
+            gin_refs[n][...] = gin[n * rows // count : (n + 1) * rows // count]
+
+
+def expert(index, total, held, z, xs, cs, wg, wu, wd, wr, experts, others=()):
+    count, (slot, width) = len(xs), xs[0].shape
+    rows = count * slot
     hidden = wg.shape[2]
     wide = 2 * TILE
-    whole = pl.BlockSpec((rows, width), lambda f: (0, 0))
-    kept = pl.BlockSpec((rows, width), lambda f: (chunk, 0))
-    thin = pl.BlockSpec((rows, TILE), lambda f: (chunk, 0))
-    tile = pl.BlockSpec((rows, wide), lambda f: (chunk, f))
-    full = lambda n, t: jax.ShapeDtypeStruct((chunks * rows, n), t)
+    whole = pl.BlockSpec((slot, width), lambda f: (0, 0))
+    kept = pl.BlockSpec((rows, width), lambda f: (index, 0))
+    thin = pl.BlockSpec((rows, TILE), lambda f: (index, 0))
+    tile = pl.BlockSpec((rows, wide), lambda f: (index, f))
+    full = lambda n, t: jax.ShapeDtypeStruct((total * slot, n), t)
     held = [] if held is None else list(held)
     return pl.pallas_call(
-        functools.partial(expert_kernel, experts, len(held) + len(others)),
+        functools.partial(expert_kernel, experts, count, len(held) + len(others)),
         grid=(hidden // wide,),
-        in_specs=[
-            SMEM, whole, whole,
+        in_specs=[SMEM] + [whole] * (2 * count) + [
             pl.BlockSpec((1, width, wide), lambda f: (0, 0, f)),
             pl.BlockSpec((1, width, wide), lambda f: (0, 0, f)),
             pl.BlockSpec((1, wide, width), lambda f: (0, f, 0)),
             pl.BlockSpec((width, TILE), lambda f: (0, 0)),
         ] + anywhere(held) + anywhere(others),
-        out_specs=[whole, kept, tile, tile, tile, kept, thin, thin],
-        out_shape=[
-            jax.ShapeDtypeStruct((rows, width), bf16),
+        out_specs=[whole] * count + [kept, tile, tile, tile, kept, thin, thin],
+        out_shape=[jax.ShapeDtypeStruct((slot, width), bf16)] * count + [
             full(width, bf16), full(hidden, bf16), full(hidden, bf16), full(hidden, bf16), full(width, bf16),
             full(TILE, f32), full(TILE, f32),
         ],
-        input_output_aliases={7 + i: 1 + i for i in range(len(held))},
+        input_output_aliases={2 * count + 5 + i: count + i for i in range(len(held))},
         scratch_shapes=[
             pltpu.VMEM((rows, width), f32), pltpu.VMEM((rows, TILE), f32), pltpu.VMEM((rows, TILE), f32),
-            pltpu.VMEM((rows, TILE), f32),
+            pltpu.VMEM((rows, TILE), f32), pltpu.VMEM((rows, width), bf16), pltpu.VMEM((rows, width), bf16),
         ],
         compiler_params=pltpu.CompilerParams(vmem_limit_bytes=VMEM),
-        cost_estimate=cost(23),
+        cost_estimate=cost(10 + 13 * count),
         name="expert",
-    )(z, x, c, wg, wu, wd, wr, *held, *others)
-
-
-def gate_up_kernel(x_ref, dgp_ref, dup_ref, gate_ref, up_ref, xt_ref):
+    )(z, *xs, *cs, wg, wu, wd, wr, *held, *others)
+
+
+def gate_up_kernel(s_ref, x_ref, dgp_ref, dup_ref, glog_ref, other_ref, mine_ref, router_ref, xt_ref):
     @pl.when(pl.program_id(0) == 0)
     def _():
         xt_ref[...] = x_ref[...].T
-
-    gate_ref[...] = dot(xt_ref[...], dgp_ref[...]).astype(bf16)
-    up_ref[...] = dot(xt_ref[...], dup_ref[...]).astype(bf16)
-
-
-def gate_up_grads(x, dgp, dup, others=()):
+        high = glog_ref[...].astype(bf16)
+        low = (glog_ref[...] - high.astype(f32)).astype(bf16)
+        router_ref[...] = dot(xt_ref[...], high) + dot(xt_ref[...], low)
+
+    first = s_ref[0] == 0
+    for n, ref in enumerate((dgp_ref, dup_ref)):
+        result = dot(xt_ref[...], ref[...]).astype(bf16).reshape((other_ref.shape[0], 2) + other_ref.shape[2:])
+        other_ref[:, n] = jnp.where(first, result[:, 1], result[:, 0])
+        mine_ref[:, n] = jnp.where(first, result[:, 0], result[:, 1])
+
+
+def gate_up_grads(side, chips, x, dgp, dup, glog, others=()):
     rows, width = x.shape
     hidden, wide = dgp.shape[1], 2 * TILE
+    part = width // chips // 2
     tile = pl.BlockSpec((rows, wide), lambda f: (0, f))
-    out = pl.BlockSpec((width, wide), lambda f: (0, f))
-    return pl.pallas_call(
-        behind(gate_up_kernel, 3, others),
+    out = pl.BlockSpec((chips, 2, part, wide), lambda f: (0, 0, 0, f))
+    shape = jax.ShapeDtypeStruct((chips, 2, part, hidden), bf16)
+    return pl.pallas_call(
+        behind(gate_up_kernel, 5, others),
         grid=(hidden // wide,),
-        in_specs=[pl.BlockSpec((rows, width), lambda f: (0, 0)), tile, tile] + anywhere(others),
+        in_specs=[
+            SMEM,
+            pl.BlockSpec((rows, width), lambda f: (0, 0)),
+            tile,
+            tile,
+            pl.BlockSpec((rows, TILE), lambda f: (0, 0)),
+        ]
+        + anywhere(others),
+        out_specs=[out, out, pl.BlockSpec((width, TILE), lambda f: (0, 0))],
+        out_shape=[shape, shape, jax.ShapeDtypeStruct((width, TILE), f32)],
+        scratch_shapes=[pltpu.VMEM((width, rows), bf16)],
+        compiler_params=pltpu.CompilerParams(vmem_limit_bytes=VMEM),
+        cost_estimate=cost(24),
+        name="gate_up_grads",
+    )(side, x, dgp, dup, glog, *others)
+
+
+def down_kernel(s_ref, act_ref, gcot_ref, other_ref, mine_ref, res_ref):
+    res_ref[...] = dot(act_ref[...].T, gcot_ref[...]).astype(bf16).reshape(res_ref.shape)
+    other_ref[...] = res_ref[:, 1 - s_ref[0]]
+    mine_ref[...] = res_ref[:, s_ref[0]]
+
+
+def down_grads(side, chips, act, gcot, others=()):
+    rows, hidden = act.shape
+    width, wide = gcot.shape[1], hidden // 2
+    part = hidden // chips // 2
+    out = pl.BlockSpec((chips // 2, part, width), lambda f: (f, 0, 0))
+    shape = jax.ShapeDtypeStruct((chips, part, width), bf16)
+    return pl.pallas_call(
+        behind(down_kernel, 3, others),
+        grid=(2,),
+        in_specs=[SMEM, pl.BlockSpec((rows, wide), lambda f: (0, f)), pl.BlockSpec((rows, width), lambda f: (0, 0))]
+        + anywhere(others),
         out_specs=[out, out],
-        out_shape=[jax.ShapeDtypeStruct((width, hidden), bf16)] * 2,
-        scratch_shapes=[pltpu.VMEM((width, rows), bf16)],
-        compiler_params=pltpu.CompilerParams(vmem_limit_bytes=VMEM),
-        cost_estimate=cost(26),
-        name="gate_up_grads",
-    )(x, dgp, dup, *others)
-
-
-def down_kernel(act_ref, gcot_ref, wd_ref, gate_ref, down_ref, *refs):
+        out_shape=[shape, shape],
+        scratch_shapes=[pltpu.VMEM((chips // 2, 2, part, width), bf16)],
+        compiler_params=pltpu.CompilerParams(vmem_limit_bytes=VMEM),
+        cost_estimate=cost(14),
+        name="down_grads",
+    )(side, act, gcot, *others)
+
+
+def out_kernel(act_ref, wd_ref, gate_ref, *refs):
     outs, acc_ref = refs[:-1], refs[-1]
     step = pl.program_id(0)
-    act = act_ref[...]
-    down_ref[...] = dot(act.T, gcot_ref[...]).astype(bf16)
-    more = dot(act, wd_ref[0])
+    more = dot(act_ref[...], wd_ref[0])
 
     @pl.when(step == 0)
     def _():
@@ -395,25 +442,24 @@
             out[...] = (acc_ref[part, :] * gate_ref[part, :1]).astype(bf16)
 
 
-def down_and_out(act, gcot, wd, gate, chunks, others=()):
+def expert_out(act, wd, gate, chunks, others=()):
     rows, hidden = act.shape
-    width, wide = gcot.shape[1], 2 * TILE
+    width, wide = wd.shape[2], hidden // 2
     fixed = lambda r, c: pl.BlockSpec((r, c), lambda f: (0, 0))
     return pl.pallas_call(
-        behind(down_kernel, 4, others),
+        behind(out_kernel, 3, others),
         grid=(hidden // wide,),
         in_specs=[
-            pl.BlockSpec((rows, wide), lambda f: (0, f)), fixed(rows, width),
+            pl.BlockSpec((rows, wide), lambda f: (0, f)),
             pl.BlockSpec((1, wide, width), lambda f: (0, f, 0)), fixed(rows, TILE),
         ] + anywhere(others),
-        out_specs=[pl.BlockSpec((wide, width), lambda f: (f, 0))] + [fixed(rows // chunks, width)] * chunks,
-        out_shape=[jax.ShapeDtypeStruct((hidden, width), bf16)]
-        + [jax.ShapeDtypeStruct((rows // chunks, width), bf16)] * chunks,
+        out_specs=[fixed(rows // chunks, width)] * chunks,
+        out_shape=[jax.ShapeDtypeStruct((rows // chunks, width), bf16)] * chunks,
         scratch_shapes=[pltpu.VMEM((rows, width), f32)],
         compiler_params=pltpu.CompilerParams(vmem_limit_bytes=VMEM),
-        cost_estimate=cost(26),
-        name="down_and_out",
-    )(act, gcot, wd, gate, *others)
+        cost_estimate=cost(14),
+        name="expert_out",
+    )(act, wd, gate, *others)
 
 
 def norm_kernel(per_block, two_ref, one_ref, own_ref, gain_ref, out_ref, turned_ref):
@@ -487,6 +533,24 @@
     )(*ins, *others)
 
 
+def pair_kernel(mine_ref, other_ref, out_ref):
+    out_ref[...] = (mine_ref[...].astype(f32) + other_ref[...].astype(f32)).astype(bf16)
+
+
+def pair_sum(mine, other, others=()):
+    block = pl.BlockSpec((1,) + mine.shape[1:], lambda f: (f,) + (0,) * (mine.ndim - 1))
+    return pl.pallas_call(
+        behind(pair_kernel, 2, others),
+        grid=mine.shape[:1],
+        in_specs=[block, block] + anywhere(others),
+        out_specs=block,
+        out_shape=jax.ShapeDtypeStruct(mine.shape, bf16),
+        compiler_params=pltpu.CompilerParams(vmem_limit_bytes=VMEM),
+        cost_estimate=cost(6),
+        name="pair_sum",
+    )(mine, other, *others)
+
+
 def cot_kernel(ks, slot, z_ref, t_ref, cot_ref, *outs):
     values = turned(cot_ref, z_ref[0])
     for k, out in zip(ks, outs):
@@ -510,7 +574,7 @@
         out[...] = dot(slot_rows(t_ref, k, slot), moe_in).astype(bf16)
 
 
-def middle_kernel(parts, z_ref, t_ref, hidden_ref, cot_ref, w_ref, gain_ref, *refs):
+def middle_kernel(z_ref, t_ref, hidden_ref, cot_ref, w_ref, gain_ref, *refs):
     pieces = cot_ref.shape[0]
     grad_ref, attn_ref, gain_grad_ref, outs = refs[pieces], refs[pieces + 1], refs[pieces + 2], refs[pieces + 3 :]
     grad_moe = collect(t_ref, refs[:pieces])
@@ -521,10 +585,9 @@
     low = grad.astype(bf16)
     attn_ref[...] = low
     context = dot_nt(low, w_ref[...]).astype(bf16)
-    rows, width = context.shape[0] // pieces, context.shape[1] // parts
-    for n in range(parts):
-        for k in range(pieces):
-            outs[n * pieces + k][...] = context[k * rows : (k + 1) * rows, n * width : (n + 1) * width]
+    rows = context.shape[0] // pieces
+    for k in range(pieces):
+        outs[k][...] = context[k * rows : (k + 1) * rows]
 
 
 def mix_kernel(z_ref, t_ref, hidden_ref, *refs):
@@ -547,30 +610,23 @@
             refs[0][...] = grad + dot_nt(flat(dq_ref), wq_ref[...])
 
         return
-    acc_ref, normed_ref, two_ref, one_ref, own_ref, gain_ref = refs
+    acc_ref, two_ref, one_ref, own_ref = refs
     grad = grad + acc_ref[...]
 
-    def gain(total):
-        return jnp.sum(total * flat(normed_ref).astype(f32), axis=0, keepdims=True)
-
     @pl.when(step == 0)
     def _():
         two_ref[...] = grad.astype(bf16)
-        gain_ref[...] = gain(grad)
 
     @pl.when(step == 1)
     def _():
         one_ref[...] = grad.astype(bf16)
-        gain_ref[...] += gain(grad)
 
     @pl.when(step == 2)
     def _():
-        total = grad + dot_nt(flat(dq_ref), wq_ref[...])
-        own_ref[...] = total
-        gain_ref[...] += gain(total)
-
-
-def input_grads(part, dq, dk, dv, wq, wk, wv, acc=None, normed=None, others=()):
+        own_ref[...] = grad + dot_nt(flat(dq_ref), wq_ref[...])
+
+
+def input_grads(part, dq, dk, dv, wq, wk, wv, acc=None, others=()):
     pieces, rows, some = dq.shape
     width = wq.shape[0]
     block = pieces * rows
@@ -581,10 +637,9 @@
     specs = [pl.BlockSpec((pieces, rows, some), lambda f: (0, 0, 0)), window, window, weight, weight, weight]
     ins, outs = [dq, dk, dv, wq, wk, wv], [(step, (3 * block, width), f32)]
     if acc is not None:
-        specs += [step, pl.BlockSpec((pieces, rows, width), lambda f: (f, 0, 0))]
-        ins += [acc, normed]
+        specs += [step]
+        ins += [acc]
         outs = [(once, (block, width), bf16)] * 2 + [(once, (block, width), f32)]
-        outs += [(pl.BlockSpec((1, width), lambda f: (0, 0)), (1, width), f32)]
     return pl.pallas_call(
         behind(functools.partial(inputs_kernel, acc is not None), len(ins), others),
         grid=(3,),
@@ -597,24 +652,66 @@
     )(*ins, *others)
 
 
-def tail_kernel(x_ref, sum_ref, swapped_ref, gain_ref, *refs):
-    count = len(refs) // 2
-    rows = x_ref.shape[1]
-    for k in range(count):
+def leave_kernel(s_ref, z_ref, two_ref, swapped_ref, parts_ref, leave_ref, keep_ref, *refs):
+    outs, total_ref = refs[:-1], refs[-1]
+    zero = jnp.zeros_like(swapped_ref)
+    swapped = swapped_ref[...]
+    add = jnp.where(s_ref[0] == 0, zero, swapped)
+    leave_ref[...] = (two_ref[...].astype(f32) + add.astype(f32)).astype(bf16)
+    keep_ref[...] = jnp.where(s_ref[0] == 0, swapped, zero)
+    total = parts_ref[0].astype(f32)
+    for i in range(1, parts_ref.shape[0]):
+        total = total + parts_ref[i].astype(f32)
+    total_ref[...] = total.astype(bf16).reshape(total_ref.shape)
+    for k, out in enumerate(outs):
+        out[...] = total_ref[z_ref[0] ^ k]
+
+
+def tail_kernel(z_ref, x_ref, sum_ref, swapped_ref, gain_ref, came_ref, *refs):
+    pieces, rows, width = x_ref.shape
+    blocks, outs, total_ref = refs[0], refs[1:-1], refs[-1]
+    total = blocks[0].astype(f32)
+    for i in range(1, blocks.shape[0]):
+        total = total + blocks[i].astype(f32)
+    total_ref[...] = total.astype(bf16).reshape(total_ref.shape)
+    share, long = total_ref.shape[1:]
+    for k in range(pieces):
         part = slice(k * rows, (k + 1) * rows)
-        grad = sum_ref[part, :] + swapped_ref[part, :].astype(f32) + refs[k][...].astype(f32)
-        refs[count + k][...] = norm_back(x_ref[k].astype(f32), gain_ref[...], grad)[0].astype(bf16)
-
-
-def end_kernel(z_ref, grad_ref, *refs):
-    out_ref = refs[-1]
-    rows = out_ref.shape[1]
-    for k in range(out_ref.shape[0]):
-        out_ref[z_ref[0] ^ k] = (grad_ref[k * rows : (k + 1) * rows, :] + refs[k][...].astype(f32)).astype(bf16)
-
-
-def projection_kernel(third, small, s_ref, nt_ref, dq_ref, dk_ref, dv_ref, *refs):
-    other_ref, mine_ref = refs[-2:]
+        grad = sum_ref[part, :] + swapped_ref[part, :].astype(f32) + came_ref[part, :].astype(f32)
+        outs[k][:rows, :] = norm_back(x_ref[k].astype(f32), gain_ref[...], grad)[0].astype(bf16)
+        theirs = total_ref[z_ref[0] ^ k]
+        outs[k][rows : rows + share, :] = theirs[:, :width]
+        outs[k][rows + share :, : long - width] = theirs[:, width:]
+        outs[k][rows + share :, long - width :] = jnp.zeros((share, 2 * width - long), bf16)
+
+
+def end_kernel(z_ref, grad_ref, wq_ref, wk_ref, wv_ref, gain_ref, *refs):
+    outs = refs[-7:]
+    pieces, rows, width = outs[0].shape
+    share, long = refs[pieces].shape
+    half = (long - width) // 3
+    first = refs[pieces][...].astype(f32)
+    for k in range(1, pieces):
+        first = first + refs[pieces + k][...].astype(f32)
+    outs[6][...] = first[:, 3 * half :]
+    total = None
+    for k in range(pieces):
+        outs[0][z_ref[0] ^ k] = (grad_ref[k * rows : (k + 1) * rows, :] + refs[k][:rows, :].astype(f32)).astype(bf16)
+        part = jnp.concatenate([refs[k][rows : rows + share, :], refs[k][rows + share :, :]], axis=1).astype(f32)
+        total = part if total is None else total + part
+    gain = jnp.zeros((share, 1), f32)
+    for i, weight in enumerate((wq_ref, wk_ref, wv_ref)):
+        parts = (first[:, i * half : (i + 1) * half], total[:, i * half : (i + 1) * half])
+        for n, part in enumerate(parts):
+            columns = slice(n * half, (n + 1) * half)
+            outs[1 + i][:, columns] = part
+            gain = gain + jnp.sum(part * weight[:, columns].astype(f32), axis=1, keepdims=True)
+    outs[4][...] = total[:, 3 * half : 3 * half + outs[4].shape[1]]
+    outs[5][...] = gain / gain_ref[...]
+
+
+def projection_kernel(third, small, pieces, s_ref, nt_ref, dq_ref, dk_ref, dv_ref, *refs):
+    other_ref, mine_ref = refs[small + pieces + (pieces > 0) :][:2]
     step = pl.program_id(0)
     keys = nt_ref.shape[3]
     own = dq_ref.shape[0]
@@ -636,6 +733,21 @@
     def _():
         put(dv_ref, 0)
 
+    if pieces:
+        turned_ref, context, attn_ref = refs[-1], refs[:pieces], refs[pieces]
+        count = context[0].shape[0]
+
+        @pl.when(step == 3 * third)
+        def _():
+            for k in range(pieces):
+                turned_ref[:, :, :, k * count : (k + 1) * count] = context[k][...].T.reshape(turned_ref.shape[:3] + (count,))
+
+        @pl.when(step >= 3 * third)
+        def _():
+            for where, ref in ((1 - s_ref[0], other_ref), (s_ref[0], mine_ref)):
+                left = turned_ref[:, where].reshape(-1, pieces * count)
+                ref[...] = dot(left, attn_ref[...]).astype(bf16).reshape(ref.shape)
+
     if small:
 
         @pl.when(step == 3 * third)
@@ -644,30 +756,38 @@
             mine_ref[...] = refs[0][:, s_ref[0]]
 
 
-def projection_grads(side, normed_t, dq, dk, dv, small=(), others=()):
+def projection_grads(side, normed_t, dq, dk, dv, small=(), context=(), attn=(), others=()):
     chips, _, rows, keys = normed_t.shape
     own, width = dq.shape
     wide = 2 * TILE
     third = width // wide
     at = lambda j: (lambda f: (0, jnp.clip(f - j * third, 0, third - 1)))
+    fixed = lambda array: pl.BlockSpec(array.shape, lambda f: (0,) * array.ndim)
+    more = len(small) + sum(array.shape[1] // wide for array in attn)
     out = pl.BlockSpec((chips, rows, wide), lambda f: (0, 0, f))
-    shape = jax.ShapeDtypeStruct((chips, rows, 3 * width + wide * len(small)), bf16)
-    return pl.pallas_call(
-        behind(functools.partial(projection_kernel, third, len(small)), 5 + len(small), others),
-        grid=(3 * third + len(small),),
+    shape = jax.ShapeDtypeStruct((chips, rows, 3 * width + wide * more), bf16)
+    ins = [side, normed_t, dq, dk, dv, *small, *context, *attn]
+    scratch = [pltpu.VMEM((chips, 2, rows, len(context) * array.shape[0]), bf16) for array in context[:1]]
+    return pl.pallas_call(
+        behind(functools.partial(projection_kernel, third, len(small), len(context)), len(ins), others),
+        grid=(3 * third + more,),
         in_specs=[
             SMEM,
-            pl.BlockSpec((chips, 2, rows, keys), lambda f: (0, 0, 0, 0)),
+            fixed(normed_t),
             pl.BlockSpec((own, wide), at(0)),
             pl.BlockSpec((keys, wide), at(1)),
             pl.BlockSpec((keys, wide), at(2)),
-        ] + [pl.BlockSpec((chips, 2, rows, wide), lambda f: (0, 0, 0, 0))] * len(small) + anywhere(others),
+        ]
+        + [fixed(array) for array in [*small, *context]]
+        + [pl.BlockSpec((array.shape[0], wide), lambda f: (0, jnp.maximum(f - 3 * third, 0))) for array in attn]
+        + anywhere(others),
         out_specs=[out, out],
         out_shape=[shape, shape],
-        compiler_params=pltpu.CompilerParams(vmem_limit_bytes=VMEM),
-        cost_estimate=cost(9.3),
+        scratch_shapes=scratch,
+        compiler_params=pltpu.CompilerParams(vmem_limit_bytes=VMEM),
+        cost_estimate=cost(9.3 + more),
         name="projection_grads",
-    )(side, normed_t, dq, dk, dv, *small, *others)
+    )(*ins, *others)
 
 
 def shift(x, by):
@@ -685,46 +805,18 @@
     return lax.ppermute(x, "exp", [(i, i ^ k) for i in range(lax.axis_size("exp"))])
 
 
-def sum_over_chips(pair):
-    chips = pair.shape[0]
+def over_chips(pair):
     count = lax.axis_size("ctx")
-    if chips > 4 or chips & (chips - 1):
-        groups = [list(range(core, count, 2)) for core in range(2)]
-        got = lax.all_to_all(pair, "ctx", split_axis=0, concat_axis=0, tiled=True, axis_index_groups=groups)
-        return jnp.sum(got.astype(f32), axis=0)
-    chip = lax.axis_index("ctx") // 2
-    total = None
-    for d in range(chips - 1, -1, -1):
-        block = lax.dynamic_index_in_dim(pair, chip ^ d, 0, keepdims=False)
-        if d:
-            block = lax.ppermute(block, "ctx", [(i, i ^ (2 * d)) for i in range(count)])
-        total = block.astype(f32) if total is None else total + block.astype(f32)
-    return total
-
-
-def sum_over_ctx(partial):
-    count = lax.axis_size("ctx")
-    rows, width = partial.shape
-    side = lax.axis_index("ctx") % 2
-    parts = partial.reshape(count // 2, 2, rows // count, width)
-    other = core_swap(lax.dynamic_index_in_dim(parts, 1 - side, 1, keepdims=False))
-    mine = lax.dynamic_index_in_dim(parts, side, 1, keepdims=False)
-    return sum_over_chips((mine.astype(f32) + other.astype(f32)).astype(bf16))
-
-
-def sum_over_exp(partial):
-    count = lax.axis_size("exp")
-    z = lax.axis_index("exp")
-    parts = partial.reshape(count, -1, partial.shape[-1])
-    total = None
-    for k in range(count - 1, -1, -1):
-        block = z_swap(lax.dynamic_index_in_dim(parts, z ^ k, 0, keepdims=False), k).astype(f32)
-        total = block if total is None else total + block
-    return total
-
-
-def sum_over_all(partial):
-    return sum_over_exp(sum_over_ctx(partial).astype(bf16))
+    groups = [list(range(core, count, 2)) for core in range(2)]
+    return lax.all_to_all(pair, "ctx", split_axis=0, concat_axis=0, tiled=True, axis_index_groups=groups)
+
+
+def summed(parts):
+    return jnp.sum(parts.astype(f32), axis=0)
+
+
+def add_pair(mine, other):
+    return (mine.astype(f32) + core_swap(other).astype(f32)).astype(bf16)
 
 
 def norm_rows(values, gain):
@@ -795,7 +887,7 @@
     hot = (bucket_of(np.clip(distance, 0, None))[None, :] == np.arange(bucket_total)[:, None]) & seen[None, :]
     vec = exact_dot(bias_table.astype(f32).reshape(heads, bucket_total), jnp.asarray(hot, f32))
     vec = jnp.where(jnp.asarray(seen)[None, :], vec, NEG).reshape(heads // 2, 2, -1)
-    bias = bias_tiles(vec)
+    bias = bias_tiles(vec, sent[:1])
 
     ends = jnp.cumsum(lax.dynamic_index_in_dim(doc_lengths, exp, 0, keepdims=False))
     piece_start = ctx * block_len + turn[:, None] * piece_len
@@ -813,7 +905,7 @@
     v_win = dot(normed, w_value).astype(bf16).reshape(-1, TILE, width)
     contexts, lses, context_rows = [None] * seqs, [], [None] * seqs
     for first in (2, 0):
-        others = [contexts[2], cot_slots[3], cot_slots[1]] if first == 0 else [cot_slots[2]]
+        others = [contexts[2], cot_slots[1]] if first == 0 else [cot_slots[2]]
         *c, l = attend((first, first + 1), z, lo[first : first + 2], q[first : first + 2], k_win, v_win, bias, others)
         lses.insert(0, l)
         for k in (first, first + 1):
@@ -824,52 +916,54 @@
     hidden, moe_in, *sent = call(
         functools.partial(hidden_kernel, [2, 0], slot),
         [z, targets, tokens, w_out, gain_two] + context_rows,
-        [((rows, width), f32), ((rows, width), bf16), slot_shape, slot_shape], 9, "hidden_rows",
+        [((rows, width), f32), ((rows, width), bf16), slot_shape, slot_shape], 9, "hidden_rows", [cot_slots[3]],
     )
     inputs = [sent[1], None, z_swap(sent[0], 2), None]
     held, returned, turns = None, [None] * experts, [0, 2, 1, 3]
-    for i, k in enumerate(turns):
-        back, *held = expert(k, experts, held, z, inputs[k], cot_slots[k], w_gate, w_up, w_down, router_wide, experts)
-        returned[k] = z_swap(back, k)
-        if i == 0:
-            sent = call(functools.partial(rows_kernel, [3, 1], slot), [targets, moe_in], [slot_shape] * 2, 3, "moe_rows", [back])
+    for ks, index in (([0], 0), ([2], 1), ([1], 2), ([3], 3)):
+        found = expert(
+            index, experts, held, z, [inputs[k] for k in ks], [cot_slots[k] for k in ks], w_gate, w_up, w_down, router_wide, experts
+        )
+        back, held = found[: len(ks)], found[len(ks) :]
+        for k, rows_k in zip(ks, back):
+            returned[k] = z_swap(rows_k, k)
+        if index == 0:
+            sent = call(functools.partial(rows_kernel, [3, 1], slot), [targets, moe_in], [slot_shape] * 2, 3, "moe_rows", back)
             inputs[3], inputs[1] = z_swap(sent[0], 3), z_swap(sent[1], 1)
     all_inputs, act_low, grad_gate_pre, grad_up_pre, grad_out_slots, gate, grad_logits = held
-    grad_logits = grad_logits[:, :experts]
-    scatter = lambda partial: lax.psum_scatter(partial, "ctx", scatter_dimension=0, tiled=True).astype(f32)
-    gate_part, up_part = gate_up_grads(all_inputs, grad_gate_pre, grad_up_pre, [returned[turns[1]], returned[turns[2]]])
-    grad_gate, grad_up = scatter(gate_part), scatter(up_part)
+    chips = ctx_count // 2
+    side_ref = jnp.reshape(side, (1,))
+    produced = expert_out(act_low, w_down, gate, experts, [returned[2]])
+    down_other, down_mine = down_grads(side_ref, chips, act_low, grad_out_slots, produced[:1])
 
     part_count = 2
     part_width = width // part_count
     grad_hidden, grad_attn, grad_gain_two, *sent_back = call(
-        functools.partial(middle_kernel, part_count),
-        [z, targets_t, hidden, cotangent, w_out, gain_two] + returned,
-        [((rows, width), f32), ((rows, width), bf16), ((1, width), f32)] + [((piece_len, part_width), bf16)] * (seqs * part_count),
-        12, "middle_rows", [gate_part],
-    )
-    arrived = [[z_swap(sent_back[n * seqs + k], k) for k in range(seqs)] for n in range(part_count)]
-    down_part, *produced = down_and_out(act_low, grad_out_slots, w_down, gate, experts, [sent_back[-1]])
-    grad_down = scatter(down_part)
-    grad_out = sum_over_ctx(dot_tn(jnp.concatenate(context_rows), grad_attn).astype(bf16)).astype(bf16)
-    grad_router_part = lax.dot_general(
-        all_inputs.astype(f32), grad_logits, (((0,), (0,)), ((), ())),
-        precision=lax.Precision.HIGHEST, preferred_element_type=f32,
-    )
-    given = [z_swap(produced[k], k) for k in range(experts)]
-
-    side_ref = jnp.reshape(side, (1,))
+        middle_kernel, [z, targets_t, hidden, cotangent, w_out, gain_two] + returned,
+        [((rows, width), f32), ((rows, width), bf16), ((1, width), f32)] + [((piece_len, width), bf16)] * seqs,
+        9, "middle_rows", [down_other],
+    )
+    arrived = [z_swap(sent_back[k], k) for k in range(seqs)]
+    other, mine, router_part = gate_up_grads(
+        side_ref, chips, all_inputs, grad_gate_pre, grad_up_pre, grad_logits, sent_back[-1:]
+    )
+    grad_router_part = router_part[:, :experts]
+    pair = pair_sum(mine, core_swap(other))
+    both = over_chips(pair)
+    down_other = core_swap(down_other)
+    given = [z_swap(produced[turns.index(k)], k) for k in range(experts)]
+
     weights = (w_query, w_key, w_value)
     flat = lambda grads: [grad.reshape(-1, part_width) for grad in grads]
-    back = lambda n, others: attend_back(n, part_count, z, lo, lses, q, k_win, v_win, bias, contexts, arrived[n], others)
-    *grads, diagonal = back(0, [down_part] + arrived[1])
-    other, mine = projection_grads(side_ref, normed_t, *flat(grads), (), [given[2], given[1]])
-    first_pair = (mine.astype(f32) + core_swap(other).astype(f32)).astype(bf16)
-    first_sum = sum_over_chips(first_pair).astype(bf16)
+    back = lambda n, others: attend_back(n, part_count, z, lo, lses, q, k_win, v_win, bias, contexts, arrived, others)
+    *grads, diagonal = back(0, [pair])
+    other, mine = projection_grads(
+        side_ref, normed_t, *flat(grads), context=context_rows, attn=[grad_attn], others=[given[2], given[1]]
+    )
+    first_pair = add_pair(mine, other)
+    first_parts = over_chips(first_pair)
     acc = input_grads(0, *grads, *weights, others=[other])[0]
-    *grads, more = back(1, [acc, grad_out, first_pair])
-    part_two, part_one, own_sum, gain_part = input_grads(1, *grads, *weights, acc, normed.reshape(-1, piece_len, width), [first_sum])
-    grad_gain_one = gain_part / gain_one
+    *grads, more = back(1, [acc, first_pair, both])
     diagonals = jnp.concatenate([diagonal, more])
     places = np.arange((TILES_SEEN) * 2 * TILE).reshape(TILES_SEEN, 2 * TILE)
     block, lane = places // (2 * TILE), places % (2 * TILE)
@@ -878,7 +972,6 @@
     to_bucket = (bucket_of(np.clip(where_dist, 0, None))[..., None] == np.arange(bucket_total)) & ok[..., None]
     table_part = exact_dot(diagonals.reshape(heads, -1), jnp.asarray(to_bucket.reshape(-1, bucket_total), f32))
     small = [
-        grad_gain_one.reshape(device_count, -1),
         grad_gain_two.reshape(device_count, -1),
         table_part.reshape(device_count, -1),
         grad_router_part.reshape(device_count, -1),
@@ -889,27 +982,41 @@
     packed = jnp.pad(packed, ((0, 0), (0, -packed.shape[1] % share))).reshape(width, -1)
     packed = jnp.pad(packed.astype(bf16), ((0, 0), (0, 2 * TILE - packed.shape[1])))
     packed = packed.reshape(ctx_count // 2, 2, -1, 2 * TILE)
-    other, mine = projection_grads(side_ref, normed_t, *flat(grads), [packed])
-    pair = (mine.astype(f32) + core_swap(other).astype(f32)).astype(bf16)
-    last_sum = sum_over_chips(pair).astype(bf16)
-    swapped = core_swap(part_one)
-    leave = jnp.where(side == 0, part_two.astype(f32), part_two.astype(f32) + swapped.astype(f32)).astype(bf16)
-    swapped = jnp.where(side == 0, swapped, jnp.zeros_like(swapped))
-    came = [shift(leave[k * piece_len : (k + 1) * piece_len], -2) for k in range(seqs)]
+    other, mine = projection_grads(side_ref, normed_t, *flat(grads), small=[packed], others=[first_parts, given[3]])
+    pair = add_pair(mine, other)
+    last = over_chips(pair)
+    part_two, part_one, own_sum = input_grads(1, *grads, *weights, acc, [pair])
+    leave, swapped, *first = call(
+        leave_kernel, [side_ref, z, part_two, core_swap(part_one), first_parts],
+        [((block_len, width), bf16)] * 2 + [((share, first_parts.shape[-1]), bf16)] * seqs, 5, "leaving_rows", [last],
+        [pltpu.VMEM((exp_count, share, first_parts.shape[-1]), bf16)],
+    )
+    first = [z_swap(piece, k) for k, piece in enumerate(first)]
+    came = shift(leave, -2)
+    down = over_chips(pair_sum(down_mine, down_other, [leave]))
     mixed = call(
-        mix_kernel, [z, targets_t, hidden] + given, [((seqs, piece_len, width), bf16)], 8, "mixed_rows", [leave, pair]
+        mix_kernel, [z, targets_t, hidden] + given, [((seqs, piece_len, width), bf16)], 8, "mixed_rows", [leave]
     )[0]
+    share = width // device_count
+    long = pair.shape[-1]
     pieces = call(
-        tail_kernel, [x_own, own_sum, swapped, gain_one[None]] + came, [((piece_len, width), bf16)] * seqs, 6, "tail_rows", [mixed, last_sum]
+        tail_kernel, [z, x_own, own_sum, swapped, gain_one[None], came, last],
+        [((piece_len + 2 * share, width), bf16)] * seqs, 8, "tail_rows", [mixed] + first[1:],
+        [pltpu.VMEM((exp_count, share, long), bf16)],
     )
     pieces = [z_swap(piece, k) for k, piece in enumerate(pieces)]
-    grad_tokens = call(end_kernel, [z, grad_hidden] + pieces, [((seqs, piece_len, width), bf16)], 4, "end_rows")[0]
-    dense = sum_over_exp(jnp.concatenate([grad_out, first_sum, last_sum], axis=1))
-    grad_out = dense[:, :width]
-    parts = [dense[:, width + i * part_width : width + (i + 1) * part_width] for i in range(3 * part_count)]
-    grad_query, grad_key, grad_value = [jnp.concatenate(parts[i::3], axis=1) for i in range(3)]
-    packed = dense[:, 4 * width :].reshape(-1, 2 * TILE)[:, : -(-cuts[-1] // share)].reshape(-1)
-    norm1_out, norm2_out, table_out, router_out = [packed[cuts[i] : cuts[i + 1]] for i in range(4)]
+    own_rows = lambda array: lax.dynamic_slice_in_dim(array, (ctx * exp_count + exp) * share, share, 0)
+    grad_tokens, grad_query, grad_key, grad_value, packed, norm1_out, grad_out = call(
+        end_kernel,
+        [z, grad_hidden] + [own_rows(array) for array in weights] + [own_rows(gain_one[:, None])] + pieces + first,
+        [((seqs, piece_len, width), bf16)] + [((share, width), f32)] * 3 + [((share, 2 * TILE), f32), ((share, 1), f32)]
+        + [((share, width), f32)],
+        6, "end_rows", [down],
+    )
+    grad_gate, grad_up, grad_down = summed(both[:, 0]), summed(both[:, 1]), summed(down)
+    packed = packed[:, : -(-cuts[-1] // share)].reshape(-1)
+    norm1_out = norm1_out[:, 0]
+    norm2_out, table_out, router_out = [packed[cuts[i] : cuts[i + 1]] for i in range(3)]
     return (
         mixed, grad_tokens, norm1_out, grad_query, grad_key, grad_value, grad_out, table_out, norm2_out,
         router_out.reshape(-1, experts), grad_gate[None], grad_up[None], grad_down[None],

time: 631 us -> 568 us (0.900)
  waiting for transfers between devices: 148 us -> 99.4 us
  Pallas kernels: 305 us -> 322 us
  between operations: 14.9 us -> 1.51 us
  starting transfers between devices: 84 us -> 72 us
    ppermute x30 -> x27, waiting for transfers between devices: 102 us -> 61.6 us  [z_swap(): lax.ppermute(x, 'exp', [(i, i ^ k) for i in range(lax.axis_size('exp'))])]
    ppermute x9 -> x0, waiting for transfers between devices: 27.1 us -> none  [sum_over_chips(): block = lax.ppermute(block, 'ctx', [(i, i ^ 2 * d) for i in range(count)])]
    all_to_all x0 -> x4, waiting for transfers between devices: none -> 24.9 us  [over_chips(): lax.all_to_all(pair, 'ctx', split_axis=0, concat_axis=0, tiled=True, axis...]
    all_to_all x0 -> x4, starting transfers between devices: none -> 19.2 us  [over_chips(): lax.all_to_all(pair, 'ctx', split_axis=0, concat_axis=0, tiled=True, axis...]
    ppermute x8 -> x5, waiting for transfers between devices: 18.1 us -> 3.49 us  [shift(): lax.ppermute(x, 'ctx', [(i, i + by) for i in range(count) if 0 <= i + by...]
    ppermute x30 -> x27, starting transfers between devices: 49.1 us -> 36.1 us  [z_swap(): lax.ppermute(x, 'exp', [(i, i ^ k) for i in range(lax.axis_size('exp'))])]
    ppermute x9 -> x0, starting transfers between devices: 12.3 us -> none  [sum_over_chips(): block = lax.ppermute(block, 'ctx', [(i, i ^ 2 * d) for i in range(count)])]
    ppermute x5 -> x6, waiting for transfers between devices: 0.01 us -> 9.37 us  [core_swap(): lax.ppermute(x, 'ctx', [(i, i ^ 1) for i in range(lax.axis_size('ctx'))])]
  transfers between devices with their start and end apart: 55 -> 42, of which waited for: 25 -> 19; matrix products, arithmetic and copies ran while one was open for 9% -> 7% of each run, Pallas kernels for 42% -> 48%
where the time goes in v3:
time: 568 us; the launch traced here: 561 us
  Pallas kernels  322 us (57%)
  waiting for transfers between devices  99.4 us (18%)
  starting transfers between devices  72 us (13%)
  local copies, waits for them, and re-layouts  33 us (6%)
  other arithmetic  21.5 us (4%)
  matrix products  11.7 us (2%)
    pallas_call x4, Pallas kernels, expert(): pl.pallas_call(functools.partial(expert_kernel, experts, count, len(held)...  88.6 us
    ppermute x27, waiting for transfers between devices, z_swap(): lax.ppermute(x, 'exp', [(i, i ^ k) for i in range(lax.axis_size('exp'))])  61.6 us
    pallas_call x2, Pallas kernels, attend_back(): pl.pallas_call(behind(functools.partial(attend_back_kernel, pieces), 8 +...  42.2 us
    pallas_call x8, Pallas kernels, call(): pl.pallas_call(behind(kernel, len(ins), others), in_specs=specs + anywher...  40.8 us
    ppermute x27, starting transfers between devices, z_swap(): lax.ppermute(x, 'exp', [(i, i ^ k) for i in range(lax.axis_size('exp'))])  36.1 us
    pallas_call x2, Pallas kernels, attend(): pl.pallas_call(behind(functools.partial(attend_kernel, ks), 6, others), g...  29.9 us
    all_to_all x4, waiting for transfers between devices, over_chips(): lax.all_to_all(pair, 'ctx', split_axis=0, concat_axis=0, tiled=True, axis...  24.9 us
    pallas_call x1, Pallas kernels, gate_up_grads(): pl.pallas_call(behind(gate_up_kernel, 5, others), grid=(hidden // wide,),...  22.8 us
  transfers between devices with their start and end apart: 42, of which 19 were waited for; matrix products, arithmetic and copies ran while one was open for 7% of the time, Pallas kernels for 48%

profile of v3, /device:TPU:10, one launch (start us, length us, event | category | flops | bytes accessed | tf_op | source)
XLA Modules:
  0.0 560.8 jit_solution(8974466222656607842)
XLA Ops:
  16.4 6.8 %collective-permute-done.3.refs_4_ = bf16[128,1024]{1,0:T(8,128)(2,1)S(1)} collective-permute-done((bf16[128,1024]{1,0:T(8,128)(2,1)S(1)}, bf16[128,1024]{1,0:T(8,128)(2,1)S(1)}, u32[]{:S(2)}, u32[]{:S(2)}) %collective-permute-start.3) | collective-permute-done | bytes 262176 | tf_op jit(solution)/shard_map/ppermute | solution.py:805
  33.6 3.5 collective-permute-done.6
  38.8 3.7 cot_rows.1
  45.9 6.4 %bias_tiles.1.refs_5_.refs_7_ = bf16[8,9,128,256]{3,2,1,0:T(8,128)(2,1)} custom-call(f32[8,2,1280]{2,1,0:T(2,128)} %reshape.303.refs_0_, bf16[320,1024]{1,0:T(8,128)(2,1)} %get-tuple-element.112.refs_1_), custom_call_target="tpu_custom_call" | custom-call | flops 6899999744 | tf_op jit(solution)/shard_map/bias_tiles/pallas_call | solution.py:165
  53.3 10.1 %norm_window.1 = (bf16[12,128,1024]{2,1,0:T(8,128)(2,1)}, bf16[4,2,128,1536]{3,2,1,0:T(8,128)(2,1)}) custom-call(bf16[4,128,1024]{2,1,0:T(8,128)(2,1)} %get-tuple-element.270.two_ref, bf16[4,128,1024]{2,1,0:T(8,128)(2,1)} %copy-done.30, bf16[4,128,1024]{2,1,0:T(8,128)(2,1)} %get-tuple-element.268.own_ref.refs_1_, f32[1,1024]{1,0:T(1,128)} %bitcast.107), custom_call_target="tpu_custom_call" | custom-call | flops 11500000256 | tf_op jit(solution)/shard_map/norm_window/pallas_call | solution.py:482
  68.0 4.8 convolution_convert_fusion.1
  72.8 4.8 convolution_convert_fusion
  78.4 14.9 %attend.2 = (bf16[128,1024]{1,0:T(8,128)(2,1)}, bf16[128,1024]{1,0:T(8,128)(2,1)}, f32[8,2,1,256]{3,2,1,0:T(1,128)}) custom-call(s32[1]{0:T(128)} %bitcast.refs_0_.z_ref.refs_1_, s32[2,1,256]{2,1,0:T(1,128)} %bitcast.113, bf16[2,128,1024]{2,1,0:T(8,128)(2,1)} %bitcast.91, bf16[12,128,1024]{2,1,0:T(8,128)(2,1)} %bitcast.116, ...), custom_call_target="tpu_custom_call" | custom-call | flops 17020000256 | tf_op jit(solution)/shard_map/attend/pallas_call | solution.py:184
  96.2 15.0 %attend.3 = (bf16[128,1024]{1,0:T(8,128)(2,1)}, bf16[128,1024]{1,0:T(8,128)(2,1)}, f32[8,2,1,256]{3,2,1,0:T(1,128)}) custom-call(s32[1]{0:T(128)} %bitcast.refs_0_.z_ref.refs_1_, s32[2,1,256]{2,1,0:T(1,128)} %bitcast.114, bf16[2,128,1024]{2,1,0:T(8,128)(2,1)} %bitcast.90, bf16[12,128,1024]{2,1,0:T(8,128)(2,1)} %bitcast.117, ...), custom_call_target="tpu_custom_call" | custom-call | flops 17020000256 | tf_op jit(solution)/shard_map/attend/pallas_call | solution.py:184
  115.1 5.6 %collective-permute-done.10.refs_6_ = bf16[128,1024]{1,0:T(8,128)(2,1)S(1)} collective-permute-done((bf16[128,1024]{1,0:T(8,128)(2,1)}, bf16[128,1024]{1,0:T(8,128)(2,1)S(1)}, u32[]{:S(2)}, u32[]{:S(2)}) %collective-permute-start.10) | collective-permute-done | bytes 262176 | tf_op jit(solution)/shard_map/ppermute | solution.py:805
  120.7 4.4 collective-permute-done.12.refs_8_
  125.8 5.6 hidden_rows.1
  133.4 22.2 %expert.4 = (bf16[320,1024]{1,0:T(8,128)(2,1)}, bf16[1280,1024]{1,0:T(8,128)(2,1)}, bf16[1280,2816]{1,0:T(8,128)(2,1)}, bf16[1280,2816]{1,0:T(8,128)(2,1)}, bf16...) custom-call(s32[1]{0:T(128)} %bitcast.refs_0_.z_ref.refs_1_, ...), custom_call_target="tpu_custom_call" | custom-call | flops 26449999872 | tf_op jit(solution)/shard_map/expert/pallas_call | solution.py:331
  161.0 22.1 %expert.5 = (bf16[320,1024]{1,0:T(8,128)(2,1)}, bf16[1280,1024]{1,0:T(8,128)(2,1)}, bf16[1280,2816]{1,0:T(8,128)(2,1)}, bf16[1280,2816]{1,0:T(8,128)(2,1)}, bf16...) custom-call(s32[1]{0:T(128)} %bitcast.refs_0_.z_ref.refs_1_, ...), custom_call_target="tpu_custom_call", output_to_operand_aliasing={{1}: (7, {}), {2}: (8, {}), {3}: (9, {}), {4}: (10, {}), {5... | custom-call | flops 26449999872 | tf_op jit(solution)/shard_map/expert/pallas_call | solution.py:331
  189.1 22.0 %expert.6 = (bf16[320,1024]{1,0:T(8,128)(2,1)}, bf16[1280,1024]{1,0:T(8,128)(2,1)}, bf16[1280,2816]{1,0:T(8,128)(2,1)}, bf16[1280,2816]{1,0:T(8,128)(2,1)}, bf16...) custom-call(s32[1]{0:T(128)} %bitcast.refs_0_.z_ref.refs_1_, ...), custom_call_target="tpu_custom_call", output_to_operand_aliasing={{1}: (7, {}), {2}: (8, {}), {3}: (9, {}), {4}: (10, {}), {5... | custom-call | flops 26449999872 | tf_op jit(solution)/shard_map/expert/pallas_call | solution.py:331
  212.0 22.2 %expert.7 = (bf16[320,1024]{1,0:T(8,128)(2,1)}, bf16[1280,1024]{1,0:T(8,128)(2,1)}, bf16[1280,2816]{1,0:T(8,128)(2,1)}, bf16[1280,2816]{1,0:T(8,128)(2,1)}, bf16...) custom-call(s32[1]{0:T(128)} %bitcast.refs_0_.z_ref.refs_1_, ...), custom_call_target="tpu_custom_call", output_to_operand_aliasing={{1}: (7, {}), {2}: (8, {}), {3}: (9, {}), {4}: (10, {}), {5... | custom-call | flops 26449999872 | tf_op jit(solution)/shard_map/expert/pallas_call | solution.py:331
  238.8 14.6 %expert_out.1 = (bf16[320,1024]{1,0:T(8,128)(2,1)}, bf16[320,1024]{1,0:T(8,128)(2,1)}, bf16[320,1024]{1,0:T(8,128)(2,1)}, bf16[320,1024]{1,0:T(8,128)(2,1)}) custom-call(bf16[1280,2816]{1,0:T(8,128)(2,1)} %get-tuple-element.148.refs_0_.refs_1_, bf16[1,2816,1024]{2,1,0:T(8,128)(2,1)} %refs_1_.1, f32[1280,128]{1,0:T(8,128)} %get-tuple-element.149.refs_2_, ...), custom_call_target="tpu_custom_call" | custom-call | flops 16099999744 | tf_op jit(solution)/shard_map/expert_out/pallas_call | solution.py:449
  253.4 12.6 %down_grads.1 = (bf16[4,352,1024]{2,1,0:T(8,128)(2,1)}, bf16[4,352,1024]{2,1,0:T(8,128)(2,1)}) custom-call(s32[1]{0:T(128)} %bitcast.36.refs_0_, bf16[1280,2816]{1,0:T(8,128)(2,1)} %get-tuple-element.148.refs_0_.refs_1_, bf16[1280,1024]{1,0:T(8,128)(2,1)} %get-tuple-element.159.refs_2_, bf16[320,1024]{1,0:T(8,128)(2,1)} %get-tuple-element.151.refs_3_), custom_call_target="tpu_custom_call" | custom-call | flops 16099999744 | tf_op jit(solution)/shard_map/down_grads/pallas_call | solution.py:410
  267.0 8.8 %middle_rows.1 = (f32[512,1024]{1,0:T(8,128)}, bf16[512,1024]{1,0:T(8,128)(2,1)}, f32[1,1024]{1,0:T(1,128)}, bf16[128,1024]{1,0:T(8,128)(2,1)}, bf16[128,1024]{1...) custom-call(s32[1]{0:T(128)} %bitcast.refs_0_.z_ref.refs_1_, s32[512,2]{1,0:T(8,128)} %bitcast.94, ...), custom_call_target="tpu_custom_call" | custom-call | flops 10350000128 | tf_op jit(solution)/shard_map/middle_rows/pallas_call | solution.py:524
  275.8 22.8 %gate_up_grads.1 = (bf16[4,2,128,2816]{3,2,1,0:T(8,128)(2,1)}, bf16[4,2,128,2816]{3,2,1,0:T(8,128)(2,1)}, f32[1024,128]{1,0:T(8,128)}) custom-call(s32[1]{0:T(128)} %bitcast.36.refs_0_, bf16[1280,1024]{1,0:T(8,128)(2,1)} %get-tuple-element.165.refs_1_, bf16[1280,2816]{1,0:T(8,128)(2,1)} %get-tuple-element.166.refs_2_, ...), custom_call_target="tpu_custom_call" | custom-call | flops 27599998976 | tf_op jit(solution)/shard_map/gate_up_grads/pallas_call | solution.py:378
  304.4 3.9 collective-permute-done.26.refs_1_
  310.7 7.3 %pair_sum.2.refs_16_ = bf16[4,2,128,2816]{3,2,1,0:T(8,128)(2,1)} custom-call(bf16[4,2,128,2816]{3,2,1,0:T(8,128)(2,1)} %get-tuple-element.169.refs_0_, bf16[4,2,128,2816]{3,2,1,0:T(8,128)(2,1)} %copy-done.28), custom_call_target="tpu_custom_call" | custom-call | flops 6899999744 | tf_op jit(solution)/shard_map/pair_sum/pallas_call | solution.py:542
  318.1 5.3 all-to-all-start
  325.6 21.0 %attend_back.2 = (bf16[4,128,512]{2,1,0:T(8,128)(2,1)}, bf16[12,128,512]{2,1,0:T(8,128)(2,1)}, bf16[12,128,512]{2,1,0:T(8,128)(2,1)}, f32[4,2,9,256]{3,2,1,0:T(8,128)}) custom-call(s32[1]{0:T(128)} %bitcast.refs_0_.z_ref.refs_1_, s32[4,1,256]{2,1,0:T(1,128)} %bitcast.111, f32[8,2,1,256]{3,2,1,0:T(1,128)} %get-tuple-element.155.refs_2_, ...), custom_call_target="tpu_custom_call" | custom-call | flops 24149999616 | tf_op jit(solution)/shard_map/attend_back/pallas_call | solution.py:217
  346.6 5.8 %collective-permute-done.19.refs_10_.refs_5_ = bf16[320,1024]{1,0:T(8,128)(2,1)S(1)} collective-permute-done((bf16[320,1024]{1,0:T(8,128)(2,1)S(1)}, bf16[320,1024]{1,0:T(8,128)(2,1)S(1)}, u32[]{:S(2)}, u32[]{:S(2)}) %collective-permute-start.19) | collective-permute-done | bytes 655392 | tf_op jit(solution)/shard_map/ppermute | solution.py:805
  353.3 12.6 %projection_grads.2 = (bf16[4,128,2560]{2,1,0:T(8,128)(2,1)}, bf16[4,128,2560]{2,1,0:T(8,128)(2,1)}) custom-call(s32[1]{0:T(128)} %bitcast.36.refs_0_, bf16[4,2,128,1536]{3,2,1,0:T(8,128)(2,1)} %get-tuple-element.174.refs_1_, bf16[512,512]{1,0:T(8,128)(2,1)} %bitcast.129, bf16[1536,512]{1,0:T(8,128)(2,1)} %bitcast.126, bf16[1536,512]{1,0:T(8,128)(2,1)} %bitcast.127, ...), custom_call_target="tpu_custom_call" | custom-call | flops 15294999552 | tf_op jit(solution)/shard_map/projection_grads/pallas_call | solution.py:771
  366.7 9.1 %input_grads.2.refs_16_.refs_6_ = f32[1536,1024]{1,0:T(8,128)} custom-call(bf16[4,128,512]{2,1,0:T(8,128)(2,1)} %get-tuple-element.171.refs_0_, bf16[12,128,512]{2,1,0:T(8,128)(2,1)} %get-tuple-element.172.refs_1_, bf16[12,128,512]{2,1,0:T(8,128)(2,1)} %get-tuple-element.173.refs_2_, bf16[1024,1024]{1,0:T(8,128)(2,1)} %refs_3_.15, ...), custom_call_target="tpu_custom_call" | custom-call | flops 8049999872 | tf_op jit(solution)/shard_map/input_grads/pallas_call | solution.py:643
  378.0 10.8 %all-to-all-done.refs_18_ = bf16[4,2,128,2816]{3,2,1,0:T(8,128)(2,1)} async-done(((bf16[4,2,128,2816]{3,2,1,0:T(8,128)(2,1)}), bf16[4,2,128,2816]{3,2,1,0:T(8,128)(2,1)}, u32[]{:S(2)}, u32[]{:S(2)}) %all-to-all-start) | async-done | bytes 5767200 | tf_op jit(solution)/shard_map/all_to_all | solution.py:811
  388.7 4.4 all-to-all-start.1
  393.2 21.3 %attend_back.3 = (bf16[4,128,512]{2,1,0:T(8,128)(2,1)}, bf16[12,128,512]{2,1,0:T(8,128)(2,1)}, bf16[12,128,512]{2,1,0:T(8,128)(2,1)}, f32[4,2,9,256]{3,2,1,0:T(8,128)}) custom-call(s32[1]{0:T(128)} %bitcast.refs_0_.z_ref.refs_1_, s32[4,1,256]{2,1,0:T(1,128)} %bitcast.112, f32[8,2,1,256]{3,2,1,0:T(1,128)} %get-tuple-element.155.refs_2_, ...), custom_call_target="tpu_custom_call" | custom-call | flops 24149999616 | tf_op jit(solution)/shard_map/attend_back/pallas_call | solution.py:217
  417.8 5.6 %all-to-all-done.1.refs_6_.refs_4_ = bf16[4,128,2560]{2,1,0:T(8,128)(2,1)S(1)} async-done(((bf16[4,128,2560]{2,1,0:T(8,128)(2,1)}), bf16[4,128,2560]{2,1,0:T(8,128)(2,1)S(1)}, u32[]{:S(2)}, u32[]{:S(2)}) %all-to-all-start.1) | async-done | bytes 2621472 | tf_op jit(solution)/shard_map/all_to_all | solution.py:811
  424.9 9.3 %projection_grads.3 = (bf16[4,128,1792]{2,1,0:T(8,128)(2,1)}, bf16[4,128,1792]{2,1,0:T(8,128)(2,1)}) custom-call(s32[1]{0:T(128)} %bitcast.36.refs_0_, bf16[4,2,128,1536]{3,2,1,0:T(8,128)(2,1)} %get-tuple-element.174.refs_1_, bf16[512,512]{1,0:T(8,128)(2,1)} %bitcast.128, bf16[1536,512]{1,0:T(8,128)(2,1)} %bitcast.124, bf16[1536,512]{1,0:T(8,128)(2,1)} %bitcast.125, ...), custom_call_target="tpu_custom_call" | custom-call | flops 11845000192 | tf_op jit(solution)/shard_map/projection_grads/pallas_call | solution.py:771
  434.7 5.5 collective-permute-done.28
  443.4 4.1 all-to-all-start.2
  447.5 10.5 %input_grads.3 = (bf16[512,1024]{1,0:T(8,128)(2,1)}, bf16[512,1024]{1,0:T(8,128)(2,1)}, f32[512,1024]{1,0:T(8,128)}) custom-call(bf16[4,128,512]{2,1,0:T(8,128)(2,1)} %get-tuple-element.178.refs_0_, bf16[12,128,512]{2,1,0:T(8,128)(2,1)} %get-tuple-element.179.refs_1_, bf16[12,128,512]{2,1,0:T(8,128)(2,1)} %get-tuple-element.180.refs_2_, ...), custom_call_target="tpu_custom_call" | custom-call | flops 8049999872 | tf_op jit(solution)/shard_map/input_grads/pallas_call | solution.py:643
  461.0 8.5 %all-to-all-done.2.refs_5_.refs_6_ = bf16[4,128,1792]{2,1,0:T(8,128)(2,1)S(1)} async-done(((bf16[4,128,1792]{2,1,0:T(8,128)(2,1)}), bf16[4,128,1792]{2,1,0:T(8,128)(2,1)S(1)}, u32[]{:S(2)}, u32[]{:S(2)}) %all-to-all-start.2) | async-done | bytes 1835040 | tf_op jit(solution)/shard_map/all_to_all | solution.py:811
  470.8 4.6 leaving_rows.1
  477.9 4.9 pair_sum.3
  482.8 5.4 all-to-all-start.3
  492.0 5.8 %mixed_rows.1.refs_7_ = bf16[4,128,1024]{2,1,0:T(8,128)(2,1)} custom-call(s32[1]{0:T(128)} %bitcast.refs_0_.z_ref.refs_1_, s32[512,2]{1,0:T(8,128)} %bitcast.95, f32[512,1024]{1,0:T(8,128)} %get-tuple-element.119.refs_2_, bf16[320,1024]{1,0:T(8,128)(2,1)} %get-tuple-element.151.refs_3_, bf16[320,1024]{1,0:T(8,128)(2,1)} %copy-done.31, ...), custom_call_target="tpu_custom_call" | custom-call | flops 9200000000 | tf_op jit(solution)/shard_map/mixed_rows/pallas_call | solution.py:524
  497.8 4.4 collective-permute-done.32.refs_9_.refs_12_
  505.7 5.7 %tail_rows.1 = (bf16[192,1024]{1,0:T(8,128)(2,1)}, bf16[192,1024]{1,0:T(8,128)(2,1)}, bf16[192,1024]{1,0:T(8,128)(2,1)}, bf16[192,1024]{1,0:T(8,128)(2,1)}) custom-call(s32[1]{0:T(128)} %bitcast.refs_0_.z_ref.refs_1_, bf16[4,128,1024]{2,1,0:T(8,128)(2,1)} %get-tuple-element.268.own_ref.refs_1_, f32[512,1024]{1,0:T(8,128)} %get-tuple-element.191.refs_2_, ...), custom_call_target="tpu_custom_call" | custom-call | flops 9200000000 | tf_op jit(solution)/shard_map/tail_rows/pallas_call | solution.py:524
  516.3 5.4 convert_reduce_fusion.1
  521.8 4.5 collective-permute-done.34.refs_7_
  526.3 15.1 %collective-permute-done.35.refs_8_ = bf16[192,1024]{1,0:T(8,128)(2,1)} collective-permute-done((bf16[192,1024]{1,0:T(8,128)(2,1)}, bf16[192,1024]{1,0:T(8,128)(2,1)}, u32[]{:S(2)}, u32[]{:S(2)}) %collective-permute-start.35) | collective-permute-done | bytes 393248 | tf_op jit(solution)/shard_map/ppermute | solution.py:805
  541.5 6.2 %collective-permute-done.36.refs_9_ = bf16[192,1024]{1,0:T(8,128)(2,1)} collective-permute-done((bf16[192,1024]{1,0:T(8,128)(2,1)}, bf16[192,1024]{1,0:T(8,128)(2,1)}, u32[]{:S(2)}, u32[]{:S(2)}) %collective-permute-start.36) | collective-permute-done | bytes 393248 | tf_op jit(solution)/shard_map/ppermute | solution.py:805
  549.2 3.7 end_rows.1
  556.9 3.6 convert_reduce_fusion
  (236 shorter events, 112.1 us)
Async XLA Ops:
  0.7 31.6 %copy-start.22 = (bf16[1024]{0:T(1024)(128)(2,1)S(1)}, bf16[1024]{0:T(1024)(128)(2,1)}, u32[]{:S(2)}) copy-start(bf16[1024]{0:T(1024)(128)(2,1)} %param.23) | copy-start | bytes 6148
  2.1 10.9 %collective-permute-start.1 = (bf16[128,1024]{1,0:T(8,128)(2,1)S(1)}, bf16[128,1024]{1,0:T(8,128)(2,1)S(1)}, u32[]{:S(2)}, u32[]{:S(2)}) collective-permute-start(bf16[128,1024]{1,0:T(8,128)(2,1)S(1)} %get-tuple-element.273), channel_id=1, source_target_pairs={{0,1},{1,0},{2,3},{3,2},{4,5},{5,4},{6,7},{7,6},{8,9},{9,8},{10,11... | collective-permute-start | bytes 786440 | tf_op jit(solution)/shard_map/ppermute | solution.py:805
  2.6 20.6 %collective-permute-start.3 = (bf16[128,1024]{1,0:T(8,128)(2,1)S(1)}, bf16[128,1024]{1,0:T(8,128)(2,1)S(1)}, u32[]{:S(2)}, u32[]{:S(2)}) collective-permute-start(bf16[128,1024]{1,0:T(8,128)(2,1)S(1)} %get-tuple-element.272), channel_id=1, source_target_pairs={{0,2},{1,3},{2,0},{3,1},{4,6},{5,7},{6,4},{7,5},{8,10},{9,11},{10,... | collective-permute-start | bytes 786440 | tf_op jit(solution)/shard_map/ppermute | solution.py:805
  5.2 23.1 %collective-permute-start.5 = (bf16[128,1024]{1,0:T(8,128)(2,1)S(1)}, bf16[128,1024]{1,0:T(8,128)(2,1)S(1)}, u32[]{:S(2)}, u32[]{:S(2)}) collective-permute-start(bf16[128,1024]{1,0:T(8,128)(2,1)S(1)} %get-tuple-element.274), channel_id=1, source_target_pairs={{0,3},{1,2},{2,1},{3,0},{4,7},{5,6},{6,5},{7,4},{8,11},{9,10},{10,... | collective-permute-start | bytes 786440 | tf_op jit(solution)/shard_map/ppermute | solution.py:805
  5.6 27.9 %collective-permute-start = (bf16[128,1024]{1,0:T(8,128)(2,1)S(1)}, bf16[128,1024]{1,0:T(8,128)(2,1)S(1)}, u32[]{:S(2)}, u32[]{:S(2)}) collective-permute-start(bf16[128,1024]{1,0:T(8,128)(2,1)S(1)} %bitcast.87), channel_id=1, source_target_pairs={{0,8},{4,12},{8,16},{12,20},{16,24},{20,28},{1,9},{5,13},{9,17},{1... | collective-permute-start | bytes 786440 | tf_op jit(solution)/shard_map/ppermute | solution.py:795
  12.3 26.4 %copy-start.16 = (s32[4,128]{1,0:T(4,128)}, s32[4,128]{1,0:T(4,128)S(1)}, u32[]{:S(2)}) copy-start(s32[4,128]{1,0:T(4,128)S(1)} %broadcast_subtract_fusion) | copy-start | bytes 6148
  13.0 25.7 %copy-start.9 = (bf16[128,1024]{1,0:T(8,128)(2,1)}, bf16[128,1024]{1,0:T(8,128)(2,1)S(1)}, u32[]{:S(2)}) copy-start(bf16[128,1024]{1,0:T(8,128)(2,1)S(1)} %collective-permute-done.1.refs_3_) | copy-start | bytes 786436
  13.0 20.6 %collective-permute-start.2 = (bf16[128,1024]{1,0:T(8,128)(2,1)S(1)}, bf16[128,1024]{1,0:T(8,128)(2,1)S(1)}, u32[]{:S(2)}, u32[]{:S(2)}) collective-permute-start(bf16[128,1024]{1,0:T(8,128)(2,1)S(1)} %collective-permute-done.1.refs_3_), channel_id=1, source_target_pairs={{0,8},{4,12},{8,16},{12,20},{16,24},{20,28},{1,9},{5,13},{9,17},{1... | collective-permute-start | bytes 786440 | tf_op jit(solution)/shard_map/ppermute | solution.py:795
  23.2 10.4 %collective-permute-start.4 = (bf16[128,1024]{1,0:T(8,128)(2,1)S(1)}, bf16[128,1024]{1,0:T(8,128)(2,1)S(1)}, u32[]{:S(2)}, u32[]{:S(2)}) collective-permute-start(bf16[128,1024]{1,0:T(8,128)(2,1)S(1)} %collective-permute-done.3.refs_4_), channel_id=1, source_target_pairs={{0,8},{4,12},{8,16},{12,20},{16,24},{20,28},{1,9},{5,13},{9,17},{1... | collective-permute-start | bytes 786440 | tf_op jit(solution)/shard_map/ppermute | solution.py:795
  28.3 8.8 %collective-permute-start.6 = (bf16[128,1024]{1,0:T(8,128)(2,1)S(1)}, bf16[128,1024]{1,0:T(8,128)(2,1)S(1)}, u32[]{:S(2)}, u32[]{:S(2)}) collective-permute-start(bf16[128,1024]{1,0:T(8,128)(2,1)S(1)} %collective-permute-done.5.refs_5_), channel_id=1, source_target_pairs={{0,8},{4,12},{8,16},{12,20},{16,24},{20,28},{1,9},{5,13},{9,17},{1... | collective-permute-start | bytes 786440 | tf_op jit(solution)/shard_map/ppermute | solution.py:795
  38.7 13.6 %collective-permute-start.7 = (bf16[4,128,1024]{2,1,0:T(8,128)(2,1)S(1)}, bf16[4,128,1024]{2,1,0:T(8,128)(2,1)S(1)}, u32[]{:S(2)}, u32[]{:S(2)}) collective-permute-start(bf16[4,128,1024]{2,1,0:T(8,128)(2,1)S(1)} %get-tuple-element.269), channel_id=1, source_target_pairs={{0,4},{4,0},{8,12},{12,8},{16,20},{20,16},{24,28},{28,24},{1,5},{5... | collective-permute-start | bytes 3145736 | tf_op jit(solution)/shard_map/ppermute | solution.py:799
  42.4 35.1 %collective-permute-start.8 = (bf16[320,1024]{1,0:T(8,128)(2,1)}, bf16[320,1024]{1,0:T(8,128)(2,1)S(1)}, u32[]{:S(2)}, u32[]{:S(2)}) collective-permute-start(bf16[320,1024]{1,0:T(8,128)(2,1)} %get-tuple-element.112.refs_1_), channel_id=1, source_target_pairs={{0,2},{1,3},{2,0},{3,1},{4,6},{5,7},{6,4},{7,5},{8,10},{9,11},{10,... | collective-permute-start | bytes 1966088 | tf_op jit(solution)/shard_map/ppermute | solution.py:805
  43.6 51.8 %collective-permute-start.9 = (bf16[320,1024]{1,0:T(8,128)(2,1)}, bf16[320,1024]{1,0:T(8,128)(2,1)S(1)}, u32[]{:S(2)}, u32[]{:S(2)}) collective-permute-start(bf16[320,1024]{1,0:T(8,128)(2,1)} %get-tuple-element.114), channel_id=1, source_target_pairs={{0,1},{1,0},{2,3},{3,2},{4,5},{5,4},{6,7},{7,6},{8,9},{9,8},{10,11... | collective-permute-start | bytes 1966088 | tf_op jit(solution)/shard_map/ppermute | solution.py:805
  45.5 69.6 %collective-permute-start.13 = (bf16[320,1024]{1,0:T(8,128)(2,1)}, bf16[320,1024]{1,0:T(8,128)(2,1)S(1)}, u32[]{:S(2)}, u32[]{:S(2)}) collective-permute-start(bf16[320,1024]{1,0:T(8,128)(2,1)} %get-tuple-element.118), channel_id=1, source_target_pairs={{0,3},{1,2},{2,1},{3,0},{4,7},{5,6},{6,5},{7,4},{8,11},{9,10},{10,... | collective-permute-start | bytes 1966088 | tf_op jit(solution)/shard_map/ppermute | solution.py:805
  93.3 27.4 %collective-permute-start.11 = (bf16[128,1024]{1,0:T(8,128)(2,1)}, bf16[128,1024]{1,0:T(8,128)(2,1)S(1)}, u32[]{:S(2)}, u32[]{:S(2)}) collective-permute-start(bf16[128,1024]{1,0:T(8,128)(2,1)} %get-tuple-element.113.refs_6_.refs_10_), channel_id=1, source_target_pairs={{0,2},{1,3},{2,0},{3,1},{4,6},{5,7},{6,4},{7,5},{8,10},{9,11},{10,... | collective-permute-start | bytes 786440 | tf_op jit(solution)/shard_map/ppermute | solution.py:805
  111.2 9.5 %collective-permute-start.10 = (bf16[128,1024]{1,0:T(8,128)(2,1)}, bf16[128,1024]{1,0:T(8,128)(2,1)S(1)}, u32[]{:S(2)}, u32[]{:S(2)}) collective-permute-start(bf16[128,1024]{1,0:T(8,128)(2,1)} %get-tuple-element.116.refs_9_), channel_id=1, source_target_pairs={{0,1},{1,0},{2,3},{3,2},{4,5},{5,4},{6,7},{7,6},{8,9},{9,8},{10,11... | collective-permute-start | bytes 786440 | tf_op jit(solution)/shard_map/ppermute | solution.py:805
  112.2 12.9 %collective-permute-start.12 = (bf16[128,1024]{1,0:T(8,128)(2,1)S(1)}, bf16[128,1024]{1,0:T(8,128)(2,1)S(1)}, u32[]{:S(2)}, u32[]{:S(2)}) collective-permute-start(bf16[128,1024]{1,0:T(8,128)(2,1)S(1)} %copy-done.45), channel_id=1, source_target_pairs={{0,3},{1,2},{2,1},{3,0},{4,7},{5,6},{6,5},{7,4},{8,11},{9,10},{10,... | collective-permute-start | bytes 786440 | tf_op jit(solution)/shard_map/ppermute | solution.py:805
  131.4 28.7 %collective-permute-start.16 = (bf16[320,1024]{1,0:T(8,128)(2,1)}, bf16[320,1024]{1,0:T(8,128)(2,1)S(1)}, u32[]{:S(2)}, u32[]{:S(2)}) collective-permute-start(bf16[320,1024]{1,0:T(8,128)(2,1)} %get-tuple-element.126), channel_id=1, source_target_pairs={{0,2},{1,3},{2,0},{3,1},{4,6},{5,7},{6,4},{7,5},{8,10},{9,11},{10,... | collective-permute-start | bytes 1966088 | tf_op jit(solution)/shard_map/ppermute | solution.py:805
  158.6 29.6 %collective-permute-start.15 = (bf16[320,1024]{1,0:T(8,128)(2,1)}, bf16[320,1024]{1,0:T(8,128)(2,1)S(1)}, u32[]{:S(2)}, u32[]{:S(2)}) collective-permute-start(bf16[320,1024]{1,0:T(8,128)(2,1)} %get-tuple-element.125), channel_id=1, source_target_pairs={{0,1},{1,0},{2,3},{3,2},{4,5},{5,4},{6,7},{7,6},{8,9},{9,8},{10,11... | collective-permute-start | bytes 1966088 | tf_op jit(solution)/shard_map/ppermute | solution.py:805
  158.6 52.5 %collective-permute-start.14 = (bf16[320,1024]{1,0:T(8,128)(2,1)}, bf16[320,1024]{1,0:T(8,128)(2,1)S(1)}, u32[]{:S(2)}, u32[]{:S(2)}) collective-permute-start(bf16[320,1024]{1,0:T(8,128)(2,1)} %get-tuple-element.124), channel_id=1, source_target_pairs={{0,3},{1,2},{2,1},{3,0},{4,7},{5,6},{6,5},{7,4},{8,11},{9,10},{10,... | collective-permute-start | bytes 1966088 | tf_op jit(solution)/shard_map/ppermute | solution.py:805
  183.0 54.9 %collective-permute-start.17 = (bf16[320,1024]{1,0:T(8,128)(2,1)}, bf16[320,1024]{1,0:T(8,128)(2,1)S(1)}, u32[]{:S(2)}, u32[]{:S(2)}) collective-permute-start(bf16[320,1024]{1,0:T(8,128)(2,1)} %get-tuple-element.150), channel_id=1, source_target_pairs={{0,2},{1,3},{2,0},{3,1},{4,6},{5,7},{6,4},{7,5},{8,10},{9,11},{10,... | collective-permute-start | bytes 1966088 | tf_op jit(solution)/shard_map/ppermute | solution.py:805
  212.0 22.5 %copy-start.39 = (bf16[320,1024]{1,0:T(8,128)(2,1)S(1)}, bf16[320,1024]{1,0:T(8,128)(2,1)}, u32[]{:S(2)}) copy-start(bf16[320,1024]{1,0:T(8,128)(2,1)} %get-tuple-element.157) | copy-start | bytes 1966084
  234.2 31.7 %collective-permute-start.22 = (bf16[320,1024]{1,0:T(8,128)(2,1)}, bf16[320,1024]{1,0:T(8,128)(2,1)S(1)}, u32[]{:S(2)}, u32[]{:S(2)}) collective-permute-start(bf16[320,1024]{1,0:T(8,128)(2,1)} %get-tuple-element.158), channel_id=1, source_target_pairs={{0,3},{1,2},{2,1},{3,0},{4,7},{5,6},{6,5},{7,4},{8,11},{9,10},{10,... | collective-permute-start | bytes 1966088 | tf_op jit(solution)/shard_map/ppermute | solution.py:805
  234.5 31.4 %collective-permute-start.21 = (bf16[320,1024]{1,0:T(8,128)(2,1)S(1)}, bf16[320,1024]{1,0:T(8,128)(2,1)S(1)}, u32[]{:S(2)}, u32[]{:S(2)}) collective-permute-start(bf16[320,1024]{1,0:T(8,128)(2,1)S(1)} %copy-done.39), channel_id=1, source_target_pairs={{0,1},{1,0},{2,3},{3,2},{4,5},{5,4},{6,7},{7,6},{8,9},{9,8},{10,11... | collective-permute-start | bytes 1966088 | tf_op jit(solution)/shard_map/ppermute | solution.py:805
  275.8 32.4 %copy-start.36 = (bf16[320,1024]{1,0:T(8,128)(2,1)S(1)}, bf16[320,1024]{1,0:T(8,128)(2,1)}, u32[]{:S(2)}) copy-start(bf16[320,1024]{1,0:T(8,128)(2,1)} %get-tuple-element.153) | copy-start | bytes 1966084
  298.6 9.6 %collective-permute-start.26 = (bf16[4,2,128,2816]{3,2,1,0:T(8,128)(2,1)}, bf16[4,2,128,2816]{3,2,1,0:T(8,128)(2,1)S(1)}, u32[]{:S(2)}, u32[]{:S(2)}) collective-permute-start(bf16[4,2,128,2816]{3,2,1,0:T(8,128)(2,1)} %get-tuple-element.170), channel_id=1, source_target_pairs={{0,4},{4,0},{8,12},{12,8},{16,20},{20,16},{24,28},{28,24},{1,5},{5... | collective-permute-start | bytes 17301512 | tf_op jit(solution)/shard_map/ppermute | solution.py:799
  298.6 26.2 %collective-permute-start.25 = (bf16[128,1024]{1,0:T(8,128)(2,1)}, bf16[128,1024]{1,0:T(8,128)(2,1)S(1)}, u32[]{:S(2)}, u32[]{:S(2)}) collective-permute-start(bf16[128,1024]{1,0:T(8,128)(2,1)} %get-tuple-element.164.refs_5_), channel_id=1, source_target_pairs={{0,3},{1,2},{2,1},{3,0},{4,7},{5,6},{6,5},{7,4},{8,11},{9,10},{10,... | collective-permute-start | bytes 786440 | tf_op jit(solution)/shard_map/ppermute | solution.py:805
  301.0 22.3 %collective-permute-start.23 = (bf16[128,1024]{1,0:T(8,128)(2,1)}, bf16[128,1024]{1,0:T(8,128)(2,1)S(1)}, u32[]{:S(2)}, u32[]{:S(2)}) collective-permute-start(bf16[128,1024]{1,0:T(8,128)(2,1)} %get-tuple-element.162), channel_id=1, source_target_pairs={{0,1},{1,0},{2,3},{3,2},{4,5},{5,4},{6,7},{7,6},{8,9},{9,8},{10,11... | collective-permute-start | bytes 786440 | tf_op jit(solution)/shard_map/ppermute | solution.py:805
  302.3 22.6 %collective-permute-start.24 = (bf16[128,1024]{1,0:T(8,128)(2,1)}, bf16[128,1024]{1,0:T(8,128)(2,1)}, u32[]{:S(2)}, u32[]{:S(2)}) collective-permute-start(bf16[128,1024]{1,0:T(8,128)(2,1)} %get-tuple-element.163), channel_id=1, source_target_pairs={{0,2},{1,3},{2,0},{3,1},{4,6},{5,7},{6,4},{7,5},{8,10},{9,11},{10,... | collective-permute-start | bytes 786440 | tf_op jit(solution)/shard_map/ppermute | solution.py:805
  302.6 44.0 %collective-permute-start.18 = (bf16[320,1024]{1,0:T(8,128)(2,1)}, bf16[320,1024]{1,0:T(8,128)(2,1)S(1)}, u32[]{:S(2)}, u32[]{:S(2)}) collective-permute-start(bf16[320,1024]{1,0:T(8,128)(2,1)} %get-tuple-element.152), channel_id=1, source_target_pairs={{0,1},{1,0},{2,3},{3,2},{4,5},{5,4},{6,7},{7,6},{8,9},{9,8},{10,11... | collective-permute-start | bytes 1966088 | tf_op jit(solution)/shard_map/ppermute | solution.py:805
  308.3 44.1 %collective-permute-start.19 = (bf16[320,1024]{1,0:T(8,128)(2,1)S(1)}, bf16[320,1024]{1,0:T(8,128)(2,1)S(1)}, u32[]{:S(2)}, u32[]{:S(2)}) collective-permute-start(bf16[320,1024]{1,0:T(8,128)(2,1)S(1)} %copy-done.36), channel_id=1, source_target_pairs={{0,2},{1,3},{2,0},{3,1},{4,6},{5,7},{6,4},{7,5},{8,10},{9,11},{10,... | collective-permute-start | bytes 1966088 | tf_op jit(solution)/shard_map/ppermute | solution.py:805
  318.1 70.7 %all-to-all-start = ((bf16[4,2,128,2816]{3,2,1,0:T(8,128)(2,1)}), bf16[4,2,128,2816]{3,2,1,0:T(8,128)(2,1)}, u32[]{:S(2)}, u32[]{:S(2)}) async-start(bf16[4,2,128,2816]{3,2,1,0:T(8,128)(2,1)} %pair_sum.2.refs_16_), calls=%async_computation | async-start | bytes 11534336 | tf_op jit(solution)/shard_map/all_to_all | solution.py:811
  365.9 9.8 %collective-permute-start.27 = (bf16[4,128,2560]{2,1,0:T(8,128)(2,1)}, bf16[4,128,2560]{2,1,0:T(8,128)(2,1)S(1)}, u32[]{:S(2)}, u32[]{:S(2)}) collective-permute-start(bf16[4,128,2560]{2,1,0:T(8,128)(2,1)} %get-tuple-element.176.refs_6_), channel_id=1, source_target_pairs={{0,4},{4,0},{8,12},{12,8},{16,20},{20,16},{24,28},{28,24},{1,5},{5... | collective-permute-start | bytes 7864328 | tf_op jit(solution)/shard_map/ppermute | solution.py:799
  366.4 51.4 %collective-permute-start.20 = (bf16[320,1024]{1,0:T(8,128)(2,1)}, bf16[320,1024]{1,0:T(8,128)(2,1)}, u32[]{:S(2)}, u32[]{:S(2)}) collective-permute-start(bf16[320,1024]{1,0:T(8,128)(2,1)} %get-tuple-element.154), channel_id=1, source_target_pairs={{0,3},{1,2},{2,1},{3,0},{4,7},{5,6},{6,5},{7,4},{8,11},{9,10},{10,... | collective-permute-start | bytes 1966088 | tf_op jit(solution)/shard_map/ppermute | solution.py:805
  388.7 34.7 %all-to-all-start.1 = ((bf16[4,128,2560]{2,1,0:T(8,128)(2,1)}), bf16[4,128,2560]{2,1,0:T(8,128)(2,1)S(1)}, u32[]{:S(2)}, u32[]{:S(2)}) async-start(bf16[4,128,2560]{2,1,0:T(8,128)(2,1)} %add_convert_fusion.refs_17_), calls=%async_computation.1 | async-start | bytes 5242880 | tf_op jit(solution)/shard_map/all_to_all | solution.py:811
  393.2 22.3 %copy-start.6 = (f32[2304,32]{1,0:T(8,128)S(1)}, f32[2304,32]{1,0:T(8,128)}, u32[]{:S(2)}) copy-start(f32[2304,32]{1,0:T(8,128)} %constant.103.clone) | copy-start | bytes 884740
  434.2 6.0 %collective-permute-start.28 = (bf16[4,128,1792]{2,1,0:T(8,128)(2,1)}, bf16[4,128,1792]{2,1,0:T(8,128)(2,1)S(1)}, u32[]{:S(2)}, u32[]{:S(2)}) collective-permute-start(bf16[4,128,1792]{2,1,0:T(8,128)(2,1)} %get-tuple-element.186), channel_id=1, source_target_pairs={{0,4},{4,0},{8,12},{12,8},{16,20},{20,16},{24,28},{28,24},{1,5},{5... | collective-permute-start | bytes 5505032 | tf_op jit(solution)/shard_map/ppermute | solution.py:799
  434.2 43.7 %collective-permute-start.37 = (bf16[4,352,1024]{2,1,0:T(8,128)(2,1)}, bf16[4,352,1024]{2,1,0:T(8,128)(2,1)}, u32[]{:S(2)}, u32[]{:S(2)}) collective-permute-start(bf16[4,352,1024]{2,1,0:T(8,128)(2,1)} %get-tuple-element.160.refs_10_), channel_id=1, source_target_pairs={{0,4},{4,0},{8,12},{12,8},{16,20},{20,16},{24,28},{28,24},{1,5},{5... | collective-permute-start | bytes 8650760 | tf_op jit(solution)/shard_map/ppermute | solution.py:799
  443.4 26.2 %all-to-all-start.2 = ((bf16[4,128,1792]{2,1,0:T(8,128)(2,1)}), bf16[4,128,1792]{2,1,0:T(8,128)(2,1)S(1)}, u32[]{:S(2)}, u32[]{:S(2)}) async-start(bf16[4,128,1792]{2,1,0:T(8,128)(2,1)} %add_convert_fusion.1.refs_7_), calls=%async_computation.2 | async-start | bytes 3670016 | tf_op jit(solution)/shard_map/all_to_all | solution.py:811
  458.0 3.0 collective-permute-start.29
  475.4 29.6 %collective-permute-start.30 = (bf16[512,1024]{1,0:T(8,128)(2,1)}, bf16[512,1024]{1,0:T(8,128)(2,1)}, u32[]{:S(2)}, u32[]{:S(2)}) collective-permute-start(bf16[512,1024]{1,0:T(8,128)(2,1)} %get-tuple-element.189.refs_7_.refs_2_), channel_id=1, source_target_pairs={{8,0},{12,4},{16,8},{20,12},{24,16},{28,20},{9,1},{13,5},{17,9},{2... | collective-permute-start | bytes 3145736 | tf_op jit(solution)/shard_map/ppermute | solution.py:795
  482.8 64.8 %all-to-all-start.3 = ((bf16[4,352,1024]{2,1,0:T(8,128)(2,1)}), bf16[4,352,1024]{2,1,0:T(8,128)(2,1)S(1)}, u32[]{:S(2)}, u32[]{:S(2)}) async-start(bf16[4,352,1024]{2,1,0:T(8,128)(2,1)} %pair_sum.3), calls=%async_computation.3 | async-start | bytes 5767168 | tf_op jit(solution)/shard_map/all_to_all | solution.py:811
  488.2 9.6 %collective-permute-start.31 = (bf16[32,2560]{1,0:T(8,128)(2,1)}, bf16[32,2560]{1,0:T(8,128)(2,1)S(1)}, u32[]{:S(2)}, u32[]{:S(2)}) collective-permute-start(bf16[32,2560]{1,0:T(8,128)(2,1)} %get-tuple-element.193), channel_id=1, source_target_pairs={{0,1},{1,0},{2,3},{3,2},{4,5},{5,4},{6,7},{7,6},{8,9},{9,8},{10,11... | collective-permute-start | bytes 491528 | tf_op jit(solution)/shard_map/ppermute | solution.py:805
  489.5 12.7 %collective-permute-start.32 = (bf16[32,2560]{1,0:T(8,128)(2,1)}, bf16[32,2560]{1,0:T(8,128)(2,1)S(1)}, u32[]{:S(2)}, u32[]{:S(2)}) collective-permute-start(bf16[32,2560]{1,0:T(8,128)(2,1)} %get-tuple-element.194), channel_id=1, source_target_pairs={{0,2},{1,3},{2,0},{3,1},{4,6},{5,7},{6,4},{7,5},{8,10},{9,11},{10,... | collective-permute-start | bytes 491528 | tf_op jit(solution)/shard_map/ppermute | solution.py:805
  492.0 13.0 %collective-permute-start.33 = (bf16[32,2560]{1,0:T(8,128)(2,1)}, bf16[32,2560]{1,0:T(8,128)(2,1)S(1)}, u32[]{:S(2)}, u32[]{:S(2)}) collective-permute-start(bf16[32,2560]{1,0:T(8,128)(2,1)} %get-tuple-element.195), channel_id=1, source_target_pairs={{0,3},{1,2},{2,1},{3,0},{4,7},{5,6},{6,5},{7,4},{8,11},{9,10},{10,... | collective-permute-start | bytes 491528 | tf_op jit(solution)/shard_map/ppermute | solution.py:805
  511.4 14.9 %collective-permute-start.34 = (bf16[192,1024]{1,0:T(8,128)(2,1)}, bf16[192,1024]{1,0:T(8,128)(2,1)S(1)}, u32[]{:S(2)}, u32[]{:S(2)}) collective-permute-start(bf16[192,1024]{1,0:T(8,128)(2,1)} %get-tuple-element.197), channel_id=1, source_target_pairs={{0,1},{1,0},{2,3},{3,2},{4,5},{5,4},{6,7},{7,6},{8,9},{9,8},{10,11... | collective-permute-start | bytes 1179656 | tf_op jit(solution)/shard_map/ppermute | solution.py:805
  511.5 29.9 %collective-permute-start.35 = (bf16[192,1024]{1,0:T(8,128)(2,1)}, bf16[192,1024]{1,0:T(8,128)(2,1)}, u32[]{:S(2)}, u32[]{:S(2)}) collective-permute-start(bf16[192,1024]{1,0:T(8,128)(2,1)} %get-tuple-element.198), channel_id=1, source_target_pairs={{0,2},{1,3},{2,0},{3,1},{4,6},{5,7},{6,4},{7,5},{8,10},{9,11},{10,... | collective-permute-start | bytes 1179656 | tf_op jit(solution)/shard_map/ppermute | solution.py:805
  514.7 32.9 %collective-permute-start.36 = (bf16[192,1024]{1,0:T(8,128)(2,1)}, bf16[192,1024]{1,0:T(8,128)(2,1)}, u32[]{:S(2)}, u32[]{:S(2)}) collective-permute-start(bf16[192,1024]{1,0:T(8,128)(2,1)} %get-tuple-element.199), channel_id=1, source_target_pairs={{0,3},{1,2},{2,1},{3,0},{4,7},{5,6},{6,5},{7,4},{8,11},{9,10},{10,... | collective-permute-start | bytes 1179656 | tf_op jit(solution)/shard_map/ppermute | solution.py:805
  (48 other events, 328.7 us)

commit v4 on v3

--- a/solution.py
+++ b/solution.py
@@ -462,39 +462,51 @@
     )(act, wd, gate, *others)
 
 
-def norm_kernel(per_block, two_ref, one_ref, own_ref, gain_ref, out_ref, turned_ref):
+def norm_kernel(two_ref, one_ref, own_ref, gain_ref, out_ref):
     step = pl.program_id(0)
 
     def put(ref):
-        x = ref[0].astype(f32)
+        x = ref[...].astype(f32)
         r = lax.rsqrt(jnp.mean(x * x, axis=-1, keepdims=True) + epsilon)
-        normed = (x * r * gain_ref[...]).astype(bf16)
-        out_ref[0] = normed
-        turned_ref[...] = normed.T.reshape(turned_ref.shape)
+        out_ref[...] = (x * r * gain_ref[...][None]).astype(bf16)
 
     for n, ref in enumerate((two_ref, one_ref, own_ref)):
-        pl.when(step // per_block == n)(functools.partial(put, ref))
-
-
-def norm_window(two, one, own, gain, chips):
+        pl.when(step // 2 == n)(functools.partial(put, ref))
+
+
+def norm_window(two, one, own, gain):
     pieces, rows, width = own.shape
-    at = lambda n: pl.BlockSpec((1, rows, width), lambda f: (jnp.clip(f - n * pieces, 0, pieces - 1), 0, 0))
-    return pl.pallas_call(
-        functools.partial(norm_kernel, pieces),
-        grid=(3 * pieces,),
+    some = pieces // 2
+    at = lambda n: pl.BlockSpec((some, rows, width), lambda f: (jnp.clip(f - 2 * n, 0, 1), 0, 0))
+    return pl.pallas_call(
+        norm_kernel,
+        grid=(6,),
         in_specs=[at(0), at(1), at(2), pl.BlockSpec((1, width), lambda f: (0, 0))],
-        out_specs=[
-            pl.BlockSpec((1, rows, width), lambda f: (f, 0, 0)),
-            pl.BlockSpec((chips, 2, width // chips // 2, rows), lambda f: (0, 0, 0, f)),
-        ],
-        out_shape=[
-            jax.ShapeDtypeStruct((3 * pieces, rows, width), bf16),
-            jax.ShapeDtypeStruct((chips, 2, width // chips // 2, 3 * pieces * rows), bf16),
-        ],
-        compiler_params=pltpu.CompilerParams(vmem_limit_bytes=VMEM),
-        cost_estimate=cost(10),
+        out_specs=pl.BlockSpec((some, rows, width), lambda f: (f, 0, 0)),
+        out_shape=jax.ShapeDtypeStruct((3 * pieces, rows, width), bf16),
+        compiler_params=pltpu.CompilerParams(vmem_limit_bytes=VMEM),
+        cost_estimate=cost(5),
         name="norm_window",
     )(two, one, own, gain)
+
+
+def turn_kernel(rows_ref, out_ref):
+    out_ref[...] = rows_ref[0].T.reshape(out_ref.shape)
+
+
+def turn_rows(normed, chips, others=()):
+    pieces, rows, width = normed.shape
+    part = width // chips // 2
+    return pl.pallas_call(
+        behind(turn_kernel, 1, others),
+        grid=(pieces,),
+        in_specs=[pl.BlockSpec((1, rows, width), lambda f: (f, 0, 0))] + anywhere(others),
+        out_specs=pl.BlockSpec((chips, 2, part, rows), lambda f: (0, 0, 0, f)),
+        out_shape=jax.ShapeDtypeStruct((chips, 2, part, pieces * rows), bf16),
+        compiler_params=pltpu.CompilerParams(vmem_limit_bytes=VMEM),
+        cost_estimate=cost(8),
+        name="turn_rows",
+    )(normed, *others)
 
 
 def slot_rows(t_ref, k, slot):
@@ -897,26 +909,27 @@
     lo = jnp.broadcast_to(lo[:, None, None, :], (seqs, 1, 2, TILE)).reshape(seqs, 1, 2 * TILE)
 
     gain_one = norm1_gain.astype(f32)
-    normed, normed_t = norm_window(x_two, x_one, x_own, gain_one[None], ctx_count // 2)
-    normed = normed.reshape(-1, width)
+    normed_pieces = norm_window(x_two, x_one, x_own, gain_one[None])
+    normed = normed_pieces.reshape(-1, width)
     normed_own = normed[2 * block_len :]
     q = (dot(normed_own, w_query).astype(bf16) * 0.125).astype(bf16).reshape(seqs, piece_len, width)
     k_win = dot(normed, w_key).astype(bf16).reshape(-1, TILE, width)
     v_win = dot(normed, w_value).astype(bf16).reshape(-1, TILE, width)
     contexts, lses, context_rows = [None] * seqs, [], [None] * seqs
     for first in (2, 0):
-        others = [contexts[2], cot_slots[1]] if first == 0 else [cot_slots[2]]
+        others = [contexts[2], cot_slots[2]] if first == 0 else []
         *c, l = attend((first, first + 1), z, lo[first : first + 2], q[first : first + 2], k_win, v_win, bias, others)
         lses.insert(0, l)
         for k in (first, first + 1):
             contexts[k] = c[k - first]
             context_rows[k] = z_swap(contexts[k], k)
+    normed_t = turn_rows(normed_pieces, ctx_count // 2, contexts[:1])
     router_wide = jnp.pad(w_router, ((0, 0), (0, TILE - experts)))
     gain_two = norm2_gain.astype(f32)[None]
     hidden, moe_in, *sent = call(
         functools.partial(hidden_kernel, [2, 0], slot),
         [z, targets, tokens, w_out, gain_two] + context_rows,
-        [((rows, width), f32), ((rows, width), bf16), slot_shape, slot_shape], 9, "hidden_rows", [cot_slots[3]],
+        [((rows, width), f32), ((rows, width), bf16), slot_shape, slot_shape], 9, "hidden_rows", [cot_slots[1], cot_slots[3], normed_t],
     )
     inputs = [sent[1], None, z_swap(sent[0], 2), None]
     held, returned, turns = None, [None] * experts, [0, 2, 1, 3]
@@ -1005,15 +1018,15 @@
         [pltpu.VMEM((exp_count, share, long), bf16)],
     )
     pieces = [z_swap(piece, k) for k, piece in enumerate(pieces)]
+    grad_gate, grad_up, grad_down = summed(both[:, 0]), summed(both[:, 1]), summed(down)
     own_rows = lambda array: lax.dynamic_slice_in_dim(array, (ctx * exp_count + exp) * share, share, 0)
     grad_tokens, grad_query, grad_key, grad_value, packed, norm1_out, grad_out = call(
         end_kernel,
         [z, grad_hidden] + [own_rows(array) for array in weights] + [own_rows(gain_one[:, None])] + pieces + first,
         [((seqs, piece_len, width), bf16)] + [((share, width), f32)] * 3 + [((share, 2 * TILE), f32), ((share, 1), f32)]
         + [((share, width), f32)],
-        6, "end_rows", [down],
-    )
-    grad_gate, grad_up, grad_down = summed(both[:, 0]), summed(both[:, 1]), summed(down)
+        6, "end_rows", [grad_down],
+    )
     packed = packed[:, : -(-cuts[-1] // share)].reshape(-1)
     norm1_out = norm1_out[:, 0]
     norm2_out, table_out, router_out = [packed[cuts[i] : cuts[i + 1]] for i in range(3)]

time: 568 us -> 566 us (level)
    ppermute x27, waiting for transfers between devices: 61.6 us -> 47.4 us  [z_swap(): lax.ppermute(x, 'exp', [(i, i ^ k) for i in range(lax.axis_size('exp'))])]
    all_to_all x4, waiting for transfers between devices: 24.9 us -> 38 us  [over_chips(): lax.all_to_all(pair, 'ctx', split_axis=0, concat_axis=0, tiled=True, axis...]
    pallas_call x1 -> x2, Pallas kernels: 10.1 us -> 14.7 us  [the longest x1 8.55 us: turn_rows(): pl.pallas_call(behind(turn_kernel, 1, others), grid=(pieces,), in_specs=[...]
    unnamed x111 -> x113, local copies, waits for them, and re-layouts: 14.8 us -> 13.1 us
  transfers between devices with their start and end apart: 42 -> 42, of which waited for: 19 -> 21; matrix products, arithmetic and copies ran while one was open for 7% -> 8% of each run, Pallas kernels for 48% -> 49%
where the time goes in v4:
time: 566 us; the launch traced here: 559 us
  Pallas kernels  326 us (58%)
  waiting for transfers between devices  96.2 us (17%)
  starting transfers between devices  73.3 us (13%)
  local copies, waits for them, and re-layouts  31.3 us (6%)
  other arithmetic  19 us (3%)
  matrix products  11.7 us (2%)
    pallas_call x4, Pallas kernels, expert(): pl.pallas_call(functools.partial(expert_kernel, experts, count, len(held)...  88.5 us
    ppermute x27, waiting for transfers between devices, z_swap(): lax.ppermute(x, 'exp', [(i, i ^ k) for i in range(lax.axis_size('exp'))])  47.4 us
    pallas_call x2, Pallas kernels, attend_back(): pl.pallas_call(behind(functools.partial(attend_back_kernel, pieces), 8 +...  42.2 us
    pallas_call x8, Pallas kernels, call(): pl.pallas_call(behind(kernel, len(ins), others), in_specs=specs + anywher...  40.8 us
    all_to_all x4, waiting for transfers between devices, over_chips(): lax.all_to_all(pair, 'ctx', split_axis=0, concat_axis=0, tiled=True, axis...  38 us
    ppermute x27, starting transfers between devices, z_swap(): lax.ppermute(x, 'exp', [(i, i ^ k) for i in range(lax.axis_size('exp'))])  37.7 us
    pallas_call x2, Pallas kernels, attend(): pl.pallas_call(behind(functools.partial(attend_kernel, ks), 6, others), g...  29.9 us
    pallas_call x1, Pallas kernels, gate_up_grads(): pl.pallas_call(behind(gate_up_kernel, 5, others), grid=(hidden // wide,),...  22.8 us
  transfers between devices with their start and end apart: 42, of which 21 were waited for; matrix products, arithmetic and copies ran while one was open for 8% of the time, Pallas kernels for 49%

profile of v4, /device:TPU:10, one launch (start us, length us, event | category | flops | bytes accessed | tf_op | source)
XLA Modules:
  0.0 559.2 jit_solution(16400715067133244832)
XLA Ops:
  5.7 3.4 collective-permute-start
  16.4 6.8 %collective-permute-done.3.refs_4_ = bf16[128,1024]{1,0:T(8,128)(2,1)S(1)} collective-permute-done((bf16[128,1024]{1,0:T(8,128)(2,1)S(1)}, bf16[128,1024]{1,0:T(8,128)(2,1)S(1)}, u32[]{:S(2)}, u32[]{:S(2)}) %collective-permute-start.3) | collective-permute-done | bytes 262176 | tf_op jit(solution)/shard_map/ppermute | solution.py:817
  28.3 3.4 collective-permute-start.6
  38.8 3.7 cot_rows.1
  45.9 6.4 %bias_tiles.1.refs_5_.refs_7_ = bf16[8,9,128,256]{3,2,1,0:T(8,128)(2,1)} custom-call(f32[8,2,1280]{2,1,0:T(2,128)} %reshape.303.refs_0_, bf16[320,1024]{1,0:T(8,128)(2,1)} %get-tuple-element.109.refs_1_), custom_call_target="tpu_custom_call" | custom-call | flops 6899999744 | tf_op jit(solution)/shard_map/bias_tiles/pallas_call | solution.py:165
  53.3 6.2 %norm_window.1.refs_0_ = bf16[12,128,1024]{2,1,0:T(8,128)(2,1)} custom-call(bf16[4,128,1024]{2,1,0:T(8,128)(2,1)} %get-tuple-element.266.two_ref, bf16[4,128,1024]{2,1,0:T(8,128)(2,1)} %copy-done.29, bf16[4,128,1024]{2,1,0:T(8,128)(2,1)} %get-tuple-element.264.own_ref.refs_1_, f32[1,1024]{1,0:T(1,128)} %bitcast.107), custom_call_target="tpu_custom_call" | custom-call | flops 5750000128 | tf_op jit(solution)/shard_map/norm_window/pallas_call | solution.py:481
  64.1 4.8 convolution_convert_fusion.1
  68.9 4.8 convolution_convert_fusion
  74.2 14.9 %attend.2 = (bf16[128,1024]{1,0:T(8,128)(2,1)}, bf16[128,1024]{1,0:T(8,128)(2,1)}, f32[8,2,1,256]{3,2,1,0:T(1,128)}) custom-call(s32[1]{0:T(128)} %bitcast.refs_0_.z_ref.refs_1_, s32[2,1,256]{2,1,0:T(1,128)} %bitcast.113, bf16[2,128,1024]{2,1,0:T(8,128)(2,1)} %bitcast.91, bf16[12,128,1024]{2,1,0:T(8,128)(2,1)} %bitcast.116, ...), custom_call_target="tpu_custom_call" | custom-call | flops 17020000256 | tf_op jit(solution)/shard_map/attend/pallas_call | solution.py:184
  92.1 15.0 %attend.3 = (bf16[128,1024]{1,0:T(8,128)(2,1)}, bf16[128,1024]{1,0:T(8,128)(2,1)}, f32[8,2,1,256]{3,2,1,0:T(1,128)}) custom-call(s32[1]{0:T(128)} %bitcast.refs_0_.z_ref.refs_1_, s32[2,1,256]{2,1,0:T(1,128)} %bitcast.114, bf16[2,128,1024]{2,1,0:T(8,128)(2,1)} %bitcast.90, bf16[12,128,1024]{2,1,0:T(8,128)(2,1)} %bitcast.117, ...), custom_call_target="tpu_custom_call" | custom-call | flops 17020000256 | tf_op jit(solution)/shard_map/attend/pallas_call | solution.py:184
  108.5 8.6 %turn_rows.1.refs_11_.refs_1_ = bf16[4,2,128,1536]{3,2,1,0:T(8,128)(2,1)} custom-call(bf16[12,128,1024]{2,1,0:T(8,128)(2,1)} %norm_window.1.refs_0_, bf16[128,1024]{1,0:T(8,128)(2,1)} %get-tuple-element.111.refs_1_.refs_5_.refs_8_), custom_call_target="tpu_custom_call" | custom-call | flops 9200000000 | tf_op jit(solution)/shard_map/turn_rows/pallas_call | solution.py:500
  117.1 6.3 %collective-permute-done.9.refs_6_ = bf16[128,1024]{1,0:T(8,128)(2,1)S(1)} collective-permute-done((bf16[128,1024]{1,0:T(8,128)(2,1)}, bf16[128,1024]{1,0:T(8,128)(2,1)S(1)}, u32[]{:S(2)}, u32[]{:S(2)}) %collective-permute-start.9) | collective-permute-done | bytes 262176 | tf_op jit(solution)/shard_map/ppermute | solution.py:817
  125.1 5.6 hidden_rows.1
  133.0 22.2 %expert.4 = (bf16[320,1024]{1,0:T(8,128)(2,1)}, bf16[1280,1024]{1,0:T(8,128)(2,1)}, bf16[1280,2816]{1,0:T(8,128)(2,1)}, bf16[1280,2816]{1,0:T(8,128)(2,1)}, bf16...) custom-call(s32[1]{0:T(128)} %bitcast.refs_0_.z_ref.refs_1_, ...), custom_call_target="tpu_custom_call" | custom-call | flops 26449999872 | tf_op jit(solution)/shard_map/expert/pallas_call | solution.py:331
  162.0 22.1 %expert.5 = (bf16[320,1024]{1,0:T(8,128)(2,1)}, bf16[1280,1024]{1,0:T(8,128)(2,1)}, bf16[1280,2816]{1,0:T(8,128)(2,1)}, bf16[1280,2816]{1,0:T(8,128)(2,1)}, bf16...) custom-call(s32[1]{0:T(128)} %bitcast.refs_0_.z_ref.refs_1_, ...), custom_call_target="tpu_custom_call", output_to_operand_aliasing={{1}: (7, {}), {2}: (8, {}), {3}: (9, {}), {4}: (10, {}), {5... | custom-call | flops 26449999872 | tf_op jit(solution)/shard_map/expert/pallas_call | solution.py:331
  190.3 22.0 %expert.6 = (bf16[320,1024]{1,0:T(8,128)(2,1)}, bf16[1280,1024]{1,0:T(8,128)(2,1)}, bf16[1280,2816]{1,0:T(8,128)(2,1)}, bf16[1280,2816]{1,0:T(8,128)(2,1)}, bf16...) custom-call(s32[1]{0:T(128)} %bitcast.refs_0_.z_ref.refs_1_, ...), custom_call_target="tpu_custom_call", output_to_operand_aliasing={{1}: (7, {}), {2}: (8, {}), {3}: (9, {}), {4}: (10, {}), {5... | custom-call | flops 26449999872 | tf_op jit(solution)/shard_map/expert/pallas_call | solution.py:331
  213.2 22.2 %expert.7 = (bf16[320,1024]{1,0:T(8,128)(2,1)}, bf16[1280,1024]{1,0:T(8,128)(2,1)}, bf16[1280,2816]{1,0:T(8,128)(2,1)}, bf16[1280,2816]{1,0:T(8,128)(2,1)}, bf16...) custom-call(s32[1]{0:T(128)} %bitcast.refs_0_.z_ref.refs_1_, ...), custom_call_target="tpu_custom_call", output_to_operand_aliasing={{1}: (7, {}), {2}: (8, {}), {3}: (9, {}), {4}: (10, {}), {5... | custom-call | flops 26449999872 | tf_op jit(solution)/shard_map/expert/pallas_call | solution.py:331
  240.7 14.6 %expert_out.1 = (bf16[320,1024]{1,0:T(8,128)(2,1)}, bf16[320,1024]{1,0:T(8,128)(2,1)}, bf16[320,1024]{1,0:T(8,128)(2,1)}, bf16[320,1024]{1,0:T(8,128)(2,1)}) custom-call(bf16[1280,2816]{1,0:T(8,128)(2,1)} %get-tuple-element.145.refs_0_.refs_1_, bf16[1,2816,1024]{2,1,0:T(8,128)(2,1)} %refs_1_.1, f32[1280,128]{1,0:T(8,128)} %get-tuple-element.146.refs_2_, ...), custom_call_target="tpu_custom_call" | custom-call | flops 16099999744 | tf_op jit(solution)/shard_map/expert_out/pallas_call | solution.py:449
  255.3 12.6 %down_grads.1 = (bf16[4,352,1024]{2,1,0:T(8,128)(2,1)}, bf16[4,352,1024]{2,1,0:T(8,128)(2,1)}) custom-call(s32[1]{0:T(128)} %bitcast.36.refs_0_, bf16[1280,2816]{1,0:T(8,128)(2,1)} %get-tuple-element.145.refs_0_.refs_1_, bf16[1280,1024]{1,0:T(8,128)(2,1)} %get-tuple-element.156.refs_2_, bf16[320,1024]{1,0:T(8,128)(2,1)} %get-tuple-element.148.refs_3_), custom_call_target="tpu_custom_call" | custom-call | flops 16099999744 | tf_op jit(solution)/shard_map/down_grads/pallas_call | solution.py:410
  269.7 8.8 %middle_rows.1 = (f32[512,1024]{1,0:T(8,128)}, bf16[512,1024]{1,0:T(8,128)(2,1)}, f32[1,1024]{1,0:T(1,128)}, bf16[128,1024]{1,0:T(8,128)(2,1)}, bf16[128,1024]{1...) custom-call(s32[1]{0:T(128)} %bitcast.refs_0_.z_ref.refs_1_, s32[512,2]{1,0:T(8,128)} %bitcast.94, ...), custom_call_target="tpu_custom_call" | custom-call | flops 10350000128 | tf_op jit(solution)/shard_map/middle_rows/pallas_call | solution.py:536
  278.4 22.8 %gate_up_grads.1 = (bf16[4,2,128,2816]{3,2,1,0:T(8,128)(2,1)}, bf16[4,2,128,2816]{3,2,1,0:T(8,128)(2,1)}, f32[1024,128]{1,0:T(8,128)}) custom-call(s32[1]{0:T(128)} %bitcast.36.refs_0_, bf16[1280,1024]{1,0:T(8,128)(2,1)} %get-tuple-element.162.refs_1_, bf16[1280,2816]{1,0:T(8,128)(2,1)} %get-tuple-element.163.refs_2_, ...), custom_call_target="tpu_custom_call" | custom-call | flops 27599998976 | tf_op jit(solution)/shard_map/gate_up_grads/pallas_call | solution.py:378
  307.2 3.7 collective-permute-done.26.refs_1_
  313.3 7.3 %pair_sum.2.refs_16_ = bf16[4,2,128,2816]{3,2,1,0:T(8,128)(2,1)} custom-call(bf16[4,2,128,2816]{3,2,1,0:T(8,128)(2,1)} %get-tuple-element.166.refs_0_, bf16[4,2,128,2816]{3,2,1,0:T(8,128)(2,1)} %copy-done.27), custom_call_target="tpu_custom_call" | custom-call | flops 6899999744 | tf_op jit(solution)/shard_map/pair_sum/pallas_call | solution.py:554
  320.7 5.3 all-to-all-start
  326.8 21.0 %attend_back.2 = (bf16[4,128,512]{2,1,0:T(8,128)(2,1)}, bf16[12,128,512]{2,1,0:T(8,128)(2,1)}, bf16[12,128,512]{2,1,0:T(8,128)(2,1)}, f32[4,2,9,256]{3,2,1,0:T(8,128)}) custom-call(s32[1]{0:T(128)} %bitcast.refs_0_.z_ref.refs_1_, s32[4,1,256]{2,1,0:T(1,128)} %bitcast.111, f32[8,2,1,256]{3,2,1,0:T(1,128)} %get-tuple-element.152.refs_2_, ...), custom_call_target="tpu_custom_call" | custom-call | flops 24149999616 | tf_op jit(solution)/shard_map/attend_back/pallas_call | solution.py:217
  347.8 5.8 %collective-permute-done.19.refs_10_.refs_5_ = bf16[320,1024]{1,0:T(8,128)(2,1)S(1)} collective-permute-done((bf16[320,1024]{1,0:T(8,128)(2,1)S(1)}, bf16[320,1024]{1,0:T(8,128)(2,1)S(1)}, u32[]{:S(2)}, u32[]{:S(2)}) %collective-permute-start.19) | collective-permute-done | bytes 655392 | tf_op jit(solution)/shard_map/ppermute | solution.py:817
  354.4 12.6 %projection_grads.2 = (bf16[4,128,2560]{2,1,0:T(8,128)(2,1)}, bf16[4,128,2560]{2,1,0:T(8,128)(2,1)}) custom-call(s32[1]{0:T(128)} %bitcast.36.refs_0_, bf16[4,2,128,1536]{3,2,1,0:T(8,128)(2,1)} %turn_rows.1.refs_11_.refs_1_, bf16[512,512]{1,0:T(8,128)(2,1)} %bitcast.129, bf16[1536,512]{1,0:T(8,128)(2,1)} %bitcast.126, bf16[1536,512]{1,0:T(8,128)(2,1)} %bitcast.127, ...), custom_call_target="tpu_custom_call" | custom-call | flops 15294999552 | tf_op jit(solution)/shard_map/projection_grads/pallas_call | solution.py:783
  368.7 8.9 %input_grads.2.refs_16_.refs_6_ = f32[1536,1024]{1,0:T(8,128)} custom-call(bf16[4,128,512]{2,1,0:T(8,128)(2,1)} %get-tuple-element.168.refs_0_, bf16[12,128,512]{2,1,0:T(8,128)(2,1)} %get-tuple-element.169.refs_1_, bf16[12,128,512]{2,1,0:T(8,128)(2,1)} %get-tuple-element.170.refs_2_, bf16[1024,1024]{1,0:T(8,128)(2,1)} %refs_3_.15, ...), custom_call_target="tpu_custom_call" | custom-call | flops 8049999872 | tf_op jit(solution)/shard_map/input_grads/pallas_call | solution.py:655
  379.9 11.5 %all-to-all-done.refs_18_ = bf16[4,2,128,2816]{3,2,1,0:T(8,128)(2,1)} async-done(((bf16[4,2,128,2816]{3,2,1,0:T(8,128)(2,1)}), bf16[4,2,128,2816]{3,2,1,0:T(8,128)(2,1)}, u32[]{:S(2)}, u32[]{:S(2)}) %all-to-all-start) | async-done | bytes 5767200 | tf_op jit(solution)/shard_map/all_to_all | solution.py:823
  391.4 3.9 all-to-all-start.1
  395.4 21.2 %attend_back.3 = (bf16[4,128,512]{2,1,0:T(8,128)(2,1)}, bf16[12,128,512]{2,1,0:T(8,128)(2,1)}, bf16[12,128,512]{2,1,0:T(8,128)(2,1)}, f32[4,2,9,256]{3,2,1,0:T(8,128)}) custom-call(s32[1]{0:T(128)} %bitcast.refs_0_.z_ref.refs_1_, s32[4,1,256]{2,1,0:T(1,128)} %bitcast.112, f32[8,2,1,256]{3,2,1,0:T(1,128)} %get-tuple-element.152.refs_2_, ...), custom_call_target="tpu_custom_call" | custom-call | flops 24149999616 | tf_op jit(solution)/shard_map/attend_back/pallas_call | solution.py:217
  420.0 5.7 %all-to-all-done.1.refs_6_.refs_4_ = bf16[4,128,2560]{2,1,0:T(8,128)(2,1)S(1)} async-done(((bf16[4,128,2560]{2,1,0:T(8,128)(2,1)}), bf16[4,128,2560]{2,1,0:T(8,128)(2,1)S(1)}, u32[]{:S(2)}, u32[]{:S(2)}) %all-to-all-start.1) | async-done | bytes 2621472 | tf_op jit(solution)/shard_map/all_to_all | solution.py:823
  427.2 9.3 %projection_grads.3 = (bf16[4,128,1792]{2,1,0:T(8,128)(2,1)}, bf16[4,128,1792]{2,1,0:T(8,128)(2,1)}) custom-call(s32[1]{0:T(128)} %bitcast.36.refs_0_, bf16[4,2,128,1536]{3,2,1,0:T(8,128)(2,1)} %turn_rows.1.refs_11_.refs_1_, bf16[512,512]{1,0:T(8,128)(2,1)} %bitcast.128, bf16[1536,512]{1,0:T(8,128)(2,1)} %bitcast.124, bf16[1536,512]{1,0:T(8,128)(2,1)} %bitcast.125, ...), custom_call_target="tpu_custom_call" | custom-call | flops 11845000192 | tf_op jit(solution)/shard_map/projection_grads/pallas_call | solution.py:783
  437.0 5.5 collective-permute-done.28
  445.6 4.1 all-to-all-start.2
  449.8 10.5 %input_grads.3 = (bf16[512,1024]{1,0:T(8,128)(2,1)}, bf16[512,1024]{1,0:T(8,128)(2,1)}, f32[512,1024]{1,0:T(8,128)}) custom-call(bf16[4,128,512]{2,1,0:T(8,128)(2,1)} %get-tuple-element.174.refs_0_, bf16[12,128,512]{2,1,0:T(8,128)(2,1)} %get-tuple-element.175.refs_1_, bf16[12,128,512]{2,1,0:T(8,128)(2,1)} %get-tuple-element.176.refs_2_, ...), custom_call_target="tpu_custom_call" | custom-call | flops 8049999872 | tf_op jit(solution)/shard_map/input_grads/pallas_call | solution.py:655
  463.3 8.6 %all-to-all-done.2.refs_5_.refs_6_ = bf16[4,128,1792]{2,1,0:T(8,128)(2,1)S(1)} async-done(((bf16[4,128,1792]{2,1,0:T(8,128)(2,1)}), bf16[4,128,1792]{2,1,0:T(8,128)(2,1)S(1)}, u32[]{:S(2)}, u32[]{:S(2)}) %all-to-all-start.2) | async-done | bytes 1835040 | tf_op jit(solution)/shard_map/all_to_all | solution.py:823
  473.1 4.6 leaving_rows.1
  480.2 4.9 pair_sum.3
  485.1 5.5 all-to-all-start.3
  495.6 5.8 %mixed_rows.1.refs_7_ = bf16[4,128,1024]{2,1,0:T(8,128)(2,1)} custom-call(s32[1]{0:T(128)} %bitcast.refs_0_.z_ref.refs_1_, s32[512,2]{1,0:T(8,128)} %bitcast.95, f32[512,1024]{1,0:T(8,128)} %get-tuple-element.116.refs_2_, bf16[320,1024]{1,0:T(8,128)(2,1)} %get-tuple-element.148.refs_3_, bf16[320,1024]{1,0:T(8,128)(2,1)} %copy-done.30, ...), custom_call_target="tpu_custom_call" | custom-call | flops 9200000000 | tf_op jit(solution)/shard_map/mixed_rows/pallas_call | solution.py:536
  501.4 3.8 collective-permute-done.32.refs_9_.refs_12_
  509.1 5.7 %tail_rows.1 = (bf16[192,1024]{1,0:T(8,128)(2,1)}, bf16[192,1024]{1,0:T(8,128)(2,1)}, bf16[192,1024]{1,0:T(8,128)(2,1)}, bf16[192,1024]{1,0:T(8,128)(2,1)}) custom-call(s32[1]{0:T(128)} %bitcast.refs_0_.z_ref.refs_1_, bf16[4,128,1024]{2,1,0:T(8,128)(2,1)} %get-tuple-element.264.own_ref.refs_1_, f32[512,1024]{1,0:T(8,128)} %get-tuple-element.187.refs_2_, ...), custom_call_target="tpu_custom_call" | custom-call | flops 9200000000 | tf_op jit(solution)/shard_map/tail_rows/pallas_call | solution.py:536
  518.3 5.4 convert_reduce_fusion
  523.8 12.2 %all-to-all-done.3 = bf16[4,352,1024]{2,1,0:T(8,128)(2,1)S(1)} async-done(((bf16[4,352,1024]{2,1,0:T(8,128)(2,1)}), bf16[4,352,1024]{2,1,0:T(8,128)(2,1)S(1)}, u32[]{:S(2)}, u32[]{:S(2)}) %all-to-all-start.3) | async-done | bytes 2883616 | tf_op jit(solution)/shard_map/all_to_all | solution.py:823
  537.6 6.6 %collective-permute-done.35.refs_8_ = bf16[192,1024]{1,0:T(8,128)(2,1)} collective-permute-done((bf16[192,1024]{1,0:T(8,128)(2,1)}, bf16[192,1024]{1,0:T(8,128)(2,1)}, u32[]{:S(2)}, u32[]{:S(2)}) %collective-permute-start.35) | collective-permute-done | bytes 393248 | tf_op jit(solution)/shard_map/ppermute | solution.py:817
  544.2 6.9 %collective-permute-done.36.refs_9_ = bf16[192,1024]{1,0:T(8,128)(2,1)} collective-permute-done((bf16[192,1024]{1,0:T(8,128)(2,1)}, bf16[192,1024]{1,0:T(8,128)(2,1)}, u32[]{:S(2)}, u32[]{:S(2)}) %collective-permute-start.36) | collective-permute-done | bytes 393248 | tf_op jit(solution)/shard_map/ppermute | solution.py:817
  551.2 3.7 end_rows.1
  (239 shorter events, 110.4 us)
Async XLA Ops:
  0.7 31.0 %copy-start.21 = (bf16[1024]{0:T(1024)(128)(2,1)S(1)}, bf16[1024]{0:T(1024)(128)(2,1)}, u32[]{:S(2)}) copy-start(bf16[1024]{0:T(1024)(128)(2,1)} %param.23) | copy-start | bytes 6148
  0.7 32.3 %copy-start.22 = (bf16[1024]{0:T(1024)(128)(2,1)S(1)}, bf16[1024]{0:T(1024)(128)(2,1)}, u32[]{:S(2)}) copy-start(bf16[1024]{0:T(1024)(128)(2,1)} %param.29) | copy-start | bytes 6148
  0.7 32.9 %copy-start.18 = (bf16[1024,4]{0,1:T(4,128)(2,1)S(1)}, bf16[1024,4]{0,1:T(4,128)(2,1)}, u32[]{:S(2)}) copy-start(bf16[1024,4]{0,1:T(4,128)(2,1)} %param.30) | copy-start | bytes 24580
  2.1 10.9 %collective-permute-start.1 = (bf16[128,1024]{1,0:T(8,128)(2,1)S(1)}, bf16[128,1024]{1,0:T(8,128)(2,1)S(1)}, u32[]{:S(2)}, u32[]{:S(2)}) collective-permute-start(bf16[128,1024]{1,0:T(8,128)(2,1)S(1)} %get-tuple-element.269), channel_id=1, source_target_pairs={{0,1},{1,0},{2,3},{3,2},{4,5},{5,4},{6,7},{7,6},{8,9},{9,8},{10,11... | collective-permute-start | bytes 786440 | tf_op jit(solution)/shard_map/ppermute | solution.py:817
  2.6 20.6 %collective-permute-start.3 = (bf16[128,1024]{1,0:T(8,128)(2,1)S(1)}, bf16[128,1024]{1,0:T(8,128)(2,1)S(1)}, u32[]{:S(2)}, u32[]{:S(2)}) collective-permute-start(bf16[128,1024]{1,0:T(8,128)(2,1)S(1)} %get-tuple-element.268), channel_id=1, source_target_pairs={{0,2},{1,3},{2,0},{3,1},{4,6},{5,7},{6,4},{7,5},{8,10},{9,11},{10,... | collective-permute-start | bytes 786440 | tf_op jit(solution)/shard_map/ppermute | solution.py:817
  5.2 23.1 %collective-permute-start.5 = (bf16[128,1024]{1,0:T(8,128)(2,1)S(1)}, bf16[128,1024]{1,0:T(8,128)(2,1)S(1)}, u32[]{:S(2)}, u32[]{:S(2)}) collective-permute-start(bf16[128,1024]{1,0:T(8,128)(2,1)S(1)} %get-tuple-element.270), channel_id=1, source_target_pairs={{0,3},{1,2},{2,1},{3,0},{4,7},{5,6},{6,5},{7,4},{8,11},{9,10},{10,... | collective-permute-start | bytes 786440 | tf_op jit(solution)/shard_map/ppermute | solution.py:817
  5.7 29.8 %collective-permute-start = (bf16[128,1024]{1,0:T(8,128)(2,1)S(1)}, bf16[128,1024]{1,0:T(8,128)(2,1)S(1)}, u32[]{:S(2)}, u32[]{:S(2)}) collective-permute-start(bf16[128,1024]{1,0:T(8,128)(2,1)S(1)} %bitcast.87), channel_id=1, source_target_pairs={{0,8},{4,12},{8,16},{12,20},{16,24},{20,28},{1,9},{5,13},{9,17},{1... | collective-permute-start | bytes 786440 | tf_op jit(solution)/shard_map/ppermute | solution.py:807
  12.3 26.4 %copy-start.15 = (s32[4,128]{1,0:T(4,128)}, s32[4,128]{1,0:T(4,128)S(1)}, u32[]{:S(2)}) copy-start(s32[4,128]{1,0:T(4,128)S(1)} %broadcast_subtract_fusion) | copy-start | bytes 6148
  13.0 25.7 %copy-start.8 = (bf16[128,1024]{1,0:T(8,128)(2,1)}, bf16[128,1024]{1,0:T(8,128)(2,1)S(1)}, u32[]{:S(2)}) copy-start(bf16[128,1024]{1,0:T(8,128)(2,1)S(1)} %collective-permute-done.1.refs_3_) | copy-start | bytes 786436
  13.0 22.4 %collective-permute-start.2 = (bf16[128,1024]{1,0:T(8,128)(2,1)S(1)}, bf16[128,1024]{1,0:T(8,128)(2,1)S(1)}, u32[]{:S(2)}, u32[]{:S(2)}) collective-permute-start(bf16[128,1024]{1,0:T(8,128)(2,1)S(1)} %collective-permute-done.1.refs_3_), channel_id=1, source_target_pairs={{0,8},{4,12},{8,16},{12,20},{16,24},{20,28},{1,9},{5,13},{9,17},{1... | collective-permute-start | bytes 786440 | tf_op jit(solution)/shard_map/ppermute | solution.py:807
  23.2 12.3 %collective-permute-start.4 = (bf16[128,1024]{1,0:T(8,128)(2,1)S(1)}, bf16[128,1024]{1,0:T(8,128)(2,1)S(1)}, u32[]{:S(2)}, u32[]{:S(2)}) collective-permute-start(bf16[128,1024]{1,0:T(8,128)(2,1)S(1)} %collective-permute-done.3.refs_4_), channel_id=1, source_target_pairs={{0,8},{4,12},{8,16},{12,20},{16,24},{20,28},{1,9},{5,13},{9,17},{1... | collective-permute-start | bytes 786440 | tf_op jit(solution)/shard_map/ppermute | solution.py:807
  28.3 8.8 %collective-permute-start.6 = (bf16[128,1024]{1,0:T(8,128)(2,1)S(1)}, bf16[128,1024]{1,0:T(8,128)(2,1)S(1)}, u32[]{:S(2)}, u32[]{:S(2)}) collective-permute-start(bf16[128,1024]{1,0:T(8,128)(2,1)S(1)} %collective-permute-done.5.refs_5_), channel_id=1, source_target_pairs={{0,8},{4,12},{8,16},{12,20},{16,24},{20,28},{1,9},{5,13},{9,17},{1... | collective-permute-start | bytes 786440 | tf_op jit(solution)/shard_map/ppermute | solution.py:807
  38.7 13.6 %collective-permute-start.7 = (bf16[4,128,1024]{2,1,0:T(8,128)(2,1)S(1)}, bf16[4,128,1024]{2,1,0:T(8,128)(2,1)S(1)}, u32[]{:S(2)}, u32[]{:S(2)}) collective-permute-start(bf16[4,128,1024]{2,1,0:T(8,128)(2,1)S(1)} %get-tuple-element.265), channel_id=1, source_target_pairs={{0,4},{4,0},{8,12},{12,8},{16,20},{20,16},{24,28},{28,24},{1,5},{5... | collective-permute-start | bytes 3145736 | tf_op jit(solution)/shard_map/ppermute | solution.py:811
  42.5 48.8 %collective-permute-start.8 = (bf16[320,1024]{1,0:T(8,128)(2,1)}, bf16[320,1024]{1,0:T(8,128)(2,1)S(1)}, u32[]{:S(2)}, u32[]{:S(2)}) collective-permute-start(bf16[320,1024]{1,0:T(8,128)(2,1)} %get-tuple-element.109.refs_1_), channel_id=1, source_target_pairs={{0,2},{1,3},{2,0},{3,1},{4,6},{5,7},{6,4},{7,5},{8,10},{9,11},{10,... | collective-permute-start | bytes 1966088 | tf_op jit(solution)/shard_map/ppermute | solution.py:817
  43.6 73.4 %collective-permute-start.12 = (bf16[320,1024]{1,0:T(8,128)(2,1)}, bf16[320,1024]{1,0:T(8,128)(2,1)S(1)}, u32[]{:S(2)}, u32[]{:S(2)}) collective-permute-start(bf16[320,1024]{1,0:T(8,128)(2,1)} %get-tuple-element.114), channel_id=1, source_target_pairs={{0,1},{1,0},{2,3},{3,2},{4,5},{5,4},{6,7},{7,6},{8,9},{9,8},{10,11... | collective-permute-start | bytes 1966088 | tf_op jit(solution)/shard_map/ppermute | solution.py:817
  45.5 71.5 %collective-permute-start.13 = (bf16[320,1024]{1,0:T(8,128)(2,1)}, bf16[320,1024]{1,0:T(8,128)(2,1)S(1)}, u32[]{:S(2)}, u32[]{:S(2)}) collective-permute-start(bf16[320,1024]{1,0:T(8,128)(2,1)} %get-tuple-element.115), channel_id=1, source_target_pairs={{0,3},{1,2},{2,1},{3,0},{4,7},{5,6},{6,5},{7,4},{8,11},{9,10},{10,... | collective-permute-start | bytes 1966088 | tf_op jit(solution)/shard_map/ppermute | solution.py:817
  89.2 34.2 %collective-permute-start.10 = (bf16[128,1024]{1,0:T(8,128)(2,1)}, bf16[128,1024]{1,0:T(8,128)(2,1)S(1)}, u32[]{:S(2)}, u32[]{:S(2)}) collective-permute-start(bf16[128,1024]{1,0:T(8,128)(2,1)} %get-tuple-element.110.refs_6_.refs_10_), channel_id=1, source_target_pairs={{0,2},{1,3},{2,0},{3,1},{4,6},{5,7},{6,4},{7,5},{8,10},{9,11},{10,... | collective-permute-start | bytes 786440 | tf_op jit(solution)/shard_map/ppermute | solution.py:817
  107.1 16.3 %collective-permute-start.9 = (bf16[128,1024]{1,0:T(8,128)(2,1)}, bf16[128,1024]{1,0:T(8,128)(2,1)S(1)}, u32[]{:S(2)}, u32[]{:S(2)}) collective-permute-start(bf16[128,1024]{1,0:T(8,128)(2,1)} %get-tuple-element.112.refs_9_), channel_id=1, source_target_pairs={{0,1},{1,0},{2,3},{3,2},{4,5},{5,4},{6,7},{7,6},{8,9},{9,8},{10,11... | collective-permute-start | bytes 786440 | tf_op jit(solution)/shard_map/ppermute | solution.py:817
  108.0 16.3 %collective-permute-start.11 = (bf16[128,1024]{1,0:T(8,128)(2,1)S(1)}, bf16[128,1024]{1,0:T(8,128)(2,1)S(1)}, u32[]{:S(2)}, u32[]{:S(2)}) collective-permute-start(bf16[128,1024]{1,0:T(8,128)(2,1)S(1)} %copy-done.44), channel_id=1, source_target_pairs={{0,3},{1,2},{2,1},{3,0},{4,7},{5,6},{6,5},{7,4},{8,11},{9,10},{10,... | collective-permute-start | bytes 786440 | tf_op jit(solution)/shard_map/ppermute | solution.py:817
  130.6 30.6 %collective-permute-start.16 = (bf16[320,1024]{1,0:T(8,128)(2,1)}, bf16[320,1024]{1,0:T(8,128)(2,1)S(1)}, u32[]{:S(2)}, u32[]{:S(2)}) collective-permute-start(bf16[320,1024]{1,0:T(8,128)(2,1)} %get-tuple-element.123), channel_id=1, source_target_pairs={{0,2},{1,3},{2,0},{3,1},{4,6},{5,7},{6,4},{7,5},{8,10},{9,11},{10,... | collective-permute-start | bytes 1966088 | tf_op jit(solution)/shard_map/ppermute | solution.py:817
  158.2 31.3 %collective-permute-start.15 = (bf16[320,1024]{1,0:T(8,128)(2,1)}, bf16[320,1024]{1,0:T(8,128)(2,1)S(1)}, u32[]{:S(2)}, u32[]{:S(2)}) collective-permute-start(bf16[320,1024]{1,0:T(8,128)(2,1)} %get-tuple-element.122), channel_id=1, source_target_pairs={{0,1},{1,0},{2,3},{3,2},{4,5},{5,4},{6,7},{7,6},{8,9},{9,8},{10,11... | collective-permute-start | bytes 1966088 | tf_op jit(solution)/shard_map/ppermute | solution.py:817
  158.6 53.7 %collective-permute-start.14 = (bf16[320,1024]{1,0:T(8,128)(2,1)}, bf16[320,1024]{1,0:T(8,128)(2,1)S(1)}, u32[]{:S(2)}, u32[]{:S(2)}) collective-permute-start(bf16[320,1024]{1,0:T(8,128)(2,1)} %get-tuple-element.121), channel_id=1, source_target_pairs={{0,3},{1,2},{2,1},{3,0},{4,7},{5,6},{6,5},{7,4},{8,11},{9,10},{10,... | collective-permute-start | bytes 1966088 | tf_op jit(solution)/shard_map/ppermute | solution.py:817
  184.1 55.8 %collective-permute-start.17 = (bf16[320,1024]{1,0:T(8,128)(2,1)}, bf16[320,1024]{1,0:T(8,128)(2,1)S(1)}, u32[]{:S(2)}, u32[]{:S(2)}) collective-permute-start(bf16[320,1024]{1,0:T(8,128)(2,1)} %get-tuple-element.147), channel_id=1, source_target_pairs={{0,2},{1,3},{2,0},{3,1},{4,6},{5,7},{6,4},{7,5},{8,10},{9,11},{10,... | collective-permute-start | bytes 1966088 | tf_op jit(solution)/shard_map/ppermute | solution.py:817
  235.4 32.5 %collective-permute-start.22 = (bf16[320,1024]{1,0:T(8,128)(2,1)}, bf16[320,1024]{1,0:T(8,128)(2,1)S(1)}, u32[]{:S(2)}, u32[]{:S(2)}) collective-permute-start(bf16[320,1024]{1,0:T(8,128)(2,1)} %get-tuple-element.155), channel_id=1, source_target_pairs={{0,3},{1,2},{2,1},{3,0},{4,7},{5,6},{6,5},{7,4},{8,11},{9,10},{10,... | collective-permute-start | bytes 1966088 | tf_op jit(solution)/shard_map/ppermute | solution.py:817
  236.7 32.2 %collective-permute-start.21 = (bf16[320,1024]{1,0:T(8,128)(2,1)S(1)}, bf16[320,1024]{1,0:T(8,128)(2,1)S(1)}, u32[]{:S(2)}, u32[]{:S(2)}) collective-permute-start(bf16[320,1024]{1,0:T(8,128)(2,1)S(1)} %copy-done.38), channel_id=1, source_target_pairs={{0,1},{1,0},{2,3},{3,2},{4,5},{5,4},{6,7},{7,6},{8,9},{9,8},{10,11... | collective-permute-start | bytes 1966088 | tf_op jit(solution)/shard_map/ppermute | solution.py:817
  278.4 32.4 %copy-start.35 = (bf16[320,1024]{1,0:T(8,128)(2,1)S(1)}, bf16[320,1024]{1,0:T(8,128)(2,1)}, u32[]{:S(2)}) copy-start(bf16[320,1024]{1,0:T(8,128)(2,1)} %get-tuple-element.150) | copy-start | bytes 1966084
  301.2 9.6 %collective-permute-start.26 = (bf16[4,2,128,2816]{3,2,1,0:T(8,128)(2,1)}, bf16[4,2,128,2816]{3,2,1,0:T(8,128)(2,1)S(1)}, u32[]{:S(2)}, u32[]{:S(2)}) collective-permute-start(bf16[4,2,128,2816]{3,2,1,0:T(8,128)(2,1)} %get-tuple-element.167), channel_id=1, source_target_pairs={{0,4},{4,0},{8,12},{12,8},{16,20},{20,16},{24,28},{28,24},{1,5},{5... | collective-permute-start | bytes 17301512 | tf_op jit(solution)/shard_map/ppermute | solution.py:811
  301.2 24.8 %collective-permute-start.25 = (bf16[128,1024]{1,0:T(8,128)(2,1)}, bf16[128,1024]{1,0:T(8,128)(2,1)S(1)}, u32[]{:S(2)}, u32[]{:S(2)}) collective-permute-start(bf16[128,1024]{1,0:T(8,128)(2,1)} %get-tuple-element.161.refs_5_), channel_id=1, source_target_pairs={{0,3},{1,2},{2,1},{3,0},{4,7},{5,6},{6,5},{7,4},{8,11},{9,10},{10,... | collective-permute-start | bytes 786440 | tf_op jit(solution)/shard_map/ppermute | solution.py:817
  302.2 23.8 %collective-permute-start.23 = (bf16[128,1024]{1,0:T(8,128)(2,1)}, bf16[128,1024]{1,0:T(8,128)(2,1)S(1)}, u32[]{:S(2)}, u32[]{:S(2)}) collective-permute-start(bf16[128,1024]{1,0:T(8,128)(2,1)} %get-tuple-element.159), channel_id=1, source_target_pairs={{0,1},{1,0},{2,3},{3,2},{4,5},{5,4},{6,7},{7,6},{8,9},{9,8},{10,11... | collective-permute-start | bytes 786440 | tf_op jit(solution)/shard_map/ppermute | solution.py:817
  304.5 21.5 %collective-permute-start.24 = (bf16[128,1024]{1,0:T(8,128)(2,1)}, bf16[128,1024]{1,0:T(8,128)(2,1)}, u32[]{:S(2)}, u32[]{:S(2)}) collective-permute-start(bf16[128,1024]{1,0:T(8,128)(2,1)} %get-tuple-element.160), channel_id=1, source_target_pairs={{0,2},{1,3},{2,0},{3,1},{4,6},{5,7},{6,4},{7,5},{8,10},{9,11},{10,... | collective-permute-start | bytes 786440 | tf_op jit(solution)/shard_map/ppermute | solution.py:817
  305.2 42.6 %collective-permute-start.18 = (bf16[320,1024]{1,0:T(8,128)(2,1)}, bf16[320,1024]{1,0:T(8,128)(2,1)S(1)}, u32[]{:S(2)}, u32[]{:S(2)}) collective-permute-start(bf16[320,1024]{1,0:T(8,128)(2,1)} %get-tuple-element.149), channel_id=1, source_target_pairs={{0,1},{1,0},{2,3},{3,2},{4,5},{5,4},{6,7},{7,6},{8,9},{9,8},{10,11... | collective-permute-start | bytes 1966088 | tf_op jit(solution)/shard_map/ppermute | solution.py:817
  310.9 42.7 %collective-permute-start.19 = (bf16[320,1024]{1,0:T(8,128)(2,1)S(1)}, bf16[320,1024]{1,0:T(8,128)(2,1)S(1)}, u32[]{:S(2)}, u32[]{:S(2)}) collective-permute-start(bf16[320,1024]{1,0:T(8,128)(2,1)S(1)} %copy-done.35), channel_id=1, source_target_pairs={{0,2},{1,3},{2,0},{3,1},{4,6},{5,7},{6,4},{7,5},{8,10},{9,11},{10,... | collective-permute-start | bytes 1966088 | tf_op jit(solution)/shard_map/ppermute | solution.py:817
  320.7 70.7 %all-to-all-start = ((bf16[4,2,128,2816]{3,2,1,0:T(8,128)(2,1)}), bf16[4,2,128,2816]{3,2,1,0:T(8,128)(2,1)}, u32[]{:S(2)}, u32[]{:S(2)}) async-start(bf16[4,2,128,2816]{3,2,1,0:T(8,128)(2,1)} %pair_sum.2.refs_16_), calls=%async_computation | async-start | bytes 11534336 | tf_op jit(solution)/shard_map/all_to_all | solution.py:823
  367.1 10.6 %collective-permute-start.27 = (bf16[4,128,2560]{2,1,0:T(8,128)(2,1)}, bf16[4,128,2560]{2,1,0:T(8,128)(2,1)S(1)}, u32[]{:S(2)}, u32[]{:S(2)}) collective-permute-start(bf16[4,128,2560]{2,1,0:T(8,128)(2,1)} %get-tuple-element.172.refs_6_), channel_id=1, source_target_pairs={{0,4},{4,0},{8,12},{12,8},{16,20},{20,16},{24,28},{28,24},{1,5},{5... | collective-permute-start | bytes 7864328 | tf_op jit(solution)/shard_map/ppermute | solution.py:811
  367.6 52.4 %collective-permute-start.20 = (bf16[320,1024]{1,0:T(8,128)(2,1)}, bf16[320,1024]{1,0:T(8,128)(2,1)}, u32[]{:S(2)}, u32[]{:S(2)}) collective-permute-start(bf16[320,1024]{1,0:T(8,128)(2,1)} %get-tuple-element.151), channel_id=1, source_target_pairs={{0,3},{1,2},{2,1},{3,0},{4,7},{5,6},{6,5},{7,4},{8,11},{9,10},{10,... | collective-permute-start | bytes 1966088 | tf_op jit(solution)/shard_map/ppermute | solution.py:817
  391.4 34.3 %all-to-all-start.1 = ((bf16[4,128,2560]{2,1,0:T(8,128)(2,1)}), bf16[4,128,2560]{2,1,0:T(8,128)(2,1)S(1)}, u32[]{:S(2)}, u32[]{:S(2)}) async-start(bf16[4,128,2560]{2,1,0:T(8,128)(2,1)} %add_convert_fusion.refs_17_), calls=%async_computation.1 | async-start | bytes 5242880 | tf_op jit(solution)/shard_map/all_to_all | solution.py:823
  436.5 6.0 %collective-permute-start.28 = (bf16[4,128,1792]{2,1,0:T(8,128)(2,1)}, bf16[4,128,1792]{2,1,0:T(8,128)(2,1)S(1)}, u32[]{:S(2)}, u32[]{:S(2)}) collective-permute-start(bf16[4,128,1792]{2,1,0:T(8,128)(2,1)} %get-tuple-element.182), channel_id=1, source_target_pairs={{0,4},{4,0},{8,12},{12,8},{16,20},{20,16},{24,28},{28,24},{1,5},{5... | collective-permute-start | bytes 5505032 | tf_op jit(solution)/shard_map/ppermute | solution.py:811
  436.5 43.7 %collective-permute-start.37 = (bf16[4,352,1024]{2,1,0:T(8,128)(2,1)}, bf16[4,352,1024]{2,1,0:T(8,128)(2,1)}, u32[]{:S(2)}, u32[]{:S(2)}) collective-permute-start(bf16[4,352,1024]{2,1,0:T(8,128)(2,1)} %get-tuple-element.157.refs_10_), channel_id=1, source_target_pairs={{0,4},{4,0},{8,12},{12,8},{16,20},{20,16},{24,28},{28,24},{1,5},{5... | collective-permute-start | bytes 8650760 | tf_op jit(solution)/shard_map/ppermute | solution.py:811
  445.6 26.2 %all-to-all-start.2 = ((bf16[4,128,1792]{2,1,0:T(8,128)(2,1)}), bf16[4,128,1792]{2,1,0:T(8,128)(2,1)S(1)}, u32[]{:S(2)}, u32[]{:S(2)}) async-start(bf16[4,128,1792]{2,1,0:T(8,128)(2,1)} %add_convert_fusion.1.refs_7_), calls=%async_computation.2 | async-start | bytes 3670016 | tf_op jit(solution)/shard_map/all_to_all | solution.py:823
  460.3 3.0 collective-permute-start.29
  477.7 30.8 %collective-permute-start.30 = (bf16[512,1024]{1,0:T(8,128)(2,1)}, bf16[512,1024]{1,0:T(8,128)(2,1)}, u32[]{:S(2)}, u32[]{:S(2)}) collective-permute-start(bf16[512,1024]{1,0:T(8,128)(2,1)} %get-tuple-element.185.refs_7_.refs_2_), channel_id=1, source_target_pairs={{8,0},{12,4},{16,8},{20,12},{24,16},{28,20},{9,1},{13,5},{17,9},{2... | collective-permute-start | bytes 3145736 | tf_op jit(solution)/shard_map/ppermute | solution.py:807
  485.1 50.9 %all-to-all-start.3 = ((bf16[4,352,1024]{2,1,0:T(8,128)(2,1)}), bf16[4,352,1024]{2,1,0:T(8,128)(2,1)S(1)}, u32[]{:S(2)}, u32[]{:S(2)}) async-start(bf16[4,352,1024]{2,1,0:T(8,128)(2,1)} %pair_sum.3), calls=%async_computation.3 | async-start | bytes 5767168 | tf_op jit(solution)/shard_map/all_to_all | solution.py:823
  492.1 9.3 %collective-permute-start.31 = (bf16[32,2560]{1,0:T(8,128)(2,1)}, bf16[32,2560]{1,0:T(8,128)(2,1)S(1)}, u32[]{:S(2)}, u32[]{:S(2)}) collective-permute-start(bf16[32,2560]{1,0:T(8,128)(2,1)} %get-tuple-element.189), channel_id=1, source_target_pairs={{0,1},{1,0},{2,3},{3,2},{4,5},{5,4},{6,7},{7,6},{8,9},{9,8},{10,11... | collective-permute-start | bytes 491528 | tf_op jit(solution)/shard_map/ppermute | solution.py:817
  493.6 11.6 %collective-permute-start.32 = (bf16[32,2560]{1,0:T(8,128)(2,1)S(1)}, bf16[32,2560]{1,0:T(8,128)(2,1)S(1)}, u32[]{:S(2)}, u32[]{:S(2)}) collective-permute-start(bf16[32,2560]{1,0:T(8,128)(2,1)S(1)} %copy-done.54), channel_id=1, source_target_pairs={{0,2},{1,3},{2,0},{3,1},{4,6},{5,7},{6,4},{7,5},{8,10},{9,11},{10,... | collective-permute-start | bytes 491528 | tf_op jit(solution)/shard_map/ppermute | solution.py:817
  494.8 13.7 %collective-permute-start.33 = (bf16[32,2560]{1,0:T(8,128)(2,1)S(1)}, bf16[32,2560]{1,0:T(8,128)(2,1)S(1)}, u32[]{:S(2)}, u32[]{:S(2)}) collective-permute-start(bf16[32,2560]{1,0:T(8,128)(2,1)S(1)} %copy-done.53), channel_id=1, source_target_pairs={{0,3},{1,2},{2,1},{3,0},{4,7},{5,6},{6,5},{7,4},{8,11},{9,10},{10,... | collective-permute-start | bytes 491528 | tf_op jit(solution)/shard_map/ppermute | solution.py:817
  514.8 22.8 %collective-permute-start.34 = (bf16[192,1024]{1,0:T(8,128)(2,1)}, bf16[192,1024]{1,0:T(8,128)(2,1)S(1)}, u32[]{:S(2)}, u32[]{:S(2)}) collective-permute-start(bf16[192,1024]{1,0:T(8,128)(2,1)} %get-tuple-element.193), channel_id=1, source_target_pairs={{0,1},{1,0},{2,3},{3,2},{4,5},{5,4},{6,7},{7,6},{8,9},{9,8},{10,11... | collective-permute-start | bytes 1179656 | tf_op jit(solution)/shard_map/ppermute | solution.py:817
  514.8 29.4 %collective-permute-start.35 = (bf16[192,1024]{1,0:T(8,128)(2,1)}, bf16[192,1024]{1,0:T(8,128)(2,1)}, u32[]{:S(2)}, u32[]{:S(2)}) collective-permute-start(bf16[192,1024]{1,0:T(8,128)(2,1)} %get-tuple-element.194), channel_id=1, source_target_pairs={{0,2},{1,3},{2,0},{3,1},{4,6},{5,7},{6,4},{7,5},{8,10},{9,11},{10,... | collective-permute-start | bytes 1179656 | tf_op jit(solution)/shard_map/ppermute | solution.py:817
  517.5 33.7 %collective-permute-start.36 = (bf16[192,1024]{1,0:T(8,128)(2,1)}, bf16[192,1024]{1,0:T(8,128)(2,1)}, u32[]{:S(2)}, u32[]{:S(2)}) collective-permute-start(bf16[192,1024]{1,0:T(8,128)(2,1)} %get-tuple-element.195), channel_id=1, source_target_pairs={{0,3},{1,2},{2,1},{3,0},{4,7},{5,6},{6,5},{7,4},{8,11},{9,10},{10,... | collective-permute-start | bytes 1179656 | tf_op jit(solution)/shard_map/ppermute | solution.py:817
  (49 other events, 326.2 us)

commit v5 on v4

--- a/solution.py
+++ b/solution.py
@@ -81,28 +81,29 @@
     outs, (lse_ref, s_ref, p_ref, v_s) = refs[: len(ks)], refs[len(ks) :]
     z = z_ref[0]
     row = lax.broadcasted_iota(jnp.int32, (TILE, 2 * TILE), 0)
-    for n, k in enumerate(ks):
-        t = z ^ k
-        q2 = split_heads(q_ref[n])
+    for i, (p, n) in enumerate((p, n) for p in range(2) for n in range(len(ks))):
+        pair = slice(p * TILE, (p + 1) * TILE)
+        t = z ^ ks[n]
+        q2 = split_heads(q_ref[n, :, pair])
         lo = lo_ref[n] - t * TILE
         top = jnp.full((8, 2 * TILE), NEG, f32)
         for a in range(TILES_SEEN):
             at = key_block(t + a, z)
-            v_s[a * TILE : (a + 1) * TILE, :] = v_ref[at]
-            s = dot_nt(k_ref[at], q2) + b_ref[0, a].astype(f32)
+            v_s[i, a * TILE : (a + 1) * TILE, :] = v_ref[at, :, pair]
+            s = dot_nt(k_ref[at, :, pair], q2) + b_ref[p, a].astype(f32)
             s = jnp.where(row >= lo - a * TILE, s, NEG)
-            s_ref[a] = s
+            s_ref[i, a] = s
             top = jnp.maximum(top, jnp.max(s.reshape(TILE // 8, 8, 2 * TILE), axis=0))
         top = jnp.max(top, axis=0, keepdims=True)
         total = jnp.zeros((8, 2 * TILE), f32)
         for a in range(TILES_SEEN):
-            p = jnp.exp(s_ref[a] - top)
-            total = total + jnp.sum(p.reshape(TILE // 8, 8, 2 * TILE), axis=0)
-            p_ref[a * TILE : (a + 1) * TILE, :] = p.astype(bf16)
+            e = jnp.exp(s_ref[i, a] - top)
+            total = total + jnp.sum(e.reshape(TILE // 8, 8, 2 * TILE), axis=0)
+            p_ref[i, a * TILE : (a + 1) * TILE, :] = e.astype(bf16)
         total = jnp.sum(total, axis=0, keepdims=True)
-        ct = dot(v_s[...].T, p_ref[...]) / total
-        outs[n][...] = merge_heads(ct).astype(bf16)
-        lse_ref[0, n] = top + jnp.log(total)
+        ct = dot(v_s[i].T, p_ref[i]) / total
+        outs[n][:, pair] = merge_heads(ct).astype(bf16)
+        lse_ref[p, n] = top + jnp.log(total)
 
 
 def attend_back_kernel(pieces, z_ref, lo_ref, lse_a, lse_b, q_ref, k_ref, v_ref, b_ref, *refs):
@@ -180,29 +181,29 @@
 def attend(ks, z, lo, q, k, v, bias, others=()):
     count, _, width = q.shape
     blocks, pairs = k.shape[0], width // TILE
-    part = lambda n: pl.BlockSpec((n, TILE, TILE), lambda g: (0, 0, g))
+    part = lambda n: pl.BlockSpec((n, TILE, 2 * TILE), lambda g: (0, 0, g))
     return pl.pallas_call(
         behind(functools.partial(attend_kernel, ks), 6, others),
-        grid=(pairs,),
+        grid=(pairs // 2,),
         in_specs=[
             SMEM,
             pl.BlockSpec((count, 1, 2 * TILE), lambda g: (0, 0, 0)),
             part(count), part(blocks), part(blocks),
-            pl.BlockSpec((1, TILES_SEEN, TILE, 2 * TILE), lambda g: (g, 0, 0, 0)),
+            pl.BlockSpec((2, TILES_SEEN, TILE, 2 * TILE), lambda g: (g, 0, 0, 0)),
         ] + anywhere(others),
-        out_specs=[pl.BlockSpec((TILE, TILE), lambda g: (0, g))] * count
-        + [pl.BlockSpec((1, count, 1, 2 * TILE), lambda g: (g, 0, 0, 0))],
+        out_specs=[pl.BlockSpec((TILE, 2 * TILE), lambda g: (0, g))] * count
+        + [pl.BlockSpec((2, count, 1, 2 * TILE), lambda g: (g, 0, 0, 0))],
         out_shape=[jax.ShapeDtypeStruct((TILE, width), bf16)] * count
         + [
             jax.ShapeDtypeStruct((pairs, count, 1, 2 * TILE), f32),
         ],
         scratch_shapes=[
-            pltpu.VMEM((TILES_SEEN, TILE, 2 * TILE), f32),
-            pltpu.VMEM((TILES_SEEN * TILE, 2 * TILE), bf16),
-            pltpu.VMEM((TILES_SEEN * TILE, TILE), bf16),
+            pltpu.VMEM((2 * count, TILES_SEEN, TILE, 2 * TILE), f32),
+            pltpu.VMEM((2 * count, TILES_SEEN * TILE, 2 * TILE), bf16),
+            pltpu.VMEM((2 * count, TILES_SEEN * TILE, TILE), bf16),
         ],
         compiler_params=pltpu.CompilerParams(vmem_limit_bytes=VMEM),
-        cost_estimate=cost(7.4 * count),
+        cost_estimate=cost(6 * count),
         name="attend",
     )(z, lo, q, k, v, bias, *others)
 
@@ -531,18 +532,25 @@
     return jnp.concatenate([ref[z ^ k] for k in range(ref.shape[0])], axis=0)
 
 
-def call(kernel, ins, outs, us, name, others=(), scratch=()):
+def call(kernel, ins, outs, us, name, others=(), scratch=(), passed=()):
     specs = [SMEM if a.ndim == 1 else pl.BlockSpec(memory_space=pltpu.VMEM) for a in ins]
-    return pl.pallas_call(
-        behind(kernel, len(ins), others),
-        in_specs=specs + anywhere(others),
-        out_specs=[pl.BlockSpec(memory_space=pltpu.VMEM)] * len(outs),
-        out_shape=[jax.ShapeDtypeStruct(shape, dtype) for shape, dtype in outs],
+    first, last = len(ins), len(ins) + len(passed) + len(others)
+
+    def body(*refs):
+        kernel(*refs[:first], *refs[last : last + len(outs)], *refs[last + len(outs) + len(passed) :])
+
+    return pl.pallas_call(
+        body,
+        in_specs=specs + anywhere(passed) + anywhere(others),
+        out_specs=[pl.BlockSpec(memory_space=pltpu.VMEM)] * len(outs) + anywhere(passed),
+        out_shape=[jax.ShapeDtypeStruct(shape, dtype) for shape, dtype in outs]
+        + [jax.ShapeDtypeStruct(array.shape, array.dtype) for array in passed],
+        input_output_aliases={first + i: len(outs) + i for i in range(len(passed))},
         scratch_shapes=list(scratch),
         compiler_params=pltpu.CompilerParams(vmem_limit_bytes=VMEM),
         cost_estimate=cost(us),
         name=name,
-    )(*ins, *others)
+    )(*ins, *passed, *others)
 
 
 def pair_kernel(mine_ref, other_ref, out_ref):
@@ -976,7 +984,8 @@
     first_pair = add_pair(mine, other)
     first_parts = over_chips(first_pair)
     acc = input_grads(0, *grads, *weights, others=[other])[0]
-    *grads, more = back(1, [acc, first_pair, both])
+    down_pair = pair_sum(down_mine, down_other)
+    *grads, more = back(1, [acc, first_pair, both, down_pair])
     diagonals = jnp.concatenate([diagonal, more])
     places = np.arange((TILES_SEEN) * 2 * TILE).reshape(TILES_SEEN, 2 * TILE)
     block, lane = places // (2 * TILE), places % (2 * TILE)
@@ -999,14 +1008,14 @@
     pair = add_pair(mine, other)
     last = over_chips(pair)
     part_two, part_one, own_sum = input_grads(1, *grads, *weights, acc, [pair])
-    leave, swapped, *first = call(
+    leave, swapped, *first, down_pair = call(
         leave_kernel, [side_ref, z, part_two, core_swap(part_one), first_parts],
         [((block_len, width), bf16)] * 2 + [((share, first_parts.shape[-1]), bf16)] * seqs, 5, "leaving_rows", [last],
-        [pltpu.VMEM((exp_count, share, first_parts.shape[-1]), bf16)],
+        [pltpu.VMEM((exp_count, share, first_parts.shape[-1]), bf16)], [down_pair],
     )
     first = [z_swap(piece, k) for k, piece in enumerate(first)]
     came = shift(leave, -2)
-    down = over_chips(pair_sum(down_mine, down_other, [leave]))
+    down = over_chips(down_pair)
     mixed = call(
         mix_kernel, [z, targets_t, hidden] + given, [((seqs, piece_len, width), bf16)], 8, "mixed_rows", [leave]
     )[0]

time: 566 us -> 563 us (level)
    all_to_all x4, waiting for transfers between devices: 38 us -> 32.4 us  [over_chips(): lax.all_to_all(pair, 'ctx', split_axis=0, concat_axis=0, tiled=True, axis...]
    unnamed x113 -> x115, local copies, waits for them, and re-layouts: 13.1 us -> 12.8 us
  transfers between devices with their start and end apart: 42 -> 42, of which waited for: 21 -> 22; matrix products, arithmetic and copies ran while one was open for 8% -> 7% of each run, Pallas kernels for 49% -> 48%
where the time goes in v5:
time: 563 us; the launch traced here: 556 us
  Pallas kernels  325 us (58%)
  waiting for transfers between devices  95.7 us (17%)
  starting transfers between devices  72.9 us (13%)
  local copies, waits for them, and re-layouts  31 us (6%)
  other arithmetic  19 us (3%)
  matrix products  11.7 us (2%)
    pallas_call x4, Pallas kernels, expert(): pl.pallas_call(functools.partial(expert_kernel, experts, count, len(held)...  88.3 us
    ppermute x27, waiting for transfers between devices, z_swap(): lax.ppermute(x, 'exp', [(i, i ^ k) for i in range(lax.axis_size('exp'))])  45.1 us
    pallas_call x2, Pallas kernels, attend_back(): pl.pallas_call(behind(functools.partial(attend_back_kernel, pieces), 8 +...  42.2 us
    pallas_call x8, Pallas kernels, call(): pl.pallas_call(body, in_specs=specs + anywhere(passed) + anywhere(others)...  40.8 us
    ppermute x27, starting transfers between devices, z_swap(): lax.ppermute(x, 'exp', [(i, i ^ k) for i in range(lax.axis_size('exp'))])  36.9 us
    all_to_all x4, waiting for transfers between devices, over_chips(): lax.all_to_all(pair, 'ctx', split_axis=0, concat_axis=0, tiled=True, axis...  32.4 us
    pallas_call x2, Pallas kernels, attend(): pl.pallas_call(behind(functools.partial(attend_kernel, ks), 6, others), g...  27.7 us
    pallas_call x1, Pallas kernels, gate_up_grads(): pl.pallas_call(behind(gate_up_kernel, 5, others), grid=(hidden // wide,),...  22.9 us
  transfers between devices with their start and end apart: 42, of which 22 were waited for; matrix products, arithmetic and copies ran while one was open for 7% of the time, Pallas kernels for 48%

profile of v5, /device:TPU:10, one launch (start us, length us, event | category | flops | bytes accessed | tf_op | source)
XLA Modules:
  0.0 556.4 jit_solution(5581468323689355139)
XLA Ops:
  16.4 6.8 %collective-permute-done.3.refs_4_ = bf16[128,1024]{1,0:T(8,128)(2,1)S(1)} collective-permute-done((bf16[128,1024]{1,0:T(8,128)(2,1)S(1)}, bf16[128,1024]{1,0:T(8,128)(2,1)S(1)}, u32[]{:S(2)}, u32[]{:S(2)}) %collective-permute-start.3) | collective-permute-done | bytes 262176 | tf_op jit(solution)/shard_map/ppermute | solution.py:825
  28.3 3.4 collective-permute-start.6
  38.8 3.7 cot_rows.1
  46.0 6.5 %bias_tiles.1.refs_5_.refs_7_ = bf16[8,9,128,256]{3,2,1,0:T(8,128)(2,1)} custom-call(f32[8,2,1280]{2,1,0:T(2,128)} %reshape.303.refs_0_, bf16[320,1024]{1,0:T(8,128)(2,1)} %get-tuple-element.110.refs_1_), custom_call_target="tpu_custom_call" | custom-call | flops 6899999744 | tf_op jit(solution)/shard_map/bias_tiles/pallas_call | solution.py:166
  53.5 6.2 %norm_window.1.refs_0_ = bf16[12,128,1024]{2,1,0:T(8,128)(2,1)} custom-call(bf16[4,128,1024]{2,1,0:T(8,128)(2,1)} %get-tuple-element.268.two_ref, bf16[4,128,1024]{2,1,0:T(8,128)(2,1)} %copy-done.29, bf16[4,128,1024]{2,1,0:T(8,128)(2,1)} %get-tuple-element.266.own_ref.refs_1_, f32[1,1024]{1,0:T(1,128)} %bitcast.107), custom_call_target="tpu_custom_call" | custom-call | flops 5750000128 | tf_op jit(solution)/shard_map/norm_window/pallas_call | solution.py:482
  64.3 4.8 convolution_convert_fusion.1
  69.1 4.8 convolution_convert_fusion
  74.4 13.9 %attend.2 = (bf16[128,1024]{1,0:T(8,128)(2,1)}, bf16[128,1024]{1,0:T(8,128)(2,1)}, f32[8,2,1,256]{3,2,1,0:T(1,128)}) custom-call(s32[1]{0:T(128)} %bitcast.refs_0_.z_ref.refs_1_, s32[2,1,256]{2,1,0:T(1,128)} %bitcast.113, bf16[2,128,1024]{2,1,0:T(8,128)(2,1)} %bitcast.91, bf16[12,128,1024]{2,1,0:T(8,128)(2,1)} %bitcast.116, ...), custom_call_target="tpu_custom_call" | custom-call | flops 13799999488 | tf_op jit(solution)/shard_map/attend/pallas_call | solution.py:185
  91.2 13.8 %attend.3 = (bf16[128,1024]{1,0:T(8,128)(2,1)}, bf16[128,1024]{1,0:T(8,128)(2,1)}, f32[8,2,1,256]{3,2,1,0:T(1,128)}) custom-call(s32[1]{0:T(128)} %bitcast.refs_0_.z_ref.refs_1_, s32[2,1,256]{2,1,0:T(1,128)} %bitcast.114, bf16[2,128,1024]{2,1,0:T(8,128)(2,1)} %bitcast.90, bf16[12,128,1024]{2,1,0:T(8,128)(2,1)} %bitcast.117, ...), custom_call_target="tpu_custom_call" | custom-call | flops 13799999488 | tf_op jit(solution)/shard_map/attend/pallas_call | solution.py:185
  106.5 9.1 %turn_rows.1.refs_11_.refs_1_ = bf16[4,2,128,1536]{3,2,1,0:T(8,128)(2,1)} custom-call(bf16[12,128,1024]{2,1,0:T(8,128)(2,1)} %norm_window.1.refs_0_, bf16[128,1024]{1,0:T(8,128)(2,1)} %get-tuple-element.112.refs_1_.refs_5_.refs_8_), custom_call_target="tpu_custom_call" | custom-call | flops 9200000000 | tf_op jit(solution)/shard_map/turn_rows/pallas_call | solution.py:501
  115.6 7.1 %collective-permute-done.9.refs_6_ = bf16[128,1024]{1,0:T(8,128)(2,1)S(1)} collective-permute-done((bf16[128,1024]{1,0:T(8,128)(2,1)}, bf16[128,1024]{1,0:T(8,128)(2,1)S(1)}, u32[]{:S(2)}, u32[]{:S(2)}) %collective-permute-start.9) | collective-permute-done | bytes 262176 | tf_op jit(solution)/shard_map/ppermute | solution.py:825
  125.0 5.6 %hidden_rows.1 = (f32[512,1024]{1,0:T(8,128)}, bf16[512,1024]{1,0:T(8,128)(2,1)}, bf16[320,1024]{1,0:T(8,128)(2,1)}, bf16[320,1024]{1,0:T(8,128)(2,1)}) custom-call(s32[1]{0:T(128)} %bitcast.refs_0_.z_ref.refs_1_, s32[2,512]{1,0:T(2,128)} %copy-done.17, bf16[4,128,1024]{2,1,0:T(8,128)(2,1)} %refs_2_.7, bf16[1024,1024]{1,0:T(8,128)(2,1)} %refs_4_.11, ...), custom_call_target="tpu_custom_call" | custom-call | flops 10350000128 | tf_op jit(solution)/shard_map/hidden_rows/pallas_call | solution.py:542
  131.4 22.0 %expert.4 = (bf16[320,1024]{1,0:T(8,128)(2,1)}, bf16[1280,1024]{1,0:T(8,128)(2,1)}, bf16[1280,2816]{1,0:T(8,128)(2,1)}, bf16[1280,2816]{1,0:T(8,128)(2,1)}, bf16...) custom-call(s32[1]{0:T(128)} %bitcast.refs_0_.z_ref.refs_1_, ...), custom_call_target="tpu_custom_call" | custom-call | flops 26449999872 | tf_op jit(solution)/shard_map/expert/pallas_call | solution.py:332
  160.5 22.1 %expert.5 = (bf16[320,1024]{1,0:T(8,128)(2,1)}, bf16[1280,1024]{1,0:T(8,128)(2,1)}, bf16[1280,2816]{1,0:T(8,128)(2,1)}, bf16[1280,2816]{1,0:T(8,128)(2,1)}, bf16...) custom-call(s32[1]{0:T(128)} %bitcast.refs_0_.z_ref.refs_1_, ...), custom_call_target="tpu_custom_call", output_to_operand_aliasing={{1}: (7, {}), {2}: (8, {}), {3}: (9, {}), {4}: (10, {}), {5... | custom-call | flops 26449999872 | tf_op jit(solution)/shard_map/expert/pallas_call | solution.py:332
  188.7 22.0 %expert.6 = (bf16[320,1024]{1,0:T(8,128)(2,1)}, bf16[1280,1024]{1,0:T(8,128)(2,1)}, bf16[1280,2816]{1,0:T(8,128)(2,1)}, bf16[1280,2816]{1,0:T(8,128)(2,1)}, bf16...) custom-call(s32[1]{0:T(128)} %bitcast.refs_0_.z_ref.refs_1_, ...), custom_call_target="tpu_custom_call", output_to_operand_aliasing={{1}: (7, {}), {2}: (8, {}), {3}: (9, {}), {4}: (10, {}), {5... | custom-call | flops 26449999872 | tf_op jit(solution)/shard_map/expert/pallas_call | solution.py:332
  211.6 22.2 %expert.7 = (bf16[320,1024]{1,0:T(8,128)(2,1)}, bf16[1280,1024]{1,0:T(8,128)(2,1)}, bf16[1280,2816]{1,0:T(8,128)(2,1)}, bf16[1280,2816]{1,0:T(8,128)(2,1)}, bf16...) custom-call(s32[1]{0:T(128)} %bitcast.refs_0_.z_ref.refs_1_, ...), custom_call_target="tpu_custom_call", output_to_operand_aliasing={{1}: (7, {}), {2}: (8, {}), {3}: (9, {}), {4}: (10, {}), {5... | custom-call | flops 26449999872 | tf_op jit(solution)/shard_map/expert/pallas_call | solution.py:332
  234.6 3.4 collective-permute-start.21
  238.8 14.4 %expert_out.1 = (bf16[320,1024]{1,0:T(8,128)(2,1)}, bf16[320,1024]{1,0:T(8,128)(2,1)}, bf16[320,1024]{1,0:T(8,128)(2,1)}, bf16[320,1024]{1,0:T(8,128)(2,1)}) custom-call(bf16[1280,2816]{1,0:T(8,128)(2,1)} %get-tuple-element.146.refs_0_.refs_1_, bf16[1,2816,1024]{2,1,0:T(8,128)(2,1)} %refs_1_.1, f32[1280,128]{1,0:T(8,128)} %get-tuple-element.147.refs_2_, ...), custom_call_target="tpu_custom_call" | custom-call | flops 16099999744 | tf_op jit(solution)/shard_map/expert_out/pallas_call | solution.py:450
  253.2 12.6 %down_grads.1 = (bf16[4,352,1024]{2,1,0:T(8,128)(2,1)}, bf16[4,352,1024]{2,1,0:T(8,128)(2,1)}) custom-call(s32[1]{0:T(128)} %bitcast.36.refs_0_, bf16[1280,2816]{1,0:T(8,128)(2,1)} %get-tuple-element.146.refs_0_.refs_1_, bf16[1280,1024]{1,0:T(8,128)(2,1)} %get-tuple-element.157.refs_2_, bf16[320,1024]{1,0:T(8,128)(2,1)} %get-tuple-element.149.refs_3_), custom_call_target="tpu_custom_call" | custom-call | flops 16099999744 | tf_op jit(solution)/shard_map/down_grads/pallas_call | solution.py:411
  267.6 8.8 %middle_rows.1 = (f32[512,1024]{1,0:T(8,128)}, bf16[512,1024]{1,0:T(8,128)(2,1)}, f32[1,1024]{1,0:T(1,128)}, bf16[128,1024]{1,0:T(8,128)(2,1)}, bf16[128,1024]{1...) custom-call(s32[1]{0:T(128)} %bitcast.refs_0_.z_ref.refs_1_, s32[512,2]{1,0:T(8,128)} %bitcast.94, ...), custom_call_target="tpu_custom_call" | custom-call | flops 10350000128 | tf_op jit(solution)/shard_map/middle_rows/pallas_call | solution.py:542
  276.4 22.9 %gate_up_grads.1 = (bf16[4,2,128,2816]{3,2,1,0:T(8,128)(2,1)}, bf16[4,2,128,2816]{3,2,1,0:T(8,128)(2,1)}, f32[1024,128]{1,0:T(8,128)}) custom-call(s32[1]{0:T(128)} %bitcast.36.refs_0_, bf16[1280,1024]{1,0:T(8,128)(2,1)} %get-tuple-element.163.refs_1_, bf16[1280,2816]{1,0:T(8,128)(2,1)} %get-tuple-element.164.refs_2_, ...), custom_call_target="tpu_custom_call" | custom-call | flops 27599998976 | tf_op jit(solution)/shard_map/gate_up_grads/pallas_call | solution.py:379
  303.7 9.4 %collective-permute-done.26.refs_1_ = bf16[4,2,128,2816]{3,2,1,0:T(8,128)(2,1)S(1)} collective-permute-done((bf16[4,2,128,2816]{3,2,1,0:T(8,128)(2,1)}, bf16[4,2,128,2816]{3,2,1,0:T(8,128)(2,1)S(1)}, u32[]{:S(2)}, u32[]{:S(2)}) %collective-permute-start.26) | collective-permute-done | bytes 5767200 | tf_op jit(solution)/shard_map/ppermute | solution.py:819
  315.5 7.4 %pair_sum.2.refs_16_ = bf16[4,2,128,2816]{3,2,1,0:T(8,128)(2,1)} custom-call(bf16[4,2,128,2816]{3,2,1,0:T(8,128)(2,1)} %get-tuple-element.167.refs_0_, bf16[4,2,128,2816]{3,2,1,0:T(8,128)(2,1)} %copy-done.27), custom_call_target="tpu_custom_call" | custom-call | flops 6899999744 | tf_op jit(solution)/shard_map/pair_sum/pallas_call | solution.py:562
  322.9 5.3 all-to-all-start
  331.3 21.0 %attend_back.2 = (bf16[4,128,512]{2,1,0:T(8,128)(2,1)}, bf16[12,128,512]{2,1,0:T(8,128)(2,1)}, bf16[12,128,512]{2,1,0:T(8,128)(2,1)}, f32[4,2,9,256]{3,2,1,0:T(8,128)}) custom-call(s32[1]{0:T(128)} %bitcast.refs_0_.z_ref.refs_1_, s32[4,1,256]{2,1,0:T(1,128)} %bitcast.111, f32[8,2,1,256]{3,2,1,0:T(1,128)} %get-tuple-element.153.refs_2_, ...), custom_call_target="tpu_custom_call" | custom-call | flops 24149999616 | tf_op jit(solution)/shard_map/attend_back/pallas_call | solution.py:218
  352.3 6.6 %collective-permute-done.19.refs_10_.refs_5_ = bf16[320,1024]{1,0:T(8,128)(2,1)S(1)} collective-permute-done((bf16[320,1024]{1,0:T(8,128)(2,1)S(1)}, bf16[320,1024]{1,0:T(8,128)(2,1)S(1)}, u32[]{:S(2)}, u32[]{:S(2)}) %collective-permute-start.19) | collective-permute-done | bytes 655392 | tf_op jit(solution)/shard_map/ppermute | solution.py:825
  359.7 12.6 %projection_grads.2 = (bf16[4,128,2560]{2,1,0:T(8,128)(2,1)}, bf16[4,128,2560]{2,1,0:T(8,128)(2,1)}) custom-call(s32[1]{0:T(128)} %bitcast.36.refs_0_, bf16[4,2,128,1536]{3,2,1,0:T(8,128)(2,1)} %turn_rows.1.refs_11_.refs_1_, bf16[512,512]{1,0:T(8,128)(2,1)} %bitcast.129, bf16[1536,512]{1,0:T(8,128)(2,1)} %bitcast.126, bf16[1536,512]{1,0:T(8,128)(2,1)} %bitcast.127, ...), custom_call_target="tpu_custom_call" | custom-call | flops 15294999552 | tf_op jit(solution)/shard_map/projection_grads/pallas_call | solution.py:791
  373.6 4.9 pair_sum.3.refs_19_.refs_5_
  378.5 9.1 %input_grads.2.refs_16_.refs_6_ = f32[1536,1024]{1,0:T(8,128)} custom-call(bf16[4,128,512]{2,1,0:T(8,128)(2,1)} %get-tuple-element.169.refs_0_, bf16[12,128,512]{2,1,0:T(8,128)(2,1)} %get-tuple-element.170.refs_1_, bf16[12,128,512]{2,1,0:T(8,128)(2,1)} %get-tuple-element.171.refs_2_, bf16[1024,1024]{1,0:T(8,128)(2,1)} %refs_3_.15, ...), custom_call_target="tpu_custom_call" | custom-call | flops 8049999872 | tf_op jit(solution)/shard_map/input_grads/pallas_call | solution.py:663
  389.7 3.9 all-to-all-done.refs_18_
  393.6 4.6 all-to-all-start.1
  398.3 21.3 %attend_back.3 = (bf16[4,128,512]{2,1,0:T(8,128)(2,1)}, bf16[12,128,512]{2,1,0:T(8,128)(2,1)}, bf16[12,128,512]{2,1,0:T(8,128)(2,1)}, f32[4,2,9,256]{3,2,1,0:T(8,128)}) custom-call(s32[1]{0:T(128)} %bitcast.refs_0_.z_ref.refs_1_, s32[4,1,256]{2,1,0:T(1,128)} %bitcast.112, f32[8,2,1,256]{3,2,1,0:T(1,128)} %get-tuple-element.153.refs_2_, ...), custom_call_target="tpu_custom_call" | custom-call | flops 24149999616 | tf_op jit(solution)/shard_map/attend_back/pallas_call | solution.py:218
  422.9 5.4 all-to-all-done.1.refs_6_.refs_4_
  429.7 9.4 %projection_grads.3 = (bf16[4,128,1792]{2,1,0:T(8,128)(2,1)}, bf16[4,128,1792]{2,1,0:T(8,128)(2,1)}) custom-call(s32[1]{0:T(128)} %bitcast.36.refs_0_, bf16[4,2,128,1536]{3,2,1,0:T(8,128)(2,1)} %turn_rows.1.refs_11_.refs_1_, bf16[512,512]{1,0:T(8,128)(2,1)} %bitcast.128, bf16[1536,512]{1,0:T(8,128)(2,1)} %bitcast.124, bf16[1536,512]{1,0:T(8,128)(2,1)} %bitcast.125, ...), custom_call_target="tpu_custom_call" | custom-call | flops 11845000192 | tf_op jit(solution)/shard_map/projection_grads/pallas_call | solution.py:791
  439.1 4.0 collective-permute-done.29
  446.3 4.1 all-to-all-start.2
  450.4 10.5 %input_grads.3 = (bf16[512,1024]{1,0:T(8,128)(2,1)}, bf16[512,1024]{1,0:T(8,128)(2,1)}, f32[512,1024]{1,0:T(8,128)}) custom-call(bf16[4,128,512]{2,1,0:T(8,128)(2,1)} %get-tuple-element.176.refs_0_, bf16[12,128,512]{2,1,0:T(8,128)(2,1)} %get-tuple-element.177.refs_1_, bf16[12,128,512]{2,1,0:T(8,128)(2,1)} %get-tuple-element.178.refs_2_, ...), custom_call_target="tpu_custom_call" | custom-call | flops 8049999872 | tf_op jit(solution)/shard_map/input_grads/pallas_call | solution.py:663
  463.8 8.7 %all-to-all-done.2.refs_6_ = bf16[4,128,1792]{2,1,0:T(8,128)(2,1)S(1)} async-done(((bf16[4,128,1792]{2,1,0:T(8,128)(2,1)}), bf16[4,128,1792]{2,1,0:T(8,128)(2,1)S(1)}, u32[]{:S(2)}, u32[]{:S(2)}) %all-to-all-start.2) | async-done | bytes 1835040 | tf_op jit(solution)/shard_map/all_to_all | solution.py:831
  473.7 4.6 leaving_rows.1
  482.4 5.3 all-to-all-start.3
  492.7 5.8 %mixed_rows.1.refs_7_ = bf16[4,128,1024]{2,1,0:T(8,128)(2,1)} custom-call(s32[1]{0:T(128)} %bitcast.refs_0_.z_ref.refs_1_, s32[512,2]{1,0:T(8,128)} %bitcast.95, f32[512,1024]{1,0:T(8,128)} %get-tuple-element.117.refs_2_, bf16[320,1024]{1,0:T(8,128)(2,1)} %get-tuple-element.149.refs_3_, bf16[320,1024]{1,0:T(8,128)(2,1)} %copy-done.30, ...), custom_call_target="tpu_custom_call" | custom-call | flops 9200000000 | tf_op jit(solution)/shard_map/mixed_rows/pallas_call | solution.py:542
  498.5 4.4 collective-permute-done.33.refs_9_.refs_12_
  507.6 5.7 %tail_rows.1 = (bf16[192,1024]{1,0:T(8,128)(2,1)}, bf16[192,1024]{1,0:T(8,128)(2,1)}, bf16[192,1024]{1,0:T(8,128)(2,1)}, bf16[192,1024]{1,0:T(8,128)(2,1)}) custom-call(s32[1]{0:T(128)} %bitcast.refs_0_.z_ref.refs_1_, bf16[4,128,1024]{2,1,0:T(8,128)(2,1)} %get-tuple-element.266.own_ref.refs_1_, f32[512,1024]{1,0:T(8,128)} %get-tuple-element.189.refs_2_, ...), custom_call_target="tpu_custom_call" | custom-call | flops 9200000000 | tf_op jit(solution)/shard_map/tail_rows/pallas_call | solution.py:542
  516.8 5.4 convert_reduce_fusion
  522.2 14.4 %all-to-all-done.3 = bf16[4,352,1024]{2,1,0:T(8,128)(2,1)S(1)} async-done(((bf16[4,352,1024]{2,1,0:T(8,128)(2,1)}), bf16[4,352,1024]{2,1,0:T(8,128)(2,1)S(1)}, u32[]{:S(2)}, u32[]{:S(2)}) %all-to-all-start.3) | async-done | bytes 2883616 | tf_op jit(solution)/shard_map/all_to_all | solution.py:831
  538.3 4.4 collective-permute-done.36.refs_8_
  542.7 5.7 %collective-permute-done.37.refs_9_ = bf16[192,1024]{1,0:T(8,128)(2,1)} collective-permute-done((bf16[192,1024]{1,0:T(8,128)(2,1)}, bf16[192,1024]{1,0:T(8,128)(2,1)}, u32[]{:S(2)}, u32[]{:S(2)}) %collective-permute-start.37) | collective-permute-done | bytes 393248 | tf_op jit(solution)/shard_map/ppermute | solution.py:825
  548.4 3.7 end_rows.1
  (241 shorter events, 111.4 us)
Async XLA Ops:
  0.7 31.0 %copy-start.21 = (bf16[1024]{0:T(1024)(128)(2,1)S(1)}, bf16[1024]{0:T(1024)(128)(2,1)}, u32[]{:S(2)}) copy-start(bf16[1024]{0:T(1024)(128)(2,1)} %param.23) | copy-start | bytes 6148
  0.7 32.3 %copy-start.22 = (bf16[1024]{0:T(1024)(128)(2,1)S(1)}, bf16[1024]{0:T(1024)(128)(2,1)}, u32[]{:S(2)}) copy-start(bf16[1024]{0:T(1024)(128)(2,1)} %param.29) | copy-start | bytes 6148
  0.7 32.9 %copy-start.18 = (bf16[1024,4]{0,1:T(4,128)(2,1)S(1)}, bf16[1024,4]{0,1:T(4,128)(2,1)}, u32[]{:S(2)}) copy-start(bf16[1024,4]{0,1:T(4,128)(2,1)} %param.30) | copy-start | bytes 24580
  2.1 10.9 %collective-permute-start.1 = (bf16[128,1024]{1,0:T(8,128)(2,1)S(1)}, bf16[128,1024]{1,0:T(8,128)(2,1)S(1)}, u32[]{:S(2)}, u32[]{:S(2)}) collective-permute-start(bf16[128,1024]{1,0:T(8,128)(2,1)S(1)} %get-tuple-element.271), channel_id=1, source_target_pairs={{0,1},{1,0},{2,3},{3,2},{4,5},{5,4},{6,7},{7,6},{8,9},{9,8},{10,11... | collective-permute-start | bytes 786440 | tf_op jit(solution)/shard_map/ppermute | solution.py:825
  2.6 20.6 %collective-permute-start.3 = (bf16[128,1024]{1,0:T(8,128)(2,1)S(1)}, bf16[128,1024]{1,0:T(8,128)(2,1)S(1)}, u32[]{:S(2)}, u32[]{:S(2)}) collective-permute-start(bf16[128,1024]{1,0:T(8,128)(2,1)S(1)} %get-tuple-element.270), channel_id=1, source_target_pairs={{0,2},{1,3},{2,0},{3,1},{4,6},{5,7},{6,4},{7,5},{8,10},{9,11},{10,... | collective-permute-start | bytes 786440 | tf_op jit(solution)/shard_map/ppermute | solution.py:825
  5.2 23.1 %collective-permute-start.5 = (bf16[128,1024]{1,0:T(8,128)(2,1)S(1)}, bf16[128,1024]{1,0:T(8,128)(2,1)S(1)}, u32[]{:S(2)}, u32[]{:S(2)}) collective-permute-start(bf16[128,1024]{1,0:T(8,128)(2,1)S(1)} %get-tuple-element.272), channel_id=1, source_target_pairs={{0,3},{1,2},{2,1},{3,0},{4,7},{5,6},{6,5},{7,4},{8,11},{9,10},{10,... | collective-permute-start | bytes 786440 | tf_op jit(solution)/shard_map/ppermute | solution.py:825
  5.7 29.8 %collective-permute-start = (bf16[128,1024]{1,0:T(8,128)(2,1)S(1)}, bf16[128,1024]{1,0:T(8,128)(2,1)S(1)}, u32[]{:S(2)}, u32[]{:S(2)}) collective-permute-start(bf16[128,1024]{1,0:T(8,128)(2,1)S(1)} %bitcast.87), channel_id=1, source_target_pairs={{0,8},{4,12},{8,16},{12,20},{16,24},{20,28},{1,9},{5,13},{9,17},{1... | collective-permute-start | bytes 786440 | tf_op jit(solution)/shard_map/ppermute | solution.py:815
  12.3 26.4 %copy-start.15 = (s32[4,128]{1,0:T(4,128)}, s32[4,128]{1,0:T(4,128)S(1)}, u32[]{:S(2)}) copy-start(s32[4,128]{1,0:T(4,128)S(1)} %broadcast_subtract_fusion) | copy-start | bytes 6148
  13.0 25.7 %copy-start.8 = (bf16[128,1024]{1,0:T(8,128)(2,1)}, bf16[128,1024]{1,0:T(8,128)(2,1)S(1)}, u32[]{:S(2)}) copy-start(bf16[128,1024]{1,0:T(8,128)(2,1)S(1)} %collective-permute-done.1.refs_3_) | copy-start | bytes 786436
  13.0 22.4 %collective-permute-start.2 = (bf16[128,1024]{1,0:T(8,128)(2,1)S(1)}, bf16[128,1024]{1,0:T(8,128)(2,1)S(1)}, u32[]{:S(2)}, u32[]{:S(2)}) collective-permute-start(bf16[128,1024]{1,0:T(8,128)(2,1)S(1)} %collective-permute-done.1.refs_3_), channel_id=1, source_target_pairs={{0,8},{4,12},{8,16},{12,20},{16,24},{20,28},{1,9},{5,13},{9,17},{1... | collective-permute-start | bytes 786440 | tf_op jit(solution)/shard_map/ppermute | solution.py:815
  23.2 12.3 %collective-permute-start.4 = (bf16[128,1024]{1,0:T(8,128)(2,1)S(1)}, bf16[128,1024]{1,0:T(8,128)(2,1)S(1)}, u32[]{:S(2)}, u32[]{:S(2)}) collective-permute-start(bf16[128,1024]{1,0:T(8,128)(2,1)S(1)} %collective-permute-done.3.refs_4_), channel_id=1, source_target_pairs={{0,8},{4,12},{8,16},{12,20},{16,24},{20,28},{1,9},{5,13},{9,17},{1... | collective-permute-start | bytes 786440 | tf_op jit(solution)/shard_map/ppermute | solution.py:815
  28.3 8.8 %collective-permute-start.6 = (bf16[128,1024]{1,0:T(8,128)(2,1)S(1)}, bf16[128,1024]{1,0:T(8,128)(2,1)S(1)}, u32[]{:S(2)}, u32[]{:S(2)}) collective-permute-start(bf16[128,1024]{1,0:T(8,128)(2,1)S(1)} %collective-permute-done.5.refs_5_), channel_id=1, source_target_pairs={{0,8},{4,12},{8,16},{12,20},{16,24},{20,28},{1,9},{5,13},{9,17},{1... | collective-permute-start | bytes 786440 | tf_op jit(solution)/shard_map/ppermute | solution.py:815
  38.7 13.8 %collective-permute-start.7 = (bf16[4,128,1024]{2,1,0:T(8,128)(2,1)S(1)}, bf16[4,128,1024]{2,1,0:T(8,128)(2,1)S(1)}, u32[]{:S(2)}, u32[]{:S(2)}) collective-permute-start(bf16[4,128,1024]{2,1,0:T(8,128)(2,1)S(1)} %get-tuple-element.267), channel_id=1, source_target_pairs={{0,4},{4,0},{8,12},{12,8},{16,20},{20,16},{24,28},{28,24},{1,5},{5... | collective-permute-start | bytes 3145736 | tf_op jit(solution)/shard_map/ppermute | solution.py:819
  42.5 47.9 %collective-permute-start.8 = (bf16[320,1024]{1,0:T(8,128)(2,1)}, bf16[320,1024]{1,0:T(8,128)(2,1)S(1)}, u32[]{:S(2)}, u32[]{:S(2)}) collective-permute-start(bf16[320,1024]{1,0:T(8,128)(2,1)} %get-tuple-element.110.refs_1_), channel_id=1, source_target_pairs={{0,2},{1,3},{2,0},{3,1},{4,6},{5,7},{6,4},{7,5},{8,10},{9,11},{10,... | collective-permute-start | bytes 1966088 | tf_op jit(solution)/shard_map/ppermute | solution.py:825
  43.6 71.9 %collective-permute-start.12 = (bf16[320,1024]{1,0:T(8,128)(2,1)}, bf16[320,1024]{1,0:T(8,128)(2,1)S(1)}, u32[]{:S(2)}, u32[]{:S(2)}) collective-permute-start(bf16[320,1024]{1,0:T(8,128)(2,1)} %get-tuple-element.115), channel_id=1, source_target_pairs={{0,1},{1,0},{2,3},{3,2},{4,5},{5,4},{6,7},{7,6},{8,9},{9,8},{10,11... | collective-permute-start | bytes 1966088 | tf_op jit(solution)/shard_map/ppermute | solution.py:825
  45.5 70.1 %collective-permute-start.13 = (bf16[320,1024]{1,0:T(8,128)(2,1)}, bf16[320,1024]{1,0:T(8,128)(2,1)S(1)}, u32[]{:S(2)}, u32[]{:S(2)}) collective-permute-start(bf16[320,1024]{1,0:T(8,128)(2,1)} %get-tuple-element.116), channel_id=1, source_target_pairs={{0,3},{1,2},{2,1},{3,0},{4,7},{5,6},{6,5},{7,4},{8,11},{9,10},{10,... | collective-permute-start | bytes 1966088 | tf_op jit(solution)/shard_map/ppermute | solution.py:825
  88.3 34.4 %collective-permute-start.10 = (bf16[128,1024]{1,0:T(8,128)(2,1)}, bf16[128,1024]{1,0:T(8,128)(2,1)S(1)}, u32[]{:S(2)}, u32[]{:S(2)}) collective-permute-start(bf16[128,1024]{1,0:T(8,128)(2,1)} %get-tuple-element.111.refs_6_.refs_10_), channel_id=1, source_target_pairs={{0,2},{1,3},{2,0},{3,1},{4,6},{5,7},{6,4},{7,5},{8,10},{9,11},{10,... | collective-permute-start | bytes 786440 | tf_op jit(solution)/shard_map/ppermute | solution.py:825
  105.0 17.6 %collective-permute-start.9 = (bf16[128,1024]{1,0:T(8,128)(2,1)}, bf16[128,1024]{1,0:T(8,128)(2,1)S(1)}, u32[]{:S(2)}, u32[]{:S(2)}) collective-permute-start(bf16[128,1024]{1,0:T(8,128)(2,1)} %get-tuple-element.113.refs_9_), channel_id=1, source_target_pairs={{0,1},{1,0},{2,3},{3,2},{4,5},{5,4},{6,7},{7,6},{8,9},{9,8},{10,11... | collective-permute-start | bytes 786440 | tf_op jit(solution)/shard_map/ppermute | solution.py:825
  106.0 18.3 %collective-permute-start.11 = (bf16[128,1024]{1,0:T(8,128)(2,1)S(1)}, bf16[128,1024]{1,0:T(8,128)(2,1)S(1)}, u32[]{:S(2)}, u32[]{:S(2)}) collective-permute-start(bf16[128,1024]{1,0:T(8,128)(2,1)S(1)} %copy-done.45), channel_id=1, source_target_pairs={{0,3},{1,2},{2,1},{3,0},{4,7},{5,6},{6,5},{7,4},{8,11},{9,10},{10,... | collective-permute-start | bytes 786440 | tf_op jit(solution)/shard_map/ppermute | solution.py:825
  130.6 29.0 %collective-permute-start.16 = (bf16[320,1024]{1,0:T(8,128)(2,1)}, bf16[320,1024]{1,0:T(8,128)(2,1)S(1)}, u32[]{:S(2)}, u32[]{:S(2)}) collective-permute-start(bf16[320,1024]{1,0:T(8,128)(2,1)} %get-tuple-element.124), channel_id=1, source_target_pairs={{0,2},{1,3},{2,0},{3,1},{4,6},{5,7},{6,4},{7,5},{8,10},{9,11},{10,... | collective-permute-start | bytes 1966088 | tf_op jit(solution)/shard_map/ppermute | solution.py:825
  156.4 31.4 %collective-permute-start.15 = (bf16[320,1024]{1,0:T(8,128)(2,1)}, bf16[320,1024]{1,0:T(8,128)(2,1)S(1)}, u32[]{:S(2)}, u32[]{:S(2)}) collective-permute-start(bf16[320,1024]{1,0:T(8,128)(2,1)} %get-tuple-element.123), channel_id=1, source_target_pairs={{0,1},{1,0},{2,3},{3,2},{4,5},{5,4},{6,7},{7,6},{8,9},{9,8},{10,11... | collective-permute-start | bytes 1966088 | tf_op jit(solution)/shard_map/ppermute | solution.py:825
  158.4 52.3 %collective-permute-start.14 = (bf16[320,1024]{1,0:T(8,128)(2,1)}, bf16[320,1024]{1,0:T(8,128)(2,1)S(1)}, u32[]{:S(2)}, u32[]{:S(2)}) collective-permute-start(bf16[320,1024]{1,0:T(8,128)(2,1)} %get-tuple-element.122), channel_id=1, source_target_pairs={{0,3},{1,2},{2,1},{3,0},{4,7},{5,6},{6,5},{7,4},{8,11},{9,10},{10,... | collective-permute-start | bytes 1966088 | tf_op jit(solution)/shard_map/ppermute | solution.py:825
  182.6 55.4 %collective-permute-start.17 = (bf16[320,1024]{1,0:T(8,128)(2,1)}, bf16[320,1024]{1,0:T(8,128)(2,1)S(1)}, u32[]{:S(2)}, u32[]{:S(2)}) collective-permute-start(bf16[320,1024]{1,0:T(8,128)(2,1)} %get-tuple-element.148), channel_id=1, source_target_pairs={{0,2},{1,3},{2,0},{3,1},{4,6},{5,7},{6,4},{7,5},{8,10},{9,11},{10,... | collective-permute-start | bytes 1966088 | tf_op jit(solution)/shard_map/ppermute | solution.py:825
  233.8 32.0 %collective-permute-start.22 = (bf16[320,1024]{1,0:T(8,128)(2,1)}, bf16[320,1024]{1,0:T(8,128)(2,1)S(1)}, u32[]{:S(2)}, u32[]{:S(2)}) collective-permute-start(bf16[320,1024]{1,0:T(8,128)(2,1)} %get-tuple-element.156), channel_id=1, source_target_pairs={{0,3},{1,2},{2,1},{3,0},{4,7},{5,6},{6,5},{7,4},{8,11},{9,10},{10,... | collective-permute-start | bytes 1966088 | tf_op jit(solution)/shard_map/ppermute | solution.py:825
  234.6 32.2 %collective-permute-start.21 = (bf16[320,1024]{1,0:T(8,128)(2,1)S(1)}, bf16[320,1024]{1,0:T(8,128)(2,1)S(1)}, u32[]{:S(2)}, u32[]{:S(2)}) collective-permute-start(bf16[320,1024]{1,0:T(8,128)(2,1)S(1)} %copy-done.39), channel_id=1, source_target_pairs={{0,1},{1,0},{2,3},{3,2},{4,5},{5,4},{6,7},{7,6},{8,9},{9,8},{10,11... | collective-permute-start | bytes 1966088 | tf_op jit(solution)/shard_map/ppermute | solution.py:825
  276.4 36.6 %copy-start.36 = (bf16[320,1024]{1,0:T(8,128)(2,1)S(1)}, bf16[320,1024]{1,0:T(8,128)(2,1)}, u32[]{:S(2)}) copy-start(bf16[320,1024]{1,0:T(8,128)(2,1)} %get-tuple-element.150) | copy-start | bytes 1966084
  299.3 13.7 %collective-permute-start.26 = (bf16[4,2,128,2816]{3,2,1,0:T(8,128)(2,1)}, bf16[4,2,128,2816]{3,2,1,0:T(8,128)(2,1)S(1)}, u32[]{:S(2)}, u32[]{:S(2)}) collective-permute-start(bf16[4,2,128,2816]{3,2,1,0:T(8,128)(2,1)} %get-tuple-element.168), channel_id=1, source_target_pairs={{0,4},{4,0},{8,12},{12,8},{16,20},{20,16},{24,28},{28,24},{1,5},{5... | collective-permute-start | bytes 17301512 | tf_op jit(solution)/shard_map/ppermute | solution.py:819
  299.3 74.2 %collective-permute-start.28 = (bf16[4,352,1024]{2,1,0:T(8,128)(2,1)}, bf16[4,352,1024]{2,1,0:T(8,128)(2,1)}, u32[]{:S(2)}, u32[]{:S(2)}) collective-permute-start(bf16[4,352,1024]{2,1,0:T(8,128)(2,1)} %get-tuple-element.158.refs_10_), channel_id=1, source_target_pairs={{0,4},{4,0},{8,12},{12,8},{16,20},{20,16},{24,28},{28,24},{1,5},{5... | collective-permute-start | bytes 8650760 | tf_op jit(solution)/shard_map/ppermute | solution.py:819
  299.8 30.6 %collective-permute-start.25 = (bf16[128,1024]{1,0:T(8,128)(2,1)S(1)}, bf16[128,1024]{1,0:T(8,128)(2,1)S(1)}, u32[]{:S(2)}, u32[]{:S(2)}) collective-permute-start(bf16[128,1024]{1,0:T(8,128)(2,1)S(1)} %copy-done.52), channel_id=1, source_target_pairs={{0,3},{1,2},{2,1},{3,0},{4,7},{5,6},{6,5},{7,4},{8,11},{9,10},{10,... | collective-permute-start | bytes 786440 | tf_op jit(solution)/shard_map/ppermute | solution.py:825
  301.1 27.1 %collective-permute-start.23 = (bf16[128,1024]{1,0:T(8,128)(2,1)}, bf16[128,1024]{1,0:T(8,128)(2,1)S(1)}, u32[]{:S(2)}, u32[]{:S(2)}) collective-permute-start(bf16[128,1024]{1,0:T(8,128)(2,1)} %get-tuple-element.160), channel_id=1, source_target_pairs={{0,1},{1,0},{2,3},{3,2},{4,5},{5,4},{6,7},{7,6},{8,9},{9,8},{10,11... | collective-permute-start | bytes 786440 | tf_op jit(solution)/shard_map/ppermute | solution.py:825
  303.5 27.0 %collective-permute-start.24 = (bf16[128,1024]{1,0:T(8,128)(2,1)}, bf16[128,1024]{1,0:T(8,128)(2,1)S(1)}, u32[]{:S(2)}, u32[]{:S(2)}) collective-permute-start(bf16[128,1024]{1,0:T(8,128)(2,1)} %get-tuple-element.161), channel_id=1, source_target_pairs={{0,2},{1,3},{2,0},{3,1},{4,6},{5,7},{6,4},{7,5},{8,10},{9,11},{10,... | collective-permute-start | bytes 786440 | tf_op jit(solution)/shard_map/ppermute | solution.py:825
  313.1 39.2 %collective-permute-start.18 = (bf16[320,1024]{1,0:T(8,128)(2,1)S(1)}, bf16[320,1024]{1,0:T(8,128)(2,1)S(1)}, u32[]{:S(2)}, u32[]{:S(2)}) collective-permute-start(bf16[320,1024]{1,0:T(8,128)(2,1)S(1)} %copy-done.36), channel_id=1, source_target_pairs={{0,1},{1,0},{2,3},{3,2},{4,5},{5,4},{6,7},{7,6},{8,9},{9,8},{10,11... | collective-permute-start | bytes 1966088 | tf_op jit(solution)/shard_map/ppermute | solution.py:825
  322.9 70.7 %all-to-all-start = ((bf16[4,2,128,2816]{3,2,1,0:T(8,128)(2,1)}), bf16[4,2,128,2816]{3,2,1,0:T(8,128)(2,1)}, u32[]{:S(2)}, u32[]{:S(2)}) async-start(bf16[4,2,128,2816]{3,2,1,0:T(8,128)(2,1)} %pair_sum.2.refs_16_), calls=%async_computation | async-start | bytes 11534336 | tf_op jit(solution)/shard_map/all_to_all | solution.py:831
  328.2 30.6 %collective-permute-start.19 = (bf16[320,1024]{1,0:T(8,128)(2,1)S(1)}, bf16[320,1024]{1,0:T(8,128)(2,1)S(1)}, u32[]{:S(2)}, u32[]{:S(2)}) collective-permute-start(bf16[320,1024]{1,0:T(8,128)(2,1)S(1)} %copy-done.35), channel_id=1, source_target_pairs={{0,2},{1,3},{2,0},{3,1},{4,6},{5,7},{6,4},{7,5},{8,10},{9,11},{10,... | collective-permute-start | bytes 1966088 | tf_op jit(solution)/shard_map/ppermute | solution.py:825
  372.3 15.3 %collective-permute-start.27 = (bf16[4,128,2560]{2,1,0:T(8,128)(2,1)}, bf16[4,128,2560]{2,1,0:T(8,128)(2,1)S(1)}, u32[]{:S(2)}, u32[]{:S(2)}) collective-permute-start(bf16[4,128,2560]{2,1,0:T(8,128)(2,1)} %get-tuple-element.173.refs_6_), channel_id=1, source_target_pairs={{0,4},{4,0},{8,12},{12,8},{16,20},{20,16},{24,28},{28,24},{1,5},{5... | collective-permute-start | bytes 7864328 | tf_op jit(solution)/shard_map/ppermute | solution.py:819
  372.8 50.1 %collective-permute-start.20 = (bf16[320,1024]{1,0:T(8,128)(2,1)}, bf16[320,1024]{1,0:T(8,128)(2,1)}, u32[]{:S(2)}, u32[]{:S(2)}) collective-permute-start(bf16[320,1024]{1,0:T(8,128)(2,1)} %get-tuple-element.152), channel_id=1, source_target_pairs={{0,3},{1,2},{2,1},{3,0},{4,7},{5,6},{6,5},{7,4},{8,11},{9,10},{10,... | collective-permute-start | bytes 1966088 | tf_op jit(solution)/shard_map/ppermute | solution.py:825
  393.6 34.6 %all-to-all-start.1 = ((bf16[4,128,2560]{2,1,0:T(8,128)(2,1)}), bf16[4,128,2560]{2,1,0:T(8,128)(2,1)S(1)}, u32[]{:S(2)}, u32[]{:S(2)}) async-start(bf16[4,128,2560]{2,1,0:T(8,128)(2,1)} %add_convert_fusion.refs_17_), calls=%async_computation.1 | async-start | bytes 5242880 | tf_op jit(solution)/shard_map/all_to_all | solution.py:831
  439.1 4.0 collective-permute-start.29
  446.3 26.2 %all-to-all-start.2 = ((bf16[4,128,1792]{2,1,0:T(8,128)(2,1)}), bf16[4,128,1792]{2,1,0:T(8,128)(2,1)S(1)}, u32[]{:S(2)}, u32[]{:S(2)}) async-start(bf16[4,128,1792]{2,1,0:T(8,128)(2,1)} %add_convert_fusion.1.refs_7_), calls=%async_computation.2 | async-start | bytes 3670016 | tf_op jit(solution)/shard_map/all_to_all | solution.py:831
  460.9 2.9 collective-permute-start.30
  478.3 29.2 %collective-permute-start.31 = (bf16[512,1024]{1,0:T(8,128)(2,1)}, bf16[512,1024]{1,0:T(8,128)(2,1)}, u32[]{:S(2)}, u32[]{:S(2)}) collective-permute-start(bf16[512,1024]{1,0:T(8,128)(2,1)} %get-tuple-element.187.refs_7_), channel_id=1, source_target_pairs={{8,0},{12,4},{16,8},{20,12},{24,16},{28,20},{9,1},{13,5},{17,9},{2... | collective-permute-start | bytes 3145736 | tf_op jit(solution)/shard_map/ppermute | solution.py:815
  482.4 54.3 %all-to-all-start.3 = ((bf16[4,352,1024]{2,1,0:T(8,128)(2,1)}), bf16[4,352,1024]{2,1,0:T(8,128)(2,1)S(1)}, u32[]{:S(2)}, u32[]{:S(2)}) async-start(bf16[4,352,1024]{2,1,0:T(8,128)(2,1)} %get-tuple-element.199), calls=%async_computation.3 | async-start | bytes 5767168 | tf_op jit(solution)/shard_map/all_to_all | solution.py:831
  489.2 9.3 %collective-permute-start.32 = (bf16[32,2560]{1,0:T(8,128)(2,1)}, bf16[32,2560]{1,0:T(8,128)(2,1)S(1)}, u32[]{:S(2)}, u32[]{:S(2)}) collective-permute-start(bf16[32,2560]{1,0:T(8,128)(2,1)} %get-tuple-element.191), channel_id=1, source_target_pairs={{0,1},{1,0},{2,3},{3,2},{4,5},{5,4},{6,7},{7,6},{8,9},{9,8},{10,11... | collective-permute-start | bytes 491528 | tf_op jit(solution)/shard_map/ppermute | solution.py:825
  490.7 12.2 %collective-permute-start.33 = (bf16[32,2560]{1,0:T(8,128)(2,1)}, bf16[32,2560]{1,0:T(8,128)(2,1)S(1)}, u32[]{:S(2)}, u32[]{:S(2)}) collective-permute-start(bf16[32,2560]{1,0:T(8,128)(2,1)} %get-tuple-element.192), channel_id=1, source_target_pairs={{0,2},{1,3},{2,0},{3,1},{4,6},{5,7},{6,4},{7,5},{8,10},{9,11},{10,... | collective-permute-start | bytes 491528 | tf_op jit(solution)/shard_map/ppermute | solution.py:825
  492.0 13.7 %collective-permute-start.34 = (bf16[32,2560]{1,0:T(8,128)(2,1)}, bf16[32,2560]{1,0:T(8,128)(2,1)S(1)}, u32[]{:S(2)}, u32[]{:S(2)}) collective-permute-start(bf16[32,2560]{1,0:T(8,128)(2,1)} %get-tuple-element.193), channel_id=1, source_target_pairs={{0,3},{1,2},{2,1},{3,0},{4,7},{5,6},{6,5},{7,4},{8,11},{9,10},{10,... | collective-permute-start | bytes 491528 | tf_op jit(solution)/shard_map/ppermute | solution.py:825
  513.3 25.0 %collective-permute-start.35 = (bf16[192,1024]{1,0:T(8,128)(2,1)}, bf16[192,1024]{1,0:T(8,128)(2,1)S(1)}, u32[]{:S(2)}, u32[]{:S(2)}) collective-permute-start(bf16[192,1024]{1,0:T(8,128)(2,1)} %get-tuple-element.195), channel_id=1, source_target_pairs={{0,1},{1,0},{2,3},{3,2},{4,5},{5,4},{6,7},{7,6},{8,9},{9,8},{10,11... | collective-permute-start | bytes 1179656 | tf_op jit(solution)/shard_map/ppermute | solution.py:825
  514.8 27.9 %collective-permute-start.36 = (bf16[192,1024]{1,0:T(8,128)(2,1)}, bf16[192,1024]{1,0:T(8,128)(2,1)}, u32[]{:S(2)}, u32[]{:S(2)}) collective-permute-start(bf16[192,1024]{1,0:T(8,128)(2,1)} %get-tuple-element.196), channel_id=1, source_target_pairs={{0,2},{1,3},{2,0},{3,1},{4,6},{5,7},{6,4},{7,5},{8,10},{9,11},{10,... | collective-permute-start | bytes 1179656 | tf_op jit(solution)/shard_map/ppermute | solution.py:825
  516.1 32.3 %collective-permute-start.37 = (bf16[192,1024]{1,0:T(8,128)(2,1)}, bf16[192,1024]{1,0:T(8,128)(2,1)}, u32[]{:S(2)}, u32[]{:S(2)}) collective-permute-start(bf16[192,1024]{1,0:T(8,128)(2,1)} %get-tuple-element.197), channel_id=1, source_target_pairs={{0,3},{1,2},{2,1},{3,0},{4,7},{5,6},{6,5},{7,4},{8,11},{9,10},{10,... | collective-permute-start | bytes 1179656 | tf_op jit(solution)/shard_map/ppermute | solution.py:825
  (50 other events, 345.9 us)

commit v6 on v5

--- a/solution.py
+++ b/solution.py
@@ -993,15 +993,9 @@
     ok = (where_dist >= 0) & (where_dist < WINDOW)
     to_bucket = (bucket_of(np.clip(where_dist, 0, None))[..., None] == np.arange(bucket_total)) & ok[..., None]
     table_part = exact_dot(diagonals.reshape(heads, -1), jnp.asarray(to_bucket.reshape(-1, bucket_total), f32))
-    small = [
-        grad_gain_two.reshape(device_count, -1),
-        table_part.reshape(device_count, -1),
-        grad_router_part.reshape(device_count, -1),
-    ]
-    cuts = np.cumsum([0] + [item.shape[1] for item in small])
-    packed = jnp.concatenate(small, axis=1)
-    share = width // device_count
-    packed = jnp.pad(packed, ((0, 0), (0, -packed.shape[1] % share))).reshape(width, -1)
+    share, table_share = width // device_count, heads * bucket_total // device_count
+    table_rows = jnp.pad(table_part.reshape(device_count, table_share), ((0, 0), (0, share - table_share)))
+    packed = jnp.concatenate([grad_gain_two.reshape(width, 1), grad_router_part, table_rows.reshape(width, 1)], axis=1)
     packed = jnp.pad(packed.astype(bf16), ((0, 0), (0, 2 * TILE - packed.shape[1])))
     packed = packed.reshape(ctx_count // 2, 2, -1, 2 * TILE)
     other, mine = projection_grads(side_ref, normed_t, *flat(grads), small=[packed], others=[first_parts, given[3]])
@@ -1036,9 +1030,8 @@
         + [((share, width), f32)],
         6, "end_rows", [grad_down],
     )
-    packed = packed[:, : -(-cuts[-1] // share)].reshape(-1)
-    norm1_out = norm1_out[:, 0]
-    norm2_out, table_out, router_out = [packed[cuts[i] : cuts[i + 1]] for i in range(3)]
+    norm1_out, norm2_out = norm1_out[:, 0], packed[:, 0]
+    router_out, table_out = packed[:, 1 : 1 + experts], packed[:table_share, 1 + experts]
     return (
         mixed, grad_tokens, norm1_out, grad_query, grad_key, grad_value, grad_out, table_out, norm2_out,
         router_out.reshape(-1, experts), grad_gate[None], grad_up[None], grad_down[None],

time: 563 us -> 565 us (level)
    unnamed x115 -> x114, local copies, waits for them, and re-layouts: 12.8 us -> 12.9 us
where the time goes in v6:
time: 565 us; the launch traced here: 558 us
  Pallas kernels  324 us (57%)
  waiting for transfers between devices  96.6 us (17%)
  starting transfers between devices  73 us (13%)
  local copies, waits for them, and re-layouts  31.8 us (6%)
  other arithmetic  18.9 us (3%)
  matrix products  11.7 us (2%)
    pallas_call x4, Pallas kernels, expert(): pl.pallas_call(functools.partial(expert_kernel, experts, count, len(held)...  88.4 us
    ppermute x27, waiting for transfers between devices, z_swap(): lax.ppermute(x, 'exp', [(i, i ^ k) for i in range(lax.axis_size('exp'))])  45.3 us
    pallas_call x2, Pallas kernels, attend_back(): pl.pallas_call(behind(functools.partial(attend_back_kernel, pieces), 8 +...  42.2 us
    pallas_call x8, Pallas kernels, call(): pl.pallas_call(body, in_specs=specs + anywhere(passed) + anywhere(others)...  40.8 us
    ppermute x27, starting transfers between devices, z_swap(): lax.ppermute(x, 'exp', [(i, i ^ k) for i in range(lax.axis_size('exp'))])  37.1 us
    all_to_all x4, waiting for transfers between devices, over_chips(): lax.all_to_all(pair, 'ctx', split_axis=0, concat_axis=0, tiled=True, axis...  33 us
    pallas_call x2, Pallas kernels, attend(): pl.pallas_call(behind(functools.partial(attend_kernel, ks), 6, others), g...  27.7 us
    pallas_call x1, Pallas kernels, gate_up_grads(): pl.pallas_call(behind(gate_up_kernel, 5, others), grid=(hidden // wide,),...  22.8 us
  transfers between devices with their start and end apart: 42, of which 22 were waited for; matrix products, arithmetic and copies ran while one was open for 7% of the time, Pallas kernels for 48%

profile of v6, /device:TPU:10, one launch (start us, length us, event | category | flops | bytes accessed | tf_op | source)
XLA Modules:
  0.0 558.0 jit_solution(2092920170493587388)
XLA Ops:
  16.4 6.8 %collective-permute-done.3.refs_4_ = bf16[128,1024]{1,0:T(8,128)(2,1)S(1)} collective-permute-done((bf16[128,1024]{1,0:T(8,128)(2,1)S(1)}, bf16[128,1024]{1,0:T(8,128)(2,1)S(1)}, u32[]{:S(2)}, u32[]{:S(2)}) %collective-permute-start.3) | collective-permute-done | bytes 262176 | tf_op jit(solution)/shard_map/ppermute | solution.py:825
  28.3 3.4 collective-permute-start.6
  38.8 3.7 cot_rows.1
  46.0 6.5 %bias_tiles.1.refs_5_.refs_7_ = bf16[8,9,128,256]{3,2,1,0:T(8,128)(2,1)} custom-call(f32[8,2,1280]{2,1,0:T(2,128)} %reshape.295.refs_0_, bf16[320,1024]{1,0:T(8,128)(2,1)} %get-tuple-element.110.refs_1_), custom_call_target="tpu_custom_call" | custom-call | flops 6899999744 | tf_op jit(solution)/shard_map/bias_tiles/pallas_call | solution.py:166
  53.5 6.2 %norm_window.1.refs_0_ = bf16[12,128,1024]{2,1,0:T(8,128)(2,1)} custom-call(bf16[4,128,1024]{2,1,0:T(8,128)(2,1)} %get-tuple-element.281.two_ref, bf16[4,128,1024]{2,1,0:T(8,128)(2,1)} %copy-done.29, bf16[4,128,1024]{2,1,0:T(8,128)(2,1)} %get-tuple-element.279.own_ref.refs_1_, f32[1,1024]{1,0:T(1,128)} %bitcast.109), custom_call_target="tpu_custom_call" | custom-call | flops 5750000128 | tf_op jit(solution)/shard_map/norm_window/pallas_call | solution.py:482
  64.3 4.8 convolution_convert_fusion.1
  69.0 4.8 convolution_convert_fusion
  74.4 13.9 %attend.2 = (bf16[128,1024]{1,0:T(8,128)(2,1)}, bf16[128,1024]{1,0:T(8,128)(2,1)}, f32[8,2,1,256]{3,2,1,0:T(1,128)}) custom-call(s32[1]{0:T(128)} %bitcast.refs_0_.z_ref.refs_1_, s32[2,1,256]{2,1,0:T(1,128)} %bitcast.115, bf16[2,128,1024]{2,1,0:T(8,128)(2,1)} %bitcast.93, bf16[12,128,1024]{2,1,0:T(8,128)(2,1)} %bitcast.118, ...), custom_call_target="tpu_custom_call" | custom-call | flops 13799999488 | tf_op jit(solution)/shard_map/attend/pallas_call | solution.py:185
  91.2 13.9 %attend.3 = (bf16[128,1024]{1,0:T(8,128)(2,1)}, bf16[128,1024]{1,0:T(8,128)(2,1)}, f32[8,2,1,256]{3,2,1,0:T(1,128)}) custom-call(s32[1]{0:T(128)} %bitcast.refs_0_.z_ref.refs_1_, s32[2,1,256]{2,1,0:T(1,128)} %bitcast.116, bf16[2,128,1024]{2,1,0:T(8,128)(2,1)} %bitcast.92, bf16[12,128,1024]{2,1,0:T(8,128)(2,1)} %bitcast.119, ...), custom_call_target="tpu_custom_call" | custom-call | flops 13799999488 | tf_op jit(solution)/shard_map/attend/pallas_call | solution.py:185
  106.4 9.0 %turn_rows.1.refs_11_.refs_1_ = bf16[4,2,128,1536]{3,2,1,0:T(8,128)(2,1)} custom-call(bf16[12,128,1024]{2,1,0:T(8,128)(2,1)} %norm_window.1.refs_0_, bf16[128,1024]{1,0:T(8,128)(2,1)} %get-tuple-element.112.refs_1_.refs_5_.refs_8_), custom_call_target="tpu_custom_call" | custom-call | flops 9200000000 | tf_op jit(solution)/shard_map/turn_rows/pallas_call | solution.py:501
  115.5 7.1 %collective-permute-done.9.refs_6_ = bf16[128,1024]{1,0:T(8,128)(2,1)S(1)} collective-permute-done((bf16[128,1024]{1,0:T(8,128)(2,1)}, bf16[128,1024]{1,0:T(8,128)(2,1)S(1)}, u32[]{:S(2)}, u32[]{:S(2)}) %collective-permute-start.9) | collective-permute-done | bytes 262176 | tf_op jit(solution)/shard_map/ppermute | solution.py:825
  125.0 5.6 %hidden_rows.1 = (f32[512,1024]{1,0:T(8,128)}, bf16[512,1024]{1,0:T(8,128)(2,1)}, bf16[320,1024]{1,0:T(8,128)(2,1)}, bf16[320,1024]{1,0:T(8,128)(2,1)}) custom-call(s32[1]{0:T(128)} %bitcast.refs_0_.z_ref.refs_1_, s32[2,512]{1,0:T(2,128)} %copy-done.17, bf16[4,128,1024]{2,1,0:T(8,128)(2,1)} %refs_2_.7, bf16[1024,1024]{1,0:T(8,128)(2,1)} %refs_4_.11, ...), custom_call_target="tpu_custom_call" | custom-call | flops 10350000128 | tf_op jit(solution)/shard_map/hidden_rows/pallas_call | solution.py:542
  131.4 22.0 %expert.4 = (bf16[320,1024]{1,0:T(8,128)(2,1)}, bf16[1280,1024]{1,0:T(8,128)(2,1)}, bf16[1280,2816]{1,0:T(8,128)(2,1)}, bf16[1280,2816]{1,0:T(8,128)(2,1)}, bf16...) custom-call(s32[1]{0:T(128)} %bitcast.refs_0_.z_ref.refs_1_, ...), custom_call_target="tpu_custom_call" | custom-call | flops 26449999872 | tf_op jit(solution)/shard_map/expert/pallas_call | solution.py:332
  160.5 22.1 %expert.5 = (bf16[320,1024]{1,0:T(8,128)(2,1)}, bf16[1280,1024]{1,0:T(8,128)(2,1)}, bf16[1280,2816]{1,0:T(8,128)(2,1)}, bf16[1280,2816]{1,0:T(8,128)(2,1)}, bf16...) custom-call(s32[1]{0:T(128)} %bitcast.refs_0_.z_ref.refs_1_, ...), custom_call_target="tpu_custom_call", output_to_operand_aliasing={{1}: (7, {}), {2}: (8, {}), {3}: (9, {}), {4}: (10, {}), {5... | custom-call | flops 26449999872 | tf_op jit(solution)/shard_map/expert/pallas_call | solution.py:332
  188.6 22.0 %expert.6 = (bf16[320,1024]{1,0:T(8,128)(2,1)}, bf16[1280,1024]{1,0:T(8,128)(2,1)}, bf16[1280,2816]{1,0:T(8,128)(2,1)}, bf16[1280,2816]{1,0:T(8,128)(2,1)}, bf16...) custom-call(s32[1]{0:T(128)} %bitcast.refs_0_.z_ref.refs_1_, ...), custom_call_target="tpu_custom_call", output_to_operand_aliasing={{1}: (7, {}), {2}: (8, {}), {3}: (9, {}), {4}: (10, {}), {5... | custom-call | flops 26449999872 | tf_op jit(solution)/shard_map/expert/pallas_call | solution.py:332
  211.5 22.3 %expert.7 = (bf16[320,1024]{1,0:T(8,128)(2,1)}, bf16[1280,1024]{1,0:T(8,128)(2,1)}, bf16[1280,2816]{1,0:T(8,128)(2,1)}, bf16[1280,2816]{1,0:T(8,128)(2,1)}, bf16...) custom-call(s32[1]{0:T(128)} %bitcast.refs_0_.z_ref.refs_1_, ...), custom_call_target="tpu_custom_call", output_to_operand_aliasing={{1}: (7, {}), {2}: (8, {}), {3}: (9, {}), {4}: (10, {}), {5... | custom-call | flops 26449999872 | tf_op jit(solution)/shard_map/expert/pallas_call | solution.py:332
  234.7 3.4 collective-permute-start.21
  238.9 14.4 %expert_out.1 = (bf16[320,1024]{1,0:T(8,128)(2,1)}, bf16[320,1024]{1,0:T(8,128)(2,1)}, bf16[320,1024]{1,0:T(8,128)(2,1)}, bf16[320,1024]{1,0:T(8,128)(2,1)}) custom-call(bf16[1280,2816]{1,0:T(8,128)(2,1)} %get-tuple-element.146.refs_0_.refs_1_, bf16[1,2816,1024]{2,1,0:T(8,128)(2,1)} %refs_1_.1, f32[1280,128]{1,0:T(8,128)} %get-tuple-element.147.refs_2_, ...), custom_call_target="tpu_custom_call" | custom-call | flops 16099999744 | tf_op jit(solution)/shard_map/expert_out/pallas_call | solution.py:450
  253.3 12.6 %down_grads.1 = (bf16[4,352,1024]{2,1,0:T(8,128)(2,1)}, bf16[4,352,1024]{2,1,0:T(8,128)(2,1)}) custom-call(s32[1]{0:T(128)} %bitcast.36.refs_0_, bf16[1280,2816]{1,0:T(8,128)(2,1)} %get-tuple-element.146.refs_0_.refs_1_, bf16[1280,1024]{1,0:T(8,128)(2,1)} %get-tuple-element.157.refs_2_, bf16[320,1024]{1,0:T(8,128)(2,1)} %get-tuple-element.149.refs_3_), custom_call_target="tpu_custom_call" | custom-call | flops 16099999744 | tf_op jit(solution)/shard_map/down_grads/pallas_call | solution.py:411
  267.7 8.8 %middle_rows.1 = (f32[512,1024]{1,0:T(8,128)}, bf16[512,1024]{1,0:T(8,128)(2,1)}, f32[1,1024]{1,0:T(1,128)}, bf16[128,1024]{1,0:T(8,128)(2,1)}, bf16[128,1024]{1...) custom-call(s32[1]{0:T(128)} %bitcast.refs_0_.z_ref.refs_1_, s32[512,2]{1,0:T(8,128)} %bitcast.96, ...), custom_call_target="tpu_custom_call" | custom-call | flops 10350000128 | tf_op jit(solution)/shard_map/middle_rows/pallas_call | solution.py:542
  276.5 22.8 %gate_up_grads.1 = (bf16[4,2,128,2816]{3,2,1,0:T(8,128)(2,1)}, bf16[4,2,128,2816]{3,2,1,0:T(8,128)(2,1)}, f32[1024,128]{1,0:T(8,128)}) custom-call(s32[1]{0:T(128)} %bitcast.36.refs_0_, bf16[1280,1024]{1,0:T(8,128)(2,1)} %get-tuple-element.163.refs_1_, bf16[1280,2816]{1,0:T(8,128)(2,1)} %get-tuple-element.164.refs_2_, ...), custom_call_target="tpu_custom_call" | custom-call | flops 27599998976 | tf_op jit(solution)/shard_map/gate_up_grads/pallas_call | solution.py:379
  303.7 9.4 %collective-permute-done.26.refs_1_ = bf16[4,2,128,2816]{3,2,1,0:T(8,128)(2,1)S(1)} collective-permute-done((bf16[4,2,128,2816]{3,2,1,0:T(8,128)(2,1)}, bf16[4,2,128,2816]{3,2,1,0:T(8,128)(2,1)S(1)}, u32[]{:S(2)}, u32[]{:S(2)}) %collective-permute-start.26) | collective-permute-done | bytes 5767200 | tf_op jit(solution)/shard_map/ppermute | solution.py:819
  315.6 7.4 %pair_sum.2.refs_16_ = bf16[4,2,128,2816]{3,2,1,0:T(8,128)(2,1)} custom-call(bf16[4,2,128,2816]{3,2,1,0:T(8,128)(2,1)} %get-tuple-element.167.refs_0_, bf16[4,2,128,2816]{3,2,1,0:T(8,128)(2,1)} %copy-done.27), custom_call_target="tpu_custom_call" | custom-call | flops 6899999744 | tf_op jit(solution)/shard_map/pair_sum/pallas_call | solution.py:562
  322.9 5.3 all-to-all-start
  331.1 21.0 %attend_back.2 = (bf16[4,128,512]{2,1,0:T(8,128)(2,1)}, bf16[12,128,512]{2,1,0:T(8,128)(2,1)}, bf16[12,128,512]{2,1,0:T(8,128)(2,1)}, f32[4,2,9,256]{3,2,1,0:T(8,128)}) custom-call(s32[1]{0:T(128)} %bitcast.refs_0_.z_ref.refs_1_, s32[4,1,256]{2,1,0:T(1,128)} %bitcast.113, f32[8,2,1,256]{3,2,1,0:T(1,128)} %get-tuple-element.153.refs_2_, ...), custom_call_target="tpu_custom_call" | custom-call | flops 24149999616 | tf_op jit(solution)/shard_map/attend_back/pallas_call | solution.py:218
  352.1 6.7 %collective-permute-done.19.refs_10_.refs_5_ = bf16[320,1024]{1,0:T(8,128)(2,1)S(1)} collective-permute-done((bf16[320,1024]{1,0:T(8,128)(2,1)S(1)}, bf16[320,1024]{1,0:T(8,128)(2,1)S(1)}, u32[]{:S(2)}, u32[]{:S(2)}) %collective-permute-start.19) | collective-permute-done | bytes 655392 | tf_op jit(solution)/shard_map/ppermute | solution.py:825
  359.6 12.6 %projection_grads.2 = (bf16[4,128,2560]{2,1,0:T(8,128)(2,1)}, bf16[4,128,2560]{2,1,0:T(8,128)(2,1)}) custom-call(s32[1]{0:T(128)} %bitcast.36.refs_0_, bf16[4,2,128,1536]{3,2,1,0:T(8,128)(2,1)} %turn_rows.1.refs_11_.refs_1_, bf16[512,512]{1,0:T(8,128)(2,1)} %bitcast.131, bf16[1536,512]{1,0:T(8,128)(2,1)} %bitcast.128, bf16[1536,512]{1,0:T(8,128)(2,1)} %bitcast.129, ...), custom_call_target="tpu_custom_call" | custom-call | flops 15294999552 | tf_op jit(solution)/shard_map/projection_grads/pallas_call | solution.py:791
  373.4 4.9 pair_sum.3.refs_19_.refs_5_
  378.3 9.1 %input_grads.2.refs_16_.refs_6_ = f32[1536,1024]{1,0:T(8,128)} custom-call(bf16[4,128,512]{2,1,0:T(8,128)(2,1)} %get-tuple-element.169.refs_0_, bf16[12,128,512]{2,1,0:T(8,128)(2,1)} %get-tuple-element.170.refs_1_, bf16[12,128,512]{2,1,0:T(8,128)(2,1)} %get-tuple-element.171.refs_2_, bf16[1024,1024]{1,0:T(8,128)(2,1)} %refs_3_.15, ...), custom_call_target="tpu_custom_call" | custom-call | flops 8049999872 | tf_op jit(solution)/shard_map/input_grads/pallas_call | solution.py:663
  389.6 4.1 all-to-all-done.refs_18_
  393.7 4.6 all-to-all-start.1
  398.3 21.3 %attend_back.3 = (bf16[4,128,512]{2,1,0:T(8,128)(2,1)}, bf16[12,128,512]{2,1,0:T(8,128)(2,1)}, bf16[12,128,512]{2,1,0:T(8,128)(2,1)}, f32[4,2,9,256]{3,2,1,0:T(8,128)}) custom-call(s32[1]{0:T(128)} %bitcast.refs_0_.z_ref.refs_1_, s32[4,1,256]{2,1,0:T(1,128)} %bitcast.114, f32[8,2,1,256]{3,2,1,0:T(1,128)} %get-tuple-element.153.refs_2_, ...), custom_call_target="tpu_custom_call" | custom-call | flops 24149999616 | tf_op jit(solution)/shard_map/attend_back/pallas_call | solution.py:218
  422.6 5.8 %all-to-all-done.1.refs_6_.refs_4_ = bf16[4,128,2560]{2,1,0:T(8,128)(2,1)S(1)} async-done(((bf16[4,128,2560]{2,1,0:T(8,128)(2,1)}), bf16[4,128,2560]{2,1,0:T(8,128)(2,1)S(1)}, u32[]{:S(2)}, u32[]{:S(2)}) %all-to-all-start.1) | async-done | bytes 2621472 | tf_op jit(solution)/shard_map/all_to_all | solution.py:831
  429.9 9.3 %projection_grads.3 = (bf16[4,128,1792]{2,1,0:T(8,128)(2,1)}, bf16[4,128,1792]{2,1,0:T(8,128)(2,1)}) custom-call(s32[1]{0:T(128)} %bitcast.36.refs_0_, bf16[4,2,128,1536]{3,2,1,0:T(8,128)(2,1)} %turn_rows.1.refs_11_.refs_1_, bf16[512,512]{1,0:T(8,128)(2,1)} %bitcast.130, bf16[1536,512]{1,0:T(8,128)(2,1)} %bitcast.126, bf16[1536,512]{1,0:T(8,128)(2,1)} %bitcast.127, ...), custom_call_target="tpu_custom_call" | custom-call | flops 11845000192 | tf_op jit(solution)/shard_map/projection_grads/pallas_call | solution.py:791
  439.2 4.0 collective-permute-done.29
  446.4 4.1 all-to-all-start.2
  450.5 10.5 %input_grads.3 = (bf16[512,1024]{1,0:T(8,128)(2,1)}, bf16[512,1024]{1,0:T(8,128)(2,1)}, f32[512,1024]{1,0:T(8,128)}) custom-call(bf16[4,128,512]{2,1,0:T(8,128)(2,1)} %get-tuple-element.176.refs_0_, bf16[12,128,512]{2,1,0:T(8,128)(2,1)} %get-tuple-element.177.refs_1_, bf16[12,128,512]{2,1,0:T(8,128)(2,1)} %get-tuple-element.178.refs_2_, ...), custom_call_target="tpu_custom_call" | custom-call | flops 8049999872 | tf_op jit(solution)/shard_map/input_grads/pallas_call | solution.py:663
  463.9 8.7 %all-to-all-done.2.refs_6_ = bf16[4,128,1792]{2,1,0:T(8,128)(2,1)S(1)} async-done(((bf16[4,128,1792]{2,1,0:T(8,128)(2,1)}), bf16[4,128,1792]{2,1,0:T(8,128)(2,1)S(1)}, u32[]{:S(2)}, u32[]{:S(2)}) %all-to-all-start.2) | async-done | bytes 1835040 | tf_op jit(solution)/shard_map/all_to_all | solution.py:831
  473.8 4.6 leaving_rows.1
  482.4 5.3 all-to-all-start.3
  492.7 5.8 %mixed_rows.1.refs_7_ = bf16[4,128,1024]{2,1,0:T(8,128)(2,1)} custom-call(s32[1]{0:T(128)} %bitcast.refs_0_.z_ref.refs_1_, s32[512,2]{1,0:T(8,128)} %bitcast.97, f32[512,1024]{1,0:T(8,128)} %get-tuple-element.117.refs_2_, bf16[320,1024]{1,0:T(8,128)(2,1)} %get-tuple-element.149.refs_3_, bf16[320,1024]{1,0:T(8,128)(2,1)} %copy-done.30, ...), custom_call_target="tpu_custom_call" | custom-call | flops 9200000000 | tf_op jit(solution)/shard_map/mixed_rows/pallas_call | solution.py:542
  498.5 3.9 collective-permute-done.33.refs_9_.refs_12_
  507.6 5.7 %tail_rows.1 = (bf16[192,1024]{1,0:T(8,128)(2,1)}, bf16[192,1024]{1,0:T(8,128)(2,1)}, bf16[192,1024]{1,0:T(8,128)(2,1)}, bf16[192,1024]{1,0:T(8,128)(2,1)}) custom-call(s32[1]{0:T(128)} %bitcast.refs_0_.z_ref.refs_1_, bf16[4,128,1024]{2,1,0:T(8,128)(2,1)} %get-tuple-element.279.own_ref.refs_1_, f32[512,1024]{1,0:T(8,128)} %get-tuple-element.189.refs_2_, ...), custom_call_target="tpu_custom_call" | custom-call | flops 9200000000 | tf_op jit(solution)/shard_map/tail_rows/pallas_call | solution.py:542
  516.8 5.4 convert_reduce_fusion
  522.2 14.4 %all-to-all-done.3 = bf16[4,352,1024]{2,1,0:T(8,128)(2,1)S(1)} async-done(((bf16[4,352,1024]{2,1,0:T(8,128)(2,1)}), bf16[4,352,1024]{2,1,0:T(8,128)(2,1)S(1)}, u32[]{:S(2)}, u32[]{:S(2)}) %all-to-all-start.3) | async-done | bytes 2883616 | tf_op jit(solution)/shard_map/all_to_all | solution.py:831
  538.3 4.2 collective-permute-done.36.refs_8_
  542.6 6.0 %collective-permute-done.37.refs_9_ = bf16[192,1024]{1,0:T(8,128)(2,1)} collective-permute-done((bf16[192,1024]{1,0:T(8,128)(2,1)}, bf16[192,1024]{1,0:T(8,128)(2,1)}, u32[]{:S(2)}, u32[]{:S(2)}) %collective-permute-start.37) | collective-permute-done | bytes 393248 | tf_op jit(solution)/shard_map/ppermute | solution.py:825
  548.6 3.7 end_rows.1
  (237 shorter events, 112.8 us)
Async XLA Ops:
  0.7 31.0 %copy-start.21 = (bf16[1024]{0:T(1024)(128)(2,1)S(1)}, bf16[1024]{0:T(1024)(128)(2,1)}, u32[]{:S(2)}) copy-start(bf16[1024]{0:T(1024)(128)(2,1)} %param.23) | copy-start | bytes 6148
  0.7 32.3 %copy-start.22 = (bf16[1024]{0:T(1024)(128)(2,1)S(1)}, bf16[1024]{0:T(1024)(128)(2,1)}, u32[]{:S(2)}) copy-start(bf16[1024]{0:T(1024)(128)(2,1)} %param.29) | copy-start | bytes 6148
  0.7 32.9 %copy-start.18 = (bf16[1024,4]{0,1:T(4,128)(2,1)S(1)}, bf16[1024,4]{0,1:T(4,128)(2,1)}, u32[]{:S(2)}) copy-start(bf16[1024,4]{0,1:T(4,128)(2,1)} %param.30) | copy-start | bytes 24580
  2.1 10.9 %collective-permute-start.1 = (bf16[128,1024]{1,0:T(8,128)(2,1)S(1)}, bf16[128,1024]{1,0:T(8,128)(2,1)S(1)}, u32[]{:S(2)}, u32[]{:S(2)}) collective-permute-start(bf16[128,1024]{1,0:T(8,128)(2,1)S(1)} %get-tuple-element.284), channel_id=1, source_target_pairs={{0,1},{1,0},{2,3},{3,2},{4,5},{5,4},{6,7},{7,6},{8,9},{9,8},{10,11... | collective-permute-start | bytes 786440 | tf_op jit(solution)/shard_map/ppermute | solution.py:825
  2.6 20.6 %collective-permute-start.3 = (bf16[128,1024]{1,0:T(8,128)(2,1)S(1)}, bf16[128,1024]{1,0:T(8,128)(2,1)S(1)}, u32[]{:S(2)}, u32[]{:S(2)}) collective-permute-start(bf16[128,1024]{1,0:T(8,128)(2,1)S(1)} %get-tuple-element.283), channel_id=1, source_target_pairs={{0,2},{1,3},{2,0},{3,1},{4,6},{5,7},{6,4},{7,5},{8,10},{9,11},{10,... | collective-permute-start | bytes 786440 | tf_op jit(solution)/shard_map/ppermute | solution.py:825
  5.2 23.1 %collective-permute-start.5 = (bf16[128,1024]{1,0:T(8,128)(2,1)S(1)}, bf16[128,1024]{1,0:T(8,128)(2,1)S(1)}, u32[]{:S(2)}, u32[]{:S(2)}) collective-permute-start(bf16[128,1024]{1,0:T(8,128)(2,1)S(1)} %get-tuple-element.285), channel_id=1, source_target_pairs={{0,3},{1,2},{2,1},{3,0},{4,7},{5,6},{6,5},{7,4},{8,11},{9,10},{10,... | collective-permute-start | bytes 786440 | tf_op jit(solution)/shard_map/ppermute | solution.py:825
  5.7 29.8 %collective-permute-start = (bf16[128,1024]{1,0:T(8,128)(2,1)S(1)}, bf16[128,1024]{1,0:T(8,128)(2,1)S(1)}, u32[]{:S(2)}, u32[]{:S(2)}) collective-permute-start(bf16[128,1024]{1,0:T(8,128)(2,1)S(1)} %bitcast.89), channel_id=1, source_target_pairs={{0,8},{4,12},{8,16},{12,20},{16,24},{20,28},{1,9},{5,13},{9,17},{1... | collective-permute-start | bytes 786440 | tf_op jit(solution)/shard_map/ppermute | solution.py:815
  12.3 26.4 %copy-start.15 = (s32[4,128]{1,0:T(4,128)}, s32[4,128]{1,0:T(4,128)S(1)}, u32[]{:S(2)}) copy-start(s32[4,128]{1,0:T(4,128)S(1)} %broadcast_subtract_fusion) | copy-start | bytes 6148
  13.0 25.7 %copy-start.8 = (bf16[128,1024]{1,0:T(8,128)(2,1)}, bf16[128,1024]{1,0:T(8,128)(2,1)S(1)}, u32[]{:S(2)}) copy-start(bf16[128,1024]{1,0:T(8,128)(2,1)S(1)} %collective-permute-done.1.refs_3_) | copy-start | bytes 786436
  13.0 22.4 %collective-permute-start.2 = (bf16[128,1024]{1,0:T(8,128)(2,1)S(1)}, bf16[128,1024]{1,0:T(8,128)(2,1)S(1)}, u32[]{:S(2)}, u32[]{:S(2)}) collective-permute-start(bf16[128,1024]{1,0:T(8,128)(2,1)S(1)} %collective-permute-done.1.refs_3_), channel_id=1, source_target_pairs={{0,8},{4,12},{8,16},{12,20},{16,24},{20,28},{1,9},{5,13},{9,17},{1... | collective-permute-start | bytes 786440 | tf_op jit(solution)/shard_map/ppermute | solution.py:815
  23.2 12.3 %collective-permute-start.4 = (bf16[128,1024]{1,0:T(8,128)(2,1)S(1)}, bf16[128,1024]{1,0:T(8,128)(2,1)S(1)}, u32[]{:S(2)}, u32[]{:S(2)}) collective-permute-start(bf16[128,1024]{1,0:T(8,128)(2,1)S(1)} %collective-permute-done.3.refs_4_), channel_id=1, source_target_pairs={{0,8},{4,12},{8,16},{12,20},{16,24},{20,28},{1,9},{5,13},{9,17},{1... | collective-permute-start | bytes 786440 | tf_op jit(solution)/shard_map/ppermute | solution.py:815
  28.3 8.8 %collective-permute-start.6 = (bf16[128,1024]{1,0:T(8,128)(2,1)S(1)}, bf16[128,1024]{1,0:T(8,128)(2,1)S(1)}, u32[]{:S(2)}, u32[]{:S(2)}) collective-permute-start(bf16[128,1024]{1,0:T(8,128)(2,1)S(1)} %collective-permute-done.5.refs_5_), channel_id=1, source_target_pairs={{0,8},{4,12},{8,16},{12,20},{16,24},{20,28},{1,9},{5,13},{9,17},{1... | collective-permute-start | bytes 786440 | tf_op jit(solution)/shard_map/ppermute | solution.py:815
  38.7 13.8 %collective-permute-start.7 = (bf16[4,128,1024]{2,1,0:T(8,128)(2,1)S(1)}, bf16[4,128,1024]{2,1,0:T(8,128)(2,1)S(1)}, u32[]{:S(2)}, u32[]{:S(2)}) collective-permute-start(bf16[4,128,1024]{2,1,0:T(8,128)(2,1)S(1)} %get-tuple-element.280), channel_id=1, source_target_pairs={{0,4},{4,0},{8,12},{12,8},{16,20},{20,16},{24,28},{28,24},{1,5},{5... | collective-permute-start | bytes 3145736 | tf_op jit(solution)/shard_map/ppermute | solution.py:819
  42.5 47.9 %collective-permute-start.8 = (bf16[320,1024]{1,0:T(8,128)(2,1)}, bf16[320,1024]{1,0:T(8,128)(2,1)S(1)}, u32[]{:S(2)}, u32[]{:S(2)}) collective-permute-start(bf16[320,1024]{1,0:T(8,128)(2,1)} %get-tuple-element.110.refs_1_), channel_id=1, source_target_pairs={{0,2},{1,3},{2,0},{3,1},{4,6},{5,7},{6,4},{7,5},{8,10},{9,11},{10,... | collective-permute-start | bytes 1966088 | tf_op jit(solution)/shard_map/ppermute | solution.py:825
  43.6 71.8 %collective-permute-start.12 = (bf16[320,1024]{1,0:T(8,128)(2,1)}, bf16[320,1024]{1,0:T(8,128)(2,1)S(1)}, u32[]{:S(2)}, u32[]{:S(2)}) collective-permute-start(bf16[320,1024]{1,0:T(8,128)(2,1)} %get-tuple-element.115), channel_id=1, source_target_pairs={{0,1},{1,0},{2,3},{3,2},{4,5},{5,4},{6,7},{7,6},{8,9},{9,8},{10,11... | collective-permute-start | bytes 1966088 | tf_op jit(solution)/shard_map/ppermute | solution.py:825
  45.5 70.0 %collective-permute-start.13 = (bf16[320,1024]{1,0:T(8,128)(2,1)}, bf16[320,1024]{1,0:T(8,128)(2,1)S(1)}, u32[]{:S(2)}, u32[]{:S(2)}) collective-permute-start(bf16[320,1024]{1,0:T(8,128)(2,1)} %get-tuple-element.116), channel_id=1, source_target_pairs={{0,3},{1,2},{2,1},{3,0},{4,7},{5,6},{6,5},{7,4},{8,11},{9,10},{10,... | collective-permute-start | bytes 1966088 | tf_op jit(solution)/shard_map/ppermute | solution.py:825
  88.3 34.4 %collective-permute-start.10 = (bf16[128,1024]{1,0:T(8,128)(2,1)}, bf16[128,1024]{1,0:T(8,128)(2,1)S(1)}, u32[]{:S(2)}, u32[]{:S(2)}) collective-permute-start(bf16[128,1024]{1,0:T(8,128)(2,1)} %get-tuple-element.111.refs_6_.refs_10_), channel_id=1, source_target_pairs={{0,2},{1,3},{2,0},{3,1},{4,6},{5,7},{6,4},{7,5},{8,10},{9,11},{10,... | collective-permute-start | bytes 786440 | tf_op jit(solution)/shard_map/ppermute | solution.py:825
  105.0 17.6 %collective-permute-start.9 = (bf16[128,1024]{1,0:T(8,128)(2,1)}, bf16[128,1024]{1,0:T(8,128)(2,1)S(1)}, u32[]{:S(2)}, u32[]{:S(2)}) collective-permute-start(bf16[128,1024]{1,0:T(8,128)(2,1)} %get-tuple-element.113.refs_9_), channel_id=1, source_target_pairs={{0,1},{1,0},{2,3},{3,2},{4,5},{5,4},{6,7},{7,6},{8,9},{9,8},{10,11... | collective-permute-start | bytes 786440 | tf_op jit(solution)/shard_map/ppermute | solution.py:825
  106.0 18.3 %collective-permute-start.11 = (bf16[128,1024]{1,0:T(8,128)(2,1)S(1)}, bf16[128,1024]{1,0:T(8,128)(2,1)S(1)}, u32[]{:S(2)}, u32[]{:S(2)}) collective-permute-start(bf16[128,1024]{1,0:T(8,128)(2,1)S(1)} %copy-done.45), channel_id=1, source_target_pairs={{0,3},{1,2},{2,1},{3,0},{4,7},{5,6},{6,5},{7,4},{8,11},{9,10},{10,... | collective-permute-start | bytes 786440 | tf_op jit(solution)/shard_map/ppermute | solution.py:825
  130.6 29.0 %collective-permute-start.16 = (bf16[320,1024]{1,0:T(8,128)(2,1)}, bf16[320,1024]{1,0:T(8,128)(2,1)S(1)}, u32[]{:S(2)}, u32[]{:S(2)}) collective-permute-start(bf16[320,1024]{1,0:T(8,128)(2,1)} %get-tuple-element.124), channel_id=1, source_target_pairs={{0,2},{1,3},{2,0},{3,1},{4,6},{5,7},{6,4},{7,5},{8,10},{9,11},{10,... | collective-permute-start | bytes 1966088 | tf_op jit(solution)/shard_map/ppermute | solution.py:825
  156.4 31.4 %collective-permute-start.15 = (bf16[320,1024]{1,0:T(8,128)(2,1)}, bf16[320,1024]{1,0:T(8,128)(2,1)S(1)}, u32[]{:S(2)}, u32[]{:S(2)}) collective-permute-start(bf16[320,1024]{1,0:T(8,128)(2,1)} %get-tuple-element.123), channel_id=1, source_target_pairs={{0,1},{1,0},{2,3},{3,2},{4,5},{5,4},{6,7},{7,6},{8,9},{9,8},{10,11... | collective-permute-start | bytes 1966088 | tf_op jit(solution)/shard_map/ppermute | solution.py:825
  158.4 52.3 %collective-permute-start.14 = (bf16[320,1024]{1,0:T(8,128)(2,1)}, bf16[320,1024]{1,0:T(8,128)(2,1)S(1)}, u32[]{:S(2)}, u32[]{:S(2)}) collective-permute-start(bf16[320,1024]{1,0:T(8,128)(2,1)} %get-tuple-element.122), channel_id=1, source_target_pairs={{0,3},{1,2},{2,1},{3,0},{4,7},{5,6},{6,5},{7,4},{8,11},{9,10},{10,... | collective-permute-start | bytes 1966088 | tf_op jit(solution)/shard_map/ppermute | solution.py:825
  182.6 55.5 %collective-permute-start.17 = (bf16[320,1024]{1,0:T(8,128)(2,1)}, bf16[320,1024]{1,0:T(8,128)(2,1)S(1)}, u32[]{:S(2)}, u32[]{:S(2)}) collective-permute-start(bf16[320,1024]{1,0:T(8,128)(2,1)} %get-tuple-element.148), channel_id=1, source_target_pairs={{0,2},{1,3},{2,0},{3,1},{4,6},{5,7},{6,4},{7,5},{8,10},{9,11},{10,... | collective-permute-start | bytes 1966088 | tf_op jit(solution)/shard_map/ppermute | solution.py:825
  233.8 32.1 %collective-permute-start.22 = (bf16[320,1024]{1,0:T(8,128)(2,1)}, bf16[320,1024]{1,0:T(8,128)(2,1)S(1)}, u32[]{:S(2)}, u32[]{:S(2)}) collective-permute-start(bf16[320,1024]{1,0:T(8,128)(2,1)} %get-tuple-element.156), channel_id=1, source_target_pairs={{0,3},{1,2},{2,1},{3,0},{4,7},{5,6},{6,5},{7,4},{8,11},{9,10},{10,... | collective-permute-start | bytes 1966088 | tf_op jit(solution)/shard_map/ppermute | solution.py:825
  234.7 32.2 %collective-permute-start.21 = (bf16[320,1024]{1,0:T(8,128)(2,1)S(1)}, bf16[320,1024]{1,0:T(8,128)(2,1)S(1)}, u32[]{:S(2)}, u32[]{:S(2)}) collective-permute-start(bf16[320,1024]{1,0:T(8,128)(2,1)S(1)} %copy-done.39), channel_id=1, source_target_pairs={{0,1},{1,0},{2,3},{3,2},{4,5},{5,4},{6,7},{7,6},{8,9},{9,8},{10,11... | collective-permute-start | bytes 1966088 | tf_op jit(solution)/shard_map/ppermute | solution.py:825
  276.5 36.6 %copy-start.36 = (bf16[320,1024]{1,0:T(8,128)(2,1)S(1)}, bf16[320,1024]{1,0:T(8,128)(2,1)}, u32[]{:S(2)}) copy-start(bf16[320,1024]{1,0:T(8,128)(2,1)} %get-tuple-element.150) | copy-start | bytes 1966084
  299.4 13.7 %collective-permute-start.26 = (bf16[4,2,128,2816]{3,2,1,0:T(8,128)(2,1)}, bf16[4,2,128,2816]{3,2,1,0:T(8,128)(2,1)S(1)}, u32[]{:S(2)}, u32[]{:S(2)}) collective-permute-start(bf16[4,2,128,2816]{3,2,1,0:T(8,128)(2,1)} %get-tuple-element.168), channel_id=1, source_target_pairs={{0,4},{4,0},{8,12},{12,8},{16,20},{20,16},{24,28},{28,24},{1,5},{5... | collective-permute-start | bytes 17301512 | tf_op jit(solution)/shard_map/ppermute | solution.py:819
  299.4 74.0 %collective-permute-start.28 = (bf16[4,352,1024]{2,1,0:T(8,128)(2,1)}, bf16[4,352,1024]{2,1,0:T(8,128)(2,1)}, u32[]{:S(2)}, u32[]{:S(2)}) collective-permute-start(bf16[4,352,1024]{2,1,0:T(8,128)(2,1)} %get-tuple-element.158.refs_10_), channel_id=1, source_target_pairs={{0,4},{4,0},{8,12},{12,8},{16,20},{20,16},{24,28},{28,24},{1,5},{5... | collective-permute-start | bytes 8650760 | tf_op jit(solution)/shard_map/ppermute | solution.py:819
  299.9 30.5 %collective-permute-start.25 = (bf16[128,1024]{1,0:T(8,128)(2,1)}, bf16[128,1024]{1,0:T(8,128)(2,1)S(1)}, u32[]{:S(2)}, u32[]{:S(2)}) collective-permute-start(bf16[128,1024]{1,0:T(8,128)(2,1)} %get-tuple-element.162.refs_5_), channel_id=1, source_target_pairs={{0,3},{1,2},{2,1},{3,0},{4,7},{5,6},{6,5},{7,4},{8,11},{9,10},{10,... | collective-permute-start | bytes 786440 | tf_op jit(solution)/shard_map/ppermute | solution.py:825
  301.0 27.2 %collective-permute-start.23 = (bf16[128,1024]{1,0:T(8,128)(2,1)S(1)}, bf16[128,1024]{1,0:T(8,128)(2,1)S(1)}, u32[]{:S(2)}, u32[]{:S(2)}) collective-permute-start(bf16[128,1024]{1,0:T(8,128)(2,1)S(1)} %copy-done.51), channel_id=1, source_target_pairs={{0,1},{1,0},{2,3},{3,2},{4,5},{5,4},{6,7},{7,6},{8,9},{9,8},{10,11... | collective-permute-start | bytes 786440 | tf_op jit(solution)/shard_map/ppermute | solution.py:825
  303.4 27.0 %collective-permute-start.24 = (bf16[128,1024]{1,0:T(8,128)(2,1)}, bf16[128,1024]{1,0:T(8,128)(2,1)}, u32[]{:S(2)}, u32[]{:S(2)}) collective-permute-start(bf16[128,1024]{1,0:T(8,128)(2,1)} %get-tuple-element.161), channel_id=1, source_target_pairs={{0,2},{1,3},{2,0},{3,1},{4,6},{5,7},{6,4},{7,5},{8,10},{9,11},{10,... | collective-permute-start | bytes 786440 | tf_op jit(solution)/shard_map/ppermute | solution.py:825
  313.1 38.9 %collective-permute-start.18 = (bf16[320,1024]{1,0:T(8,128)(2,1)S(1)}, bf16[320,1024]{1,0:T(8,128)(2,1)S(1)}, u32[]{:S(2)}, u32[]{:S(2)}) collective-permute-start(bf16[320,1024]{1,0:T(8,128)(2,1)S(1)} %copy-done.36), channel_id=1, source_target_pairs={{0,1},{1,0},{2,3},{3,2},{4,5},{5,4},{6,7},{7,6},{8,9},{9,8},{10,11... | collective-permute-start | bytes 1966088 | tf_op jit(solution)/shard_map/ppermute | solution.py:825
  322.9 70.7 %all-to-all-start = ((bf16[4,2,128,2816]{3,2,1,0:T(8,128)(2,1)}), bf16[4,2,128,2816]{3,2,1,0:T(8,128)(2,1)}, u32[]{:S(2)}, u32[]{:S(2)}) async-start(bf16[4,2,128,2816]{3,2,1,0:T(8,128)(2,1)} %pair_sum.2.refs_16_), calls=%async_computation | async-start | bytes 11534336 | tf_op jit(solution)/shard_map/all_to_all | solution.py:831
  328.2 30.5 %collective-permute-start.19 = (bf16[320,1024]{1,0:T(8,128)(2,1)S(1)}, bf16[320,1024]{1,0:T(8,128)(2,1)S(1)}, u32[]{:S(2)}, u32[]{:S(2)}) collective-permute-start(bf16[320,1024]{1,0:T(8,128)(2,1)S(1)} %copy-done.35), channel_id=1, source_target_pairs={{0,2},{1,3},{2,0},{3,1},{4,6},{5,7},{6,4},{7,5},{8,10},{9,11},{10,... | collective-permute-start | bytes 1966088 | tf_op jit(solution)/shard_map/ppermute | solution.py:825
  372.2 15.2 %collective-permute-start.27 = (bf16[4,128,2560]{2,1,0:T(8,128)(2,1)}, bf16[4,128,2560]{2,1,0:T(8,128)(2,1)S(1)}, u32[]{:S(2)}, u32[]{:S(2)}) collective-permute-start(bf16[4,128,2560]{2,1,0:T(8,128)(2,1)} %get-tuple-element.173.refs_6_), channel_id=1, source_target_pairs={{0,4},{4,0},{8,12},{12,8},{16,20},{20,16},{24,28},{28,24},{1,5},{5... | collective-permute-start | bytes 7864328 | tf_op jit(solution)/shard_map/ppermute | solution.py:819
  372.4 50.2 %collective-permute-start.20 = (bf16[320,1024]{1,0:T(8,128)(2,1)}, bf16[320,1024]{1,0:T(8,128)(2,1)}, u32[]{:S(2)}, u32[]{:S(2)}) collective-permute-start(bf16[320,1024]{1,0:T(8,128)(2,1)} %get-tuple-element.152), channel_id=1, source_target_pairs={{0,3},{1,2},{2,1},{3,0},{4,7},{5,6},{6,5},{7,4},{8,11},{9,10},{10,... | collective-permute-start | bytes 1966088 | tf_op jit(solution)/shard_map/ppermute | solution.py:825
  393.7 34.7 %all-to-all-start.1 = ((bf16[4,128,2560]{2,1,0:T(8,128)(2,1)}), bf16[4,128,2560]{2,1,0:T(8,128)(2,1)S(1)}, u32[]{:S(2)}, u32[]{:S(2)}) async-start(bf16[4,128,2560]{2,1,0:T(8,128)(2,1)} %add_convert_fusion.refs_17_), calls=%async_computation.1 | async-start | bytes 5242880 | tf_op jit(solution)/shard_map/all_to_all | solution.py:831
  439.2 4.0 collective-permute-start.29
  446.4 26.2 %all-to-all-start.2 = ((bf16[4,128,1792]{2,1,0:T(8,128)(2,1)}), bf16[4,128,1792]{2,1,0:T(8,128)(2,1)S(1)}, u32[]{:S(2)}, u32[]{:S(2)}) async-start(bf16[4,128,1792]{2,1,0:T(8,128)(2,1)} %add_convert_fusion.1.refs_7_), calls=%async_computation.2 | async-start | bytes 3670016 | tf_op jit(solution)/shard_map/all_to_all | solution.py:831
  461.0 2.9 collective-permute-start.30
  478.4 29.2 %collective-permute-start.31 = (bf16[512,1024]{1,0:T(8,128)(2,1)}, bf16[512,1024]{1,0:T(8,128)(2,1)}, u32[]{:S(2)}, u32[]{:S(2)}) collective-permute-start(bf16[512,1024]{1,0:T(8,128)(2,1)} %get-tuple-element.187.refs_7_), channel_id=1, source_target_pairs={{8,0},{12,4},{16,8},{20,12},{24,16},{28,20},{9,1},{13,5},{17,9},{2... | collective-permute-start | bytes 3145736 | tf_op jit(solution)/shard_map/ppermute | solution.py:815
  482.4 54.3 %all-to-all-start.3 = ((bf16[4,352,1024]{2,1,0:T(8,128)(2,1)}), bf16[4,352,1024]{2,1,0:T(8,128)(2,1)S(1)}, u32[]{:S(2)}, u32[]{:S(2)}) async-start(bf16[4,352,1024]{2,1,0:T(8,128)(2,1)} %get-tuple-element.199), calls=%async_computation.3 | async-start | bytes 5767168 | tf_op jit(solution)/shard_map/all_to_all | solution.py:831
  489.2 9.3 %collective-permute-start.32 = (bf16[32,2560]{1,0:T(8,128)(2,1)}, bf16[32,2560]{1,0:T(8,128)(2,1)S(1)}, u32[]{:S(2)}, u32[]{:S(2)}) collective-permute-start(bf16[32,2560]{1,0:T(8,128)(2,1)} %get-tuple-element.191), channel_id=1, source_target_pairs={{0,1},{1,0},{2,3},{3,2},{4,5},{5,4},{6,7},{7,6},{8,9},{9,8},{10,11... | collective-permute-start | bytes 491528 | tf_op jit(solution)/shard_map/ppermute | solution.py:825
  490.7 11.7 %collective-permute-start.33 = (bf16[32,2560]{1,0:T(8,128)(2,1)}, bf16[32,2560]{1,0:T(8,128)(2,1)S(1)}, u32[]{:S(2)}, u32[]{:S(2)}) collective-permute-start(bf16[32,2560]{1,0:T(8,128)(2,1)} %get-tuple-element.192), channel_id=1, source_target_pairs={{0,2},{1,3},{2,0},{3,1},{4,6},{5,7},{6,4},{7,5},{8,10},{9,11},{10,... | collective-permute-start | bytes 491528 | tf_op jit(solution)/shard_map/ppermute | solution.py:825
  491.7 14.0 %collective-permute-start.34 = (bf16[32,2560]{1,0:T(8,128)(2,1)}, bf16[32,2560]{1,0:T(8,128)(2,1)S(1)}, u32[]{:S(2)}, u32[]{:S(2)}) collective-permute-start(bf16[32,2560]{1,0:T(8,128)(2,1)} %get-tuple-element.193), channel_id=1, source_target_pairs={{0,3},{1,2},{2,1},{3,0},{4,7},{5,6},{6,5},{7,4},{8,11},{9,10},{10,... | collective-permute-start | bytes 491528 | tf_op jit(solution)/shard_map/ppermute | solution.py:825
  513.3 25.0 %collective-permute-start.35 = (bf16[192,1024]{1,0:T(8,128)(2,1)}, bf16[192,1024]{1,0:T(8,128)(2,1)S(1)}, u32[]{:S(2)}, u32[]{:S(2)}) collective-permute-start(bf16[192,1024]{1,0:T(8,128)(2,1)} %get-tuple-element.195), channel_id=1, source_target_pairs={{0,1},{1,0},{2,3},{3,2},{4,5},{5,4},{6,7},{7,6},{8,9},{9,8},{10,11... | collective-permute-start | bytes 1179656 | tf_op jit(solution)/shard_map/ppermute | solution.py:825
  514.8 27.8 %collective-permute-start.36 = (bf16[192,1024]{1,0:T(8,128)(2,1)}, bf16[192,1024]{1,0:T(8,128)(2,1)}, u32[]{:S(2)}, u32[]{:S(2)}) collective-permute-start(bf16[192,1024]{1,0:T(8,128)(2,1)} %get-tuple-element.196), channel_id=1, source_target_pairs={{0,2},{1,3},{2,0},{3,1},{4,6},{5,7},{6,4},{7,5},{8,10},{9,11},{10,... | collective-permute-start | bytes 1179656 | tf_op jit(solution)/shard_map/ppermute | solution.py:825
  515.8 32.8 %collective-permute-start.37 = (bf16[192,1024]{1,0:T(8,128)(2,1)}, bf16[192,1024]{1,0:T(8,128)(2,1)}, u32[]{:S(2)}, u32[]{:S(2)}) collective-permute-start(bf16[192,1024]{1,0:T(8,128)(2,1)} %get-tuple-element.197), channel_id=1, source_target_pairs={{0,3},{1,2},{2,1},{3,0},{4,7},{5,6},{6,5},{7,4},{8,11},{9,10},{10,... | collective-permute-start | bytes 1179656 | tf_op jit(solution)/shard_map/ppermute | solution.py:825
  (49 other events, 349.3 us)
